TPU v7x, 32 devices: a whole 2x2x4 slice. The times are simulated.
32 devices in a mesh: gx: 4 (over z), gy: 2 (over y), gz: 4 (over x, core).
Axes of the slice: x: 2, y: 2, z: 4, core: 2. Of those that a mesh axis runs over, the one named last changes fastest.
Arguments:
- snapshot: float32 [512, 320, 512], P('gx', 'gy', 'gz'), may hold values from -40 to 40
Outputs:
- basis: float32 [512, 128], P('gx')
- core: float32 [128, 320, 512], P('gx', 'gy', 'gz')
All inputs are finite; a program needn't handle non-finite values.
Results may differ from a plain program's by a relative error of at most 0.0002.
Values sent between devices are 32-bit elements; how exact they have to be, the bound alone decides.
No kernel may reach another device: no remote copies, remote signals or barrier semaphores. Data moves between devices by JAX's collectives and lax.ppermute only.
A program may use at most 64 MiB of HBM per device.

v0:
```python
import jax
import jax.numpy as jnp
from jax import lax
from jax.sharding import PartitionSpec as P

RANK = 128
ITERS = 2


def product(left, right):
    return jnp.dot(left, right, precision=lax.Precision.HIGHEST, preferred_element_type=jnp.float32)


def orthonormal(matrix):
    lower = jnp.linalg.cholesky(product(matrix.T, matrix))
    return jax.scipy.linalg.solve_triangular(lower, matrix.T, lower=True).T


def local(snapshot):
    xlocal, ylocal, zlocal = snapshot.shape
    flat = snapshot.reshape(xlocal, ylocal * zlocal)
    fibres = lax.all_to_all(flat, "gx", split_axis=1, concat_axis=0, tiled=True)
    gram = product(fibres, fibres.T)
    factor = jnp.linalg.cholesky(lax.psum(gram, ("gx", "gy", "gz")))
    basis = orthonormal(factor[:, :RANK])
    for step in range(ITERS):
        basis = orthonormal(product(factor, product(factor.T, basis)))
    groups = lax.axis_size("gx")
    own_rows = basis.shape[0] // groups
    mine = lax.dynamic_slice_in_dim(basis, lax.axis_index("gx") * own_rows, own_rows, 0)
    projected = product(basis.T, fibres)
    returned = lax.all_to_all(projected, "gx", split_axis=0, concat_axis=1, tiled=True)
    return (mine, returned.reshape(RANK // groups, ylocal, zlocal))


def solution(mesh):
    in_specs = (P("gx", "gy", "gz"),)
    out_specs = (P("gx", None), P("gx", "gy", "gz"))
    return jax.shard_map(local, mesh=mesh, in_specs=in_specs, out_specs=out_specs, check_vma=False)
```

profile of v0, /device:TPU:0, one launch (start us, length us, event | category | flops | bytes accessed | tf_op | source)
XLA Modules:
  0.0 667.9 jit_solution(7144745280773873583)
XLA Ops:
  7.2 12.6 %all_to_all.24 = f32[128,4,5120]{2,1,0:T(4,128)} reshape(f32[128,160,128]{2,1,0:T(8,128)} %param.4) | data formatting | bytes 20971520 | tf_op jit(solution)/shard_map/all_to_all | solution.py:22
  19.8 10.0 %copy.10 = f32[128,4,5120]{2,0,1:T(8,128)S(1)} copy(f32[128,4,5120]{2,1,0:T(4,128)} %all_to_all.24) | data formatting | bytes 20971520 | tf_op jit(solution)/shard_map/all_to_all | solution.py:22
  29.8 234.5 %all_to_all.32 = f32[128,4,5120]{2,0,1:T(8,128)S(1)} all-to-all(f32[128,4,5120]{2,0,1:T(8,128)S(1)} %copy.10), channel_id=1, replica_groups=mesh['gx'=4,'gy'=2,'gz'=4] {'gx'}, dimensions={1} | all-to-all | bytes 20971520 | tf_op jit(solution)/shard_map/all_to_all | solution.py:22
  264.4 4.0 copy-done
  268.4 18.4 %fusion.48 = f32[512,512]{0,1:T(8,128)} fusion(f32[512,5120]{1,0:T(8,128)S(1)} %bitcast.83), kind=kOutput, calls=%fused_computation.77 | convolution fusion | flops 16106127360 | bytes 11534336 | tf_op jit(solution)/shard_map/dot_general | solution.py:11
  286.8 129.7 %all-reduce.3.cloned.1.call-done = f32[512,512]{0,1:T(8,128)} async-done(((f32[512,512]{0,1:T(8,128)}), f32[512,512]{0,1:T(8,128)}) %all-reduce.3.cloned.1.call-update) | async-done | bytes 1048592 | tf_op jit(solution)/shard_map/psum | solution.py:24
  416.6 1.6 copy.12
  418.1 1.4 fusion
  419.6 11.7 %cholesky.120 = f32[128,128]{1,0:T(8,128)S(1)} custom-call(f32[128,128]{1,0:T(8,128)S(1)} %cholesky.356), custom_call_target="Cholesky" | custom-call | tf_op jit(solution)/shard_map/jit(cholesky)/cholesky | solution.py:24
  431.4 9.8 %custom-call.32 = f32[1,128,128]{1,2,0:T(8,128)S(1)} custom-call(f32[1,128,128]{2,1,0:T(8,128)S(1)} %get-tuple-element.17), custom_call_target="InvertDiagBlocksLowerTriangular" | custom-call | tf_op jit(solution)/shard_map/jit(cholesky)/cholesky | solution.py:24
  442.0 11.7 %cholesky.244 = f32[128,128]{1,0:T(8,128)S(1)} custom-call(f32[128,128]{1,0:T(8,128)S(1)} %cholesky.360), custom_call_target="Cholesky" | custom-call | tf_op jit(solution)/shard_map/jit(cholesky)/cholesky | solution.py:24
  453.7 10.0 %custom-call.33 = f32[1,128,128]{1,2,0:T(8,128)S(1)} custom-call(f32[1,128,128]{2,1,0:T(8,128)S(1)} %get-tuple-element.14), custom_call_target="InvertDiagBlocksLowerTriangular" | custom-call | tf_op jit(solution)/shard_map/jit(cholesky)/cholesky | solution.py:24
  464.4 11.7 %cholesky.265 = f32[128,128]{1,0:T(8,128)S(1)} custom-call(f32[128,128]{1,0:T(8,128)S(1)} %cholesky.365), custom_call_target="Cholesky" | custom-call | tf_op jit(solution)/shard_map/jit(cholesky)/cholesky | solution.py:24
  476.8 9.8 %custom-call.34 = f32[1,128,128]{1,2,0:T(8,128)S(1)} custom-call(f32[1,128,128]{2,1,0:T(8,128)S(1)} %get-tuple-element.11), custom_call_target="InvertDiagBlocksLowerTriangular" | custom-call | tf_op jit(solution)/shard_map/jit(cholesky)/cholesky | solution.py:24
  487.2 11.7 %cholesky.282 = f32[128,128]{1,0:T(8,128)S(1)} custom-call(f32[128,128]{1,0:T(8,128)S(1)} %convolution_subtract_fusion.2), custom_call_target="Cholesky" | custom-call | tf_op jit(solution)/shard_map/jit(cholesky)/cholesky | solution.py:24
  502.9 0.8 fusion.9
  503.8 11.7 %cholesky.325 = f32[128,128]{1,0:T(8,128)S(1)} custom-call(f32[128,128]{1,0:T(8,128)S(1)} %fusion.26), custom_call_target="Cholesky" | custom-call | tf_op jit(solution)/shard_map/jit(cholesky)/cholesky | solution.py:15
  516.8 9.8 %custom-call.37 = f32[1,128,128]{1,2,0:T(8,128)S(1)} custom-call(f32[1,128,128]{2,1,0:T(8,128)S(1)} %fusion.16), custom_call_target="InvertDiagBlocksLowerTriangular" | custom-call | tf_op jit(solution)/shard_map/jit(_solve_triangular)/triangular_solve | solution.py:16
  527.1 1.8 fusion.49
  528.9 1.0 fusion.50
  530.6 12.1 %cholesky.336 = f32[128,128]{1,0:T(8,128)S(1)} custom-call(f32[128,128]{1,0:T(8,128)S(1)} %fusion.24), custom_call_target="Cholesky" | custom-call | tf_op jit(solution)/shard_map/jit(cholesky)/cholesky | solution.py:15
  544.1 9.8 %custom-call.38 = f32[1,128,128]{1,2,0:T(8,128)S(1)} custom-call(f32[1,128,128]{2,1,0:T(8,128)S(1)} %fusion.17), custom_call_target="InvertDiagBlocksLowerTriangular" | custom-call | tf_op jit(solution)/shard_map/jit(_solve_triangular)/triangular_solve | solution.py:16
  554.3 1.8 fusion.52
  556.1 1.0 fusion.53
  557.8 11.7 %cholesky.347 = f32[128,128]{1,0:T(8,128)S(1)} custom-call(f32[128,128]{1,0:T(8,128)S(1)} %fusion.22), custom_call_target="Cholesky" | custom-call | tf_op jit(solution)/shard_map/jit(cholesky)/cholesky | solution.py:15
  570.9 10.0 %custom-call.39 = f32[1,128,128]{1,2,0:T(8,128)S(1)} custom-call(f32[1,128,128]{2,1,0:T(8,128)S(1)} %fusion.18), custom_call_target="InvertDiagBlocksLowerTriangular" | custom-call | tf_op jit(solution)/shard_map/jit(_solve_triangular)/triangular_solve | solution.py:16
  581.3 9.8 %fusion.55 = f32[4,32,5120]{2,1,0:T(8,128)} fusion(f32[4,32,512]{2,1,0:T(8,128)S(1)} %bitcast.86, f32[512,5120,1]{1,0,2:T(8,128)} %bitcast.84), kind=kOutput, calls=%fused_computation.84 | convolution fusion | flops 4026531840 | bytes 13369344 | tf_op jit(solution)/shard_map/dot_general | solution.py:11
  591.1 3.7 all-to-all-start.1
  594.8 0.7 copy.17
  595.5 58.1 %all-to-all-done.1 = f32[4,32,5120]{2,1,0:T(8,128)S(1)} async-done(((f32[4,32,5120]{2,1,0:T(8,128)}), f32[4,32,5120]{2,1,0:T(8,128)S(1)}, u32[]{:S(2)}, u32[]{:S(2)}) %all-to-all-start.1) | async-done | bytes 2621472 | tf_op jit(solution)/shard_map/all_to_all | solution.py:32
  653.6 3.2 copy.16
  656.8 4.0 reshape.52
  (42 shorter events, 11.1 us)
Async XLA Ops:
  7.2 409.4 %all-reduce.3.cloned.1.call-start = ((), (), s32[]{:S(2)}) async-start(), calls=%async_computation.2 | async-start | bytes 2097152 | tf_op jit(solution)/shard_map/psum | solution.py:24
  264.4 4.0 copy-start
  591.1 62.5 %all-to-all-start.1 = ((f32[4,32,5120]{2,1,0:T(8,128)}), f32[4,32,5120]{2,1,0:T(8,128)S(1)}, u32[]{:S(2)}, u32[]{:S(2)}) async-start(f32[4,32,5120]{2,1,0:T(8,128)} %fusion.55), calls=%async_computation.1 | async-start | bytes 5242880 | tf_op jit(solution)/shard_map/all_to_all | solution.py:32
Sparse Core Ops, SparseCore 0:
  287.0 129.5 all-reduce.2
where the time goes:
time: 674 us; the launch traced here: 668 us
  blocking collectives  235 us (35%)
  waiting for transfers between devices  188 us (28%)
  other arithmetic  149 us (22%)
  matrix products  39 us (6%)
  local copies, waits for them, and re-layouts  36.6 us (5%)
  between operations  17 us (3%)
    all_to_all x1, blocking collectives, local(): fibres = lax.all_to_all(flat, 'gx', split_axis=1, concat_axis=0, tiled=True)  235 us
    psum x1, waiting for transfers between devices, local(): factor = jnp.linalg.cholesky(lax.psum(gram, ('gx', 'gy', 'gz')))  130 us
    another operation x14, other arithmetic, local(): factor = jnp.linalg.cholesky(lax.psum(gram, ('gx', 'gy', 'gz')))  78.5 us
    all_to_all x1, waiting for transfers between devices, local(): lax.all_to_all(projected, 'gx', split_axis=0, concat_axis=1, tiled=True)  58.1 us
    another operation x9, other arithmetic, orthonormal(): lower = jnp.linalg.cholesky(product(matrix.T, matrix))  37.6 us
    dot_general x9, matrix products, product(): jnp.dot(left, right, precision=lax.Precision.HIGHEST, preferred_element_t...  35.9 us
    another operation x6, other arithmetic, orthonormal(): return jax.scipy.linalg.solve_triangular(lower, matrix.T, lower=True).T  31.5 us
    all_to_all x2, local copies, waits for them, and re-layouts, local(): fibres = lax.all_to_all(flat, 'gx', split_axis=1, concat_axis=0, tiled=True)  22.6 us
  transfers between devices with their start and end apart: 2, of which 2 were waited for; matrix products, arithmetic and copies ran while one was open for 0% of the time, Pallas kernels for 0%

commit v1 on v0

v1 whole, which is shorter than its diff:
```python
import functools

import jax
import jax.numpy as jnp
from jax import lax
from jax.experimental import pallas as pl
from jax.experimental.pallas import tpu as pltpu
from jax.sharding import PartitionSpec as P

RANK = 128
ITERS = 2
BLOCK = 128
AXES = ("gx", "gy", "gz")


def product(left, right):
    return jnp.dot(left, right, precision=lax.Precision.HIGHEST, preferred_element_type=jnp.float32)


def split(value):
    high = value.astype(jnp.bfloat16)
    low = (value - high.astype(jnp.float32)).astype(jnp.bfloat16)
    return high, low


def dot_t(left, right):
    return lax.dot_general(left, right, (((1,), (1,)), ((), ())), preferred_element_type=jnp.float32)


def dot_n(left, right):
    return lax.dot_general(left, right, (((1,), (0,)), ((), ())), preferred_element_type=jnp.float32)


def gram_kernel(first, groups, steps, xlocal, zlocal, *refs):
    if first:
        rows_ref, out_ref, high_ref, low_ref = refs
        old_ref = None
    else:
        rows_ref, old_ref, out_ref, high_ref, low_ref = refs
    for group in range(groups):
        for step in range(steps):
            high, low = split(rows_ref[group, step])
            at = (slice(group * xlocal, (group + 1) * xlocal), slice(step * zlocal, (step + 1) * zlocal))
            high_ref[at] = high
            low_ref[at] = low
    count = groups * xlocal // BLOCK
    slot = 0
    for row in range(count):
        mine = slice(row * BLOCK, (row + 1) * BLOCK)
        upto = slice(0, (row + 1) * BLOCK)
        total = dot_t(high_ref[mine, :], high_ref[upto, :])
        total += dot_t(high_ref[mine, :], low_ref[upto, :])
        total += dot_t(low_ref[mine, :], high_ref[upto, :])
        for column in range(row + 1):
            block = total[:, column * BLOCK : (column + 1) * BLOCK]
            out_ref[slot] = block if old_ref is None else block + old_ref[slot]
            slot += 1


def gram_step(rows, old):
    groups, steps, xlocal, zlocal = rows.shape
    order = groups * xlocal
    count = order // BLOCK
    slots = count * (count + 1) // 2
    first = old is None
    vmem = pl.BlockSpec(memory_space=pltpu.VMEM)
    half = jax.ShapeDtypeStruct((order, steps * zlocal), jnp.bfloat16)
    operands = (rows,) if first else (rows, old)
    return pl.pallas_call(
        functools.partial(gram_kernel, first, groups, steps, xlocal, zlocal),
        out_shape=(jax.ShapeDtypeStruct((slots, BLOCK, BLOCK), jnp.float32), half, half),
        in_specs=[vmem] * len(operands),
        out_specs=(vmem, vmem, vmem),
        input_output_aliases={} if first else {1: 0},
        compiler_params=pltpu.CompilerParams(vmem_limit_bytes=48 * 2**20),
        cost_estimate=pl.CostEstimate(flops=6 * order * order * steps * zlocal, bytes_accessed=rows.size * 8, transcendentals=0),
    )(*operands)


def core_kernel(steps, zlocal, turned_ref, high_ref, low_ref, out_ref):
    high, low = split(turned_ref[...])
    total = dot_n(high, high_ref[...]) + dot_n(high, low_ref[...]) + dot_n(low, high_ref[...])
    for step in range(steps):
        out_ref[:, step, :] = total[:, step * zlocal : (step + 1) * zlocal]


def core_step(turned, high, low, zlocal):
    steps = high.shape[1] // zlocal
    vmem = pl.BlockSpec(memory_space=pltpu.VMEM)
    return pl.pallas_call(
        functools.partial(core_kernel, steps, zlocal),
        out_shape=jax.ShapeDtypeStruct((turned.shape[0], steps, zlocal), jnp.float32),
        in_specs=[vmem] * 3,
        out_specs=vmem,
        compiler_params=pltpu.CompilerParams(vmem_limit_bytes=48 * 2**20),
        cost_estimate=pl.CostEstimate(flops=6 * turned.size * steps * zlocal, bytes_accessed=high.size * 6, transcendentals=0),
    )(turned, high, low)


def total_sum(blocks):
    devices = lax.axis_size(AXES)
    shape = blocks.shape
    flat = blocks.reshape(-1, BLOCK)
    rows = flat.shape[0]
    share = -(-rows // devices)
    flat = jnp.pad(flat, ((0, share * devices - rows), (0, 0)))
    parts = lax.all_to_all(flat.reshape(devices, share, BLOCK), AXES, split_axis=0, concat_axis=0, tiled=True)
    mine = jnp.sum(parts, axis=0)
    spread = jnp.broadcast_to(mine[None], (devices, share, BLOCK))
    whole = lax.all_to_all(spread, AXES, split_axis=0, concat_axis=0, tiled=True)
    return whole.reshape(-1, BLOCK)[:rows].reshape(shape)


def orthonormal(matrix):
    lower = jnp.linalg.cholesky(product(matrix.T, matrix))
    return jax.scipy.linalg.solve_triangular(lower, matrix.T, lower=True).T


def assemble(blocks, count):
    rows = []
    for row in range(count):
        line = []
        for column in range(count):
            high, low = max(row, column), min(row, column)
            block = blocks[high * (high + 1) // 2 + low]
            line.append(block if row >= column else block.T)
        rows.append(jnp.concatenate(line, axis=1))
    return jnp.concatenate(rows, axis=0)


def chunk_count(per):
    return max(k for k in range(1, 6) if per % k == 0)


def local(snapshot):
    xlocal, ylocal, zlocal = snapshot.shape
    groups = lax.axis_size("gx")
    order = groups * xlocal
    chunks = chunk_count(ylocal // groups)
    wide = ylocal // chunks
    steps = wide // groups
    halves = []
    total = None
    for chunk in range(chunks):
        piece = jnp.transpose(snapshot[:, chunk * wide : (chunk + 1) * wide, :], (1, 0, 2))
        rows = lax.all_to_all(piece, "gx", split_axis=0, concat_axis=0, tiled=True)
        total, high, low = gram_step(rows.reshape(groups, steps, xlocal, zlocal), total)
        halves.append((high, low))
    gram = assemble(total_sum(total), order // BLOCK)
    basis = orthonormal(gram[:, :RANK])
    for step in range(ITERS):
        basis = orthonormal(product(gram, basis))
    mine = lax.dynamic_slice_in_dim(basis, lax.axis_index("gx") * xlocal, xlocal, 0)
    turned = basis.T
    keep = RANK // groups
    outs = []
    for high, low in halves:
        part = core_step(turned, high, low, zlocal).reshape(groups, keep, steps, zlocal)
        back = lax.all_to_all(part, "gx", split_axis=0, concat_axis=0, tiled=True)
        outs.append(jnp.swapaxes(back, 0, 1).reshape(keep, wide, zlocal))
    return (mine, jnp.concatenate(outs, axis=1))


def solution(mesh):
    in_specs = (P("gx", "gy", "gz"),)
    out_specs = (P("gx", None), P("gx", "gy", "gz"))
    return jax.shard_map(local, mesh=mesh, in_specs=in_specs, out_specs=out_specs, check_vma=False)
```

time: 674 us -> 521 us (0.77)
  blocking collectives: 235 us -> 42.8 us
  other arithmetic: 149 us -> 77 us
  waiting for transfers between devices: 188 us -> 251 us
  starting transfers between devices: 3.69 us -> 43.7 us
  matrix products: 39 us -> 8.41 us
  Pallas kernels: 0 us -> 27.7 us
  local copies, waits for them, and re-layouts: 36.6 us -> 61 us
  between operations: 17 us -> 1.24 us
    all_to_all x1 -> x10, waiting for transfers between devices: 58.1 us -> 251 us  [the longest x5 199 us: local(): rows = lax.all_to_all(piece, 'gx', split_axis=0, concat_axis=0, tiled=True)]
    all_to_all x1 -> x2, blocking collectives: 235 us -> 42.8 us  [the longest x1 21.5 us: total_sum(): lax.all_to_all(flat.reshape(devices, share, BLOCK), AXES, split_axis=0, c...]
    psum x1 -> x0, waiting for transfers between devices: 130 us -> none  [local(): factor = jnp.linalg.cholesky(lax.psum(gram, ('gx', 'gy', 'gz')))]
    another operation x14 -> x0, other arithmetic: 78.5 us -> none  [local(): factor = jnp.linalg.cholesky(lax.psum(gram, ('gx', 'gy', 'gz')))]
    unnamed x3 -> x49, local copies, waits for them, and re-layouts: 4.72 us -> 50.1 us
    all_to_all x1 -> x10, starting transfers between devices: 3.65 us -> 43.7 us  [the longest x5 24.3 us: local(): rows = lax.all_to_all(piece, 'gx', split_axis=0, concat_axis=0, tiled=True)]
    dot_general x9 -> x5, matrix products: 35.9 us -> 6.21 us  [product(): jnp.dot(left, right, precision=lax.Precision.HIGHEST, preferred_element_t...]
    pallas_call x0 -> x10, Pallas kernels: none -> 27.7 us  [the longest x5 19.7 us: gram_step(): pl.pallas_call(functools.partial(gram_kernel, first, groups, steps, xloca...]
  transfers between devices with their start and end apart: 2 -> 10, of which waited for: 2 -> 10; matrix products, arithmetic and copies ran while one was open for 0% -> 5% of each run, Pallas kernels for 0% -> 4%
where the time goes in v1:
time: 521 us; the launch traced here: 513 us
  waiting for transfers between devices  251 us (48%)
  other arithmetic  77 us (15%)
  local copies, waits for them, and re-layouts  61 us (12%)
  starting transfers between devices  43.7 us (8%)
  blocking collectives  42.8 us (8%)
  Pallas kernels  27.7 us (5%)
  matrix products  8.41 us (2%)
    all_to_all x5, waiting for transfers between devices, local(): rows = lax.all_to_all(piece, 'gx', split_axis=0, concat_axis=0, tiled=True)  199 us
    all_to_all x5, waiting for transfers between devices, local(): back = lax.all_to_all(part, 'gx', split_axis=0, concat_axis=0, tiled=True)  51.5 us
    unnamed x49, local copies, waits for them, and re-layouts  50.1 us
    another operation x9, other arithmetic, orthonormal(): lower = jnp.linalg.cholesky(product(matrix.T, matrix))  39 us
    another operation x6, other arithmetic, orthonormal(): return jax.scipy.linalg.solve_triangular(lower, matrix.T, lower=True).T  31.4 us
    all_to_all x5, starting transfers between devices, local(): rows = lax.all_to_all(piece, 'gx', split_axis=0, concat_axis=0, tiled=True)  24.3 us
    all_to_all x1, blocking collectives, total_sum(): lax.all_to_all(flat.reshape(devices, share, BLOCK), AXES, split_axis=0, c...  21.5 us
    all_to_all x1, blocking collectives, total_sum(): lax.all_to_all(spread, AXES, split_axis=0, concat_axis=0, tiled=True)  21.2 us
  transfers between devices with their start and end apart: 10, of which 10 were waited for; matrix products, arithmetic and copies ran while one was open for 5% of the time, Pallas kernels for 4%

profile of v1, /device:TPU:0, one launch (start us, length us, event | category | flops | bytes accessed | tf_op | source)
XLA Modules:
  0.0 512.5 jit_solution(3439335980606067298)
XLA Ops:
  0.6 7.9 %fusion.19 = (f32[128,32,128]{2,1,0:T(8,128)S(1)}, f32[128,32,128]{2,1,0:T(8,128)}, f32[128,32,128]{2,1,0:T(8,128)}, f32[128,32,128]{2,1,0:T(8,128)}, f32[128,32,128]{2,1,0:T(8,128)}) fusion(f32[128,160,128]{2,1,0:T(8,128)} %param.4), kind=kLoop, calls=%fused_computation.55 | loop fusion | bytes 20971520 | tf_op jit(solution)/shard_map/slice | solution.py:145
  11.2 6.3 %all-to-all-start.4 = ((f32[32,128,128]{2,1,0:T(8,128)}), f32[32,128,128]{2,1,0:T(8,128)S(1)}, u32[]{:S(2)}, u32[]{:S(2)}) async-start(f32[32,128,128]{2,1,0:T(8,128)} %bitcast.141), calls=%async_computation.4 | async-start | bytes 4194304 | tf_op jit(solution)/shard_map/all_to_all | solution.py:146
  17.5 4.2 copy.77
  21.7 44.0 %all-to-all-done.4 = f32[32,128,128]{2,1,0:T(8,128)S(1)} async-done(((f32[32,128,128]{2,1,0:T(8,128)}), f32[32,128,128]{2,1,0:T(8,128)S(1)}, u32[]{:S(2)}, u32[]{:S(2)}) %all-to-all-start.4) | async-done | bytes 2097184 | tf_op jit(solution)/shard_map/all_to_all | solution.py:146
  65.7 4.4 all-to-all-start.3
  74.3 43.6 %all-to-all-done.3 = f32[32,128,128]{2,1,0:T(8,128)} async-done(((f32[32,128,128]{2,1,0:T(8,128)}), f32[32,128,128]{2,1,0:T(8,128)}, u32[]{:S(2)}, u32[]{:S(2)}) %all-to-all-start.3) | async-done | bytes 2097184 | tf_op jit(solution)/shard_map/all_to_all | solution.py:146
  117.9 4.5 all-to-all-start.2
  122.4 4.2 copy.79
  126.6 43.5 %all-to-all-done.2 = f32[32,128,128]{2,1,0:T(8,128)} async-done(((f32[32,128,128]{2,1,0:T(8,128)}), f32[32,128,128]{2,1,0:T(8,128)}, u32[]{:S(2)}, u32[]{:S(2)}) %all-to-all-start.2) | async-done | bytes 2097184 | tf_op jit(solution)/shard_map/all_to_all | solution.py:146
  170.1 4.4 all-to-all-start.1
  178.7 43.6 %all-to-all-done.1 = f32[32,128,128]{2,1,0:T(8,128)} async-done(((f32[32,128,128]{2,1,0:T(8,128)}), f32[32,128,128]{2,1,0:T(8,128)}, u32[]{:S(2)}, u32[]{:S(2)}) %all-to-all-start.1) | async-done | bytes 2097184 | tf_op jit(solution)/shard_map/all_to_all | solution.py:146
  222.3 4.7 all-to-all-start
  230.6 4.3 shard_map.31
  236.9 4.3 shard_map.32
  243.1 4.3 shard_map.33
  250.2 24.5 %all-to-all-done = f32[32,128,128]{2,1,0:T(8,128)} async-done(((f32[32,128,128]{2,1,0:T(8,128)}), f32[32,128,128]{2,1,0:T(8,128)}, u32[]{:S(2)}, u32[]{:S(2)}) %all-to-all-start) | async-done | bytes 2097184 | tf_op jit(solution)/shard_map/all_to_all | solution.py:146
  275.8 4.3 shard_map.34
  280.1 21.5 %all_to_all.60 = f32[32,40,128]{2,1,0:T(8,128)} all-to-all(f32[32,40,128]{2,1,0:T(8,128)S(1)} %bitcast.136), channel_id=1, replica_groups=mesh['gx'=4,'gy'=2,'gz'=4] {'gx','gy','gz'}, dimensions={0} | all-to-all | bytes 1310720 | tf_op jit(solution)/shard_map/all_to_all | solution.py:107
  302.8 21.2 %all_to_all.61 = f32[32,40,128]{2,1,0:T(8,128)S(1)} all-to-all(f32[32,40,128]{2,1,0:T(8,128)S(1)} %broadcast_in_dim.2), channel_id=1, replica_groups=mesh['gx'=4,'gy'=2,'gz'=4] {'gx','gy','gz'}, dimensions={0} | all-to-all | bytes 1310720 | tf_op jit(solution)/shard_map/all_to_all | solution.py:110
  336.7 12.5 %cholesky.59 = f32[128,128]{1,0:T(8,128)S(1)} custom-call(f32[128,128]{1,0:T(8,128)} %fusion.14), custom_call_target="Cholesky" | custom-call | tf_op jit(solution)/shard_map/jit(cholesky)/cholesky | solution.py:115
  350.6 9.8 %custom-call.7 = f32[1,128,128]{1,2,0:T(8,128)S(1)} custom-call(f32[1,128,128]{2,1,0:T(8,128)S(1)} %fusion.6), custom_call_target="InvertDiagBlocksLowerTriangular" | custom-call | tf_op jit(solution)/shard_map/jit(_solve_triangular)/triangular_solve | solution.py:116
  364.4 12.7 %cholesky.70 = f32[128,128]{1,0:T(8,128)S(1)} custom-call(f32[128,128]{1,0:T(8,128)} %fusion.12), custom_call_target="Cholesky" | custom-call | tf_op jit(solution)/shard_map/jit(cholesky)/cholesky | solution.py:115
  378.4 9.8 %custom-call.8 = f32[1,128,128]{1,2,0:T(8,128)S(1)} custom-call(f32[1,128,128]{2,1,0:T(8,128)S(1)} %fusion.7), custom_call_target="InvertDiagBlocksLowerTriangular" | custom-call | tf_op jit(solution)/shard_map/jit(_solve_triangular)/triangular_solve | solution.py:116
  392.3 11.7 %cholesky.81 = f32[128,128]{1,0:T(8,128)S(1)} custom-call(f32[128,128]{1,0:T(8,128)S(1)} %fusion.10), custom_call_target="Cholesky" | custom-call | tf_op jit(solution)/shard_map/jit(cholesky)/cholesky | solution.py:115
  405.4 9.8 %custom-call.9 = f32[1,128,128]{1,2,0:T(8,128)S(1)} custom-call(f32[1,128,128]{2,1,0:T(8,128)S(1)} %fusion.8), custom_call_target="InvertDiagBlocksLowerTriangular" | custom-call | tf_op jit(solution)/shard_map/jit(_solve_triangular)/triangular_solve | solution.py:116
  429.0 11.0 %all-to-all-done.10 = f32[4,32,8,128]{3,2,1,0:T(8,128)} async-done(((f32[4,32,8,128]{3,2,1,0:T(8,128)}), f32[4,32,8,128]{3,2,1,0:T(8,128)}, u32[]{:S(2)}, u32[]{:S(2)}) %all-to-all-start.10) | async-done | bytes 524320 | tf_op jit(solution)/shard_map/all_to_all | solution.py:159
  440.0 4.2 all-to-all-start.9
  448.2 10.2 %all-to-all-done.9 = f32[4,32,8,128]{3,2,1,0:T(8,128)} async-done(((f32[4,32,8,128]{3,2,1,0:T(8,128)}), f32[4,32,8,128]{3,2,1,0:T(8,128)}, u32[]{:S(2)}, u32[]{:S(2)}) %all-to-all-start.9) | async-done | bytes 524320 | tf_op jit(solution)/shard_map/all_to_all | solution.py:159
  458.4 4.1 all-to-all-start.8
  465.3 11.2 %all-to-all-done.8 = f32[4,32,8,128]{3,2,1,0:T(8,128)} async-done(((f32[4,32,8,128]{3,2,1,0:T(8,128)}), f32[4,32,8,128]{3,2,1,0:T(8,128)}, u32[]{:S(2)}, u32[]{:S(2)}) %all-to-all-start.8) | async-done | bytes 524320 | tf_op jit(solution)/shard_map/all_to_all | solution.py:159
  482.4 11.6 %all-to-all-done.7 = f32[4,32,8,128]{3,2,1,0:T(8,128)S(1)} async-done(((f32[4,32,8,128]{3,2,1,0:T(8,128)}), f32[4,32,8,128]{3,2,1,0:T(8,128)S(1)}, u32[]{:S(2)}, u32[]{:S(2)}) %all-to-all-start.7) | async-done | bytes 524320 | tf_op jit(solution)/shard_map/all_to_all | solution.py:159
  504.1 7.4 %all-to-all-done.11 = f32[4,32,8,128]{3,2,1,0:T(8,128)S(1)} async-done(((f32[4,32,8,128]{3,2,1,0:T(8,128)}), f32[4,32,8,128]{3,2,1,0:T(8,128)S(1)}, u32[]{:S(2)}, u32[]{:S(2)}) %all-to-all-start.11) | async-done | bytes 524320 | tf_op jit(solution)/shard_map/all_to_all | solution.py:159
  (88 shorter events, 85.3 us)
Async XLA Ops:
  11.2 54.5 %all-to-all-start.4 = ((f32[32,128,128]{2,1,0:T(8,128)}), f32[32,128,128]{2,1,0:T(8,128)S(1)}, u32[]{:S(2)}, u32[]{:S(2)}) async-start(f32[32,128,128]{2,1,0:T(8,128)} %bitcast.141), calls=%async_computation.4 | async-start | bytes 4194304 | tf_op jit(solution)/shard_map/all_to_all | solution.py:146
  65.7 52.2 %all-to-all-start.3 = ((f32[32,128,128]{2,1,0:T(8,128)}), f32[32,128,128]{2,1,0:T(8,128)}, u32[]{:S(2)}, u32[]{:S(2)}) async-start(f32[32,128,128]{2,1,0:T(8,128)} %bitcast.139), calls=%async_computation.3 | async-start | bytes 4194304 | tf_op jit(solution)/shard_map/all_to_all | solution.py:146
  117.9 52.2 %all-to-all-start.2 = ((f32[32,128,128]{2,1,0:T(8,128)}), f32[32,128,128]{2,1,0:T(8,128)}, u32[]{:S(2)}, u32[]{:S(2)}) async-start(f32[32,128,128]{2,1,0:T(8,128)} %bitcast.140), calls=%async_computation.2 | async-start | bytes 4194304 | tf_op jit(solution)/shard_map/all_to_all | solution.py:146
  170.1 52.2 %all-to-all-start.1 = ((f32[32,128,128]{2,1,0:T(8,128)}), f32[32,128,128]{2,1,0:T(8,128)}, u32[]{:S(2)}, u32[]{:S(2)}) async-start(f32[32,128,128]{2,1,0:T(8,128)} %bitcast.138), calls=%async_computation.1 | async-start | bytes 4194304 | tf_op jit(solution)/shard_map/all_to_all | solution.py:146
  222.3 52.4 %all-to-all-start = ((f32[32,128,128]{2,1,0:T(8,128)}), f32[32,128,128]{2,1,0:T(8,128)}, u32[]{:S(2)}, u32[]{:S(2)}) async-start(f32[32,128,128]{2,1,0:T(8,128)} %bitcast.137), calls=%async_computation | async-start | bytes 4194304 | tf_op jit(solution)/shard_map/all_to_all | solution.py:146
  229.5 1.1 copy-start
  234.9 1.0 copy-start.2
  235.8 1.1 copy-start.4
  241.2 1.0 copy-start.6
  242.2 1.0 copy-start.8
  247.4 1.0 copy-start.10
  248.4 1.0 copy-start.12
  249.4 0.8 copy-start.14
  274.7 1.1 copy-start.15
  390.9 0.7 copy-start.16
  416.6 1.2 copy-start.11
  417.8 1.2 copy-start.13
  420.8 19.2 %all-to-all-start.10 = ((f32[4,32,8,128]{3,2,1,0:T(8,128)}), f32[4,32,8,128]{3,2,1,0:T(8,128)}, u32[]{:S(2)}, u32[]{:S(2)}) async-start(f32[4,32,8,128]{3,2,1,0:T(8,128)} %bitcast.50), calls=%async_computation.10 | async-start | bytes 1048576 | tf_op jit(solution)/shard_map/all_to_all | solution.py:159
  425.0 1.2 copy-start.7
  426.2 1.2 copy-start.9
  440.0 18.4 %all-to-all-start.9 = ((f32[4,32,8,128]{3,2,1,0:T(8,128)}), f32[4,32,8,128]{3,2,1,0:T(8,128)}, u32[]{:S(2)}, u32[]{:S(2)}) async-start(f32[4,32,8,128]{3,2,1,0:T(8,128)} %bitcast.47), calls=%async_computation.9 | async-start | bytes 1048576 | tf_op jit(solution)/shard_map/all_to_all | solution.py:159
  444.2 1.2 copy-start.3
  445.4 1.2 copy-start.5
  458.4 18.2 %all-to-all-start.8 = ((f32[4,32,8,128]{3,2,1,0:T(8,128)}), f32[4,32,8,128]{3,2,1,0:T(8,128)}, u32[]{:S(2)}, u32[]{:S(2)}) async-start(f32[4,32,8,128]{3,2,1,0:T(8,128)} %bitcast.44), calls=%async_computation.8 | async-start | bytes 1048576 | tf_op jit(solution)/shard_map/all_to_all | solution.py:159
  462.6 1.2 copy-start.1
  476.6 17.4 %all-to-all-start.7 = ((f32[4,32,8,128]{3,2,1,0:T(8,128)}), f32[4,32,8,128]{3,2,1,0:T(8,128)S(1)}, u32[]{:S(2)}, u32[]{:S(2)}) async-start(f32[4,32,8,128]{3,2,1,0:T(8,128)} %bitcast.41), calls=%async_computation.7 | async-start | bytes 1048576 | tf_op jit(solution)/shard_map/all_to_all | solution.py:159
  494.0 17.4 %all-to-all-start.11 = ((f32[4,32,8,128]{3,2,1,0:T(8,128)}), f32[4,32,8,128]{3,2,1,0:T(8,128)S(1)}, u32[]{:S(2)}, u32[]{:S(2)}) async-start(f32[4,32,8,128]{3,2,1,0:T(8,128)} %bitcast.53), calls=%async_computation.11 | async-start | bytes 1048576 | tf_op jit(solution)/shard_map/all_to_all | solution.py:159

commit v2 on v0

v2 whole, which is shorter than its diff:
```python
import functools

import jax
import jax.numpy as jnp
from jax import lax
from jax.experimental import pallas as pl
from jax.experimental.pallas import tpu as pltpu
from jax.sharding import PartitionSpec as P

RANK = 128
ITERS = 2
BLOCK = 128
SUB = 8
AXES = ("gx", "gy", "gz")
VMEM = pl.BlockSpec(memory_space=pltpu.VMEM)
SMEM = pl.BlockSpec(memory_space=pltpu.SMEM)
ANY = pl.BlockSpec(memory_space=pl.ANY)
PARAMS = pltpu.CompilerParams(vmem_limit_bytes=20 * 2**20)


def product(left, right, contract=((1,), (0,))):
    return lax.dot_general(
        left, right, (contract, ((), ())), precision=lax.Precision.HIGHEST, preferred_element_type=jnp.float32
    )


def split(value):
    high = value.astype(jnp.bfloat16)
    low = (value - high.astype(jnp.float32)).astype(jnp.bfloat16)
    return high, low


def dot(left, right, contract):
    return lax.dot_general(left, right, (contract, ((), ())), preferred_element_type=jnp.float32)


def pack_kernel(groups, start, per, steps, me_ref, snapshot_ref, *refs):
    outs, held, sems = refs[:groups], refs[groups], refs[groups + 1]
    copies = []
    for shift in [*range(1, groups), 0]:
        owner = lax.rem(me_ref[0] + shift, groups)
        first = pl.multiple_of(owner * per + start, SUB)
        copy = pltpu.make_async_copy(snapshot_ref.at[:, pl.ds(first, steps), :], held.at[shift], sems.at[shift])
        copy.start()
        copies.append((shift, copy))
    for shift, copy in copies:
        copy.wait()
        for step in range(steps):
            outs[shift][step] = held[shift, :, step, :]


def pack(me, snapshot, groups, start, steps):
    xlocal, ylocal, zlocal = snapshot.shape
    per = ylocal // groups
    shape = (steps, xlocal, zlocal)
    if steps % SUB or per % SUB:
        parts = []
        for shift in range(groups):
            first = lax.rem(me[0] + shift, groups) * per + start
            parts.append(jnp.swapaxes(lax.dynamic_slice_in_dim(snapshot, first, steps, 1), 0, 1))
        return parts
    return pl.pallas_call(
        functools.partial(pack_kernel, groups, start, per, steps),
        out_shape=(jax.ShapeDtypeStruct(shape, jnp.float32),) * groups,
        in_specs=[SMEM, ANY],
        out_specs=(VMEM,) * groups,
        scratch_shapes=[
            pltpu.VMEM((groups, xlocal, steps, zlocal), jnp.float32),
            pltpu.SemaphoreType.DMA((groups,)),
        ],
        compiler_params=PARAMS,
        cost_estimate=pl.CostEstimate(flops=0, bytes_accessed=8 * groups * steps * xlocal * zlocal, transcendentals=0),
    )(me, snapshot)


def gram_kernel(first, groups, steps, xlocal, zlocal, me_ref, *refs):
    parts, refs = refs[:groups], refs[groups:]
    old_ref, (out_ref, high_ref, low_ref) = (None, refs) if first else (refs[0], refs[1:])
    for shift in range(groups):
        owner = lax.rem(me_ref[0] + groups - shift, groups)
        rows = pl.ds(pl.multiple_of(owner * xlocal, xlocal), xlocal)
        for step in range(steps):
            high, low = split(parts[shift][step])
            columns = slice(step * zlocal, (step + 1) * zlocal)
            high_ref[rows, columns] = high
            low_ref[rows, columns] = low
    order = groups * xlocal
    big = 2 * BLOCK if order % (2 * BLOCK) == 0 else BLOCK
    ratio = big // BLOCK
    last = ((1,), (1,))
    for row in range(order // big):
        left = slice(row * big, (row + 1) * big)
        for column in range(row + 1):
            right = slice(column * big, (column + 1) * big)
            total = dot(high_ref[left, :], high_ref[right, :], last)
            total += dot(high_ref[left, :], low_ref[right, :], last)
            total += dot(low_ref[left, :], high_ref[right, :], last)
            for i in range(ratio):
                for j in range(ratio):
                    r, c = row * ratio + i, column * ratio + j
                    if r < c:
                        continue
                    at = pl.ds((r * (r + 1) // 2 + c) * BLOCK, BLOCK)
                    block = total[i * BLOCK : (i + 1) * BLOCK, j * BLOCK : (j + 1) * BLOCK]
                    out_ref[at, :] = block if first else block + old_ref[at, :]


def gram_step(me, parts, old):
    groups = len(parts)
    steps, xlocal, zlocal = parts[0].shape
    order = groups * xlocal
    count = order // BLOCK
    first = old is None
    half = jax.ShapeDtypeStruct((order, steps * zlocal), jnp.bfloat16)
    operands = (me, *parts) if first else (me, *parts, old)
    return pl.pallas_call(
        functools.partial(gram_kernel, first, groups, steps, xlocal, zlocal),
        out_shape=(jax.ShapeDtypeStruct((count * (count + 1) // 2 * BLOCK, BLOCK), jnp.float32), half, half),
        in_specs=[SMEM] + [VMEM] * (len(operands) - 1),
        out_specs=(VMEM,) * 3,
        compiler_params=PARAMS,
        cost_estimate=pl.CostEstimate(
            flops=6 * order * order * steps * zlocal, bytes_accessed=8 * order * steps * zlocal, transcendentals=0
        ),
    )(*operands)


def inverse_cholesky(a_ref, b_ref, w_ref):
    order = a_ref.shape[0]
    wide = (SUB, order)
    below = lax.broadcasted_iota(jnp.int32, wide, 0)
    across = lax.broadcasted_iota(jnp.int32, wide, 1)
    for group in range(order // SUB):
        b_ref[group * SUB : (group + 1) * SUB, :] = jnp.where(across == below + group * SUB, 1.0, 0.0)

    def spread_row(value, row):
        return jnp.broadcast_to(value[row : row + 1, :], wide)

    for panel in range(order // SUB):
        at = slice(panel * SUB, (panel + 1) * SUB)
        a, b = a_ref[at, :], b_ref[at, :]
        columns = [jnp.broadcast_to(a[:, panel * SUB + k : panel * SUB + k + 1], wide) for k in range(SUB)]
        inverses, factors, scale = [], {}, jnp.zeros(wide, jnp.float32)
        for j in range(SUB):
            pivot = spread_row(columns[j], j)
            inverse = 1.0 / pivot
            inverses.append(inverse)
            scale = jnp.where(below == j, lax.rsqrt(pivot), scale)
            lower = jnp.where(below > j, columns[j], 0.0)
            for k in range(j + 1, SUB):
                factors[j, k] = spread_row(columns[k], j) * inverse
                columns[k] = columns[k] - lower * factors[j, k]
            lower = lower * inverse
            a = a - lower * spread_row(a, j)
            b = b - lower * spread_row(b, j)
        w_ref[at, :] = b * scale
        a_rows = [spread_row(a, j) * inverses[j] for j in range(SUB)]
        b_rows = [spread_row(b, j) * inverses[j] for j in range(SUB)]
        for group in range(panel + 1, order // SUB):
            rows = slice(group * SUB, (group + 1) * SUB)
            a, b = a_ref[rows, :], b_ref[rows, :]
            columns = [jnp.broadcast_to(a[:, panel * SUB + k : panel * SUB + k + 1], wide) for k in range(SUB)]
            for j in range(SUB):
                for k in range(j + 1, SUB):
                    columns[k] = columns[k] - columns[j] * factors[j, k]
                a = a - columns[j] * a_rows[j]
                b = b - columns[j] * b_rows[j]
            a_ref[rows, :] = a
            b_ref[rows, :] = b


def factor_kernel(order, xlocal, me_ref, blocks_ref, mine_ref, turned_ref, gram_ref, m_ref, a_ref, b_ref, w_ref):
    count = order // BLOCK
    for row in range(count):
        for column in range(row + 1):
            at = (row * (row + 1) // 2 + column) * BLOCK
            block = blocks_ref[at : at + BLOCK, :]
            gram_ref[row * BLOCK : (row + 1) * BLOCK, column * BLOCK : (column + 1) * BLOCK] = block
            if row != column:
                gram_ref[column * BLOCK : (column + 1) * BLOCK, row * BLOCK : (row + 1) * BLOCK] = block.T
    m_ref[...] = gram_ref[:, :RANK]

    def orthonormal():
        m = m_ref[...]
        a_ref[...] = product(m, m, ((0,), (0,)))
        inverse_cholesky(a_ref, b_ref, w_ref)
        return product(m, w_ref[...], ((1,), (1,)))

    def step(index, carry):
        basis = orthonormal()
        m_ref[...] = basis

        @pl.when(index < ITERS)
        def _():
            m_ref[...] = product(gram_ref[...], basis)

        return carry

    lax.fori_loop(0, ITERS + 1, step, 0)
    mine_ref[...] = m_ref[pl.ds(pl.multiple_of(me_ref[0] * xlocal, SUB), xlocal), :]
    turned_ref[...] = m_ref[...].T


def factor_step(me, blocks, order, xlocal):
    square = pltpu.VMEM((RANK, RANK), jnp.float32)
    return pl.pallas_call(
        functools.partial(factor_kernel, order, xlocal),
        out_shape=(
            jax.ShapeDtypeStruct((xlocal, RANK), jnp.float32),
            jax.ShapeDtypeStruct((RANK, order), jnp.float32),
        ),
        in_specs=[SMEM, VMEM],
        out_specs=(VMEM, VMEM),
        scratch_shapes=[
            pltpu.VMEM((order, order), jnp.float32),
            pltpu.VMEM((order, RANK), jnp.float32),
            square,
            square,
            square,
        ],
        compiler_params=PARAMS,
    )(me, blocks)


def core_kernel(groups, keep, steps, zlocal, me_ref, turned_ref, high_ref, low_ref, *outs):
    lines = []
    for shift in range(groups):
        owner = lax.rem(me_ref[0] + shift, groups)
        lines.append(turned_ref[pl.ds(pl.multiple_of(owner * keep, SUB), keep), :])
    high, low = split(jnp.concatenate(lines, axis=0))
    natural = ((1,), (0,))
    total = dot(high, high_ref[...], natural) + dot(high, low_ref[...], natural) + dot(low, high_ref[...], natural)
    for shift in range(groups):
        for step in range(steps):
            outs[shift][:, step, :] = total[shift * keep : (shift + 1) * keep, step * zlocal : (step + 1) * zlocal]


def core_step(me, turned, high, low, groups, zlocal):
    order, width = high.shape
    steps = width // zlocal
    keep = RANK // groups
    return pl.pallas_call(
        functools.partial(core_kernel, groups, keep, steps, zlocal),
        out_shape=(jax.ShapeDtypeStruct((keep, steps, zlocal), jnp.float32),) * groups,
        in_specs=[SMEM] + [VMEM] * 3,
        out_specs=(VMEM,) * groups,
        compiler_params=PARAMS,
        cost_estimate=pl.CostEstimate(flops=6 * RANK * order * width, bytes_accessed=6 * order * width, transcendentals=0),
    )(me, turned, high, low)


def place_kernel(groups, per, starts, steps, me_ref, *refs):
    parts, out_ref, sem = refs[:-2], refs[-2], refs[-1]
    copies = []
    for chunk, start in enumerate(starts):
        for shift in range(groups):
            owner = lax.rem(me_ref[0] + groups - shift, groups)
            first = pl.multiple_of(owner * per + start, SUB)
            index = chunk * groups + shift
            copy = pltpu.make_async_copy(parts[index], out_ref.at[:, pl.ds(first, steps), :], sem.at[index])
            copy.start()
            copies.append(copy)
    for copy in copies:
        copy.wait()


def place(me, chunks, starts, ylocal):
    groups = len(chunks[0])
    keep, steps, zlocal = chunks[0][0].shape
    per = ylocal // groups
    shape = (keep, ylocal, zlocal)
    if steps % SUB or per % SUB:
        out = jnp.zeros(shape, jnp.float32)
        for start, parts in zip(starts, chunks):
            for shift, part in enumerate(parts):
                first = lax.rem(me[0] + groups - shift, groups) * per + start
                out = lax.dynamic_update_slice_in_dim(out, part, first, 1)
        return out
    parts = [part for parts in chunks for part in parts]
    return pl.pallas_call(
        functools.partial(place_kernel, groups, per, starts, steps),
        out_shape=jax.ShapeDtypeStruct(shape, jnp.float32),
        in_specs=[SMEM] + [ANY] * len(parts),
        out_specs=ANY,
        scratch_shapes=[pltpu.SemaphoreType.DMA((len(parts),))],
        compiler_params=PARAMS,
    )(me, *parts)


def exchange(parts):
    groups = len(parts)
    moved = [parts[0]]
    for shift in range(1, groups):
        moved.append(lax.ppermute(parts[shift], "gx", [(i, (i + shift) % groups) for i in range(groups)]))
    return moved


def total_sum(blocks):
    devices = lax.axis_size(AXES)
    rows = blocks.shape[0]
    share = -(-rows // devices)
    flat = jnp.pad(blocks, ((0, share * devices - rows), (0, 0)))
    parts = lax.all_to_all(flat.reshape(devices, share, BLOCK), AXES, split_axis=0, concat_axis=0, tiled=True)
    mine = jnp.sum(parts, axis=0)
    spread = jnp.broadcast_to(mine[None], (devices, share, BLOCK))
    whole = lax.all_to_all(spread, AXES, split_axis=0, concat_axis=0, tiled=True)
    return whole.reshape(-1, BLOCK)


def chunk_count(per):
    return max(k for k in range(1, 6) if per % k == 0)


def local(snapshot):
    xlocal, ylocal, zlocal = snapshot.shape
    groups = lax.axis_size("gx")
    order = groups * xlocal
    per = ylocal // groups
    chunks = chunk_count(per)
    steps = per // chunks
    starts = [chunk * steps for chunk in range(chunks)]
    me = lax.axis_index("gx").astype(jnp.int32).reshape(1)
    halves = []
    total = None
    for start in starts:
        total, high, low = gram_step(me, exchange(pack(me, snapshot, groups, start, steps)), total)
        halves.append((high, low))
    mine, turned = factor_step(me, total_sum(total), order, xlocal)
    outs = [exchange(core_step(me, turned, high, low, groups, zlocal)) for high, low in halves]
    return (mine, place(me, outs, starts, ylocal))


def solution(mesh):
    in_specs = (P("gx", "gy", "gz"),)
    out_specs = (P("gx", None), P("gx", "gy", "gz"))
    return jax.shard_map(local, mesh=mesh, in_specs=in_specs, out_specs=out_specs, check_vma=False)
```

time: 674 us -> 369 us (0.55)
  blocking collectives: 235 us -> 54.2 us
  starting transfers between devices: 3.69 us -> 179 us
  other arithmetic: 149 us -> 1.14 us
  waiting for transfers between devices: 188 us -> 72.2 us
  Pallas kernels: 0 us -> 41.7 us
  matrix products: 39 us -> 0 us
  local copies, waits for them, and re-layouts: 36.6 us -> 19.5 us
  between operations: 17 us -> 1.05 us
    all_to_all x1 -> x2, blocking collectives: 235 us -> 54.2 us  [the longest x1 32.9 us: total_sum(): lax.all_to_all(flat.reshape(devices, share, BLOCK), AXES, split_axis=0, c...]
    ppermute x0 -> x30, starting transfers between devices: none -> 179 us  [exchange(): lax.ppermute(parts[shift], 'gx', [(i, (i + shift) % groups) for i in rang...]
    another operation x29 -> x0, other arithmetic: 148 us -> none  [the longest x14 78.5 us: local(): factor = jnp.linalg.cholesky(lax.psum(gram, ('gx', 'gy', 'gz')))]
    psum x1 -> x0, waiting for transfers between devices: 130 us -> none  [local(): factor = jnp.linalg.cholesky(lax.psum(gram, ('gx', 'gy', 'gz')))]
    ppermute x0 -> x30, waiting for transfers between devices: none -> 72.2 us  [exchange(): lax.ppermute(parts[shift], 'gx', [(i, (i + shift) % groups) for i in rang...]
    all_to_all x1 -> x0, waiting for transfers between devices: 58.1 us -> none  [local(): lax.all_to_all(projected, 'gx', split_axis=0, concat_axis=1, tiled=True)]
    pallas_call x0 -> x17, Pallas kernels: none -> 41.7 us  [the longest x1 20.6 us: factor_step(): pl.pallas_call(functools.partial(factor_kernel, order, xlocal), out_shape...]
    dot_general x9 -> x0, matrix products: 35.9 us -> none  [product(): jnp.dot(left, right, precision=lax.Precision.HIGHEST, preferred_element_t...]
  transfers between devices with their start and end apart: 2 -> 30, of which waited for: 2 -> 7; matrix products, arithmetic and copies ran while one was open for 0% -> 0% of each run, Pallas kernels for 0% -> 4%
where the time goes in v2:
time: 369 us; the launch traced here: 368 us
  starting transfers between devices  179 us (49%)
  waiting for transfers between devices  72.2 us (20%)
  blocking collectives  54.2 us (15%)
  Pallas kernels  41.7 us (11%)
  local copies, waits for them, and re-layouts  19.5 us (5%)
    ppermute x30, starting transfers between devices, exchange(): lax.ppermute(parts[shift], 'gx', [(i, (i + shift) % groups) for i in rang...  179 us
    ppermute x30, waiting for transfers between devices, exchange(): lax.ppermute(parts[shift], 'gx', [(i, (i + shift) % groups) for i in rang...  72.2 us
    all_to_all x1, blocking collectives, total_sum(): lax.all_to_all(flat.reshape(devices, share, BLOCK), AXES, split_axis=0, c...  32.9 us
    all_to_all x1, blocking collectives, total_sum(): lax.all_to_all(spread, AXES, split_axis=0, concat_axis=0, tiled=True)  21.2 us
    pallas_call x1, Pallas kernels, factor_step(): pl.pallas_call(functools.partial(factor_kernel, order, xlocal), out_shape...  20.6 us
    unnamed x30, local copies, waits for them, and re-layouts  19.4 us
    pallas_call x5, Pallas kernels, gram_step(): pl.pallas_call(functools.partial(gram_kernel, first, groups, steps, xloca...  8.5 us
  transfers between devices with their start and end apart: 30, of which 7 were waited for; matrix products, arithmetic and copies ran while one was open for 0% of the time, Pallas kernels for 4%

profile of v2, /device:TPU:0, one launch (start us, length us, event | category | flops | bytes accessed | tf_op | source)
XLA Modules:
  0.0 368.3 jit_solution(3186513297002607973)
XLA Ops:
  0.6 4.0 %copy-done = f32[128,160,128]{2,1,0:T(8,128)S(1)} copy-done((f32[128,160,128]{2,1,0:T(8,128)S(1)}, f32[128,160,128]{2,1,0:T(8,128)}, u32[]{:S(2)}) %copy-start) | copy-done | bytes 10485784
  6.1 3.1 collective-permute-start.6
  9.1 2.6 collective-permute-start.7
  16.8 7.2 %collective-permute-done.6.refs_1_ = f32[8,128,128]{2,1,0:T(8,128)S(1)} collective-permute-done((f32[8,128,128]{2,1,0:T(8,128)S(1)}, f32[8,128,128]{2,1,0:T(8,128)S(1)}, u32[]{:S(2)}, u32[]{:S(2)}) %collective-permute-start.6) | collective-permute-done | bytes 524320 | tf_op jit(solution)/shard_map/ppermute | solution.py:294
  24.1 23.4 %collective-permute-start.13 = (f32[8,128,128]{2,1,0:T(8,128)S(1)}, f32[8,128,128]{2,1,0:T(8,128)S(1)}, u32[]{:S(2)}, u32[]{:S(2)}) collective-permute-start(f32[8,128,128]{2,1,0:T(8,128)S(1)} %get-tuple-element.77), channel_id=1, source_target_pairs={{0,16},{8,24},{16,0},{24,8},{1,17},{9,25},{17,1},{25,9},{2,18},{10... | collective-permute-start | bytes 1572872 | tf_op jit(solution)/shard_map/ppermute | solution.py:294
  47.5 12.1 %collective-permute-start.14 = (f32[8,128,128]{2,1,0:T(8,128)S(1)}, f32[8,128,128]{2,1,0:T(8,128)S(1)}, u32[]{:S(2)}, u32[]{:S(2)}) collective-permute-start(f32[8,128,128]{2,1,0:T(8,128)S(1)} %get-tuple-element.78), channel_id=1, source_target_pairs={{0,24},{8,0},{16,8},{24,16},{1,25},{9,1},{17,9},{25,17},{2,26},{10... | collective-permute-start | bytes 1572872 | tf_op jit(solution)/shard_map/ppermute | solution.py:294
  61.1 30.9 %collective-permute-start.9 = (f32[8,128,128]{2,1,0:T(8,128)S(1)}, f32[8,128,128]{2,1,0:T(8,128)S(1)}, u32[]{:S(2)}, u32[]{:S(2)}) collective-permute-start(f32[8,128,128]{2,1,0:T(8,128)S(1)} %get-tuple-element.72), channel_id=1, source_target_pairs={{0,8},{8,16},{16,24},{24,0},{1,9},{9,17},{17,25},{25,1},{2,10},{10... | collective-permute-start | bytes 1572872 | tf_op jit(solution)/shard_map/ppermute | solution.py:294
  92.4 1.9 collective-permute-start.11
  94.4 30.0 %collective-permute-done.13.refs_2_ = f32[8,128,128]{2,1,0:T(8,128)S(1)} collective-permute-done((f32[8,128,128]{2,1,0:T(8,128)S(1)}, f32[8,128,128]{2,1,0:T(8,128)S(1)}, u32[]{:S(2)}, u32[]{:S(2)}) %collective-permute-start.13) | collective-permute-done | bytes 524320 | tf_op jit(solution)/shard_map/ppermute | solution.py:294
  124.4 25.2 %collective-permute-start.5 = (f32[8,128,128]{2,1,0:T(8,128)S(1)}, f32[8,128,128]{2,1,0:T(8,128)S(1)}, u32[]{:S(2)}, u32[]{:S(2)}) collective-permute-start(f32[8,128,128]{2,1,0:T(8,128)S(1)} %get-tuple-element.66), channel_id=1, source_target_pairs={{0,24},{8,0},{16,8},{24,16},{1,25},{9,1},{17,9},{25,17},{2,26},{10... | collective-permute-start | bytes 1572872 | tf_op jit(solution)/shard_map/ppermute | solution.py:294
  151.0 18.2 %collective-permute-start = (f32[8,128,128]{2,1,0:T(8,128)S(1)}, f32[8,128,128]{2,1,0:T(8,128)S(1)}, u32[]{:S(2)}, u32[]{:S(2)}) collective-permute-start(f32[8,128,128]{2,1,0:T(8,128)S(1)} %get-tuple-element.60), channel_id=1, source_target_pairs={{0,8},{8,16},{16,24},{24,0},{1,9},{9,17},{17,25},{25,1},{2,10},{10... | collective-permute-start | bytes 1572872 | tf_op jit(solution)/shard_map/ppermute | solution.py:294
  169.2 1.9 collective-permute-start.1
  171.1 29.0 %collective-permute-start.2 = (f32[8,128,128]{2,1,0:T(8,128)S(1)}, f32[8,128,128]{2,1,0:T(8,128)S(1)}, u32[]{:S(2)}, u32[]{:S(2)}) collective-permute-start(f32[8,128,128]{2,1,0:T(8,128)S(1)} %get-tuple-element.62), channel_id=1, source_target_pairs={{0,24},{8,0},{16,8},{24,16},{1,25},{9,1},{17,9},{25,17},{2,26},{10... | collective-permute-start | bytes 1572872 | tf_op jit(solution)/shard_map/ppermute | solution.py:294
  201.9 1.7 shard_map.36
  204.5 1.7 shard_map.37
  208.3 1.7 shard_map.38
  211.9 13.6 %collective-permute-done.1.refs_2_ = f32[8,128,128]{2,1,0:T(8,128)S(1)} collective-permute-done((f32[8,128,128]{2,1,0:T(8,128)S(1)}, f32[8,128,128]{2,1,0:T(8,128)S(1)}, u32[]{:S(2)}, u32[]{:S(2)}) %collective-permute-start.1) | collective-permute-done | bytes 524320 | tf_op jit(solution)/shard_map/ppermute | solution.py:294
  225.5 1.7 shard_map.39
  229.2 32.9 %all_to_all.10 = f32[32,40,128]{2,1,0:T(8,128)} all-to-all(f32[32,40,128]{2,1,0:T(8,128)S(1)} %bitcast.4), channel_id=1, replica_groups=mesh['gx'=4,'gy'=2,'gz'=4] {'gx','gy','gz'}, dimensions={0} | all-to-all | bytes 1310720 | tf_op jit(solution)/shard_map/all_to_all | solution.py:303
  263.3 21.2 %all_to_all.11 = f32[32,40,128]{2,1,0:T(8,128)S(1)} all-to-all(f32[32,40,128]{2,1,0:T(8,128)S(1)} %broadcast_in_dim.2), channel_id=1, replica_groups=mesh['gx'=4,'gy'=2,'gz'=4] {'gx','gy','gz'}, dimensions={0} | all-to-all | bytes 1310720 | tf_op jit(solution)/shard_map/all_to_all | solution.py:306
  284.6 20.6 %shard_map.40 = (f32[128,128]{1,0:T(8,128)}, f32[128,512]{1,0:T(8,128)S(1)}) custom-call(s32[1]{0:T(128)} %bitcast.me_ref, f32[1280,128]{1,0:T(8,128)S(1)} %bitcast.3), custom_call_target="tpu_custom_call" | custom-call | tf_op jit(solution)/shard_map/pallas_call | solution.py:206
  310.1 2.2 collective-permute-start.29
  316.1 2.0 collective-permute-start.25
  323.3 2.4 collective-permute-start.26
  325.8 4.2 %collective-permute-start.22 = (f32[32,8,128]{2,1,0:T(8,128)S(1)}, f32[32,8,128]{2,1,0:T(8,128)S(1)}, u32[]{:S(2)}, u32[]{:S(2)}) collective-permute-start(f32[32,8,128]{2,1,0:T(8,128)S(1)} %get-tuple-element.102), channel_id=1, source_target_pairs={{0,16},{8,24},{16,0},{24,8},{1,17},{9,25},{17,1},{25,9},{2,18},{10... | collective-permute-start | bytes 393224 | tf_op jit(solution)/shard_map/ppermute | solution.py:294
  329.9 3.7 %collective-permute-start.23 = (f32[32,8,128]{2,1,0:T(8,128)S(1)}, f32[32,8,128]{2,1,0:T(8,128)S(1)}, u32[]{:S(2)}, u32[]{:S(2)}) collective-permute-start(f32[32,8,128]{2,1,0:T(8,128)S(1)} %get-tuple-element.103), channel_id=1, source_target_pairs={{0,24},{8,0},{16,8},{24,16},{1,25},{9,1},{17,9},{25,17},{2,26},{10... | collective-permute-start | bytes 393224 | tf_op jit(solution)/shard_map/ppermute | solution.py:294
  333.7 4.7 %collective-permute-done.25.refs_14_ = f32[32,8,128]{2,1,0:T(8,128)S(1)} collective-permute-done((f32[32,8,128]{2,1,0:T(8,128)S(1)}, f32[32,8,128]{2,1,0:T(8,128)S(1)}, u32[]{:S(2)}, u32[]{:S(2)}) %collective-permute-start.25) | collective-permute-done | bytes 131104 | tf_op jit(solution)/shard_map/ppermute | solution.py:294
  339.9 3.4 collective-permute-start.19
  344.1 5.5 %collective-permute-done.22.refs_10_ = f32[32,8,128]{2,1,0:T(8,128)S(1)} collective-permute-done((f32[32,8,128]{2,1,0:T(8,128)S(1)}, f32[32,8,128]{2,1,0:T(8,128)S(1)}, u32[]{:S(2)}, u32[]{:S(2)}) %collective-permute-start.22) | collective-permute-done | bytes 131104 | tf_op jit(solution)/shard_map/ppermute | solution.py:294
  349.6 4.2 %collective-permute-start.16 = (f32[32,8,128]{2,1,0:T(8,128)S(1)}, f32[32,8,128]{2,1,0:T(8,128)S(1)}, u32[]{:S(2)}, u32[]{:S(2)}) collective-permute-start(f32[32,8,128]{2,1,0:T(8,128)S(1)} %get-tuple-element.90), channel_id=1, source_target_pairs={{0,16},{8,24},{16,0},{24,8},{1,17},{9,25},{17,1},{25,9},{2,18},{10... | collective-permute-start | bytes 393224 | tf_op jit(solution)/shard_map/ppermute | solution.py:294
  355.3 5.5 %collective-permute-done.19.refs_6_ = f32[32,8,128]{2,1,0:T(8,128)S(1)} collective-permute-done((f32[32,8,128]{2,1,0:T(8,128)S(1)}, f32[32,8,128]{2,1,0:T(8,128)S(1)}, u32[]{:S(2)}, u32[]{:S(2)}) %collective-permute-start.19) | collective-permute-done | bytes 131104 | tf_op jit(solution)/shard_map/ppermute | solution.py:294
  360.8 5.6 %collective-permute-done.16.refs_2_ = f32[32,8,128]{2,1,0:T(8,128)S(1)} collective-permute-done((f32[32,8,128]{2,1,0:T(8,128)S(1)}, f32[32,8,128]{2,1,0:T(8,128)S(1)}, u32[]{:S(2)}, u32[]{:S(2)}) %collective-permute-start.16) | collective-permute-done | bytes 131104 | tf_op jit(solution)/shard_map/ppermute | solution.py:294
  (79 shorter events, 39.0 us)
Async XLA Ops:
  0.6 4.0 %copy-start = (f32[128,160,128]{2,1,0:T(8,128)S(1)}, f32[128,160,128]{2,1,0:T(8,128)}, u32[]{:S(2)}) copy-start(f32[128,160,128]{2,1,0:T(8,128)} %snapshot_ref.9) | copy-start | bytes 31457284
  6.1 18.0 %collective-permute-start.6 = (f32[8,128,128]{2,1,0:T(8,128)S(1)}, f32[8,128,128]{2,1,0:T(8,128)S(1)}, u32[]{:S(2)}, u32[]{:S(2)}) collective-permute-start(f32[8,128,128]{2,1,0:T(8,128)S(1)} %get-tuple-element.68), channel_id=1, source_target_pairs={{0,8},{8,16},{16,24},{24,0},{1,9},{9,17},{17,25},{25,1},{2,10},{10... | collective-permute-start | bytes 1572872 | tf_op jit(solution)/shard_map/ppermute | solution.py:294
  9.1 38.3 %collective-permute-start.7 = (f32[8,128,128]{2,1,0:T(8,128)S(1)}, f32[8,128,128]{2,1,0:T(8,128)S(1)}, u32[]{:S(2)}, u32[]{:S(2)}) collective-permute-start(f32[8,128,128]{2,1,0:T(8,128)S(1)} %get-tuple-element.69), channel_id=1, source_target_pairs={{0,16},{8,24},{16,0},{24,8},{1,17},{9,25},{17,1},{25,9},{2,18},{10... | collective-permute-start | bytes 1572872 | tf_op jit(solution)/shard_map/ppermute | solution.py:294
  11.7 49.3 %collective-permute-start.8 = (f32[8,128,128]{2,1,0:T(8,128)S(1)}, f32[8,128,128]{2,1,0:T(8,128)S(1)}, u32[]{:S(2)}, u32[]{:S(2)}) collective-permute-start(f32[8,128,128]{2,1,0:T(8,128)S(1)} %get-tuple-element.70), channel_id=1, source_target_pairs={{0,24},{8,0},{16,8},{24,16},{1,25},{9,1},{17,9},{25,17},{2,26},{10... | collective-permute-start | bytes 1572872 | tf_op jit(solution)/shard_map/ppermute | solution.py:294
  14.5 77.5 %collective-permute-start.3 = (f32[8,128,128]{2,1,0:T(8,128)S(1)}, f32[8,128,128]{2,1,0:T(8,128)S(1)}, u32[]{:S(2)}, u32[]{:S(2)}) collective-permute-start(f32[8,128,128]{2,1,0:T(8,128)S(1)} %get-tuple-element.64), channel_id=1, source_target_pairs={{0,8},{8,16},{16,24},{24,0},{1,9},{9,17},{17,25},{25,1},{2,10},{10... | collective-permute-start | bytes 1572872 | tf_op jit(solution)/shard_map/ppermute | solution.py:294
  16.7 75.7 %collective-permute-start.12 = (f32[8,128,128]{2,1,0:T(8,128)S(1)}, f32[8,128,128]{2,1,0:T(8,128)S(1)}, u32[]{:S(2)}, u32[]{:S(2)}) collective-permute-start(f32[8,128,128]{2,1,0:T(8,128)S(1)} %get-tuple-element.76), channel_id=1, source_target_pairs={{0,8},{8,16},{16,24},{24,0},{1,9},{9,17},{17,25},{25,1},{2,10},{10... | collective-permute-start | bytes 1572872 | tf_op jit(solution)/shard_map/ppermute | solution.py:294
  24.1 100.3 %collective-permute-start.13 = (f32[8,128,128]{2,1,0:T(8,128)S(1)}, f32[8,128,128]{2,1,0:T(8,128)S(1)}, u32[]{:S(2)}, u32[]{:S(2)}) collective-permute-start(f32[8,128,128]{2,1,0:T(8,128)S(1)} %get-tuple-element.77), channel_id=1, source_target_pairs={{0,16},{8,24},{16,0},{24,8},{1,17},{9,25},{17,1},{25,9},{2,18},{10... | collective-permute-start | bytes 1572872 | tf_op jit(solution)/shard_map/ppermute | solution.py:294
  47.5 76.9 %collective-permute-start.14 = (f32[8,128,128]{2,1,0:T(8,128)S(1)}, f32[8,128,128]{2,1,0:T(8,128)S(1)}, u32[]{:S(2)}, u32[]{:S(2)}) collective-permute-start(f32[8,128,128]{2,1,0:T(8,128)S(1)} %get-tuple-element.78), channel_id=1, source_target_pairs={{0,24},{8,0},{16,8},{24,16},{1,25},{9,1},{17,9},{25,17},{2,26},{10... | collective-permute-start | bytes 1572872 | tf_op jit(solution)/shard_map/ppermute | solution.py:294
  61.1 89.9 %collective-permute-start.9 = (f32[8,128,128]{2,1,0:T(8,128)S(1)}, f32[8,128,128]{2,1,0:T(8,128)S(1)}, u32[]{:S(2)}, u32[]{:S(2)}) collective-permute-start(f32[8,128,128]{2,1,0:T(8,128)S(1)} %get-tuple-element.72), channel_id=1, source_target_pairs={{0,8},{8,16},{16,24},{24,0},{1,9},{9,17},{17,25},{25,1},{2,10},{10... | collective-permute-start | bytes 1572872 | tf_op jit(solution)/shard_map/ppermute | solution.py:294
  92.0 77.2 %collective-permute-start.10 = (f32[8,128,128]{2,1,0:T(8,128)S(1)}, f32[8,128,128]{2,1,0:T(8,128)S(1)}, u32[]{:S(2)}, u32[]{:S(2)}) collective-permute-start(f32[8,128,128]{2,1,0:T(8,128)S(1)} %get-tuple-element.73), channel_id=1, source_target_pairs={{0,16},{8,24},{16,0},{24,8},{1,17},{9,25},{17,1},{25,9},{2,18},{10... | collective-permute-start | bytes 1572872 | tf_op jit(solution)/shard_map/ppermute | solution.py:294
  92.4 78.7 %collective-permute-start.11 = (f32[8,128,128]{2,1,0:T(8,128)S(1)}, f32[8,128,128]{2,1,0:T(8,128)S(1)}, u32[]{:S(2)}, u32[]{:S(2)}) collective-permute-start(f32[8,128,128]{2,1,0:T(8,128)S(1)} %get-tuple-element.74), channel_id=1, source_target_pairs={{0,24},{8,0},{16,8},{24,16},{1,25},{9,1},{17,9},{25,17},{2,26},{10... | collective-permute-start | bytes 1572872 | tf_op jit(solution)/shard_map/ppermute | solution.py:294
  124.4 83.9 %collective-permute-start.4 = (f32[8,128,128]{2,1,0:T(8,128)S(1)}, f32[8,128,128]{2,1,0:T(8,128)S(1)}, u32[]{:S(2)}, u32[]{:S(2)}) collective-permute-start(f32[8,128,128]{2,1,0:T(8,128)S(1)} %get-tuple-element.65), channel_id=1, source_target_pairs={{0,16},{8,24},{16,0},{24,8},{1,17},{9,25},{17,1},{25,9},{2,18},{10... | collective-permute-start | bytes 1572872 | tf_op jit(solution)/shard_map/ppermute | solution.py:294
  124.4 83.9 %collective-permute-start.5 = (f32[8,128,128]{2,1,0:T(8,128)S(1)}, f32[8,128,128]{2,1,0:T(8,128)S(1)}, u32[]{:S(2)}, u32[]{:S(2)}) collective-permute-start(f32[8,128,128]{2,1,0:T(8,128)S(1)} %get-tuple-element.66), channel_id=1, source_target_pairs={{0,24},{8,0},{16,8},{24,16},{1,25},{9,1},{17,9},{25,17},{2,26},{10... | collective-permute-start | bytes 1572872 | tf_op jit(solution)/shard_map/ppermute | solution.py:294
  151.0 60.9 %collective-permute-start = (f32[8,128,128]{2,1,0:T(8,128)S(1)}, f32[8,128,128]{2,1,0:T(8,128)S(1)}, u32[]{:S(2)}, u32[]{:S(2)}) collective-permute-start(f32[8,128,128]{2,1,0:T(8,128)S(1)} %get-tuple-element.60), channel_id=1, source_target_pairs={{0,8},{8,16},{16,24},{24,0},{1,9},{9,17},{17,25},{25,1},{2,10},{10... | collective-permute-start | bytes 1572872 | tf_op jit(solution)/shard_map/ppermute | solution.py:294
  169.2 56.3 %collective-permute-start.1 = (f32[8,128,128]{2,1,0:T(8,128)S(1)}, f32[8,128,128]{2,1,0:T(8,128)S(1)}, u32[]{:S(2)}, u32[]{:S(2)}) collective-permute-start(f32[8,128,128]{2,1,0:T(8,128)S(1)} %get-tuple-element.61), channel_id=1, source_target_pairs={{0,16},{8,24},{16,0},{24,8},{1,17},{9,25},{17,1},{25,9},{2,18},{10... | collective-permute-start | bytes 1572872 | tf_op jit(solution)/shard_map/ppermute | solution.py:294
  171.1 54.4 %collective-permute-start.2 = (f32[8,128,128]{2,1,0:T(8,128)S(1)}, f32[8,128,128]{2,1,0:T(8,128)S(1)}, u32[]{:S(2)}, u32[]{:S(2)}) collective-permute-start(f32[8,128,128]{2,1,0:T(8,128)S(1)} %get-tuple-element.62), channel_id=1, source_target_pairs={{0,24},{8,0},{16,8},{24,16},{1,25},{9,1},{17,9},{25,17},{2,26},{10... | collective-permute-start | bytes 1572872 | tf_op jit(solution)/shard_map/ppermute | solution.py:294
  308.4 15.0 %collective-permute-start.27 = (f32[32,8,128]{2,1,0:T(8,128)S(1)}, f32[32,8,128]{2,1,0:T(8,128)S(1)}, u32[]{:S(2)}, u32[]{:S(2)}) collective-permute-start(f32[32,8,128]{2,1,0:T(8,128)S(1)} %get-tuple-element.113), channel_id=1, source_target_pairs={{0,8},{8,16},{16,24},{24,0},{1,9},{9,17},{17,25},{25,1},{2,10},{10... | collective-permute-start | bytes 393224 | tf_op jit(solution)/shard_map/ppermute | solution.py:294
  309.9 15.9 %collective-permute-start.28 = (f32[32,8,128]{2,1,0:T(8,128)S(1)}, f32[32,8,128]{2,1,0:T(8,128)S(1)}, u32[]{:S(2)}, u32[]{:S(2)}) collective-permute-start(f32[32,8,128]{2,1,0:T(8,128)S(1)} %get-tuple-element.114), channel_id=1, source_target_pairs={{0,16},{8,24},{16,0},{24,8},{1,17},{9,25},{17,1},{25,9},{2,18},{10... | collective-permute-start | bytes 393224 | tf_op jit(solution)/shard_map/ppermute | solution.py:294
  310.1 15.6 %collective-permute-start.29 = (f32[32,8,128]{2,1,0:T(8,128)S(1)}, f32[32,8,128]{2,1,0:T(8,128)S(1)}, u32[]{:S(2)}, u32[]{:S(2)}) collective-permute-start(f32[32,8,128]{2,1,0:T(8,128)S(1)} %get-tuple-element.115), channel_id=1, source_target_pairs={{0,24},{8,0},{16,8},{24,16},{1,25},{9,1},{17,9},{25,17},{2,26},{10... | collective-permute-start | bytes 393224 | tf_op jit(solution)/shard_map/ppermute | solution.py:294
  315.5 14.4 %collective-permute-start.24 = (f32[32,8,128]{2,1,0:T(8,128)S(1)}, f32[32,8,128]{2,1,0:T(8,128)S(1)}, u32[]{:S(2)}, u32[]{:S(2)}) collective-permute-start(f32[32,8,128]{2,1,0:T(8,128)S(1)} %get-tuple-element.107), channel_id=1, source_target_pairs={{0,8},{8,16},{16,24},{24,0},{1,9},{9,17},{17,25},{25,1},{2,10},{10... | collective-permute-start | bytes 393224 | tf_op jit(solution)/shard_map/ppermute | solution.py:294
  316.1 22.2 %collective-permute-start.25 = (f32[32,8,128]{2,1,0:T(8,128)S(1)}, f32[32,8,128]{2,1,0:T(8,128)S(1)}, u32[]{:S(2)}, u32[]{:S(2)}) collective-permute-start(f32[32,8,128]{2,1,0:T(8,128)S(1)} %get-tuple-element.108), channel_id=1, source_target_pairs={{0,16},{8,24},{16,0},{24,8},{1,17},{9,25},{17,1},{25,9},{2,18},{10... | collective-permute-start | bytes 393224 | tf_op jit(solution)/shard_map/ppermute | solution.py:294
  321.3 1.2 copy-start.2
  323.3 16.5 %collective-permute-start.26 = (f32[32,8,128]{2,1,0:T(8,128)S(1)}, f32[32,8,128]{2,1,0:T(8,128)S(1)}, u32[]{:S(2)}, u32[]{:S(2)}) collective-permute-start(f32[32,8,128]{2,1,0:T(8,128)S(1)} %get-tuple-element.109), channel_id=1, source_target_pairs={{0,24},{8,0},{16,8},{24,16},{1,25},{9,1},{17,9},{25,17},{2,26},{10... | collective-permute-start | bytes 393224 | tf_op jit(solution)/shard_map/ppermute | solution.py:294
  325.8 17.6 %collective-permute-start.21 = (f32[32,8,128]{2,1,0:T(8,128)S(1)}, f32[32,8,128]{2,1,0:T(8,128)S(1)}, u32[]{:S(2)}, u32[]{:S(2)}) collective-permute-start(f32[32,8,128]{2,1,0:T(8,128)S(1)} %get-tuple-element.101), channel_id=1, source_target_pairs={{0,8},{8,16},{16,24},{24,0},{1,9},{9,17},{17,25},{25,1},{2,10},{10... | collective-permute-start | bytes 393224 | tf_op jit(solution)/shard_map/ppermute | solution.py:294
  325.8 23.8 %collective-permute-start.22 = (f32[32,8,128]{2,1,0:T(8,128)S(1)}, f32[32,8,128]{2,1,0:T(8,128)S(1)}, u32[]{:S(2)}, u32[]{:S(2)}) collective-permute-start(f32[32,8,128]{2,1,0:T(8,128)S(1)} %get-tuple-element.102), channel_id=1, source_target_pairs={{0,16},{8,24},{16,0},{24,8},{1,17},{9,25},{17,1},{25,9},{2,18},{10... | collective-permute-start | bytes 393224 | tf_op jit(solution)/shard_map/ppermute | solution.py:294
  329.9 19.6 %collective-permute-start.23 = (f32[32,8,128]{2,1,0:T(8,128)S(1)}, f32[32,8,128]{2,1,0:T(8,128)S(1)}, u32[]{:S(2)}, u32[]{:S(2)}) collective-permute-start(f32[32,8,128]{2,1,0:T(8,128)S(1)} %get-tuple-element.103), channel_id=1, source_target_pairs={{0,24},{8,0},{16,8},{24,16},{1,25},{9,1},{17,9},{25,17},{2,26},{10... | collective-permute-start | bytes 393224 | tf_op jit(solution)/shard_map/ppermute | solution.py:294
  338.3 15.5 %collective-permute-start.18 = (f32[32,8,128]{2,1,0:T(8,128)S(1)}, f32[32,8,128]{2,1,0:T(8,128)S(1)}, u32[]{:S(2)}, u32[]{:S(2)}) collective-permute-start(f32[32,8,128]{2,1,0:T(8,128)S(1)} %get-tuple-element.95), channel_id=1, source_target_pairs={{0,8},{8,16},{16,24},{24,0},{1,9},{9,17},{17,25},{25,1},{2,10},{10... | collective-permute-start | bytes 393224 | tf_op jit(solution)/shard_map/ppermute | solution.py:294
  339.9 20.9 %collective-permute-start.19 = (f32[32,8,128]{2,1,0:T(8,128)S(1)}, f32[32,8,128]{2,1,0:T(8,128)S(1)}, u32[]{:S(2)}, u32[]{:S(2)}) collective-permute-start(f32[32,8,128]{2,1,0:T(8,128)S(1)} %get-tuple-element.96), channel_id=1, source_target_pairs={{0,16},{8,24},{16,0},{24,8},{1,17},{9,25},{17,1},{25,9},{2,18},{10... | collective-permute-start | bytes 393224 | tf_op jit(solution)/shard_map/ppermute | solution.py:294
  343.3 17.5 %collective-permute-start.20 = (f32[32,8,128]{2,1,0:T(8,128)S(1)}, f32[32,8,128]{2,1,0:T(8,128)S(1)}, u32[]{:S(2)}, u32[]{:S(2)}) collective-permute-start(f32[32,8,128]{2,1,0:T(8,128)S(1)} %get-tuple-element.97), channel_id=1, source_target_pairs={{0,24},{8,0},{16,8},{24,16},{1,25},{9,1},{17,9},{25,17},{2,26},{10... | collective-permute-start | bytes 393224 | tf_op jit(solution)/shard_map/ppermute | solution.py:294
  349.6 11.2 %collective-permute-start.15 = (f32[32,8,128]{2,1,0:T(8,128)S(1)}, f32[32,8,128]{2,1,0:T(8,128)S(1)}, u32[]{:S(2)}, u32[]{:S(2)}) collective-permute-start(f32[32,8,128]{2,1,0:T(8,128)S(1)} %get-tuple-element.89), channel_id=1, source_target_pairs={{0,8},{8,16},{16,24},{24,0},{1,9},{9,17},{17,25},{25,1},{2,10},{10... | collective-permute-start | bytes 393224 | tf_op jit(solution)/shard_map/ppermute | solution.py:294
  349.6 16.9 %collective-permute-start.16 = (f32[32,8,128]{2,1,0:T(8,128)S(1)}, f32[32,8,128]{2,1,0:T(8,128)S(1)}, u32[]{:S(2)}, u32[]{:S(2)}) collective-permute-start(f32[32,8,128]{2,1,0:T(8,128)S(1)} %get-tuple-element.90), channel_id=1, source_target_pairs={{0,16},{8,24},{16,0},{24,8},{1,17},{9,25},{17,1},{25,9},{2,18},{10... | collective-permute-start | bytes 393224 | tf_op jit(solution)/shard_map/ppermute | solution.py:294
  353.8 12.6 %collective-permute-start.17 = (f32[32,8,128]{2,1,0:T(8,128)S(1)}, f32[32,8,128]{2,1,0:T(8,128)S(1)}, u32[]{:S(2)}, u32[]{:S(2)}) collective-permute-start(f32[32,8,128]{2,1,0:T(8,128)S(1)} %get-tuple-element.91), channel_id=1, source_target_pairs={{0,24},{8,0},{16,8},{24,16},{1,25},{9,1},{17,9},{25,17},{2,26},{10... | collective-permute-start | bytes 393224 | tf_op jit(solution)/shard_map/ppermute | solution.py:294
  (13 other events, 14.3 us)

commit v3 on v2

--- a/solution.py
+++ b/solution.py
@@ -11,11 +11,13 @@
 ITERS = 2
 BLOCK = 128
 SUB = 8
+HALF = 16
 AXES = ("gx", "gy", "gz")
 VMEM = pl.BlockSpec(memory_space=pltpu.VMEM)
 SMEM = pl.BlockSpec(memory_space=pltpu.SMEM)
 ANY = pl.BlockSpec(memory_space=pl.ANY)
-PARAMS = pltpu.CompilerParams(vmem_limit_bytes=20 * 2**20)
+HBM = pl.BlockSpec(memory_space=pltpu.HBM)
+PARAMS = pltpu.CompilerParams(vmem_limit_bytes=12 * 2**20)
 
 
 def product(left, right, contract=((1,), (0,))):
@@ -34,13 +36,14 @@
     return lax.dot_general(left, right, (contract, ((), ())), preferred_element_type=jnp.float32)
 
 
-def pack_kernel(groups, start, per, steps, me_ref, snapshot_ref, *refs):
+def pack_kernel(groups, x0, tall, start, per, steps, me_ref, snapshot_ref, *refs):
     outs, held, sems = refs[:groups], refs[groups], refs[groups + 1]
     copies = []
     for shift in [*range(1, groups), 0]:
         owner = lax.rem(me_ref[0] + shift, groups)
         first = pl.multiple_of(owner * per + start, SUB)
-        copy = pltpu.make_async_copy(snapshot_ref.at[:, pl.ds(first, steps), :], held.at[shift], sems.at[shift])
+        source = snapshot_ref.at[pl.ds(x0, tall), pl.ds(first, steps), :]
+        copy = pltpu.make_async_copy(source, held.at[shift], sems.at[shift])
         copy.start()
         copies.append((shift, copy))
     for shift, copy in copies:
@@ -49,78 +52,79 @@
             outs[shift][step] = held[shift, :, step, :]
 
 
-def pack(me, snapshot, groups, start, steps):
-    xlocal, ylocal, zlocal = snapshot.shape
+def pack(me, snapshot, groups, x0, tall, start, steps):
+    _, ylocal, zlocal = snapshot.shape
     per = ylocal // groups
-    shape = (steps, xlocal, zlocal)
+    shape = (steps, tall, zlocal)
     if steps % SUB or per % SUB:
         parts = []
         for shift in range(groups):
             first = lax.rem(me[0] + shift, groups) * per + start
-            parts.append(jnp.swapaxes(lax.dynamic_slice_in_dim(snapshot, first, steps, 1), 0, 1))
+            piece = lax.dynamic_slice_in_dim(snapshot[x0 : x0 + tall], first, steps, 1)
+            parts.append(jnp.swapaxes(piece, 0, 1))
         return parts
     return pl.pallas_call(
-        functools.partial(pack_kernel, groups, start, per, steps),
+        functools.partial(pack_kernel, groups, x0, tall, start, per, steps),
         out_shape=(jax.ShapeDtypeStruct(shape, jnp.float32),) * groups,
-        in_specs=[SMEM, ANY],
+        in_specs=[SMEM, HBM],
         out_specs=(VMEM,) * groups,
         scratch_shapes=[
-            pltpu.VMEM((groups, xlocal, steps, zlocal), jnp.float32),
+            pltpu.VMEM((groups, tall, steps, zlocal), jnp.float32),
             pltpu.SemaphoreType.DMA((groups,)),
         ],
         compiler_params=PARAMS,
-        cost_estimate=pl.CostEstimate(flops=0, bytes_accessed=8 * groups * steps * xlocal * zlocal, transcendentals=0),
+        cost_estimate=pl.CostEstimate(flops=0, bytes_accessed=8 * groups * steps * tall * zlocal, transcendentals=0),
     )(me, snapshot)
 
 
-def gram_kernel(first, groups, steps, xlocal, zlocal, me_ref, *refs):
+def gram_kernel(first, groups, earlier, me_ref, *refs):
     parts, refs = refs[:groups], refs[groups:]
+    highs, lows, refs = list(refs[:earlier]), list(refs[earlier : 2 * earlier]), refs[2 * earlier :]
     old_ref, (out_ref, high_ref, low_ref) = (None, refs) if first else (refs[0], refs[1:])
+    steps, tall, zlocal = parts[0].shape
     for shift in range(groups):
         owner = lax.rem(me_ref[0] + groups - shift, groups)
-        rows = pl.ds(pl.multiple_of(owner * xlocal, xlocal), xlocal)
+        rows = pl.ds(pl.multiple_of(owner * tall, HALF), tall)
         for step in range(steps):
             high, low = split(parts[shift][step])
             columns = slice(step * zlocal, (step + 1) * zlocal)
             high_ref[rows, columns] = high
             low_ref[rows, columns] = low
-    order = groups * xlocal
-    big = 2 * BLOCK if order % (2 * BLOCK) == 0 else BLOCK
-    ratio = big // BLOCK
     last = ((1,), (1,))
-    for row in range(order // big):
-        left = slice(row * big, (row + 1) * big)
-        for column in range(row + 1):
-            right = slice(column * big, (column + 1) * big)
-            total = dot(high_ref[left, :], high_ref[right, :], last)
-            total += dot(high_ref[left, :], low_ref[right, :], last)
-            total += dot(low_ref[left, :], high_ref[right, :], last)
-            for i in range(ratio):
-                for j in range(ratio):
-                    r, c = row * ratio + i, column * ratio + j
-                    if r < c:
-                        continue
-                    at = pl.ds((r * (r + 1) // 2 + c) * BLOCK, BLOCK)
-                    block = total[i * BLOCK : (i + 1) * BLOCK, j * BLOCK : (j + 1) * BLOCK]
-                    out_ref[at, :] = block if first else block + old_ref[at, :]
-
-
-def gram_step(me, parts, old):
+    slot = 0
+    for row in range(groups * tall // BLOCK):
+        mine = slice(row * BLOCK, (row + 1) * BLOCK)
+        for other_high, other_low in [*zip(highs, lows), (high_ref, low_ref)]:
+            upto = slice(0, (row + 1) * BLOCK if other_high is high_ref else other_high.shape[0])
+            total = dot(high_ref[mine, :], other_high[upto, :], last)
+            total += dot(high_ref[mine, :], other_low[upto, :], last)
+            total += dot(low_ref[mine, :], other_high[upto, :], last)
+            for column in range(upto.stop // BLOCK):
+                at = slice(slot * BLOCK, (slot + 1) * BLOCK)
+                block = total[:, column * BLOCK : (column + 1) * BLOCK]
+                out_ref[at, :] = block if first else block + old_ref[at, :]
+                slot += 1
+
+
+def gram_step(me, parts, earlier, old):
     groups = len(parts)
-    steps, xlocal, zlocal = parts[0].shape
-    order = groups * xlocal
-    count = order // BLOCK
+    steps, tall, zlocal = parts[0].shape
+    rows = groups * tall
+    before = sum(high.shape[0] for high, _ in earlier)
+    done, count = before // BLOCK, rows // BLOCK
+    slots = done * count + count * (count + 1) // 2
     first = old is None
-    half = jax.ShapeDtypeStruct((order, steps * zlocal), jnp.bfloat16)
-    operands = (me, *parts) if first else (me, *parts, old)
-    return pl.pallas_call(
-        functools.partial(gram_kernel, first, groups, steps, xlocal, zlocal),
-        out_shape=(jax.ShapeDtypeStruct((count * (count + 1) // 2 * BLOCK, BLOCK), jnp.float32), half, half),
+    half = jax.ShapeDtypeStruct((rows, steps * zlocal), jnp.bfloat16)
+    operands = [me, *parts, *(high for high, _ in earlier), *(low for _, low in earlier)]
+    operands += [] if first else [old]
+    return pl.pallas_call(
+        functools.partial(gram_kernel, first, groups, len(earlier)),
+        out_shape=(jax.ShapeDtypeStruct((slots * BLOCK, BLOCK), jnp.float32), half, half),
         in_specs=[SMEM] + [VMEM] * (len(operands) - 1),
         out_specs=(VMEM,) * 3,
         compiler_params=PARAMS,
         cost_estimate=pl.CostEstimate(
-            flops=6 * order * order * steps * zlocal, bytes_accessed=8 * order * steps * zlocal, transcendentals=0
+            flops=6 * slots * BLOCK * BLOCK * steps * zlocal, bytes_accessed=8 * rows * steps * zlocal, transcendentals=0
         ),
     )(*operands)
 
@@ -169,25 +173,33 @@
             b_ref[rows, :] = b
 
 
-def factor_kernel(order, xlocal, me_ref, blocks_ref, mine_ref, turned_ref, gram_ref, m_ref, a_ref, b_ref, w_ref):
-    count = order // BLOCK
-    for row in range(count):
-        for column in range(row + 1):
-            at = (row * (row + 1) // 2 + column) * BLOCK
-            block = blocks_ref[at : at + BLOCK, :]
-            gram_ref[row * BLOCK : (row + 1) * BLOCK, column * BLOCK : (column + 1) * BLOCK] = block
-            if row != column:
-                gram_ref[column * BLOCK : (column + 1) * BLOCK, row * BLOCK : (row + 1) * BLOCK] = block.T
-    m_ref[...] = gram_ref[:, :RANK]
-
-    def orthonormal():
+def factor_kernel(groups, talls, me_ref, *refs):
+    phases = len(talls)
+    sums, refs = refs[:phases], refs[phases:]
+    mine_ref, turned_ref, gram_ref, m_ref, a_ref, b_ref, w_ref = refs
+    bases = [groups * sum(talls[:phase]) for phase in range(phases)]
+    xlocal = sum(talls)
+    for phase, tall in enumerate(talls):
+        slot = 0
+        first = bases[phase] // BLOCK
+        for row in range(first, first + groups * tall // BLOCK):
+            for column in range(row + 1):
+                block = sums[phase][slot * BLOCK : (slot + 1) * BLOCK, :]
+                slot += 1
+                gram_ref[row * BLOCK : (row + 1) * BLOCK, column * BLOCK : (column + 1) * BLOCK] = block
+                if row != column:
+                    gram_ref[column * BLOCK : (column + 1) * BLOCK, row * BLOCK : (row + 1) * BLOCK] = block.T
+    lines = []
+    for owner in range(-(-RANK // xlocal)):
+        for base, tall in zip(bases, talls):
+            lines.append(gram_ref[base + owner * tall : base + (owner + 1) * tall, :])
+    m_ref[...] = jnp.concatenate(lines, axis=0)[:RANK, :].T
+
+    def step(index, carry):
         m = m_ref[...]
         a_ref[...] = product(m, m, ((0,), (0,)))
         inverse_cholesky(a_ref, b_ref, w_ref)
-        return product(m, w_ref[...], ((1,), (1,)))
-
-    def step(index, carry):
-        basis = orthonormal()
+        basis = product(m, w_ref[...], ((1,), (1,)))
         m_ref[...] = basis
 
         @pl.when(index < ITERS)
@@ -197,19 +209,24 @@
         return carry
 
     lax.fori_loop(0, ITERS + 1, step, 0)
-    mine_ref[...] = m_ref[pl.ds(pl.multiple_of(me_ref[0] * xlocal, SUB), xlocal), :]
+    offset = 0
+    for base, tall in zip(bases, talls):
+        rows = pl.ds(pl.multiple_of(base + me_ref[0] * tall, SUB), tall)
+        mine_ref[offset : offset + tall, :] = m_ref[rows, :]
+        offset += tall
     turned_ref[...] = m_ref[...].T
 
 
-def factor_step(me, blocks, order, xlocal):
+def factor_step(me, sums, groups, talls):
+    order, xlocal = groups * sum(talls), sum(talls)
     square = pltpu.VMEM((RANK, RANK), jnp.float32)
     return pl.pallas_call(
-        functools.partial(factor_kernel, order, xlocal),
+        functools.partial(factor_kernel, groups, talls),
         out_shape=(
             jax.ShapeDtypeStruct((xlocal, RANK), jnp.float32),
             jax.ShapeDtypeStruct((RANK, order), jnp.float32),
         ),
-        in_specs=[SMEM, VMEM],
+        in_specs=[SMEM] + [VMEM] * len(sums),
         out_specs=(VMEM, VMEM),
         scratch_shapes=[
             pltpu.VMEM((order, order), jnp.float32),
@@ -219,34 +236,41 @@
             square,
         ],
         compiler_params=PARAMS,
-    )(me, blocks)
-
-
-def core_kernel(groups, keep, steps, zlocal, me_ref, turned_ref, high_ref, low_ref, *outs):
+    )(me, *sums)
+
+
+def core_kernel(groups, keep, steps, zlocal, phases, me_ref, turned_ref, *refs):
+    highs, lows, outs = refs[:phases], refs[phases : 2 * phases], refs[2 * phases :]
     lines = []
     for shift in range(groups):
         owner = lax.rem(me_ref[0] + shift, groups)
         lines.append(turned_ref[pl.ds(pl.multiple_of(owner * keep, SUB), keep), :])
     high, low = split(jnp.concatenate(lines, axis=0))
     natural = ((1,), (0,))
-    total = dot(high, high_ref[...], natural) + dot(high, low_ref[...], natural) + dot(low, high_ref[...], natural)
+    total, base = 0.0, 0
+    for high_ref, low_ref in zip(highs, lows):
+        rows = slice(base, base + high_ref.shape[0])
+        base = rows.stop
+        total += dot(high[:, rows], high_ref[...], natural)
+        total += dot(high[:, rows], low_ref[...], natural)
+        total += dot(low[:, rows], high_ref[...], natural)
     for shift in range(groups):
         for step in range(steps):
             outs[shift][:, step, :] = total[shift * keep : (shift + 1) * keep, step * zlocal : (step + 1) * zlocal]
 
 
-def core_step(me, turned, high, low, groups, zlocal):
-    order, width = high.shape
+def core_step(me, turned, halves, groups, zlocal):
+    order, width = turned.shape[1], halves[0][0].shape[1]
     steps = width // zlocal
     keep = RANK // groups
     return pl.pallas_call(
-        functools.partial(core_kernel, groups, keep, steps, zlocal),
+        functools.partial(core_kernel, groups, keep, steps, zlocal, len(halves)),
         out_shape=(jax.ShapeDtypeStruct((keep, steps, zlocal), jnp.float32),) * groups,
-        in_specs=[SMEM] + [VMEM] * 3,
+        in_specs=[SMEM] + [VMEM] * (1 + 2 * len(halves)),
         out_specs=(VMEM,) * groups,
         compiler_params=PARAMS,
         cost_estimate=pl.CostEstimate(flops=6 * RANK * order * width, bytes_accessed=6 * order * width, transcendentals=0),
-    )(me, turned, high, low)
+    )(me, turned, *(high for high, _ in halves), *(low for _, low in halves))
 
 
 def place_kernel(groups, per, starts, steps, me_ref, *refs):
@@ -311,22 +335,35 @@
     return max(k for k in range(1, 6) if per % k == 0)
 
 
+def phase_sizes(xlocal, groups):
+    short = xlocal // 4
+    if short % HALF or groups * short % BLOCK:
+        short = xlocal // 2
+    return [xlocal - short, short]
+
+
 def local(snapshot):
     xlocal, ylocal, zlocal = snapshot.shape
     groups = lax.axis_size("gx")
-    order = groups * xlocal
     per = ylocal // groups
     chunks = chunk_count(per)
     steps = per // chunks
     starts = [chunk * steps for chunk in range(chunks)]
+    talls = phase_sizes(xlocal, groups)
     me = lax.axis_index("gx").astype(jnp.int32).reshape(1)
-    halves = []
-    total = None
-    for start in starts:
-        total, high, low = gram_step(me, exchange(pack(me, snapshot, groups, start, steps)), total)
-        halves.append((high, low))
-    mine, turned = factor_step(me, total_sum(total), order, xlocal)
-    outs = [exchange(core_step(me, turned, high, low, groups, zlocal)) for high, low in halves]
+    halves = [[] for _ in starts]
+    sums = []
+    x0 = 0
+    for tall in talls:
+        total = None
+        for held, start in zip(halves, starts):
+            parts = exchange(pack(me, snapshot, groups, x0, tall, start, steps))
+            total, high, low = gram_step(me, parts, held, total)
+            held.append((high, low))
+        x0 += tall
+        sums.append(total_sum(total) if x0 == xlocal else lax.psum(total, AXES))
+    mine, turned = factor_step(me, sums, groups, talls)
+    outs = [exchange(core_step(me, turned, held, groups, zlocal)) for held in halves]
     return (mine, place(me, outs, starts, ylocal))
 
 

time: 369 us -> 500 us (1.36)
  waiting for transfers between devices: 72.2 us -> 223 us
  blocking collectives: 54.2 us -> 13.2 us
  between operations: 1.05 us -> 14.5 us
  local copies, waits for them, and re-layouts: 19.5 us -> 27.9 us
  Pallas kernels: 41.7 us -> 49.3 us
  starting transfers between devices: 179 us -> 172 us
    psum x0 -> x1, waiting for transfers between devices: none -> 134 us  [local(): sums.append(total_sum(total) if x0 == xlocal else lax.psum(total, AXES))]
    all_to_all x1 -> x0, blocking collectives: 21.2 us -> none  [total_sum(): lax.all_to_all(spread, AXES, split_axis=0, concat_axis=0, tiled=True)]
    all_to_all x1, blocking collectives: 32.9 us -> 13.2 us  [total_sum(): lax.all_to_all(flat.reshape(devices, share, BLOCK), AXES, split_axis=0, c...]
    ppermute x30 -> x45, waiting for transfers between devices: 72.2 us -> 87.9 us  [exchange(): lax.ppermute(parts[shift], 'gx', [(i, (i + shift) % groups) for i in rang...]
    ppermute x30 -> x45, starting transfers between devices: 179 us -> 169 us  [exchange(): lax.ppermute(parts[shift], 'gx', [(i, (i + shift) % groups) for i in rang...]
    unnamed x30 -> x70, local copies, waits for them, and re-layouts: 19.4 us -> 27.1 us
    pallas_call x11 -> x21, Pallas kernels: 36.2 us -> 42.6 us  [the longest x1 20.6 us: factor_step(): pl.pallas_call(functools.partial(factor_kernel, groups, talls), out_shape...]
  transfers between devices with their start and end apart: 30 -> 47, of which waited for: 7 -> 13; matrix products, arithmetic and copies ran while one was open for 0% -> 0% of each run, Pallas kernels for 4% -> 5%
where the time goes in v3:
time: 500 us; the launch traced here: 499 us
  waiting for transfers between devices  223 us (45%)
  starting transfers between devices  172 us (34%)
  Pallas kernels  49.3 us (10%)
  local copies, waits for them, and re-layouts  27.9 us (6%)
  between operations  14.5 us (3%)
  blocking collectives  13.2 us (3%)
    ppermute x45, starting transfers between devices, exchange(): lax.ppermute(parts[shift], 'gx', [(i, (i + shift) % groups) for i in rang...  169 us
    psum x1, waiting for transfers between devices, local(): sums.append(total_sum(total) if x0 == xlocal else lax.psum(total, AXES))  134 us
    ppermute x45, waiting for transfers between devices, exchange(): lax.ppermute(parts[shift], 'gx', [(i, (i + shift) % groups) for i in rang...  87.9 us
    unnamed x70, local copies, waits for them, and re-layouts  27.1 us
    pallas_call x1, Pallas kernels, factor_step(): pl.pallas_call(functools.partial(factor_kernel, groups, talls), out_shape...  20.6 us
    pallas_call x10, Pallas kernels, gram_step(): pl.pallas_call(functools.partial(gram_kernel, first, groups, len(earlier)...  14.5 us
    all_to_all x1, blocking collectives, total_sum(): lax.all_to_all(flat.reshape(devices, share, BLOCK), AXES, split_axis=0, c...  13.2 us
  transfers between devices with their start and end apart: 47, of which 13 were waited for; matrix products, arithmetic and copies ran while one was open for 0% of the time, Pallas kernels for 5%

profile of v3, /device:TPU:0, one launch (start us, length us, event | category | flops | bytes accessed | tf_op | source)
XLA Modules:
  0.0 499.4 jit_solution(16878562985958197259)
XLA Ops:
  7.2 4.0 copy-done
  11.6 3.1 collective-permute-start.18
  14.7 2.6 collective-permute-start.19
  21.1 6.6 %collective-permute-start.25 = (f32[8,32,128]{2,1,0:T(8,128)S(1)}, f32[8,32,128]{2,1,0:T(8,128)S(1)}, u32[]{:S(2)}, u32[]{:S(2)}) collective-permute-start(f32[8,32,128]{2,1,0:T(8,128)S(1)} %get-tuple-element.139), channel_id=1, source_target_pairs={{0,16},{8,24},{16,0},{24,8},{1,17},{9,25},{17,1},{25,9},{2,18},{10... | collective-permute-start | bytes 393224 | tf_op jit(solution)/shard_map/ppermute | solution.py:318
  27.7 3.7 collective-permute-start.26
  32.5 6.0 %collective-permute-start.3 = (f32[8,96,128]{2,1,0:T(8,128)S(1)}, f32[8,96,128]{2,1,0:T(8,128)S(1)}, u32[]{:S(2)}, u32[]{:S(2)}) collective-permute-start(f32[8,96,128]{2,1,0:T(8,128)S(1)} %get-tuple-element.99), channel_id=1, source_target_pairs={{0,8},{8,16},{16,24},{24,0},{1,9},{9,17},{17,25},{25,1},{2,10},{10... | collective-permute-start | bytes 1179656 | tf_op jit(solution)/shard_map/ppermute | solution.py:318
  39.8 22.6 %collective-permute-done.25.refs_2_ = f32[8,32,128]{2,1,0:T(8,128)S(1)} collective-permute-done((f32[8,32,128]{2,1,0:T(8,128)S(1)}, f32[8,32,128]{2,1,0:T(8,128)S(1)}, u32[]{:S(2)}, u32[]{:S(2)}) %collective-permute-start.25) | collective-permute-done | bytes 131104 | tf_op jit(solution)/shard_map/ppermute | solution.py:318
  62.4 4.4 collective-permute-start.5
  69.0 7.5 %collective-permute-done.28.refs_2_ = f32[8,32,128]{2,1,0:T(8,128)S(1)} collective-permute-done((f32[8,32,128]{2,1,0:T(8,128)S(1)}, f32[8,32,128]{2,1,0:T(8,128)S(1)}, u32[]{:S(2)}, u32[]{:S(2)}) %collective-permute-start.28) | collective-permute-done | bytes 131104 | tf_op jit(solution)/shard_map/ppermute | solution.py:318
  76.5 10.6 %collective-permute-start.6 = (f32[8,96,128]{2,1,0:T(8,128)S(1)}, f32[8,96,128]{2,1,0:T(8,128)S(1)}, u32[]{:S(2)}, u32[]{:S(2)}) collective-permute-start(f32[8,96,128]{2,1,0:T(8,128)S(1)} %get-tuple-element.103), channel_id=1, source_target_pairs={{0,8},{8,16},{16,24},{24,0},{1,9},{9,17},{17,25},{25,1},{2,10},{10... | collective-permute-start | bytes 1179656 | tf_op jit(solution)/shard_map/ppermute | solution.py:318
  87.1 2.5 collective-permute-start.9
  91.1 2.9 collective-permute-start.11
  95.0 2.7 collective-permute-done.5.refs_3_
  97.7 23.3 %collective-permute-start.12 = (f32[8,96,128]{2,1,0:T(8,128)S(1)}, f32[8,96,128]{2,1,0:T(8,128)S(1)}, u32[]{:S(2)}, u32[]{:S(2)}) collective-permute-start(f32[8,96,128]{2,1,0:T(8,128)S(1)} %get-tuple-element.111), channel_id=1, source_target_pairs={{0,8},{8,16},{16,24},{24,0},{1,9},{9,17},{17,25},{25,1},{2,10},{10... | collective-permute-start | bytes 1179656 | tf_op jit(solution)/shard_map/ppermute | solution.py:318
  123.4 22.4 %collective-permute-done.10.refs_2_ = f32[8,96,128]{2,1,0:T(8,128)S(1)} collective-permute-done((f32[8,96,128]{2,1,0:T(8,128)S(1)}, f32[8,96,128]{2,1,0:T(8,128)S(1)}, u32[]{:S(2)}, u32[]{:S(2)}) %collective-permute-start.10) | collective-permute-done | bytes 393248 | tf_op jit(solution)/shard_map/ppermute | solution.py:318
  145.8 19.3 %collective-permute-start.8 = (f32[8,96,128]{2,1,0:T(8,128)S(1)}, f32[8,96,128]{2,1,0:T(8,128)S(1)}, u32[]{:S(2)}, u32[]{:S(2)}) collective-permute-start(f32[8,96,128]{2,1,0:T(8,128)S(1)} %get-tuple-element.105), channel_id=1, source_target_pairs={{0,24},{8,0},{16,8},{24,16},{1,25},{9,1},{17,9},{25,17},{2,26},{10... | collective-permute-start | bytes 1179656 | tf_op jit(solution)/shard_map/ppermute | solution.py:318
  166.3 12.8 %collective-permute-start = (f32[8,96,128]{2,1,0:T(8,128)S(1)}, f32[8,96,128]{2,1,0:T(8,128)S(1)}, u32[]{:S(2)}, u32[]{:S(2)}) collective-permute-start(f32[8,96,128]{2,1,0:T(8,128)S(1)} %get-tuple-element.95), channel_id=1, source_target_pairs={{0,8},{8,16},{16,24},{24,0},{1,9},{9,17},{17,25},{25,1},{2,10},{10... | collective-permute-start | bytes 1179656 | tf_op jit(solution)/shard_map/ppermute | solution.py:318
  181.1 17.8 %collective-permute-start.2 = (f32[8,96,128]{2,1,0:T(8,128)S(1)}, f32[8,96,128]{2,1,0:T(8,128)S(1)}, u32[]{:S(2)}, u32[]{:S(2)}) collective-permute-start(f32[8,96,128]{2,1,0:T(8,128)S(1)} %get-tuple-element.97), channel_id=1, source_target_pairs={{0,24},{8,0},{16,8},{24,16},{1,25},{9,1},{17,9},{25,17},{2,26},{10... | collective-permute-start | bytes 1179656 | tf_op jit(solution)/shard_map/ppermute | solution.py:318
  207.7 8.0 %collective-permute-start.23 = (f32[8,32,128]{2,1,0:T(8,128)S(1)}, f32[8,32,128]{2,1,0:T(8,128)S(1)}, u32[]{:S(2)}, u32[]{:S(2)}) collective-permute-start(f32[8,32,128]{2,1,0:T(8,128)S(1)} %get-tuple-element.134), channel_id=1, source_target_pairs={{0,24},{8,0},{16,8},{24,16},{1,25},{9,1},{17,9},{25,17},{2,26},{10... | collective-permute-start | bytes 393224 | tf_op jit(solution)/shard_map/ppermute | solution.py:318
  222.0 17.5 %collective-permute-done.22.refs_2_ = f32[8,32,128]{2,1,0:T(8,128)S(1)} collective-permute-done((f32[8,32,128]{2,1,0:T(8,128)S(1)}, f32[8,32,128]{2,1,0:T(8,128)S(1)}, u32[]{:S(2)}, u32[]{:S(2)}) %collective-permute-start.22) | collective-permute-done | bytes 131104 | tf_op jit(solution)/shard_map/ppermute | solution.py:318
  241.9 3.4 collective-permute-start.17
  255.6 13.2 %all_to_all.10 = f32[32,16,128]{2,1,0:T(8,128)S(1)} all-to-all(f32[32,16,128]{2,1,0:T(8,128)S(1)} %bitcast.4), channel_id=1, replica_groups=mesh['gx'=4,'gy'=2,'gz'=4] {'gx','gy','gz'}, dimensions={0} | all-to-all | bytes 524288 | tf_op jit(solution)/shard_map/all_to_all | solution.py:327
  269.5 2.6 all-to-all-start.1
  272.9 134.1 %all-reduce.2.cloned.1.call-done.refs_0_ = f32[768,128]{1,0:T(8,128)} async-done(((f32[768,128]{1,0:T(8,128)}), f32[768,128]{1,0:T(8,128)}) %all-reduce.2.cloned.1.call-update) | async-done | bytes 393232 | tf_op jit(solution)/shard_map/psum | solution.py:364
  408.1 20.6 %shard_map.50 = (f32[128,128]{1,0:T(8,128)}, f32[128,512]{1,0:T(8,128)S(1)}) custom-call(s32[1]{0:T(128)} %bitcast.me_ref, f32[768,128]{1,0:T(8,128)S(1)} %copy-done.14, f32[512,128]{1,0:T(8,128)S(1)} %bitcast.3), custom_call_target="tpu_custom_call" | custom-call | tf_op jit(solution)/shard_map/pallas_call | solution.py:223
  455.3 2.9 collective-permute-start.38
  458.2 2.6 collective-permute-done.34.refs_6_
  464.3 3.6 collective-permute-start.40
  468.0 4.5 collective-permute-start.41
  474.2 3.4 collective-permute-start.43
  477.6 6.0 %collective-permute-start.44 = (f32[32,8,128]{2,1,0:T(8,128)S(1)}, f32[32,8,128]{2,1,0:T(8,128)S(1)}, u32[]{:S(2)}, u32[]{:S(2)}) collective-permute-start(f32[32,8,128]{2,1,0:T(8,128)S(1)} %get-tuple-element.185), channel_id=1, source_target_pairs={{0,24},{8,0},{16,8},{24,16},{1,25},{9,1},{17,9},{25,17},{2,26},{10... | collective-permute-start | bytes 393224 | tf_op jit(solution)/shard_map/ppermute | solution.py:318
  483.9 7.0 %collective-permute-done.43.refs_18_ = f32[32,8,128]{2,1,0:T(8,128)S(1)} collective-permute-done((f32[32,8,128]{2,1,0:T(8,128)S(1)}, f32[32,8,128]{2,1,0:T(8,128)S(1)}, u32[]{:S(2)}, u32[]{:S(2)}) %collective-permute-start.43) | collective-permute-done | bytes 131104 | tf_op jit(solution)/shard_map/ppermute | solution.py:318
  (163 shorter events, 81.0 us)
Async XLA Ops:
  19.0 19.5 %collective-permute-start.21 = (f32[8,32,128]{2,1,0:T(8,128)S(1)}, f32[8,32,128]{2,1,0:T(8,128)S(1)}, u32[]{:S(2)}, u32[]{:S(2)}) collective-permute-start(f32[8,32,128]{2,1,0:T(8,128)S(1)} %get-tuple-element.132), channel_id=1, source_target_pairs={{0,8},{8,16},{16,24},{24,0},{1,9},{9,17},{17,25},{25,1},{2,10},{10... | collective-permute-start | bytes 393224 | tf_op jit(solution)/shard_map/ppermute | solution.py:318
  20.2 19.2 %collective-permute-start.24 = (f32[8,32,128]{2,1,0:T(8,128)S(1)}, f32[8,32,128]{2,1,0:T(8,128)S(1)}, u32[]{:S(2)}, u32[]{:S(2)}) collective-permute-start(f32[8,32,128]{2,1,0:T(8,128)S(1)} %get-tuple-element.138), channel_id=1, source_target_pairs={{0,8},{8,16},{16,24},{24,0},{1,9},{9,17},{17,25},{25,1},{2,10},{10... | collective-permute-start | bytes 393224 | tf_op jit(solution)/shard_map/ppermute | solution.py:318
  21.1 41.3 %collective-permute-start.25 = (f32[8,32,128]{2,1,0:T(8,128)S(1)}, f32[8,32,128]{2,1,0:T(8,128)S(1)}, u32[]{:S(2)}, u32[]{:S(2)}) collective-permute-start(f32[8,32,128]{2,1,0:T(8,128)S(1)} %get-tuple-element.139), channel_id=1, source_target_pairs={{0,16},{8,24},{16,0},{24,8},{1,17},{9,25},{17,1},{25,9},{2,18},{10... | collective-permute-start | bytes 393224 | tf_op jit(solution)/shard_map/ppermute | solution.py:318
  27.7 34.7 %collective-permute-start.26 = (f32[8,32,128]{2,1,0:T(8,128)S(1)}, f32[8,32,128]{2,1,0:T(8,128)S(1)}, u32[]{:S(2)}, u32[]{:S(2)}) collective-permute-start(f32[8,32,128]{2,1,0:T(8,128)S(1)} %get-tuple-element.140), channel_id=1, source_target_pairs={{0,24},{8,0},{16,8},{24,16},{1,25},{9,1},{17,9},{25,17},{2,26},{10... | collective-permute-start | bytes 393224 | tf_op jit(solution)/shard_map/ppermute | solution.py:318
  32.5 57.0 %collective-permute-start.3 = (f32[8,96,128]{2,1,0:T(8,128)S(1)}, f32[8,96,128]{2,1,0:T(8,128)S(1)}, u32[]{:S(2)}, u32[]{:S(2)}) collective-permute-start(f32[8,96,128]{2,1,0:T(8,128)S(1)} %get-tuple-element.99), channel_id=1, source_target_pairs={{0,8},{8,16},{16,24},{24,0},{1,9},{9,17},{17,25},{25,1},{2,10},{10... | collective-permute-start | bytes 1179656 | tf_op jit(solution)/shard_map/ppermute | solution.py:318
  38.5 52.6 %collective-permute-start.4 = (f32[8,96,128]{2,1,0:T(8,128)S(1)}, f32[8,96,128]{2,1,0:T(8,128)S(1)}, u32[]{:S(2)}, u32[]{:S(2)}) collective-permute-start(f32[8,96,128]{2,1,0:T(8,128)S(1)} %get-tuple-element.100), channel_id=1, source_target_pairs={{0,16},{8,24},{16,0},{24,8},{1,17},{9,25},{17,1},{25,9},{2,18},{10... | collective-permute-start | bytes 1179656 | tf_op jit(solution)/shard_map/ppermute | solution.py:318
  39.4 23.0 %collective-permute-start.27 = (f32[8,32,128]{2,1,0:T(8,128)S(1)}, f32[8,32,128]{2,1,0:T(8,128)S(1)}, u32[]{:S(2)}, u32[]{:S(2)}) collective-permute-start(f32[8,32,128]{2,1,0:T(8,128)S(1)} %get-tuple-element.144), channel_id=1, source_target_pairs={{0,8},{8,16},{16,24},{24,0},{1,9},{9,17},{17,25},{25,1},{2,10},{10... | collective-permute-start | bytes 393224 | tf_op jit(solution)/shard_map/ppermute | solution.py:318
  62.4 24.6 %collective-permute-start.29 = (f32[8,32,128]{2,1,0:T(8,128)S(1)}, f32[8,32,128]{2,1,0:T(8,128)S(1)}, u32[]{:S(2)}, u32[]{:S(2)}) collective-permute-start(f32[8,32,128]{2,1,0:T(8,128)S(1)} %get-tuple-element.146), channel_id=1, source_target_pairs={{0,24},{8,0},{16,8},{24,16},{1,25},{9,1},{17,9},{25,17},{2,26},{10... | collective-permute-start | bytes 393224 | tf_op jit(solution)/shard_map/ppermute | solution.py:318
  62.4 35.3 %collective-permute-start.5 = (f32[8,96,128]{2,1,0:T(8,128)S(1)}, f32[8,96,128]{2,1,0:T(8,128)S(1)}, u32[]{:S(2)}, u32[]{:S(2)}) collective-permute-start(f32[8,96,128]{2,1,0:T(8,128)S(1)} %get-tuple-element.101), channel_id=1, source_target_pairs={{0,24},{8,0},{16,8},{24,16},{1,25},{9,1},{17,9},{25,17},{2,26},{10... | collective-permute-start | bytes 1179656 | tf_op jit(solution)/shard_map/ppermute | solution.py:318
  76.5 44.6 %collective-permute-start.6 = (f32[8,96,128]{2,1,0:T(8,128)S(1)}, f32[8,96,128]{2,1,0:T(8,128)S(1)}, u32[]{:S(2)}, u32[]{:S(2)}) collective-permute-start(f32[8,96,128]{2,1,0:T(8,128)S(1)} %get-tuple-element.103), channel_id=1, source_target_pairs={{0,8},{8,16},{16,24},{24,0},{1,9},{9,17},{17,25},{25,1},{2,10},{10... | collective-permute-start | bytes 1179656 | tf_op jit(solution)/shard_map/ppermute | solution.py:318
  87.1 34.0 %collective-permute-start.9 = (f32[8,96,128]{2,1,0:T(8,128)S(1)}, f32[8,96,128]{2,1,0:T(8,128)S(1)}, u32[]{:S(2)}, u32[]{:S(2)}) collective-permute-start(f32[8,96,128]{2,1,0:T(8,128)S(1)} %get-tuple-element.107), channel_id=1, source_target_pairs={{0,8},{8,16},{16,24},{24,0},{1,9},{9,17},{17,25},{25,1},{2,10},{10... | collective-permute-start | bytes 1179656 | tf_op jit(solution)/shard_map/ppermute | solution.py:318
  89.6 56.3 %collective-permute-start.10 = (f32[8,96,128]{2,1,0:T(8,128)S(1)}, f32[8,96,128]{2,1,0:T(8,128)S(1)}, u32[]{:S(2)}, u32[]{:S(2)}) collective-permute-start(f32[8,96,128]{2,1,0:T(8,128)S(1)} %get-tuple-element.108), channel_id=1, source_target_pairs={{0,16},{8,24},{16,0},{24,8},{1,17},{9,25},{17,1},{25,9},{2,18},{10... | collective-permute-start | bytes 1179656 | tf_op jit(solution)/shard_map/ppermute | solution.py:318
  91.1 54.7 %collective-permute-start.11 = (f32[8,96,128]{2,1,0:T(8,128)S(1)}, f32[8,96,128]{2,1,0:T(8,128)S(1)}, u32[]{:S(2)}, u32[]{:S(2)}) collective-permute-start(f32[8,96,128]{2,1,0:T(8,128)S(1)} %get-tuple-element.109), channel_id=1, source_target_pairs={{0,24},{8,0},{16,8},{24,16},{1,25},{9,1},{17,9},{25,17},{2,26},{10... | collective-permute-start | bytes 1179656 | tf_op jit(solution)/shard_map/ppermute | solution.py:318
  97.7 68.5 %collective-permute-start.12 = (f32[8,96,128]{2,1,0:T(8,128)S(1)}, f32[8,96,128]{2,1,0:T(8,128)S(1)}, u32[]{:S(2)}, u32[]{:S(2)}) collective-permute-start(f32[8,96,128]{2,1,0:T(8,128)S(1)} %get-tuple-element.111), channel_id=1, source_target_pairs={{0,8},{8,16},{16,24},{24,0},{1,9},{9,17},{17,25},{25,1},{2,10},{10... | collective-permute-start | bytes 1179656 | tf_op jit(solution)/shard_map/ppermute | solution.py:318
  121.1 60.0 %collective-permute-start.13 = (f32[8,96,128]{2,1,0:T(8,128)S(1)}, f32[8,96,128]{2,1,0:T(8,128)S(1)}, u32[]{:S(2)}, u32[]{:S(2)}) collective-permute-start(f32[8,96,128]{2,1,0:T(8,128)S(1)} %get-tuple-element.112), channel_id=1, source_target_pairs={{0,16},{8,24},{16,0},{24,8},{1,17},{9,25},{17,1},{25,9},{2,18},{10... | collective-permute-start | bytes 1179656 | tf_op jit(solution)/shard_map/ppermute | solution.py:318
  121.1 60.0 %collective-permute-start.14 = (f32[8,96,128]{2,1,0:T(8,128)S(1)}, f32[8,96,128]{2,1,0:T(8,128)S(1)}, u32[]{:S(2)}, u32[]{:S(2)}) collective-permute-start(f32[8,96,128]{2,1,0:T(8,128)S(1)} %get-tuple-element.113), channel_id=1, source_target_pairs={{0,24},{8,0},{16,8},{24,16},{1,25},{9,1},{17,9},{25,17},{2,26},{10... | collective-permute-start | bytes 1179656 | tf_op jit(solution)/shard_map/ppermute | solution.py:318
  145.8 61.9 %collective-permute-start.7 = (f32[8,96,128]{2,1,0:T(8,128)S(1)}, f32[8,96,128]{2,1,0:T(8,128)S(1)}, u32[]{:S(2)}, u32[]{:S(2)}) collective-permute-start(f32[8,96,128]{2,1,0:T(8,128)S(1)} %get-tuple-element.104), channel_id=1, source_target_pairs={{0,16},{8,24},{16,0},{24,8},{1,17},{9,25},{17,1},{25,9},{2,18},{10... | collective-permute-start | bytes 1179656 | tf_op jit(solution)/shard_map/ppermute | solution.py:318
  145.8 61.9 %collective-permute-start.8 = (f32[8,96,128]{2,1,0:T(8,128)S(1)}, f32[8,96,128]{2,1,0:T(8,128)S(1)}, u32[]{:S(2)}, u32[]{:S(2)}) collective-permute-start(f32[8,96,128]{2,1,0:T(8,128)S(1)} %get-tuple-element.105), channel_id=1, source_target_pairs={{0,24},{8,0},{16,8},{24,16},{1,25},{9,1},{17,9},{25,17},{2,26},{10... | collective-permute-start | bytes 1179656 | tf_op jit(solution)/shard_map/ppermute | solution.py:318
  166.3 75.6 %collective-permute-start = (f32[8,96,128]{2,1,0:T(8,128)S(1)}, f32[8,96,128]{2,1,0:T(8,128)S(1)}, u32[]{:S(2)}, u32[]{:S(2)}) collective-permute-start(f32[8,96,128]{2,1,0:T(8,128)S(1)} %get-tuple-element.95), channel_id=1, source_target_pairs={{0,8},{8,16},{16,24},{24,0},{1,9},{9,17},{17,25},{25,1},{2,10},{10... | collective-permute-start | bytes 1179656 | tf_op jit(solution)/shard_map/ppermute | solution.py:318
  181.0 69.2 %collective-permute-start.1 = (f32[8,96,128]{2,1,0:T(8,128)S(1)}, f32[8,96,128]{2,1,0:T(8,128)S(1)}, u32[]{:S(2)}, u32[]{:S(2)}) collective-permute-start(f32[8,96,128]{2,1,0:T(8,128)S(1)} %get-tuple-element.96), channel_id=1, source_target_pairs={{0,16},{8,24},{16,0},{24,8},{1,17},{9,25},{17,1},{25,9},{2,18},{10... | collective-permute-start | bytes 1179656 | tf_op jit(solution)/shard_map/ppermute | solution.py:318
  181.1 69.1 %collective-permute-start.2 = (f32[8,96,128]{2,1,0:T(8,128)S(1)}, f32[8,96,128]{2,1,0:T(8,128)S(1)}, u32[]{:S(2)}, u32[]{:S(2)}) collective-permute-start(f32[8,96,128]{2,1,0:T(8,128)S(1)} %get-tuple-element.97), channel_id=1, source_target_pairs={{0,24},{8,0},{16,8},{24,16},{1,25},{9,1},{17,9},{25,17},{2,26},{10... | collective-permute-start | bytes 1179656 | tf_op jit(solution)/shard_map/ppermute | solution.py:318
  207.7 31.8 %collective-permute-start.22 = (f32[8,32,128]{2,1,0:T(8,128)S(1)}, f32[8,32,128]{2,1,0:T(8,128)S(1)}, u32[]{:S(2)}, u32[]{:S(2)}) collective-permute-start(f32[8,32,128]{2,1,0:T(8,128)S(1)} %get-tuple-element.133), channel_id=1, source_target_pairs={{0,16},{8,24},{16,0},{24,8},{1,17},{9,25},{17,1},{25,9},{2,18},{10... | collective-permute-start | bytes 393224 | tf_op jit(solution)/shard_map/ppermute | solution.py:318
  207.7 31.8 %collective-permute-start.23 = (f32[8,32,128]{2,1,0:T(8,128)S(1)}, f32[8,32,128]{2,1,0:T(8,128)S(1)}, u32[]{:S(2)}, u32[]{:S(2)}) collective-permute-start(f32[8,32,128]{2,1,0:T(8,128)S(1)} %get-tuple-element.134), channel_id=1, source_target_pairs={{0,24},{8,0},{16,8},{24,16},{1,25},{9,1},{17,9},{25,17},{2,26},{10... | collective-permute-start | bytes 393224 | tf_op jit(solution)/shard_map/ppermute | solution.py:318
  269.5 137.4 %all-to-all-start.1 = ((f32[32,16,128]{2,1,0:T(8,128)}), f32[32,16,128]{2,1,0:T(8,128)S(1)}, u32[]{:S(2)}, u32[]{:S(2)}) async-start(f32[32,16,128]{2,1,0:T(8,128)} %broadcast_in_dim.2), calls=%async_computation.1 | async-start | bytes 524288 | tf_op jit(solution)/shard_map/all_to_all | solution.py:330
  272.1 134.8 %all-reduce.2.cloned.1.call-start = ((), (), s32[]{:S(2)}) async-start(), calls=%async_computation.2 | async-start | bytes 786432 | tf_op jit(solution)/shard_map/psum | solution.py:364
  433.9 17.5 %collective-permute-start.30 = (f32[32,8,128]{2,1,0:T(8,128)S(1)}, f32[32,8,128]{2,1,0:T(8,128)S(1)}, u32[]{:S(2)}, u32[]{:S(2)}) collective-permute-start(f32[32,8,128]{2,1,0:T(8,128)S(1)} %get-tuple-element.159), channel_id=1, source_target_pairs={{0,8},{8,16},{16,24},{24,0},{1,9},{9,17},{17,25},{25,1},{2,10},{10... | collective-permute-start | bytes 393224 | tf_op jit(solution)/shard_map/ppermute | solution.py:318
  435.4 18.4 %collective-permute-start.31 = (f32[32,8,128]{2,1,0:T(8,128)S(1)}, f32[32,8,128]{2,1,0:T(8,128)S(1)}, u32[]{:S(2)}, u32[]{:S(2)}) collective-permute-start(f32[32,8,128]{2,1,0:T(8,128)S(1)} %get-tuple-element.160), channel_id=1, source_target_pairs={{0,16},{8,24},{16,0},{24,8},{1,17},{9,25},{17,1},{25,9},{2,18},{10... | collective-permute-start | bytes 393224 | tf_op jit(solution)/shard_map/ppermute | solution.py:318
  436.8 17.1 %collective-permute-start.32 = (f32[32,8,128]{2,1,0:T(8,128)S(1)}, f32[32,8,128]{2,1,0:T(8,128)S(1)}, u32[]{:S(2)}, u32[]{:S(2)}) collective-permute-start(f32[32,8,128]{2,1,0:T(8,128)S(1)} %get-tuple-element.161), channel_id=1, source_target_pairs={{0,24},{8,0},{16,8},{24,16},{1,25},{9,1},{17,9},{25,17},{2,26},{10... | collective-permute-start | bytes 393224 | tf_op jit(solution)/shard_map/ppermute | solution.py:318
  441.8 19.0 %collective-permute-start.34 = (f32[32,8,128]{2,1,0:T(8,128)S(1)}, f32[32,8,128]{2,1,0:T(8,128)S(1)}, u32[]{:S(2)}, u32[]{:S(2)}) collective-permute-start(f32[32,8,128]{2,1,0:T(8,128)S(1)} %get-tuple-element.166), channel_id=1, source_target_pairs={{0,16},{8,24},{16,0},{24,8},{1,17},{9,25},{17,1},{25,9},{2,18},{10... | collective-permute-start | bytes 393224 | tf_op jit(solution)/shard_map/ppermute | solution.py:318
  453.8 18.8 %collective-permute-start.37 = (f32[32,8,128]{2,1,0:T(8,128)S(1)}, f32[32,8,128]{2,1,0:T(8,128)S(1)}, u32[]{:S(2)}, u32[]{:S(2)}) collective-permute-start(f32[32,8,128]{2,1,0:T(8,128)S(1)} %get-tuple-element.172), channel_id=1, source_target_pairs={{0,16},{8,24},{16,0},{24,8},{1,17},{9,25},{17,1},{25,9},{2,18},{10... | collective-permute-start | bytes 393224 | tf_op jit(solution)/shard_map/ppermute | solution.py:318
  455.3 18.9 %collective-permute-start.38 = (f32[32,8,128]{2,1,0:T(8,128)S(1)}, f32[32,8,128]{2,1,0:T(8,128)S(1)}, u32[]{:S(2)}, u32[]{:S(2)}) collective-permute-start(f32[32,8,128]{2,1,0:T(8,128)S(1)} %get-tuple-element.173), channel_id=1, source_target_pairs={{0,24},{8,0},{16,8},{24,16},{1,25},{9,1},{17,9},{25,17},{2,26},{10... | collective-permute-start | bytes 393224 | tf_op jit(solution)/shard_map/ppermute | solution.py:318
  464.3 19.5 %collective-permute-start.40 = (f32[32,8,128]{2,1,0:T(8,128)S(1)}, f32[32,8,128]{2,1,0:T(8,128)S(1)}, u32[]{:S(2)}, u32[]{:S(2)}) collective-permute-start(f32[32,8,128]{2,1,0:T(8,128)S(1)} %get-tuple-element.178), channel_id=1, source_target_pairs={{0,16},{8,24},{16,0},{24,8},{1,17},{9,25},{17,1},{25,9},{2,18},{10... | collective-permute-start | bytes 393224 | tf_op jit(solution)/shard_map/ppermute | solution.py:318
  (50 other events, 433.8 us)
Sparse Core Ops, SparseCore 0:
  278.3 128.6 all-reduce.1

commit v4 on v3

--- a/solution.py
+++ b/solution.py
@@ -36,97 +36,114 @@
     return lax.dot_general(left, right, (contract, ((), ())), preferred_element_type=jnp.float32)
 
 
-def pack_kernel(groups, x0, tall, start, per, steps, me_ref, snapshot_ref, *refs):
-    outs, held, sems = refs[:groups], refs[groups], refs[groups + 1]
+def pack_kernel(groups, per, pieces, me_ref, snapshot_ref, *refs):
+    outs, refs = refs[: groups * len(pieces)], refs[groups * len(pieces) :]
+    helds, sems = refs[:-1], refs[-1]
     copies = []
-    for shift in [*range(1, groups), 0]:
-        owner = lax.rem(me_ref[0] + shift, groups)
-        first = pl.multiple_of(owner * per + start, SUB)
-        source = snapshot_ref.at[pl.ds(x0, tall), pl.ds(first, steps), :]
-        copy = pltpu.make_async_copy(source, held.at[shift], sems.at[shift])
-        copy.start()
-        copies.append((shift, copy))
-    for shift, copy in copies:
+    for index, (x0, tall, start, steps) in enumerate(pieces):
+        for shift in [*range(1, groups), 0]:
+            owner = lax.rem(me_ref[0] + shift, groups)
+            first = pl.multiple_of(owner * per + start, SUB)
+            source = snapshot_ref.at[pl.ds(x0, tall), pl.ds(first, steps), :]
+            copy = pltpu.make_async_copy(source, helds[index].at[shift], sems.at[index * groups + shift])
+            copy.start()
+            copies.append((index, shift, copy))
+    for index, shift, copy in copies:
         copy.wait()
-        for step in range(steps):
-            outs[shift][step] = held[shift, :, step, :]
-
-
-def pack(me, snapshot, groups, x0, tall, start, steps):
+        for step in range(pieces[index][3]):
+            outs[index * groups + shift][step] = helds[index][shift, :, step, :]
+
+
+def pack(me, snapshot, groups, pieces, limit):
     _, ylocal, zlocal = snapshot.shape
     per = ylocal // groups
-    shape = (steps, tall, zlocal)
-    if steps % SUB or per % SUB:
+    if per % SUB or any(steps % SUB for _, _, _, steps in pieces):
         parts = []
+        for x0, tall, start, steps in pieces:
+            for shift in range(groups):
+                first = lax.rem(me[0] + shift, groups) * per + start
+                piece = lax.dynamic_slice_in_dim(snapshot[x0 : x0 + tall], first, steps, 1)
+                parts.append(jnp.swapaxes(piece, 0, 1))
+    else:
+        outs, helds = [], []
+        for _, tall, _, steps in pieces:
+            outs += [jax.ShapeDtypeStruct((steps, tall, zlocal), jnp.float32)] * groups
+            helds.append(pltpu.VMEM((groups, tall, steps, zlocal), jnp.float32))
+        parts = pl.pallas_call(
+            functools.partial(pack_kernel, groups, per, tuple(pieces)),
+            out_shape=tuple(outs),
+            in_specs=[SMEM, HBM],
+            out_specs=(VMEM,) * len(outs),
+            scratch_shapes=[*helds, pltpu.SemaphoreType.DMA((len(outs),))],
+            compiler_params=pltpu.CompilerParams(vmem_limit_bytes=limit),
+            cost_estimate=pl.CostEstimate(
+                flops=0, bytes_accessed=8 * sum(groups * tall * steps * zlocal for _, tall, _, steps in pieces), transcendentals=0
+            ),
+        )(me, snapshot)
+    return [list(parts[at : at + groups]) for at in range(0, len(parts), groups)]
+
+
+def gram_kernel(first, groups, chunks, earlier, me_ref, *refs):
+    parts, refs = refs[:groups], refs[groups:]
+    held, refs = refs[: 2 * chunks * earlier], refs[2 * chunks * earlier :]
+    old_ref, refs = (None, refs) if first else (refs[0], refs[1:])
+    out_ref, made = refs[0], refs[1:]
+    wide, tall, zlocal = parts[0].shape
+    steps = wide // chunks
+    last = ((1,), (1,))
+    for chunk in range(chunks):
+        high_ref, low_ref = made[2 * chunk : 2 * chunk + 2]
         for shift in range(groups):
-            first = lax.rem(me[0] + shift, groups) * per + start
-            piece = lax.dynamic_slice_in_dim(snapshot[x0 : x0 + tall], first, steps, 1)
-            parts.append(jnp.swapaxes(piece, 0, 1))
-        return parts
-    return pl.pallas_call(
-        functools.partial(pack_kernel, groups, x0, tall, start, per, steps),
-        out_shape=(jax.ShapeDtypeStruct(shape, jnp.float32),) * groups,
-        in_specs=[SMEM, HBM],
-        out_specs=(VMEM,) * groups,
-        scratch_shapes=[
-            pltpu.VMEM((groups, tall, steps, zlocal), jnp.float32),
-            pltpu.SemaphoreType.DMA((groups,)),
-        ],
-        compiler_params=PARAMS,
-        cost_estimate=pl.CostEstimate(flops=0, bytes_accessed=8 * groups * steps * tall * zlocal, transcendentals=0),
-    )(me, snapshot)
-
-
-def gram_kernel(first, groups, earlier, me_ref, *refs):
-    parts, refs = refs[:groups], refs[groups:]
-    highs, lows, refs = list(refs[:earlier]), list(refs[earlier : 2 * earlier]), refs[2 * earlier :]
-    old_ref, (out_ref, high_ref, low_ref) = (None, refs) if first else (refs[0], refs[1:])
-    steps, tall, zlocal = parts[0].shape
-    for shift in range(groups):
-        owner = lax.rem(me_ref[0] + groups - shift, groups)
-        rows = pl.ds(pl.multiple_of(owner * tall, HALF), tall)
-        for step in range(steps):
-            high, low = split(parts[shift][step])
-            columns = slice(step * zlocal, (step + 1) * zlocal)
-            high_ref[rows, columns] = high
-            low_ref[rows, columns] = low
-    last = ((1,), (1,))
-    slot = 0
-    for row in range(groups * tall // BLOCK):
-        mine = slice(row * BLOCK, (row + 1) * BLOCK)
-        for other_high, other_low in [*zip(highs, lows), (high_ref, low_ref)]:
-            upto = slice(0, (row + 1) * BLOCK if other_high is high_ref else other_high.shape[0])
-            total = dot(high_ref[mine, :], other_high[upto, :], last)
-            total += dot(high_ref[mine, :], other_low[upto, :], last)
-            total += dot(low_ref[mine, :], other_high[upto, :], last)
-            for column in range(upto.stop // BLOCK):
-                at = slice(slot * BLOCK, (slot + 1) * BLOCK)
-                block = total[:, column * BLOCK : (column + 1) * BLOCK]
-                out_ref[at, :] = block if first else block + old_ref[at, :]
-                slot += 1
+            owner = lax.rem(me_ref[0] + groups - shift, groups)
+            rows = pl.ds(pl.multiple_of(owner * tall, HALF), tall)
+            for step in range(steps):
+                high, low = split(parts[shift][chunk * steps + step])
+                columns = slice(step * zlocal, (step + 1) * zlocal)
+                high_ref[rows, columns] = high
+                low_ref[rows, columns] = low
+        pairs = held[2 * chunk * earlier : 2 * (chunk + 1) * earlier]
+        pairs = [*zip(pairs[::2], pairs[1::2]), (high_ref, low_ref)]
+        slot = 0
+        for row in range(groups * tall // BLOCK):
+            mine = slice(row * BLOCK, (row + 1) * BLOCK)
+            for other_high, other_low in pairs:
+                upto = slice(0, (row + 1) * BLOCK if other_high is high_ref else other_high.shape[0])
+                total = dot(high_ref[mine, :], other_high[upto, :], last)
+                total += dot(high_ref[mine, :], other_low[upto, :], last)
+                total += dot(low_ref[mine, :], other_high[upto, :], last)
+                for column in range(upto.stop // BLOCK):
+                    at = slice(slot * BLOCK, (slot + 1) * BLOCK)
+                    block = total[:, column * BLOCK : (column + 1) * BLOCK]
+                    if chunk:
+                        block += out_ref[at, :]
+                    elif not first:
+                        block += old_ref[at, :]
+                    out_ref[at, :] = block
+                    slot += 1
 
 
 def gram_step(me, parts, earlier, old):
-    groups = len(parts)
-    steps, tall, zlocal = parts[0].shape
+    groups, chunks = len(parts), len(earlier)
+    wide, tall, zlocal = parts[0].shape
     rows = groups * tall
-    before = sum(high.shape[0] for high, _ in earlier)
+    before = sum(high.shape[0] for high, _ in earlier[0])
     done, count = before // BLOCK, rows // BLOCK
     slots = done * count + count * (count + 1) // 2
     first = old is None
-    half = jax.ShapeDtypeStruct((rows, steps * zlocal), jnp.bfloat16)
-    operands = [me, *parts, *(high for high, _ in earlier), *(low for _, low in earlier)]
+    half = jax.ShapeDtypeStruct((rows, wide // chunks * zlocal), jnp.bfloat16)
+    operands = [me, *parts, *(half for held in earlier for pair in held for half in pair)]
     operands += [] if first else [old]
-    return pl.pallas_call(
-        functools.partial(gram_kernel, first, groups, len(earlier)),
-        out_shape=(jax.ShapeDtypeStruct((slots * BLOCK, BLOCK), jnp.float32), half, half),
+    total, *made = pl.pallas_call(
+        functools.partial(gram_kernel, first, groups, chunks, len(earlier[0])),
+        out_shape=(jax.ShapeDtypeStruct((slots * BLOCK, BLOCK), jnp.float32),) + (half,) * (2 * chunks),
         in_specs=[SMEM] + [VMEM] * (len(operands) - 1),
-        out_specs=(VMEM,) * 3,
+        out_specs=(VMEM,) * (1 + 2 * chunks),
         compiler_params=PARAMS,
         cost_estimate=pl.CostEstimate(
-            flops=6 * slots * BLOCK * BLOCK * steps * zlocal, bytes_accessed=8 * rows * steps * zlocal, transcendentals=0
+            flops=6 * slots * BLOCK * BLOCK * wide * zlocal, bytes_accessed=8 * rows * wide * zlocal, transcendentals=0
         ),
     )(*operands)
+    return total, list(zip(made[::2], made[1::2]))
 
 
 def inverse_cholesky(a_ref, b_ref, w_ref):
@@ -319,16 +336,20 @@
     return moved
 
 
-def total_sum(blocks):
-    devices = lax.axis_size(AXES)
+def total_sum(blocks, stages):
     rows = blocks.shape[0]
-    share = -(-rows // devices)
-    flat = jnp.pad(blocks, ((0, share * devices - rows), (0, 0)))
-    parts = lax.all_to_all(flat.reshape(devices, share, BLOCK), AXES, split_axis=0, concat_axis=0, tiled=True)
-    mine = jnp.sum(parts, axis=0)
-    spread = jnp.broadcast_to(mine[None], (devices, share, BLOCK))
-    whole = lax.all_to_all(spread, AXES, split_axis=0, concat_axis=0, tiled=True)
-    return whole.reshape(-1, BLOCK)
+    flat = jnp.pad(blocks, ((0, -rows % lax.axis_size(AXES)), (0, 0)))
+    for axes in stages:
+        parts = flat.reshape(lax.axis_size(axes), -1, BLOCK)
+        flat = jnp.sum(lax.all_to_all(parts, axes, split_axis=0, concat_axis=0, tiled=True), axis=0)
+    for axes in reversed(stages):
+        spread = jnp.broadcast_to(flat[None], (lax.axis_size(axes), *flat.shape))
+        flat = lax.all_to_all(spread, axes, split_axis=0, concat_axis=0, tiled=True).reshape(-1, BLOCK)
+    return flat
+
+
+def hold(values, after):
+    return list(lax.optimization_barrier((values, after))[0])
 
 
 def chunk_count(per):
@@ -351,17 +372,35 @@
     starts = [chunk * steps for chunk in range(chunks)]
     talls = phase_sizes(xlocal, groups)
     me = lax.axis_index("gx").astype(jnp.int32).reshape(1)
-    halves = [[] for _ in starts]
-    sums = []
-    x0 = 0
-    for tall in talls:
-        total = None
-        for held, start in zip(halves, starts):
-            parts = exchange(pack(me, snapshot, groups, x0, tall, start, steps))
-            total, high, low = gram_step(me, parts, held, total)
-            held.append((high, low))
-        x0 += tall
-        sums.append(total_sum(total) if x0 == xlocal else lax.psum(total, AXES))
+
+    long = [(0, talls[0], start, steps) for start in starts]
+    cut = per - steps if chunks > 1 else per
+    short = [(talls[0], talls[1], 0, cut)]
+    short += [(talls[0], talls[1], cut, steps)] if chunks > 1 else []
+    packed = pack(me, snapshot, groups, long[:1], 54 * 2**20)
+    packed += pack(me, snapshot, groups, long[1:] + short, 44 * 2**20)
+
+    moved = []
+    for index, parts in enumerate(packed):
+        if index >= 2:
+            parts = hold(parts, moved[index - 2])
+        moved.append(exchange(parts))
+
+    halves = []
+    total = None
+    for parts in moved[:chunks]:
+        total, made = gram_step(me, parts, [[]], total)
+        halves.append(made)
+    sums = [total_sum(total, [("gy", "gz"), "gx"])]
+    total, at = None, 0
+    for parts in moved[chunks:]:
+        count = parts[0].shape[0] // steps
+        total, made = gram_step(me, hold(parts, sums[0]), halves[at : at + count], total)
+        for held, pair in zip(halves[at : at + count], made):
+            held.append(pair)
+        at += count
+    sums.append(total_sum(total, [AXES]))
+
     mine, turned = factor_step(me, sums, groups, talls)
     outs = [exchange(core_step(me, turned, held, groups, zlocal)) for held in halves]
     return (mine, place(me, outs, starts, ylocal))

time: 500 us -> 397 us (0.79)
  waiting for transfers between devices: 223 us -> 106 us
  blocking collectives: 13.2 us -> 82.4 us
  starting transfers between devices: 172 us -> 115 us
  between operations: 14.5 us -> 1.2 us
  local copies, waits for them, and re-layouts: 27.9 us -> 35.7 us
    psum x1 -> x0, waiting for transfers between devices: 134 us -> none  [local(): sums.append(total_sum(total) if x0 == xlocal else lax.psum(total, AXES))]
    all_to_all x1 -> x4, blocking collectives: 13.2 us -> 82.4 us  [the longest x2 61.5 us: total_sum(): lax.all_to_all(parts, axes, split_axis=0, concat_axis=0, tiled=True)]
    ppermute x45 -> x36, starting transfers between devices: 169 us -> 108 us  [exchange(): lax.ppermute(parts[shift], 'gx', [(i, (i + shift) % groups) for i in rang...]
    ppermute x45 -> x36, waiting for transfers between devices: 87.9 us -> 102 us  [exchange(): lax.ppermute(parts[shift], 'gx', [(i, (i + shift) % groups) for i in rang...]
    unnamed x70 -> x98, local copies, waits for them, and re-layouts: 27.1 us -> 34.9 us
    all_to_all x1 -> x2, starting transfers between devices: 2.58 us -> 7.6 us  [the longest x1 3.84 us: total_sum(): lax.all_to_all(spread, axes, split_axis=0, concat_axis=0, tiled=True)]
    pallas_call x20 -> x9, Pallas kernels: 22 us -> 26 us  [the longest x7 17 us: gram_step(): pl.pallas_call(functools.partial(gram_kernel, first, groups, chunks, len(...]
  transfers between devices with their start and end apart: 47 -> 38, of which waited for: 13 -> 12; matrix products, arithmetic and copies ran while one was open for 0% -> 0% of each run, Pallas kernels for 5% -> 4%
where the time goes in v4:
time: 397 us; the launch traced here: 396 us
  starting transfers between devices  115 us (29%)
  waiting for transfers between devices  106 us (27%)
  blocking collectives  82.4 us (21%)
  Pallas kernels  53.2 us (13%)
  local copies, waits for them, and re-layouts  35.7 us (9%)
    ppermute x36, starting transfers between devices, exchange(): lax.ppermute(parts[shift], 'gx', [(i, (i + shift) % groups) for i in rang...  108 us
    ppermute x36, waiting for transfers between devices, exchange(): lax.ppermute(parts[shift], 'gx', [(i, (i + shift) % groups) for i in rang...  102 us
    all_to_all x2, blocking collectives, total_sum(): lax.all_to_all(parts, axes, split_axis=0, concat_axis=0, tiled=True)  61.5 us
    unnamed x98, local copies, waits for them, and re-layouts  34.9 us
    all_to_all x2, blocking collectives, total_sum(): lax.all_to_all(spread, axes, split_axis=0, concat_axis=0, tiled=True)  20.9 us
    pallas_call x1, Pallas kernels, factor_step(): pl.pallas_call(functools.partial(factor_kernel, groups, talls), out_shape...  20.6 us
    pallas_call x7, Pallas kernels, gram_step(): pl.pallas_call(functools.partial(gram_kernel, first, groups, chunks, len(...  17 us
    pallas_call x2, Pallas kernels, pack(): pl.pallas_call(functools.partial(pack_kernel, groups, per, tuple(pieces))...  9 us
  transfers between devices with their start and end apart: 38, of which 12 were waited for; matrix products, arithmetic and copies ran while one was open for 0% of the time, Pallas kernels for 4%

profile of v4, /device:TPU:0, one launch (start us, length us, event | category | flops | bytes accessed | tf_op | source)
XLA Modules:
  0.0 395.7 jit_solution(10911284084920876992)
XLA Ops:
  0.6 3.0 shard_map.31
  3.7 3.1 collective-permute-start
  10.7 6.0 %shard_map.30 = (f32[8,96,128]{2,1,0:T(8,128)S(1)}, f32[8,96,128]{2,1,0:T(8,128)S(1)}, f32[8,96,128]{2,1,0:T(8,128)S(1)}, f32[8,96,128]{2,1,0:T(8,128)S(1)}, f32...) custom-call(s32[1]{0:T(128)} %bitcast.me_ref, ...), custom_call_target="tpu_custom_call" | custom-call | bytes 17825792 | tf_op jit(solution)/shard_map/pallas_call | solution.py:72
  22.1 2.8 collective-permute-start.11
  24.9 11.0 %collective-permute-done.1.refs_2_ = f32[8,96,128]{2,1,0:T(8,128)S(1)} collective-permute-done((f32[8,96,128]{2,1,0:T(8,128)}, f32[8,96,128]{2,1,0:T(8,128)S(1)}, u32[]{:S(2)}, u32[]{:S(2)}) %collective-permute-start.1) | collective-permute-done | bytes 393248 | tf_op jit(solution)/shard_map/ppermute | solution.py:335
  36.0 25.8 %collective-permute-start.3 = (f32[8,96,128]{2,1,0:T(8,128)S(1)}, f32[8,96,128]{2,1,0:T(8,128)S(1)}, u32[]{:S(2)}, u32[]{:S(2)}) collective-permute-start(f32[8,96,128]{2,1,0:T(8,128)S(1)} %get-tuple-element.120), channel_id=1, source_target_pairs={{0,8},{8,16},{16,24},{24,0},{1,9},{9,17},{17,25},{25,1},{2,10},{10... | collective-permute-start | bytes 1179656 | tf_op jit(solution)/shard_map/ppermute | solution.py:335
  64.2 21.5 %collective-permute-done.10.refs_2_ = f32[8,96,128]{2,1,0:T(8,128)S(1)} collective-permute-done((f32[8,96,128]{2,1,0:T(8,128)S(1)}, f32[8,96,128]{2,1,0:T(8,128)S(1)}, u32[]{:S(2)}, u32[]{:S(2)}) %collective-permute-start.10) | collective-permute-done | bytes 393248 | tf_op jit(solution)/shard_map/ppermute | solution.py:335
  85.7 9.0 %collective-permute-start.12 = (f32[8,96,128]{2,1,0:T(8,128)S(1)}, f32[8,96,128]{2,1,0:T(8,128)S(1)}, u32[]{:S(2)}, u32[]{:S(2)}) collective-permute-start(f32[8,96,128]{2,1,0:T(8,128)S(1)} %get-tuple-element.136), channel_id=1, source_target_pairs={{0,8},{8,16},{16,24},{24,0},{1,9},{9,17},{17,25},{25,1},{2,10},{10... | collective-permute-start | bytes 1179656 | tf_op jit(solution)/shard_map/ppermute | solution.py:335
  97.3 22.0 %collective-permute-done.4.refs_2_ = f32[8,96,128]{2,1,0:T(8,128)S(1)} collective-permute-done((f32[8,96,128]{2,1,0:T(8,128)S(1)}, f32[8,96,128]{2,1,0:T(8,128)S(1)}, u32[]{:S(2)}, u32[]{:S(2)}) %collective-permute-start.4) | collective-permute-done | bytes 393248 | tf_op jit(solution)/shard_map/ppermute | solution.py:335
  119.4 9.0 %collective-permute-start.6 = (f32[8,96,128]{2,1,0:T(8,128)S(1)}, f32[8,96,128]{2,1,0:T(8,128)S(1)}, u32[]{:S(2)}, u32[]{:S(2)}) collective-permute-start(f32[8,96,128]{2,1,0:T(8,128)S(1)} %get-tuple-element.124), channel_id=1, source_target_pairs={{0,8},{8,16},{16,24},{24,0},{1,9},{9,17},{17,25},{25,1},{2,10},{10... | collective-permute-start | bytes 1179656 | tf_op jit(solution)/shard_map/ppermute | solution.py:335
  128.4 2.7 collective-permute-start.7
  138.4 14.7 %collective-permute-done.13.refs_2_ = f32[8,96,128]{2,1,0:T(8,128)S(1)} collective-permute-done((f32[8,96,128]{2,1,0:T(8,128)S(1)}, f32[8,96,128]{2,1,0:T(8,128)S(1)}, u32[]{:S(2)}, u32[]{:S(2)}) %collective-permute-start.13) | collective-permute-done | bytes 393248 | tf_op jit(solution)/shard_map/ppermute | solution.py:335
  156.7 13.2 %collective-permute-done.7.refs_2_ = f32[8,96,128]{2,1,0:T(8,128)S(1)} collective-permute-done((f32[8,96,128]{2,1,0:T(8,128)S(1)}, f32[8,96,128]{2,1,0:T(8,128)S(1)}, u32[]{:S(2)}, u32[]{:S(2)}) %collective-permute-start.7) | collective-permute-done | bytes 393248 | tf_op jit(solution)/shard_map/ppermute | solution.py:335
  174.4 3.8 all-to-all-start
  178.1 8.9 %collective-permute-start.18 = (f32[32,32,128]{2,1,0:T(8,128)}, f32[32,32,128]{2,1,0:T(8,128)}, u32[]{:S(2)}, u32[]{:S(2)}) collective-permute-start(f32[32,32,128]{2,1,0:T(8,128)} %copy-done.44), channel_id=1, source_target_pairs={{0,8},{8,16},{16,24},{24,0},{1,9},{9,17},{17,25},{25,1},{2,10},{10... | collective-permute-start | bytes 1572872 | tf_op jit(solution)/shard_map/ppermute | solution.py:335
  190.1 45.7 %all_to_all.30 = f32[4,24,128]{2,1,0:T(8,128)S(1)} all-to-all(f32[4,24,128]{2,1,0:T(8,128)} %bitcast.11), channel_id=1, replica_groups=mesh['gx'=4,'gy'=2,'gz'=4] {'gx'}, dimensions={0} | all-to-all | bytes 98304 | tf_op jit(solution)/shard_map/all_to_all | solution.py:344
  235.8 8.1 %all_to_all.31 = f32[4,24,128]{2,1,0:T(8,128)S(1)} all-to-all(f32[4,24,128]{2,1,0:T(8,128)S(1)} %broadcast_in_dim.8), channel_id=1, replica_groups=mesh['gx'=4,'gy'=2,'gz'=4] {'gx'}, dimensions={0} | all-to-all | bytes 98304 | tf_op jit(solution)/shard_map/all_to_all | solution.py:347
  244.7 3.8 all-to-all-start.3
  252.3 4.5 %all-to-all-done.3 = f32[8,96,128]{2,1,0:T(8,128)S(1)} async-done(((f32[8,96,128]{2,1,0:T(8,128)}), f32[8,96,128]{2,1,0:T(8,128)S(1)}, u32[]{:S(2)}, u32[]{:S(2)}) %all-to-all-start.3) | async-done | bytes 393248 | tf_op jit(solution)/shard_map/all_to_all | solution.py:347
  257.1 5.2 %collective-permute-done.16.refs_2_ = f32[8,32,128]{2,1,0:T(8,128)} collective-permute-done((f32[8,32,128]{2,1,0:T(8,128)}, f32[8,32,128]{2,1,0:T(8,128)}, u32[]{:S(2)}, u32[]{:S(2)}) %collective-permute-start.16) | collective-permute-done | bytes 131104 | tf_op jit(solution)/shard_map/ppermute | solution.py:335
  267.8 4.9 %shard_map.37 = (f32[512,128]{1,0:T(8,128)S(1)}, bf16[128,1024]{1,0:T(8,128)(2,1)S(1)}, bf16[128,1024]{1,0:T(8,128)(2,1)S(1)}, bf16[128,1024]{1,0:T(8,128)(2,1)S...) custom-call(s32[1]{0:T(128)} %bitcast.me_ref, ...), custom_call_target="tpu_custom_call" | custom-call | flops 1610612736 | bytes 4194304 | tf_op jit(solution)/shard_map/pallas_call | solution.py:136
  280.1 15.8 %all_to_all.32 = f32[32,16,128]{2,1,0:T(8,128)} all-to-all(f32[32,16,128]{2,1,0:T(8,128)S(1)} %bitcast.9), channel_id=1, replica_groups=mesh['gx'=4,'gy'=2,'gz'=4] {'gx','gy','gz'}, dimensions={0} | all-to-all | bytes 524288 | tf_op jit(solution)/shard_map/all_to_all | solution.py:344
  297.0 12.8 %all_to_all.33 = f32[32,16,128]{2,1,0:T(8,128)S(1)} all-to-all(f32[32,16,128]{2,1,0:T(8,128)S(1)} %broadcast_in_dim.22), channel_id=1, replica_groups=mesh['gx'=4,'gy'=2,'gz'=4] {'gx','gy','gz'}, dimensions={0} | all-to-all | bytes 524288 | tf_op jit(solution)/shard_map/all_to_all | solution.py:347
  309.8 20.6 %shard_map.39 = (f32[128,128]{1,0:T(8,128)}, f32[128,512]{1,0:T(8,128)S(1)}) custom-call(s32[1]{0:T(128)} %bitcast.me_ref, f32[768,128]{1,0:T(8,128)S(1)} %bitcast.7, f32[512,128]{1,0:T(8,128)S(1)} %bitcast.8), custom_call_target="tpu_custom_call" | custom-call | tf_op jit(solution)/shard_map/pallas_call | solution.py:240
  355.1 2.9 collective-permute-start.32
  359.0 2.9 collective-permute-start.29
  364.4 5.6 %collective-permute-start.25 = (f32[32,8,128]{2,1,0:T(8,128)S(1)}, f32[32,8,128]{2,1,0:T(8,128)S(1)}, u32[]{:S(2)}, u32[]{:S(2)}) collective-permute-start(f32[32,8,128]{2,1,0:T(8,128)S(1)} %get-tuple-element.192), channel_id=1, source_target_pairs={{0,16},{8,24},{16,0},{24,8},{1,17},{9,25},{17,1},{25,9},{2,18},{10... | collective-permute-start | bytes 393224 | tf_op jit(solution)/shard_map/ppermute | solution.py:335
  370.0 3.9 collective-permute-start.26
  373.9 4.9 %collective-permute-done.28.refs_10_ = f32[32,8,128]{2,1,0:T(8,128)S(1)} collective-permute-done((f32[32,8,128]{2,1,0:T(8,128)S(1)}, f32[32,8,128]{2,1,0:T(8,128)S(1)}, u32[]{:S(2)}, u32[]{:S(2)}) %collective-permute-start.28) | collective-permute-done | bytes 131104 | tf_op jit(solution)/shard_map/ppermute | solution.py:335
  378.8 3.8 collective-permute-start.22
  382.6 3.4 collective-permute-start.23
  387.4 6.5 %collective-permute-done.22.refs_2_ = f32[32,8,128]{2,1,0:T(8,128)S(1)} collective-permute-done((f32[32,8,128]{2,1,0:T(8,128)S(1)}, f32[32,8,128]{2,1,0:T(8,128)S(1)}, u32[]{:S(2)}, u32[]{:S(2)}) %collective-permute-start.22) | collective-permute-done | bytes 131104 | tf_op jit(solution)/shard_map/ppermute | solution.py:335
  (168 shorter events, 82.6 us)
Async XLA Ops:
  3.7 18.4 %collective-permute-start = (f32[8,96,128]{2,1,0:T(8,128)}, f32[8,96,128]{2,1,0:T(8,128)S(1)}, u32[]{:S(2)}, u32[]{:S(2)}) collective-permute-start(f32[8,96,128]{2,1,0:T(8,128)} %get-tuple-element.116), channel_id=1, source_target_pairs={{0,8},{8,16},{16,24},{24,0},{1,9},{9,17},{17,25},{25,1},{2,10},{10... | collective-permute-start | bytes 1179656 | tf_op jit(solution)/shard_map/ppermute | solution.py:335
  6.7 29.2 %collective-permute-start.1 = (f32[8,96,128]{2,1,0:T(8,128)}, f32[8,96,128]{2,1,0:T(8,128)S(1)}, u32[]{:S(2)}, u32[]{:S(2)}) collective-permute-start(f32[8,96,128]{2,1,0:T(8,128)} %get-tuple-element.117), channel_id=1, source_target_pairs={{0,16},{8,24},{16,0},{24,8},{1,17},{9,25},{17,1},{25,9},{2,18},{10... | collective-permute-start | bytes 1179656 | tf_op jit(solution)/shard_map/ppermute | solution.py:335
  9.3 26.6 %collective-permute-start.2 = (f32[8,96,128]{2,1,0:T(8,128)}, f32[8,96,128]{2,1,0:T(8,128)S(1)}, u32[]{:S(2)}, u32[]{:S(2)}) collective-permute-start(f32[8,96,128]{2,1,0:T(8,128)} %get-tuple-element.118), channel_id=1, source_target_pairs={{0,24},{8,0},{16,8},{24,16},{1,25},{9,1},{17,9},{25,17},{2,26},{10... | collective-permute-start | bytes 1179656 | tf_op jit(solution)/shard_map/ppermute | solution.py:335
  21.1 42.5 %collective-permute-start.9 = (f32[8,96,128]{2,1,0:T(8,128)S(1)}, f32[8,96,128]{2,1,0:T(8,128)S(1)}, u32[]{:S(2)}, u32[]{:S(2)}) collective-permute-start(f32[8,96,128]{2,1,0:T(8,128)S(1)} %get-tuple-element.132), channel_id=1, source_target_pairs={{0,8},{8,16},{16,24},{24,0},{1,9},{9,17},{17,25},{25,1},{2,10},{10... | collective-permute-start | bytes 1179656 | tf_op jit(solution)/shard_map/ppermute | solution.py:335
  21.8 63.9 %collective-permute-start.10 = (f32[8,96,128]{2,1,0:T(8,128)S(1)}, f32[8,96,128]{2,1,0:T(8,128)S(1)}, u32[]{:S(2)}, u32[]{:S(2)}) collective-permute-start(f32[8,96,128]{2,1,0:T(8,128)S(1)} %get-tuple-element.133), channel_id=1, source_target_pairs={{0,16},{8,24},{16,0},{24,8},{1,17},{9,25},{17,1},{25,9},{2,18},{10... | collective-permute-start | bytes 1179656 | tf_op jit(solution)/shard_map/ppermute | solution.py:335
  22.1 63.6 %collective-permute-start.11 = (f32[8,96,128]{2,1,0:T(8,128)S(1)}, f32[8,96,128]{2,1,0:T(8,128)S(1)}, u32[]{:S(2)}, u32[]{:S(2)}) collective-permute-start(f32[8,96,128]{2,1,0:T(8,128)S(1)} %get-tuple-element.134), channel_id=1, source_target_pairs={{0,24},{8,0},{16,8},{24,16},{1,25},{9,1},{17,9},{25,17},{2,26},{10... | collective-permute-start | bytes 1179656 | tf_op jit(solution)/shard_map/ppermute | solution.py:335
  36.0 61.4 %collective-permute-start.3 = (f32[8,96,128]{2,1,0:T(8,128)S(1)}, f32[8,96,128]{2,1,0:T(8,128)S(1)}, u32[]{:S(2)}, u32[]{:S(2)}) collective-permute-start(f32[8,96,128]{2,1,0:T(8,128)S(1)} %get-tuple-element.120), channel_id=1, source_target_pairs={{0,8},{8,16},{16,24},{24,0},{1,9},{9,17},{17,25},{25,1},{2,10},{10... | collective-permute-start | bytes 1179656 | tf_op jit(solution)/shard_map/ppermute | solution.py:335
  61.8 57.6 %collective-permute-start.4 = (f32[8,96,128]{2,1,0:T(8,128)S(1)}, f32[8,96,128]{2,1,0:T(8,128)S(1)}, u32[]{:S(2)}, u32[]{:S(2)}) collective-permute-start(f32[8,96,128]{2,1,0:T(8,128)S(1)} %get-tuple-element.121), channel_id=1, source_target_pairs={{0,16},{8,24},{16,0},{24,8},{1,17},{9,25},{17,1},{25,9},{2,18},{10... | collective-permute-start | bytes 1179656 | tf_op jit(solution)/shard_map/ppermute | solution.py:335
  63.6 55.8 %collective-permute-start.5 = (f32[8,96,128]{2,1,0:T(8,128)S(1)}, f32[8,96,128]{2,1,0:T(8,128)S(1)}, u32[]{:S(2)}, u32[]{:S(2)}) collective-permute-start(f32[8,96,128]{2,1,0:T(8,128)S(1)} %get-tuple-element.122), channel_id=1, source_target_pairs={{0,24},{8,0},{16,8},{24,16},{1,25},{9,1},{17,9},{25,17},{2,26},{10... | collective-permute-start | bytes 1179656 | tf_op jit(solution)/shard_map/ppermute | solution.py:335
  85.7 45.4 %collective-permute-start.12 = (f32[8,96,128]{2,1,0:T(8,128)S(1)}, f32[8,96,128]{2,1,0:T(8,128)S(1)}, u32[]{:S(2)}, u32[]{:S(2)}) collective-permute-start(f32[8,96,128]{2,1,0:T(8,128)S(1)} %get-tuple-element.136), channel_id=1, source_target_pairs={{0,8},{8,16},{16,24},{24,0},{1,9},{9,17},{17,25},{25,1},{2,10},{10... | collective-permute-start | bytes 1179656 | tf_op jit(solution)/shard_map/ppermute | solution.py:335
  94.7 58.4 %collective-permute-start.13 = (f32[8,96,128]{2,1,0:T(8,128)S(1)}, f32[8,96,128]{2,1,0:T(8,128)S(1)}, u32[]{:S(2)}, u32[]{:S(2)}) collective-permute-start(f32[8,96,128]{2,1,0:T(8,128)S(1)} %get-tuple-element.137), channel_id=1, source_target_pairs={{0,16},{8,24},{16,0},{24,8},{1,17},{9,25},{17,1},{25,9},{2,18},{10... | collective-permute-start | bytes 1179656 | tf_op jit(solution)/shard_map/ppermute | solution.py:335
  97.3 55.7 %collective-permute-start.14 = (f32[8,96,128]{2,1,0:T(8,128)S(1)}, f32[8,96,128]{2,1,0:T(8,128)S(1)}, u32[]{:S(2)}, u32[]{:S(2)}) collective-permute-start(f32[8,96,128]{2,1,0:T(8,128)S(1)} %get-tuple-element.138), channel_id=1, source_target_pairs={{0,24},{8,0},{16,8},{24,16},{1,25},{9,1},{17,9},{25,17},{2,26},{10... | collective-permute-start | bytes 1179656 | tf_op jit(solution)/shard_map/ppermute | solution.py:335
  119.4 37.3 %collective-permute-start.6 = (f32[8,96,128]{2,1,0:T(8,128)S(1)}, f32[8,96,128]{2,1,0:T(8,128)S(1)}, u32[]{:S(2)}, u32[]{:S(2)}) collective-permute-start(f32[8,96,128]{2,1,0:T(8,128)S(1)} %get-tuple-element.124), channel_id=1, source_target_pairs={{0,8},{8,16},{16,24},{24,0},{1,9},{9,17},{17,25},{25,1},{2,10},{10... | collective-permute-start | bytes 1179656 | tf_op jit(solution)/shard_map/ppermute | solution.py:335
  128.4 41.6 %collective-permute-start.7 = (f32[8,96,128]{2,1,0:T(8,128)S(1)}, f32[8,96,128]{2,1,0:T(8,128)S(1)}, u32[]{:S(2)}, u32[]{:S(2)}) collective-permute-start(f32[8,96,128]{2,1,0:T(8,128)S(1)} %get-tuple-element.125), channel_id=1, source_target_pairs={{0,16},{8,24},{16,0},{24,8},{1,17},{9,25},{17,1},{25,9},{2,18},{10... | collective-permute-start | bytes 1179656 | tf_op jit(solution)/shard_map/ppermute | solution.py:335
  131.1 38.8 %collective-permute-start.8 = (f32[8,96,128]{2,1,0:T(8,128)S(1)}, f32[8,96,128]{2,1,0:T(8,128)S(1)}, u32[]{:S(2)}, u32[]{:S(2)}) collective-permute-start(f32[8,96,128]{2,1,0:T(8,128)S(1)} %get-tuple-element.126), channel_id=1, source_target_pairs={{0,24},{8,0},{16,8},{24,16},{1,25},{9,1},{17,9},{25,17},{2,26},{10... | collective-permute-start | bytes 1179656 | tf_op jit(solution)/shard_map/ppermute | solution.py:335
  174.4 15.1 %all-to-all-start = ((f32[8,96,128]{2,1,0:T(8,128)}), f32[8,96,128]{2,1,0:T(8,128)S(1)}, u32[]{:S(2)}, u32[]{:S(2)}) async-start(f32[8,96,128]{2,1,0:T(8,128)} %bitcast.1), calls=%async_computation | async-start | bytes 786432 | tf_op jit(solution)/shard_map/all_to_all | solution.py:344
  178.1 71.6 %collective-permute-start.18 = (f32[32,32,128]{2,1,0:T(8,128)}, f32[32,32,128]{2,1,0:T(8,128)}, u32[]{:S(2)}, u32[]{:S(2)}) collective-permute-start(f32[32,32,128]{2,1,0:T(8,128)} %copy-done.44), channel_id=1, source_target_pairs={{0,8},{8,16},{16,24},{24,0},{1,9},{9,17},{17,25},{25,1},{2,10},{10... | collective-permute-start | bytes 1572872 | tf_op jit(solution)/shard_map/ppermute | solution.py:335
  187.0 65.3 %collective-permute-start.19 = (f32[32,32,128]{2,1,0:T(8,128)}, f32[32,32,128]{2,1,0:T(8,128)}, u32[]{:S(2)}, u32[]{:S(2)}) collective-permute-start(f32[32,32,128]{2,1,0:T(8,128)} %copy-done.43), channel_id=1, source_target_pairs={{0,16},{8,24},{16,0},{24,8},{1,17},{9,25},{17,1},{25,9},{2,18},{10... | collective-permute-start | bytes 1572872 | tf_op jit(solution)/shard_map/ppermute | solution.py:335
  188.7 63.6 %collective-permute-start.20 = (f32[32,32,128]{2,1,0:T(8,128)}, f32[32,32,128]{2,1,0:T(8,128)}, u32[]{:S(2)}, u32[]{:S(2)}) collective-permute-start(f32[32,32,128]{2,1,0:T(8,128)} %copy-done.42), channel_id=1, source_target_pairs={{0,24},{8,0},{16,8},{24,16},{1,25},{9,1},{17,9},{25,17},{2,26},{10... | collective-permute-start | bytes 1572872 | tf_op jit(solution)/shard_map/ppermute | solution.py:335
  249.3 12.9 %collective-permute-start.16 = (f32[8,32,128]{2,1,0:T(8,128)}, f32[8,32,128]{2,1,0:T(8,128)}, u32[]{:S(2)}, u32[]{:S(2)}) collective-permute-start(f32[8,32,128]{2,1,0:T(8,128)} %copy-done.47), channel_id=1, source_target_pairs={{0,16},{8,24},{16,0},{24,8},{1,17},{9,25},{17,1},{25,9},{2,18},{10... | collective-permute-start | bytes 393224 | tf_op jit(solution)/shard_map/ppermute | solution.py:335
  249.8 12.5 %collective-permute-start.17 = (f32[8,32,128]{2,1,0:T(8,128)}, f32[8,32,128]{2,1,0:T(8,128)}, u32[]{:S(2)}, u32[]{:S(2)}) collective-permute-start(f32[8,32,128]{2,1,0:T(8,128)} %copy-done.46), channel_id=1, source_target_pairs={{0,24},{8,0},{16,8},{24,16},{1,25},{9,1},{17,9},{25,17},{2,26},{10... | collective-permute-start | bytes 393224 | tf_op jit(solution)/shard_map/ppermute | solution.py:335
  335.6 19.6 %collective-permute-start.33 = (f32[32,8,128]{2,1,0:T(8,128)S(1)}, f32[32,8,128]{2,1,0:T(8,128)S(1)}, u32[]{:S(2)}, u32[]{:S(2)}) collective-permute-start(f32[32,8,128]{2,1,0:T(8,128)S(1)} %get-tuple-element.209), channel_id=1, source_target_pairs={{0,8},{8,16},{16,24},{24,0},{1,9},{9,17},{17,25},{25,1},{2,10},{10... | collective-permute-start | bytes 393224 | tf_op jit(solution)/shard_map/ppermute | solution.py:335
  336.5 21.5 %collective-permute-start.34 = (f32[32,8,128]{2,1,0:T(8,128)S(1)}, f32[32,8,128]{2,1,0:T(8,128)S(1)}, u32[]{:S(2)}, u32[]{:S(2)}) collective-permute-start(f32[32,8,128]{2,1,0:T(8,128)S(1)} %get-tuple-element.210), channel_id=1, source_target_pairs={{0,16},{8,24},{16,0},{24,8},{1,17},{9,25},{17,1},{25,9},{2,18},{10... | collective-permute-start | bytes 393224 | tf_op jit(solution)/shard_map/ppermute | solution.py:335
  337.5 20.5 %collective-permute-start.35 = (f32[32,8,128]{2,1,0:T(8,128)S(1)}, f32[32,8,128]{2,1,0:T(8,128)S(1)}, u32[]{:S(2)}, u32[]{:S(2)}) collective-permute-start(f32[32,8,128]{2,1,0:T(8,128)S(1)} %get-tuple-element.211), channel_id=1, source_target_pairs={{0,24},{8,0},{16,8},{24,16},{1,25},{9,1},{17,9},{25,17},{2,26},{10... | collective-permute-start | bytes 393224 | tf_op jit(solution)/shard_map/ppermute | solution.py:335
  344.6 14.4 %collective-permute-start.30 = (f32[32,8,128]{2,1,0:T(8,128)S(1)}, f32[32,8,128]{2,1,0:T(8,128)S(1)}, u32[]{:S(2)}, u32[]{:S(2)}) collective-permute-start(f32[32,8,128]{2,1,0:T(8,128)S(1)} %get-tuple-element.203), channel_id=1, source_target_pairs={{0,8},{8,16},{16,24},{24,0},{1,9},{9,17},{17,25},{25,1},{2,10},{10... | collective-permute-start | bytes 393224 | tf_op jit(solution)/shard_map/ppermute | solution.py:335
  345.5 16.5 %collective-permute-start.31 = (f32[32,8,128]{2,1,0:T(8,128)S(1)}, f32[32,8,128]{2,1,0:T(8,128)S(1)}, u32[]{:S(2)}, u32[]{:S(2)}) collective-permute-start(f32[32,8,128]{2,1,0:T(8,128)S(1)} %get-tuple-element.204), channel_id=1, source_target_pairs={{0,16},{8,24},{16,0},{24,8},{1,17},{9,25},{17,1},{25,9},{2,18},{10... | collective-permute-start | bytes 393224 | tf_op jit(solution)/shard_map/ppermute | solution.py:335
  358.1 20.7 %collective-permute-start.28 = (f32[32,8,128]{2,1,0:T(8,128)S(1)}, f32[32,8,128]{2,1,0:T(8,128)S(1)}, u32[]{:S(2)}, u32[]{:S(2)}) collective-permute-start(f32[32,8,128]{2,1,0:T(8,128)S(1)} %get-tuple-element.198), channel_id=1, source_target_pairs={{0,16},{8,24},{16,0},{24,8},{1,17},{9,25},{17,1},{25,9},{2,18},{10... | collective-permute-start | bytes 393224 | tf_op jit(solution)/shard_map/ppermute | solution.py:335
  359.0 19.8 %collective-permute-start.29 = (f32[32,8,128]{2,1,0:T(8,128)S(1)}, f32[32,8,128]{2,1,0:T(8,128)S(1)}, u32[]{:S(2)}, u32[]{:S(2)}) collective-permute-start(f32[32,8,128]{2,1,0:T(8,128)S(1)} %get-tuple-element.199), channel_id=1, source_target_pairs={{0,24},{8,0},{16,8},{24,16},{1,25},{9,1},{17,9},{25,17},{2,26},{10... | collective-permute-start | bytes 393224 | tf_op jit(solution)/shard_map/ppermute | solution.py:335
  361.9 20.6 %collective-permute-start.24 = (f32[32,8,128]{2,1,0:T(8,128)S(1)}, f32[32,8,128]{2,1,0:T(8,128)S(1)}, u32[]{:S(2)}, u32[]{:S(2)}) collective-permute-start(f32[32,8,128]{2,1,0:T(8,128)S(1)} %get-tuple-element.191), channel_id=1, source_target_pairs={{0,8},{8,16},{16,24},{24,0},{1,9},{9,17},{17,25},{25,1},{2,10},{10... | collective-permute-start | bytes 393224 | tf_op jit(solution)/shard_map/ppermute | solution.py:335
  364.4 23.0 %collective-permute-start.25 = (f32[32,8,128]{2,1,0:T(8,128)S(1)}, f32[32,8,128]{2,1,0:T(8,128)S(1)}, u32[]{:S(2)}, u32[]{:S(2)}) collective-permute-start(f32[32,8,128]{2,1,0:T(8,128)S(1)} %get-tuple-element.192), channel_id=1, source_target_pairs={{0,16},{8,24},{16,0},{24,8},{1,17},{9,25},{17,1},{25,9},{2,18},{10... | collective-permute-start | bytes 393224 | tf_op jit(solution)/shard_map/ppermute | solution.py:335
  370.0 17.3 %collective-permute-start.26 = (f32[32,8,128]{2,1,0:T(8,128)S(1)}, f32[32,8,128]{2,1,0:T(8,128)S(1)}, u32[]{:S(2)}, u32[]{:S(2)}) collective-permute-start(f32[32,8,128]{2,1,0:T(8,128)S(1)} %get-tuple-element.193), channel_id=1, source_target_pairs={{0,24},{8,0},{16,8},{24,16},{1,25},{9,1},{17,9},{25,17},{2,26},{10... | collective-permute-start | bytes 393224 | tf_op jit(solution)/shard_map/ppermute | solution.py:335
  378.8 15.1 %collective-permute-start.22 = (f32[32,8,128]{2,1,0:T(8,128)S(1)}, f32[32,8,128]{2,1,0:T(8,128)S(1)}, u32[]{:S(2)}, u32[]{:S(2)}) collective-permute-start(f32[32,8,128]{2,1,0:T(8,128)S(1)} %get-tuple-element.186), channel_id=1, source_target_pairs={{0,16},{8,24},{16,0},{24,8},{1,17},{9,25},{17,1},{25,9},{2,18},{10... | collective-permute-start | bytes 393224 | tf_op jit(solution)/shard_map/ppermute | solution.py:335
  (55 other events, 716.7 us)

commit v5 on v4

--- a/solution.py
+++ b/solution.py
@@ -17,7 +17,8 @@
 SMEM = pl.BlockSpec(memory_space=pltpu.SMEM)
 ANY = pl.BlockSpec(memory_space=pl.ANY)
 HBM = pl.BlockSpec(memory_space=pltpu.HBM)
-PARAMS = pltpu.CompilerParams(vmem_limit_bytes=12 * 2**20)
+SMALL, LARGE = 12 * 2**20, 56 * 2**20
+PARAMS = pltpu.CompilerParams(vmem_limit_bytes=SMALL)
 
 
 def product(left, right, contract=((1,), (0,))):
@@ -122,7 +123,7 @@
                     slot += 1
 
 
-def gram_step(me, parts, earlier, old):
+def gram_step(me, parts, earlier, old, limit):
     groups, chunks = len(parts), len(earlier)
     wide, tall, zlocal = parts[0].shape
     rows = groups * tall
@@ -138,7 +139,7 @@
         out_shape=(jax.ShapeDtypeStruct((slots * BLOCK, BLOCK), jnp.float32),) + (half,) * (2 * chunks),
         in_specs=[SMEM] + [VMEM] * (len(operands) - 1),
         out_specs=(VMEM,) * (1 + 2 * chunks),
-        compiler_params=PARAMS,
+        compiler_params=pltpu.CompilerParams(vmem_limit_bytes=limit),
         cost_estimate=pl.CostEstimate(
             flops=6 * slots * BLOCK * BLOCK * wide * zlocal, bytes_accessed=8 * rows * wide * zlocal, transcendentals=0
         ),
@@ -356,13 +357,6 @@
     return max(k for k in range(1, 6) if per % k == 0)
 
 
-def phase_sizes(xlocal, groups):
-    short = xlocal // 4
-    if short % HALF or groups * short % BLOCK:
-        short = xlocal // 2
-    return [xlocal - short, short]
-
-
 def local(snapshot):
     xlocal, ylocal, zlocal = snapshot.shape
     groups = lax.axis_size("gx")
@@ -370,15 +364,13 @@
     chunks = chunk_count(per)
     steps = per // chunks
     starts = [chunk * steps for chunk in range(chunks)]
-    talls = phase_sizes(xlocal, groups)
+    talls = [xlocal]
     me = lax.axis_index("gx").astype(jnp.int32).reshape(1)
 
-    long = [(0, talls[0], start, steps) for start in starts]
-    cut = per - steps if chunks > 1 else per
-    short = [(talls[0], talls[1], 0, cut)]
-    short += [(talls[0], talls[1], cut, steps)] if chunks > 1 else []
-    packed = pack(me, snapshot, groups, long[:1], 54 * 2**20)
-    packed += pack(me, snapshot, groups, long[1:] + short, 44 * 2**20)
+    pieces = [(0, xlocal, start, steps) for start in starts]
+    packed = pack(me, snapshot, groups, pieces[:1], 54 * 2**20)
+    if chunks > 1:
+        packed += pack(me, snapshot, groups, pieces[1:], 44 * 2**20)
 
     moved = []
     for index, parts in enumerate(packed):
@@ -388,22 +380,20 @@
 
     halves = []
     total = None
-    for parts in moved[:chunks]:
-        total, made = gram_step(me, parts, [[]], total)
+    for index, parts in enumerate(moved):
+        limit = SMALL if index == chunks - 1 else LARGE
+        total, made = gram_step(me, parts, [[]], total, limit)
         halves.append(made)
-    sums = [total_sum(total, [("gy", "gz"), "gx"])]
-    total, at = None, 0
-    for parts in moved[chunks:]:
-        count = parts[0].shape[0] // steps
-        total, made = gram_step(me, hold(parts, sums[0]), halves[at : at + count], total)
-        for held, pair in zip(halves[at : at + count], made):
-            held.append(pair)
-        at += count
-    sums.append(total_sum(total, [AXES]))
+    sums = [total_sum(total, [AXES])]
 
     mine, turned = factor_step(me, sums, groups, talls)
-    outs = [exchange(core_step(me, turned, held, groups, zlocal)) for held in halves]
-    return (mine, place(me, outs, starts, ylocal))
+    outs = []
+    for held in halves[-1:] + halves[:-1]:
+        if len(outs) == 1:
+            (turned,) = hold([turned], parts[0])
+        parts = core_step(me, turned, held, groups, zlocal)
+        outs.append(exchange(hold(parts, outs[-2]) if len(outs) >= 2 else parts))
+    return (mine, place(me, outs, starts[-1:] + starts[:-1], ylocal))
 
 
 def solution(mesh):

time: 397 us -> 370 us (0.932)
  blocking collectives: 82.4 us -> 54.2 us
  waiting for transfers between devices: 106 us -> 134 us
  local copies, waits for them, and re-layouts: 35.7 us -> 14.9 us
  starting transfers between devices: 115 us -> 104 us
  Pallas kernels: 53.2 us -> 59.8 us
    ppermute x36 -> x30, waiting for transfers between devices: 102 us -> 134 us  [exchange(): lax.ppermute(parts[shift], 'gx', [(i, (i + shift) % groups) for i in rang...]
    all_to_all x2 -> x1, blocking collectives: 61.5 us -> 32.9 us  [total_sum(): lax.all_to_all(parts, axes, split_axis=0, concat_axis=0, tiled=True)]
    unnamed x98 -> x50, local copies, waits for them, and re-layouts: 34.9 us -> 14.8 us
    pallas_call x7 -> x5, Pallas kernels: 17 us -> 24.7 us  [gram_step(): pl.pallas_call(functools.partial(gram_kernel, first, groups, chunks, len(...]
    all_to_all x2 -> x0, starting transfers between devices: 7.6 us -> none  [the longest x1 3.84 us: total_sum(): lax.all_to_all(spread, axes, split_axis=0, concat_axis=0, tiled=True)]
    all_to_all x2 -> x0, waiting for transfers between devices: 4.5 us -> none  [the longest x1 4.5 us: total_sum(): lax.all_to_all(spread, axes, split_axis=0, concat_axis=0, tiled=True)]
    ppermute x36 -> x30, starting transfers between devices: 108 us -> 104 us  [exchange(): lax.ppermute(parts[shift], 'gx', [(i, (i + shift) % groups) for i in rang...]
    all_to_all x2 -> x1, blocking collectives: 20.9 us -> 21.2 us  [total_sum(): lax.all_to_all(spread, axes, split_axis=0, concat_axis=0, tiled=True)]
  transfers between devices with their start and end apart: 38 -> 30, of which waited for: 12 -> 11; matrix products, arithmetic and copies ran while one was open for 0% -> 0% of each run, Pallas kernels for 4% -> 8%
where the time goes in v5:
time: 370 us; the launch traced here: 369 us
  waiting for transfers between devices  134 us (36%)
  starting transfers between devices  104 us (28%)
  Pallas kernels  59.8 us (16%)
  blocking collectives  54.2 us (15%)
  local copies, waits for them, and re-layouts  14.9 us (4%)
    ppermute x30, waiting for transfers between devices, exchange(): lax.ppermute(parts[shift], 'gx', [(i, (i + shift) % groups) for i in rang...  134 us
    ppermute x30, starting transfers between devices, exchange(): lax.ppermute(parts[shift], 'gx', [(i, (i + shift) % groups) for i in rang...  104 us
    all_to_all x1, blocking collectives, total_sum(): lax.all_to_all(parts, axes, split_axis=0, concat_axis=0, tiled=True)  32.9 us
    pallas_call x5, Pallas kernels, gram_step(): pl.pallas_call(functools.partial(gram_kernel, first, groups, chunks, len(...  24.7 us
    all_to_all x1, blocking collectives, total_sum(): lax.all_to_all(spread, axes, split_axis=0, concat_axis=0, tiled=True)  21.2 us
    pallas_call x1, Pallas kernels, factor_step(): pl.pallas_call(functools.partial(factor_kernel, groups, talls), out_shape...  20.6 us
    unnamed x50, local copies, waits for them, and re-layouts  14.8 us
    pallas_call x2, Pallas kernels, pack(): pl.pallas_call(functools.partial(pack_kernel, groups, per, tuple(pieces))...  9.07 us
  transfers between devices with their start and end apart: 30, of which 11 were waited for; matrix products, arithmetic and copies ran while one was open for 0% of the time, Pallas kernels for 8%

profile of v5, /device:TPU:0, one launch (start us, length us, event | category | flops | bytes accessed | tf_op | source)
XLA Modules:
  0.0 368.9 jit_solution(4114296571302235423)
XLA Ops:
  0.6 3.5 shard_map.31
  4.1 3.1 collective-permute-start
  7.2 2.6 collective-permute-start.1
  11.1 5.6 %shard_map.30 = (f32[8,128,128]{2,1,0:T(8,128)S(1)}, f32[8,128,128]{2,1,0:T(8,128)S(1)}, f32[8,128,128]{2,1,0:T(8,128)S(1)}, f32[8,128,128]{2,1,0:T(8,128)S(1)},...) custom-call(s32[1]{0:T(128)} %bitcast.me_ref, ...), custom_call_target="tpu_custom_call" | custom-call | bytes 16777216 | tf_op jit(solution)/shard_map/pallas_call | solution.py:73
  22.3 2.5 collective-permute-start.11
  24.8 20.0 %collective-permute-done.1.refs_2_ = f32[8,128,128]{2,1,0:T(8,128)S(1)} collective-permute-done((f32[8,128,128]{2,1,0:T(8,128)}, f32[8,128,128]{2,1,0:T(8,128)S(1)}, u32[]{:S(2)}, u32[]{:S(2)}) %collective-permute-start.1) | collective-permute-done | bytes 524320 | tf_op jit(solution)/shard_map/ppermute | solution.py:336
  44.9 34.3 %collective-permute-start.3 = (f32[8,128,128]{2,1,0:T(8,128)S(1)}, f32[8,128,128]{2,1,0:T(8,128)S(1)}, u32[]{:S(2)}, u32[]{:S(2)}) collective-permute-start(f32[8,128,128]{2,1,0:T(8,128)S(1)} %get-tuple-element.97), channel_id=1, source_target_pairs={{0,8},{8,16},{16,24},{24,0},{1,9},{9,17},{17,25},{25,1},{2,10},{10... | collective-permute-start | bytes 1572872 | tf_op jit(solution)/shard_map/ppermute | solution.py:336
  81.5 30.0 %collective-permute-done.10.refs_2_ = f32[8,128,128]{2,1,0:T(8,128)S(1)} collective-permute-done((f32[8,128,128]{2,1,0:T(8,128)S(1)}, f32[8,128,128]{2,1,0:T(8,128)S(1)}, u32[]{:S(2)}, u32[]{:S(2)}) %collective-permute-start.10) | collective-permute-done | bytes 524320 | tf_op jit(solution)/shard_map/ppermute | solution.py:336
  111.5 11.8 %collective-permute-start.12 = (f32[8,128,128]{2,1,0:T(8,128)S(1)}, f32[8,128,128]{2,1,0:T(8,128)}, u32[]{:S(2)}, u32[]{:S(2)}) collective-permute-start(f32[8,128,128]{2,1,0:T(8,128)S(1)} %get-tuple-element.113), channel_id=1, source_target_pairs={{0,8},{8,16},{16,24},{24,0},{1,9},{9,17},{17,25},{25,1},{2,10},{10... | collective-permute-start | bytes 1572872 | tf_op jit(solution)/shard_map/ppermute | solution.py:336
  123.3 2.7 collective-permute-start.13
  126.0 30.4 %collective-permute-done.4.refs_2_ = f32[8,128,128]{2,1,0:T(8,128)S(1)} collective-permute-done((f32[8,128,128]{2,1,0:T(8,128)S(1)}, f32[8,128,128]{2,1,0:T(8,128)S(1)}, u32[]{:S(2)}, u32[]{:S(2)}) %collective-permute-start.4) | collective-permute-done | bytes 524320 | tf_op jit(solution)/shard_map/ppermute | solution.py:336
  157.2 11.1 %collective-permute-start.6 = (f32[8,128,128]{2,1,0:T(8,128)S(1)}, f32[8,128,128]{2,1,0:T(8,128)S(1)}, u32[]{:S(2)}, u32[]{:S(2)}) collective-permute-start(f32[8,128,128]{2,1,0:T(8,128)S(1)} %get-tuple-element.101), channel_id=1, source_target_pairs={{0,8},{8,16},{16,24},{24,0},{1,9},{9,17},{17,25},{25,1},{2,10},{10... | collective-permute-start | bytes 1572872 | tf_op jit(solution)/shard_map/ppermute | solution.py:336
  168.3 3.4 collective-permute-start.7
  171.7 5.0 %shard_map.32 = (f32[1280,128]{1,0:T(8,128)}, bf16[512,1024]{1,0:T(8,128)(2,1)}, bf16[512,1024]{1,0:T(8,128)(2,1)}) custom-call(s32[1]{0:T(128)} %bitcast.me_ref, f32[8,128,128]{2,1,0:T(8,128)} %get-tuple-element.92.refs_0_, f32[8,128,128]{2,1,0:T(8,128)} %copy-done.16, f32[8,128,128]{2,1,0:T(8,128)} %copy-done.17, f32[8,128,128]{2,1,0:T(8,128)} %copy-done.18), custom_call_target="tpu_custom_call" | custom-call | flops 1006632960 | bytes 4194304 | tf_op jit(solution)/shard_map/pallas_call | solution.py:137
  176.8 5.6 %shard_map.33 = (f32[1280,128]{1,0:T(8,128)}, bf16[512,1024]{1,0:T(8,128)(2,1)}, bf16[512,1024]{1,0:T(8,128)(2,1)}) custom-call(s32[1]{0:T(128)} %bitcast.me_ref, f32[8,128,128]{2,1,0:T(8,128)} %copy-done.14, f32[8,128,128]{2,1,0:T(8,128)} %copy-done.19, f32[8,128,128]{2,1,0:T(8,128)} %copy-done.20, f32[8,128,128]{2,1,0:T(8,128)} %copy-done.21, ...), custom_call_target="tpu_custom_call" | custom-call | flops 1006632960 | bytes 4194304 | tf_op jit(solution)/shard_map/pallas_call | solution.py:137
  182.3 5.5 %shard_map.34 = (f32[1280,128]{1,0:T(8,128)}, bf16[512,1024]{1,0:T(8,128)(2,1)}, bf16[512,1024]{1,0:T(8,128)(2,1)}) custom-call(s32[1]{0:T(128)} %bitcast.me_ref, f32[8,128,128]{2,1,0:T(8,128)} %copy-done.13, f32[8,128,128]{2,1,0:T(8,128)} %copy-done.22, f32[8,128,128]{2,1,0:T(8,128)} %copy-done.23, f32[8,128,128]{2,1,0:T(8,128)} %copy-done.24, ...), custom_call_target="tpu_custom_call" | custom-call | flops 1006632960 | bytes 4194304 | tf_op jit(solution)/shard_map/pallas_call | solution.py:137
  187.9 13.6 %collective-permute-done.13.refs_2_ = f32[8,128,128]{2,1,0:T(8,128)} collective-permute-done((f32[8,128,128]{2,1,0:T(8,128)S(1)}, f32[8,128,128]{2,1,0:T(8,128)}, u32[]{:S(2)}, u32[]{:S(2)}) %collective-permute-start.13) | collective-permute-done | bytes 524320 | tf_op jit(solution)/shard_map/ppermute | solution.py:336
  201.5 5.6 %shard_map.35 = (f32[1280,128]{1,0:T(8,128)}, bf16[512,1024]{1,0:T(8,128)(2,1)}, bf16[512,1024]{1,0:T(8,128)(2,1)}) custom-call(s32[1]{0:T(128)} %bitcast.me_ref, f32[8,128,128]{2,1,0:T(8,128)} %copy-done.12, f32[8,128,128]{2,1,0:T(8,128)} %collective-permute-done.12.refs_1_, f32[8,128,128]{2,1,0:T(8,128)} %collective-permute-done.13.refs_2_, ...), custom_call_target="tpu_custom_call" | custom-call | flops 1006632960 | bytes 4194304 | tf_op jit(solution)/shard_map/pallas_call | solution.py:137
  207.0 16.8 %collective-permute-done.7.refs_2_ = f32[8,128,128]{2,1,0:T(8,128)S(1)} collective-permute-done((f32[8,128,128]{2,1,0:T(8,128)S(1)}, f32[8,128,128]{2,1,0:T(8,128)S(1)}, u32[]{:S(2)}, u32[]{:S(2)}) %collective-permute-start.7) | collective-permute-done | bytes 524320 | tf_op jit(solution)/shard_map/ppermute | solution.py:336
  224.9 3.0 shard_map.36
  229.9 32.9 %all_to_all.10 = f32[32,40,128]{2,1,0:T(8,128)} all-to-all(f32[32,40,128]{2,1,0:T(8,128)S(1)} %bitcast.4), channel_id=1, replica_groups=mesh['gx'=4,'gy'=2,'gz'=4] {'gx','gy','gz'}, dimensions={0} | all-to-all | bytes 1310720 | tf_op jit(solution)/shard_map/all_to_all | solution.py:345
  264.0 21.2 %all_to_all.11 = f32[32,40,128]{2,1,0:T(8,128)S(1)} all-to-all(f32[32,40,128]{2,1,0:T(8,128)S(1)} %broadcast_in_dim.2), channel_id=1, replica_groups=mesh['gx'=4,'gy'=2,'gz'=4] {'gx','gy','gz'}, dimensions={0} | all-to-all | bytes 1310720 | tf_op jit(solution)/shard_map/all_to_all | solution.py:348
  285.2 20.6 %shard_map.37 = (f32[128,128]{1,0:T(8,128)}, f32[128,512]{1,0:T(8,128)S(1)}) custom-call(s32[1]{0:T(128)} %bitcast.me_ref, f32[1280,128]{1,0:T(8,128)S(1)} %bitcast.3), custom_call_target="tpu_custom_call" | custom-call | tf_op jit(solution)/shard_map/pallas_call | solution.py:241
  318.8 2.4 collective-permute-start.20
  324.4 2.6 collective-permute-done.16.refs_2_
  327.0 5.0 %collective-permute-start.21 = (f32[32,8,128]{2,1,0:T(8,128)S(1)}, f32[32,8,128]{2,1,0:T(8,128)S(1)}, u32[]{:S(2)}, u32[]{:S(2)}) collective-permute-start(f32[32,8,128]{2,1,0:T(8,128)S(1)} %get-tuple-element.143), channel_id=1, source_target_pairs={{0,8},{8,16},{16,24},{24,0},{1,9},{9,17},{17,25},{25,1},{2,10},{10... | collective-permute-start | bytes 393224 | tf_op jit(solution)/shard_map/ppermute | solution.py:336
  336.4 2.6 collective-permute-done.19.refs_6_
  339.0 3.4 collective-permute-start.24
  345.6 4.6 %collective-permute-done.22.refs_10_ = f32[32,8,128]{2,1,0:T(8,128)S(1)} collective-permute-done((f32[32,8,128]{2,1,0:T(8,128)S(1)}, f32[32,8,128]{2,1,0:T(8,128)S(1)}, u32[]{:S(2)}, u32[]{:S(2)}) %collective-permute-start.22) | collective-permute-done | bytes 131104 | tf_op jit(solution)/shard_map/ppermute | solution.py:336
  350.3 3.4 collective-permute-start.27
  356.0 5.5 %collective-permute-done.25.refs_14_ = f32[32,8,128]{2,1,0:T(8,128)S(1)} collective-permute-done((f32[32,8,128]{2,1,0:T(8,128)S(1)}, f32[32,8,128]{2,1,0:T(8,128)S(1)}, u32[]{:S(2)}, u32[]{:S(2)}) %collective-permute-start.25) | collective-permute-done | bytes 131104 | tf_op jit(solution)/shard_map/ppermute | solution.py:336
  361.5 5.6 %collective-permute-done.28.refs_18_ = f32[32,8,128]{2,1,0:T(8,128)S(1)} collective-permute-done((f32[32,8,128]{2,1,0:T(8,128)S(1)}, f32[32,8,128]{2,1,0:T(8,128)S(1)}, u32[]{:S(2)}, u32[]{:S(2)}) %collective-permute-start.28) | collective-permute-done | bytes 131104 | tf_op jit(solution)/shard_map/ppermute | solution.py:336
  (96 shorter events, 42.1 us)
Async XLA Ops:
  4.1 18.2 %collective-permute-start = (f32[8,128,128]{2,1,0:T(8,128)}, f32[8,128,128]{2,1,0:T(8,128)S(1)}, u32[]{:S(2)}, u32[]{:S(2)}) collective-permute-start(f32[8,128,128]{2,1,0:T(8,128)} %get-tuple-element.93), channel_id=1, source_target_pairs={{0,8},{8,16},{16,24},{24,0},{1,9},{9,17},{17,25},{25,1},{2,10},{10... | collective-permute-start | bytes 1572872 | tf_op jit(solution)/shard_map/ppermute | solution.py:336
  7.2 37.6 %collective-permute-start.1 = (f32[8,128,128]{2,1,0:T(8,128)}, f32[8,128,128]{2,1,0:T(8,128)S(1)}, u32[]{:S(2)}, u32[]{:S(2)}) collective-permute-start(f32[8,128,128]{2,1,0:T(8,128)} %get-tuple-element.94), channel_id=1, source_target_pairs={{0,16},{8,24},{16,0},{24,8},{1,17},{9,25},{17,1},{25,9},{2,18},{10... | collective-permute-start | bytes 1572872 | tf_op jit(solution)/shard_map/ppermute | solution.py:336
  9.8 35.1 %collective-permute-start.2 = (f32[8,128,128]{2,1,0:T(8,128)}, f32[8,128,128]{2,1,0:T(8,128)S(1)}, u32[]{:S(2)}, u32[]{:S(2)}) collective-permute-start(f32[8,128,128]{2,1,0:T(8,128)} %get-tuple-element.95), channel_id=1, source_target_pairs={{0,24},{8,0},{16,8},{24,16},{1,25},{9,1},{17,9},{25,17},{2,26},{10... | collective-permute-start | bytes 1572872 | tf_op jit(solution)/shard_map/ppermute | solution.py:336
  19.1 61.8 %collective-permute-start.9 = (f32[8,128,128]{2,1,0:T(8,128)S(1)}, f32[8,128,128]{2,1,0:T(8,128)S(1)}, u32[]{:S(2)}, u32[]{:S(2)}) collective-permute-start(f32[8,128,128]{2,1,0:T(8,128)S(1)} %get-tuple-element.109), channel_id=1, source_target_pairs={{0,8},{8,16},{16,24},{24,0},{1,9},{9,17},{17,25},{25,1},{2,10},{10... | collective-permute-start | bytes 1572872 | tf_op jit(solution)/shard_map/ppermute | solution.py:336
  19.8 91.6 %collective-permute-start.10 = (f32[8,128,128]{2,1,0:T(8,128)S(1)}, f32[8,128,128]{2,1,0:T(8,128)S(1)}, u32[]{:S(2)}, u32[]{:S(2)}) collective-permute-start(f32[8,128,128]{2,1,0:T(8,128)S(1)} %get-tuple-element.110), channel_id=1, source_target_pairs={{0,16},{8,24},{16,0},{24,8},{1,17},{9,25},{17,1},{25,9},{2,18},{10... | collective-permute-start | bytes 1572872 | tf_op jit(solution)/shard_map/ppermute | solution.py:336
  22.3 149.4 %copy-start.16 = (f32[8,128,128]{2,1,0:T(8,128)}, f32[8,128,128]{2,1,0:T(8,128)S(1)}, u32[]{:S(2)}) copy-start(f32[8,128,128]{2,1,0:T(8,128)S(1)} %collective-permute-done.refs_1_) | copy-start | bytes 1572868
  22.3 89.1 %collective-permute-start.11 = (f32[8,128,128]{2,1,0:T(8,128)S(1)}, f32[8,128,128]{2,1,0:T(8,128)S(1)}, u32[]{:S(2)}, u32[]{:S(2)}) collective-permute-start(f32[8,128,128]{2,1,0:T(8,128)S(1)} %get-tuple-element.111), channel_id=1, source_target_pairs={{0,24},{8,0},{16,8},{24,16},{1,25},{9,1},{17,9},{25,17},{2,26},{10... | collective-permute-start | bytes 1572872 | tf_op jit(solution)/shard_map/ppermute | solution.py:336
  44.9 81.1 %collective-permute-start.3 = (f32[8,128,128]{2,1,0:T(8,128)S(1)}, f32[8,128,128]{2,1,0:T(8,128)S(1)}, u32[]{:S(2)}, u32[]{:S(2)}) collective-permute-start(f32[8,128,128]{2,1,0:T(8,128)S(1)} %get-tuple-element.97), channel_id=1, source_target_pairs={{0,8},{8,16},{16,24},{24,0},{1,9},{9,17},{17,25},{25,1},{2,10},{10... | collective-permute-start | bytes 1572872 | tf_op jit(solution)/shard_map/ppermute | solution.py:336
  79.1 77.3 %collective-permute-start.4 = (f32[8,128,128]{2,1,0:T(8,128)S(1)}, f32[8,128,128]{2,1,0:T(8,128)S(1)}, u32[]{:S(2)}, u32[]{:S(2)}) collective-permute-start(f32[8,128,128]{2,1,0:T(8,128)S(1)} %get-tuple-element.98), channel_id=1, source_target_pairs={{0,16},{8,24},{16,0},{24,8},{1,17},{9,25},{17,1},{25,9},{2,18},{10... | collective-permute-start | bytes 1572872 | tf_op jit(solution)/shard_map/ppermute | solution.py:336
  81.0 75.4 %collective-permute-start.5 = (f32[8,128,128]{2,1,0:T(8,128)S(1)}, f32[8,128,128]{2,1,0:T(8,128)S(1)}, u32[]{:S(2)}, u32[]{:S(2)}) collective-permute-start(f32[8,128,128]{2,1,0:T(8,128)S(1)} %get-tuple-element.99), channel_id=1, source_target_pairs={{0,24},{8,0},{16,8},{24,16},{1,25},{9,1},{17,9},{25,17},{2,26},{10... | collective-permute-start | bytes 1572872 | tf_op jit(solution)/shard_map/ppermute | solution.py:336
  111.5 60.2 %collective-permute-start.12 = (f32[8,128,128]{2,1,0:T(8,128)S(1)}, f32[8,128,128]{2,1,0:T(8,128)}, u32[]{:S(2)}, u32[]{:S(2)}) collective-permute-start(f32[8,128,128]{2,1,0:T(8,128)S(1)} %get-tuple-element.113), channel_id=1, source_target_pairs={{0,8},{8,16},{16,24},{24,0},{1,9},{9,17},{17,25},{25,1},{2,10},{10... | collective-permute-start | bytes 1572872 | tf_op jit(solution)/shard_map/ppermute | solution.py:336
  123.3 78.2 %collective-permute-start.13 = (f32[8,128,128]{2,1,0:T(8,128)S(1)}, f32[8,128,128]{2,1,0:T(8,128)}, u32[]{:S(2)}, u32[]{:S(2)}) collective-permute-start(f32[8,128,128]{2,1,0:T(8,128)S(1)} %get-tuple-element.114), channel_id=1, source_target_pairs={{0,16},{8,24},{16,0},{24,8},{1,17},{9,25},{17,1},{25,9},{2,18},{10... | collective-permute-start | bytes 1572872 | tf_op jit(solution)/shard_map/ppermute | solution.py:336
  126.0 75.5 %collective-permute-start.14 = (f32[8,128,128]{2,1,0:T(8,128)S(1)}, f32[8,128,128]{2,1,0:T(8,128)}, u32[]{:S(2)}, u32[]{:S(2)}) collective-permute-start(f32[8,128,128]{2,1,0:T(8,128)S(1)} %get-tuple-element.115), channel_id=1, source_target_pairs={{0,24},{8,0},{16,8},{24,16},{1,25},{9,1},{17,9},{25,17},{2,26},{10... | collective-permute-start | bytes 1572872 | tf_op jit(solution)/shard_map/ppermute | solution.py:336
  157.2 49.8 %collective-permute-start.6 = (f32[8,128,128]{2,1,0:T(8,128)S(1)}, f32[8,128,128]{2,1,0:T(8,128)S(1)}, u32[]{:S(2)}, u32[]{:S(2)}) collective-permute-start(f32[8,128,128]{2,1,0:T(8,128)S(1)} %get-tuple-element.101), channel_id=1, source_target_pairs={{0,8},{8,16},{16,24},{24,0},{1,9},{9,17},{17,25},{25,1},{2,10},{10... | collective-permute-start | bytes 1572872 | tf_op jit(solution)/shard_map/ppermute | solution.py:336
  168.3 55.5 %collective-permute-start.7 = (f32[8,128,128]{2,1,0:T(8,128)S(1)}, f32[8,128,128]{2,1,0:T(8,128)S(1)}, u32[]{:S(2)}, u32[]{:S(2)}) collective-permute-start(f32[8,128,128]{2,1,0:T(8,128)S(1)} %get-tuple-element.102), channel_id=1, source_target_pairs={{0,16},{8,24},{16,0},{24,8},{1,17},{9,25},{17,1},{25,9},{2,18},{10... | collective-permute-start | bytes 1572872 | tf_op jit(solution)/shard_map/ppermute | solution.py:336
  171.7 52.1 %collective-permute-start.8 = (f32[8,128,128]{2,1,0:T(8,128)S(1)}, f32[8,128,128]{2,1,0:T(8,128)S(1)}, u32[]{:S(2)}, u32[]{:S(2)}) collective-permute-start(f32[8,128,128]{2,1,0:T(8,128)S(1)} %get-tuple-element.103), channel_id=1, source_target_pairs={{0,24},{8,0},{16,8},{24,16},{1,25},{9,1},{17,9},{25,17},{2,26},{10... | collective-permute-start | bytes 1572872 | tf_op jit(solution)/shard_map/ppermute | solution.py:336
  187.9 146.5 %copy-start.2 = (bf16[512,1024]{1,0:T(8,128)(2,1)S(1)}, bf16[512,1024]{1,0:T(8,128)(2,1)}, u32[]{:S(2)}) copy-start(bf16[512,1024]{1,0:T(8,128)(2,1)} %get-tuple-element.146.refs_0_) | copy-start | bytes 3145732
  309.1 9.7 %collective-permute-start.15 = (f32[32,8,128]{2,1,0:T(8,128)S(1)}, f32[32,8,128]{2,1,0:T(8,128)S(1)}, u32[]{:S(2)}, u32[]{:S(2)}) collective-permute-start(f32[32,8,128]{2,1,0:T(8,128)S(1)} %get-tuple-element.126), channel_id=1, source_target_pairs={{0,8},{8,16},{16,24},{24,0},{1,9},{9,17},{17,25},{25,1},{2,10},{10... | collective-permute-start | bytes 393224 | tf_op jit(solution)/shard_map/ppermute | solution.py:336
  310.6 16.4 %collective-permute-start.16 = (f32[32,8,128]{2,1,0:T(8,128)S(1)}, f32[32,8,128]{2,1,0:T(8,128)S(1)}, u32[]{:S(2)}, u32[]{:S(2)}) collective-permute-start(f32[32,8,128]{2,1,0:T(8,128)S(1)} %get-tuple-element.127), channel_id=1, source_target_pairs={{0,16},{8,24},{16,0},{24,8},{1,17},{9,25},{17,1},{25,9},{2,18},{10... | collective-permute-start | bytes 393224 | tf_op jit(solution)/shard_map/ppermute | solution.py:336
  310.8 16.2 %collective-permute-start.17 = (f32[32,8,128]{2,1,0:T(8,128)S(1)}, f32[32,8,128]{2,1,0:T(8,128)S(1)}, u32[]{:S(2)}, u32[]{:S(2)}) collective-permute-start(f32[32,8,128]{2,1,0:T(8,128)S(1)} %get-tuple-element.128), channel_id=1, source_target_pairs={{0,24},{8,0},{16,8},{24,16},{1,25},{9,1},{17,9},{25,17},{2,26},{10... | collective-permute-start | bytes 393224 | tf_op jit(solution)/shard_map/ppermute | solution.py:336
  316.2 15.8 %collective-permute-start.18 = (f32[32,8,128]{2,1,0:T(8,128)S(1)}, f32[32,8,128]{2,1,0:T(8,128)S(1)}, u32[]{:S(2)}, u32[]{:S(2)}) collective-permute-start(f32[32,8,128]{2,1,0:T(8,128)S(1)} %get-tuple-element.133), channel_id=1, source_target_pairs={{0,8},{8,16},{16,24},{24,0},{1,9},{9,17},{17,25},{25,1},{2,10},{10... | collective-permute-start | bytes 393224 | tf_op jit(solution)/shard_map/ppermute | solution.py:336
  316.8 22.2 %collective-permute-start.19 = (f32[32,8,128]{2,1,0:T(8,128)S(1)}, f32[32,8,128]{2,1,0:T(8,128)S(1)}, u32[]{:S(2)}, u32[]{:S(2)}) collective-permute-start(f32[32,8,128]{2,1,0:T(8,128)S(1)} %get-tuple-element.134), channel_id=1, source_target_pairs={{0,16},{8,24},{16,0},{24,8},{1,17},{9,25},{17,1},{25,9},{2,18},{10... | collective-permute-start | bytes 393224 | tf_op jit(solution)/shard_map/ppermute | solution.py:336
  318.8 20.2 %collective-permute-start.20 = (f32[32,8,128]{2,1,0:T(8,128)S(1)}, f32[32,8,128]{2,1,0:T(8,128)S(1)}, u32[]{:S(2)}, u32[]{:S(2)}) collective-permute-start(f32[32,8,128]{2,1,0:T(8,128)S(1)} %get-tuple-element.135), channel_id=1, source_target_pairs={{0,24},{8,0},{16,8},{24,16},{1,25},{9,1},{17,9},{25,17},{2,26},{10... | collective-permute-start | bytes 393224 | tf_op jit(solution)/shard_map/ppermute | solution.py:336
  327.0 16.3 %collective-permute-start.21 = (f32[32,8,128]{2,1,0:T(8,128)S(1)}, f32[32,8,128]{2,1,0:T(8,128)S(1)}, u32[]{:S(2)}, u32[]{:S(2)}) collective-permute-start(f32[32,8,128]{2,1,0:T(8,128)S(1)} %get-tuple-element.143), channel_id=1, source_target_pairs={{0,8},{8,16},{16,24},{24,0},{1,9},{9,17},{17,25},{25,1},{2,10},{10... | collective-permute-start | bytes 393224 | tf_op jit(solution)/shard_map/ppermute | solution.py:336
  332.0 18.2 %collective-permute-start.22 = (f32[32,8,128]{2,1,0:T(8,128)S(1)}, f32[32,8,128]{2,1,0:T(8,128)S(1)}, u32[]{:S(2)}, u32[]{:S(2)}) collective-permute-start(f32[32,8,128]{2,1,0:T(8,128)S(1)} %get-tuple-element.144), channel_id=1, source_target_pairs={{0,16},{8,24},{16,0},{24,8},{1,17},{9,25},{17,1},{25,9},{2,18},{10... | collective-permute-start | bytes 393224 | tf_op jit(solution)/shard_map/ppermute | solution.py:336
  332.0 18.2 %collective-permute-start.23 = (f32[32,8,128]{2,1,0:T(8,128)S(1)}, f32[32,8,128]{2,1,0:T(8,128)S(1)}, u32[]{:S(2)}, u32[]{:S(2)}) collective-permute-start(f32[32,8,128]{2,1,0:T(8,128)S(1)} %get-tuple-element.145), channel_id=1, source_target_pairs={{0,24},{8,0},{16,8},{24,16},{1,25},{9,1},{17,9},{25,17},{2,26},{10... | collective-permute-start | bytes 393224 | tf_op jit(solution)/shard_map/ppermute | solution.py:336
  339.0 14.6 %collective-permute-start.24 = (f32[32,8,128]{2,1,0:T(8,128)S(1)}, f32[32,8,128]{2,1,0:T(8,128)S(1)}, u32[]{:S(2)}, u32[]{:S(2)}) collective-permute-start(f32[32,8,128]{2,1,0:T(8,128)S(1)} %get-tuple-element.153), channel_id=1, source_target_pairs={{0,8},{8,16},{16,24},{24,0},{1,9},{9,17},{17,25},{25,1},{2,10},{10... | collective-permute-start | bytes 393224 | tf_op jit(solution)/shard_map/ppermute | solution.py:336
  343.2 18.3 %collective-permute-start.25 = (f32[32,8,128]{2,1,0:T(8,128)S(1)}, f32[32,8,128]{2,1,0:T(8,128)S(1)}, u32[]{:S(2)}, u32[]{:S(2)}) collective-permute-start(f32[32,8,128]{2,1,0:T(8,128)S(1)} %get-tuple-element.154), channel_id=1, source_target_pairs={{0,16},{8,24},{16,0},{24,8},{1,17},{9,25},{17,1},{25,9},{2,18},{10... | collective-permute-start | bytes 393224 | tf_op jit(solution)/shard_map/ppermute | solution.py:336
  343.3 18.2 %collective-permute-start.26 = (f32[32,8,128]{2,1,0:T(8,128)S(1)}, f32[32,8,128]{2,1,0:T(8,128)S(1)}, u32[]{:S(2)}, u32[]{:S(2)}) collective-permute-start(f32[32,8,128]{2,1,0:T(8,128)S(1)} %get-tuple-element.155), channel_id=1, source_target_pairs={{0,24},{8,0},{16,8},{24,16},{1,25},{9,1},{17,9},{25,17},{2,26},{10... | collective-permute-start | bytes 393224 | tf_op jit(solution)/shard_map/ppermute | solution.py:336
  350.3 11.2 %collective-permute-start.27 = (f32[32,8,128]{2,1,0:T(8,128)S(1)}, f32[32,8,128]{2,1,0:T(8,128)S(1)}, u32[]{:S(2)}, u32[]{:S(2)}) collective-permute-start(f32[32,8,128]{2,1,0:T(8,128)S(1)} %get-tuple-element.163), channel_id=1, source_target_pairs={{0,8},{8,16},{16,24},{24,0},{1,9},{9,17},{17,25},{25,1},{2,10},{10... | collective-permute-start | bytes 393224 | tf_op jit(solution)/shard_map/ppermute | solution.py:336
  353.6 13.5 %collective-permute-start.28 = (f32[32,8,128]{2,1,0:T(8,128)S(1)}, f32[32,8,128]{2,1,0:T(8,128)S(1)}, u32[]{:S(2)}, u32[]{:S(2)}) collective-permute-start(f32[32,8,128]{2,1,0:T(8,128)S(1)} %get-tuple-element.164), channel_id=1, source_target_pairs={{0,16},{8,24},{16,0},{24,8},{1,17},{9,25},{17,1},{25,9},{2,18},{10... | collective-permute-start | bytes 393224 | tf_op jit(solution)/shard_map/ppermute | solution.py:336
  353.6 13.5 %collective-permute-start.29 = (f32[32,8,128]{2,1,0:T(8,128)S(1)}, f32[32,8,128]{2,1,0:T(8,128)S(1)}, u32[]{:S(2)}, u32[]{:S(2)}) collective-permute-start(f32[32,8,128]{2,1,0:T(8,128)S(1)} %get-tuple-element.165), channel_id=1, source_target_pairs={{0,24},{8,0},{16,8},{24,16},{1,25},{9,1},{17,9},{25,17},{2,26},{10... | collective-permute-start | bytes 393224 | tf_op jit(solution)/shard_map/ppermute | solution.py:336
  (23 other events, 811.4 us)

commit v6 on v5

--- a/solution.py
+++ b/solution.py
@@ -1,4 +1,5 @@
 import functools
+import math
 
 import jax
 import jax.numpy as jnp
@@ -12,7 +13,8 @@
 BLOCK = 128
 SUB = 8
 HALF = 16
-AXES = ("gx", "gy", "gz")
+CHIPS = ("gx", "gy", "gu")
+CORES = "gc"
 VMEM = pl.BlockSpec(memory_space=pltpu.VMEM)
 SMEM = pl.BlockSpec(memory_space=pltpu.SMEM)
 ANY = pl.BlockSpec(memory_space=pl.ANY)
@@ -163,18 +165,26 @@
         a, b = a_ref[at, :], b_ref[at, :]
         columns = [jnp.broadcast_to(a[:, panel * SUB + k : panel * SUB + k + 1], wide) for k in range(SUB)]
         inverses, factors, scale = [], {}, jnp.zeros(wide, jnp.float32)
-        for j in range(SUB):
-            pivot = spread_row(columns[j], j)
+        for j in range(0, SUB, 2):
+            pivot, beside, corner = spread_row(columns[j], j), spread_row(columns[j + 1], j), spread_row(columns[j + 1], j + 1)
+            minor = pivot * corner - beside * beside
             inverse = 1.0 / pivot
-            inverses.append(inverse)
+            second = pivot * (1.0 / minor)
+            inverses += [inverse, second]
             scale = jnp.where(below == j, lax.rsqrt(pivot), scale)
+            scale = jnp.where(below == j + 1, lax.rsqrt(minor * inverse), scale)
+            factors[j, j + 1] = beside * inverse
             lower = jnp.where(below > j, columns[j], 0.0)
-            for k in range(j + 1, SUB):
+            after = jnp.where(below > j + 1, columns[j + 1] - columns[j] * factors[j, j + 1], 0.0)
+            for k in range(j + 2, SUB):
                 factors[j, k] = spread_row(columns[k], j) * inverse
-                columns[k] = columns[k] - lower * factors[j, k]
-            lower = lower * inverse
+                factors[j + 1, k] = (spread_row(columns[k], j + 1) - beside * factors[j, k]) * second
+                columns[k] = columns[k] - lower * factors[j, k] - after * factors[j + 1, k]
+            lower, after = lower * inverse, after * second
             a = a - lower * spread_row(a, j)
             b = b - lower * spread_row(b, j)
+            a = a - after * spread_row(a, j + 1)
+            b = b - after * spread_row(b, j + 1)
         w_ref[at, :] = b * scale
         a_rows = [spread_row(a, j) * inverses[j] for j in range(SUB)]
         b_rows = [spread_row(b, j) * inverses[j] for j in range(SUB)]
@@ -191,33 +201,31 @@
             b_ref[rows, :] = b
 
 
-def factor_kernel(groups, talls, me_ref, *refs):
-    phases = len(talls)
-    sums, refs = refs[:phases], refs[phases:]
-    mine_ref, turned_ref, gram_ref, m_ref, a_ref, b_ref, w_ref = refs
-    bases = [groups * sum(talls[:phase]) for phase in range(phases)]
-    xlocal = sum(talls)
-    for phase, tall in enumerate(talls):
-        slot = 0
-        first = bases[phase] // BLOCK
-        for row in range(first, first + groups * tall // BLOCK):
-            for column in range(row + 1):
-                block = sums[phase][slot * BLOCK : (slot + 1) * BLOCK, :]
-                slot += 1
-                gram_ref[row * BLOCK : (row + 1) * BLOCK, column * BLOCK : (column + 1) * BLOCK] = block
-                if row != column:
-                    gram_ref[column * BLOCK : (column + 1) * BLOCK, row * BLOCK : (row + 1) * BLOCK] = block.T
-    lines = []
-    for owner in range(-(-RANK // xlocal)):
-        for base, tall in zip(bases, talls):
-            lines.append(gram_ref[base + owner * tall : base + (owner + 1) * tall, :])
-    m_ref[...] = jnp.concatenate(lines, axis=0)[:RANK, :].T
+def factor_kernel(groups, xlocal, me_ref, core_ref, own_ref, other_ref, mine_ref, turned_ref, gram_ref, m_ref, a_ref, b_ref, w_ref):
+    first = core_ref[0] == 0
+    halves = own_ref.shape[0]
+    for row in range(groups * xlocal // BLOCK):
+        for column in range(row + 1):
+            at = (row * (row + 1) // 2 + column) * BLOCK
+            low = at < halves
+            at = slice(at % halves, at % halves + BLOCK)
+            own, other = own_ref[at, :], other_ref[at, :]
+            block = jnp.where(first, own, other) if low else jnp.where(first, other, own)
+            gram_ref[row * BLOCK : (row + 1) * BLOCK, column * BLOCK : (column + 1) * BLOCK] = block
+            if row != column:
+                gram_ref[column * BLOCK : (column + 1) * BLOCK, row * BLOCK : (row + 1) * BLOCK] = block.T
+    m_ref[...] = gram_ref[:, :RANK]
 
     def step(index, carry):
         m = m_ref[...]
-        a_ref[...] = product(m, m, ((0,), (0,)))
+        cross = product(m, m, ((0,), (0,)))
+        diagonal = lax.broadcasted_iota(jnp.int32, cross.shape, 0) == lax.broadcasted_iota(jnp.int32, cross.shape, 1)
+        diagonal = jnp.where(diagonal, cross, 0.0)
+        across = lax.rsqrt(jnp.sum(diagonal, axis=0, keepdims=True))
+        down = lax.rsqrt(jnp.sum(diagonal, axis=1, keepdims=True))
+        a_ref[...] = cross * across * down
         inverse_cholesky(a_ref, b_ref, w_ref)
-        basis = product(m, w_ref[...], ((1,), (1,)))
+        basis = product(m, w_ref[...] * across, ((1,), (1,)))
         m_ref[...] = basis
 
         @pl.when(index < ITERS)
@@ -227,24 +235,20 @@
         return carry
 
     lax.fori_loop(0, ITERS + 1, step, 0)
-    offset = 0
-    for base, tall in zip(bases, talls):
-        rows = pl.ds(pl.multiple_of(base + me_ref[0] * tall, SUB), tall)
-        mine_ref[offset : offset + tall, :] = m_ref[rows, :]
-        offset += tall
+    mine_ref[...] = m_ref[pl.ds(pl.multiple_of(me_ref[0] * xlocal, SUB), xlocal), :]
     turned_ref[...] = m_ref[...].T
 
 
-def factor_step(me, sums, groups, talls):
-    order, xlocal = groups * sum(talls), sum(talls)
+def factor_step(me, core, own, other, groups, xlocal):
+    order = groups * xlocal
     square = pltpu.VMEM((RANK, RANK), jnp.float32)
     return pl.pallas_call(
-        functools.partial(factor_kernel, groups, talls),
+        functools.partial(factor_kernel, groups, xlocal),
         out_shape=(
             jax.ShapeDtypeStruct((xlocal, RANK), jnp.float32),
             jax.ShapeDtypeStruct((RANK, order), jnp.float32),
         ),
-        in_specs=[SMEM] + [VMEM] * len(sums),
+        in_specs=[SMEM, SMEM, VMEM, VMEM],
         out_specs=(VMEM, VMEM),
         scratch_shapes=[
             pltpu.VMEM((order, order), jnp.float32),
@@ -254,7 +258,7 @@
             square,
         ],
         compiler_params=PARAMS,
-    )(me, *sums)
+    )(me, core, own, other)
 
 
 def core_kernel(groups, keep, steps, zlocal, phases, me_ref, turned_ref, *refs):
@@ -337,16 +341,19 @@
     return moved
 
 
-def total_sum(blocks, stages):
-    rows = blocks.shape[0]
-    flat = jnp.pad(blocks, ((0, -rows % lax.axis_size(AXES)), (0, 0)))
-    for axes in stages:
-        parts = flat.reshape(lax.axis_size(axes), -1, BLOCK)
-        flat = jnp.sum(lax.all_to_all(parts, axes, split_axis=0, concat_axis=0, tiled=True), axis=0)
-    for axes in reversed(stages):
-        spread = jnp.broadcast_to(flat[None], (lax.axis_size(axes), *flat.shape))
-        flat = lax.all_to_all(spread, axes, split_axis=0, concat_axis=0, tiled=True).reshape(-1, BLOCK)
-    return flat
+def total_sum(blocks, core):
+    chips = lax.axis_size(CHIPS)
+    swap = [(0, 1), (1, 0)]
+    unit = math.lcm(2 * chips, 2 * BLOCK)
+    blocks = jnp.pad(blocks, ((0, -blocks.shape[0] % unit), (0, 0)))
+    half = blocks.shape[0] // 2
+    other = lax.ppermute(lax.dynamic_slice_in_dim(blocks, (1 - core[0]) * half, half), CORES, swap)
+    own = lax.dynamic_slice_in_dim(blocks, core[0] * half, half) + other
+    parts = own.reshape(chips, -1, BLOCK)
+    share = jnp.sum(lax.all_to_all(parts, CHIPS, split_axis=0, concat_axis=0, tiled=True), axis=0)
+    spread = jnp.broadcast_to(share[None], parts.shape)
+    own = lax.all_to_all(spread, CHIPS, split_axis=0, concat_axis=0, tiled=True).reshape(half, BLOCK)
+    return own, lax.ppermute(own, CORES, swap)
 
 
 def hold(values, after):
@@ -364,8 +371,8 @@
     chunks = chunk_count(per)
     steps = per // chunks
     starts = [chunk * steps for chunk in range(chunks)]
-    talls = [xlocal]
     me = lax.axis_index("gx").astype(jnp.int32).reshape(1)
+    core = lax.axis_index(CORES).astype(jnp.int32).reshape(1)
 
     pieces = [(0, xlocal, start, steps) for start in starts]
     packed = pack(me, snapshot, groups, pieces[:1], 54 * 2**20)
@@ -380,13 +387,11 @@
 
     halves = []
     total = None
-    for index, parts in enumerate(moved):
-        limit = SMALL if index == chunks - 1 else LARGE
-        total, made = gram_step(me, parts, [[]], total, limit)
+    for parts in moved:
+        total, made = gram_step(me, parts, [[]], total, SMALL)
         halves.append(made)
-    sums = [total_sum(total, [AXES])]
-
-    mine, turned = factor_step(me, sums, groups, talls)
+    own, other = total_sum(total, core)
+    mine, turned = factor_step(me, core, own, other, groups, xlocal)
     outs = []
     for held in halves[-1:] + halves[:-1]:
         if len(outs) == 1:
@@ -397,6 +402,7 @@
 
 
 def solution(mesh):
-    in_specs = (P("gx", "gy", "gz"),)
-    out_specs = (P("gx", None), P("gx", "gy", "gz"))
-    return jax.shard_map(local, mesh=mesh, in_specs=in_specs, out_specs=out_specs, check_vma=False)
+    gx, gy, gz = mesh.devices.shape
+    mesh = jax.sharding.Mesh(mesh.devices.reshape(gx, gy, gz // 2, 2), (*CHIPS, CORES))
+    grid = P("gx", "gy", ("gu", CORES))
+    return jax.shard_map(local, mesh=mesh, in_specs=(grid,), out_specs=(P("gx", None), grid), check_vma=False)

time: 370 us -> 360 us (0.973)
  local copies, waits for them, and re-layouts: 14.9 us -> 33.6 us
  blocking collectives: 54.2 us -> 41.7 us
  Pallas kernels: 59.8 us -> 50.4 us
  waiting for transfers between devices: 134 us -> 127 us
    unnamed x50 -> x76, local copies, waits for them, and re-layouts: 14.8 us -> 32.8 us
    all_to_all x2, blocking collectives: 54.2 us -> 41.7 us  [the longest x1 27.5 us: total_sum(): lax.all_to_all(parts, CHIPS, split_axis=0, concat_axis=0, tiled=True)]
    ppermute x30, waiting for transfers between devices: 134 us -> 124 us  [exchange(): lax.ppermute(parts[shift], 'gx', [(i, (i + shift) % groups) for i in rang...]
    pallas_call x5, Pallas kernels: 24.7 us -> 17.3 us  [gram_step(): pl.pallas_call(functools.partial(gram_kernel, first, groups, chunks, len(...]
  transfers between devices with their start and end apart: 30 -> 32, of which waited for: 11 -> 13; matrix products, arithmetic and copies ran while one was open for 0% -> 0% of each run, Pallas kernels for 8% -> 6%
where the time goes in v6:
time: 360 us; the launch traced here: 359 us
  waiting for transfers between devices  127 us (35%)
  starting transfers between devices  104 us (29%)
  Pallas kernels  50.4 us (14%)
  blocking collectives  41.7 us (12%)
  local copies, waits for them, and re-layouts  33.6 us (9%)
    ppermute x30, waiting for transfers between devices, exchange(): lax.ppermute(parts[shift], 'gx', [(i, (i + shift) % groups) for i in rang...  124 us
    ppermute x30, starting transfers between devices, exchange(): lax.ppermute(parts[shift], 'gx', [(i, (i + shift) % groups) for i in rang...  104 us
    unnamed x76, local copies, waits for them, and re-layouts  32.8 us
    all_to_all x1, blocking collectives, total_sum(): lax.all_to_all(parts, CHIPS, split_axis=0, concat_axis=0, tiled=True)  27.5 us
    pallas_call x1, Pallas kernels, factor_step(): pl.pallas_call(functools.partial(factor_kernel, groups, xlocal), out_shap...  17.5 us
    pallas_call x5, Pallas kernels, gram_step(): pl.pallas_call(functools.partial(gram_kernel, first, groups, chunks, len(...  17.3 us
    all_to_all x1, blocking collectives, total_sum(): lax.all_to_all(spread, CHIPS, split_axis=0, concat_axis=0, tiled=True)  14.1 us
    pallas_call x2, Pallas kernels, pack(): pl.pallas_call(functools.partial(pack_kernel, groups, per, tuple(pieces))...  10.1 us
  transfers between devices with their start and end apart: 32, of which 13 were waited for; matrix products, arithmetic and copies ran while one was open for 0% of the time, Pallas kernels for 6%

profile of v6, /device:TPU:0, one launch (start us, length us, event | category | flops | bytes accessed | tf_op | source)
XLA Modules:
  0.0 358.8 jit_solution(13506129520597978285)
XLA Ops:
  0.6 3.6 shard_map.31
  4.2 3.1 collective-permute-start
  7.3 2.6 collective-permute-start.1
  11.2 6.6 %shard_map.30 = (f32[8,128,128]{2,1,0:T(8,128)S(1)}, f32[8,128,128]{2,1,0:T(8,128)S(1)}, f32[8,128,128]{2,1,0:T(8,128)S(1)}, f32[8,128,128]{2,1,0:T(8,128)S(1)},...) custom-call(s32[1]{0:T(128)} %bitcast.me_ref, ...), custom_call_target="tpu_custom_call" | custom-call | bytes 16777216 | tf_op jit(solution)/shard_map/pallas_call | solution.py:75
  22.4 2.5 collective-permute-start.11
  24.9 20.0 %collective-permute-done.1.refs_2_ = f32[8,128,128]{2,1,0:T(8,128)S(1)} collective-permute-done((f32[8,128,128]{2,1,0:T(8,128)}, f32[8,128,128]{2,1,0:T(8,128)S(1)}, u32[]{:S(2)}, u32[]{:S(2)}) %collective-permute-start.1) | collective-permute-done | bytes 524320 | tf_op jit(solution)/shard_map/ppermute | solution.py:340
  44.9 34.3 %collective-permute-start.3 = (f32[8,128,128]{2,1,0:T(8,128)S(1)}, f32[8,128,128]{2,1,0:T(8,128)S(1)}, u32[]{:S(2)}, u32[]{:S(2)}) collective-permute-start(f32[8,128,128]{2,1,0:T(8,128)S(1)} %get-tuple-element.97), channel_id=1, source_target_pairs={{0,8},{8,16},{16,24},{24,0},{1,9},{9,17},{17,25},{25,1},{2,10},{10... | collective-permute-start | bytes 1572872 | tf_op jit(solution)/shard_map/ppermute | solution.py:340
  82.4 29.2 %collective-permute-done.10.refs_2_ = f32[8,128,128]{2,1,0:T(8,128)S(1)} collective-permute-done((f32[8,128,128]{2,1,0:T(8,128)S(1)}, f32[8,128,128]{2,1,0:T(8,128)S(1)}, u32[]{:S(2)}, u32[]{:S(2)}) %collective-permute-start.10) | collective-permute-done | bytes 524320 | tf_op jit(solution)/shard_map/ppermute | solution.py:340
  113.1 11.1 %collective-permute-start.12 = (f32[8,128,128]{2,1,0:T(8,128)S(1)}, f32[8,128,128]{2,1,0:T(8,128)S(1)}, u32[]{:S(2)}, u32[]{:S(2)}) collective-permute-start(f32[8,128,128]{2,1,0:T(8,128)S(1)} %get-tuple-element.113), channel_id=1, source_target_pairs={{0,8},{8,16},{16,24},{24,0},{1,9},{9,17},{17,25},{25,1},{2,10},{10... | collective-permute-start | bytes 1572872 | tf_op jit(solution)/shard_map/ppermute | solution.py:340
  124.2 3.4 collective-permute-start.13
  128.4 28.1 %collective-permute-done.4.refs_2_ = f32[8,128,128]{2,1,0:T(8,128)S(1)} collective-permute-done((f32[8,128,128]{2,1,0:T(8,128)S(1)}, f32[8,128,128]{2,1,0:T(8,128)S(1)}, u32[]{:S(2)}, u32[]{:S(2)}) %collective-permute-start.4) | collective-permute-done | bytes 524320 | tf_op jit(solution)/shard_map/ppermute | solution.py:340
  158.1 11.1 %collective-permute-start.6 = (f32[8,128,128]{2,1,0:T(8,128)}, f32[8,128,128]{2,1,0:T(8,128)}, u32[]{:S(2)}, u32[]{:S(2)}) collective-permute-start(f32[8,128,128]{2,1,0:T(8,128)} %get-tuple-element.101), channel_id=1, source_target_pairs={{0,8},{8,16},{16,24},{24,0},{1,9},{9,17},{17,25},{25,1},{2,10},{10... | collective-permute-start | bytes 1572872 | tf_op jit(solution)/shard_map/ppermute | solution.py:340
  169.2 3.4 collective-permute-start.7
  173.4 2.8 shard_map.32
  182.4 3.0 shard_map.33
  190.9 3.0 shard_map.34
  194.8 6.7 %collective-permute-done.13.refs_2_ = f32[8,128,128]{2,1,0:T(8,128)} collective-permute-done((f32[8,128,128]{2,1,0:T(8,128)S(1)}, f32[8,128,128]{2,1,0:T(8,128)}, u32[]{:S(2)}, u32[]{:S(2)}) %collective-permute-start.13) | collective-permute-done | bytes 524320 | tf_op jit(solution)/shard_map/ppermute | solution.py:340
  201.6 4.2 %shard_map.35 = (f32[1280,128]{1,0:T(8,128)S(1)}, bf16[512,1024]{1,0:T(8,128)(2,1)S(1)}, bf16[512,1024]{1,0:T(8,128)(2,1)S(1)}) custom-call(s32[1]{0:T(128)} %bitcast.me_ref, f32[8,128,128]{2,1,0:T(8,128)S(1)} %copy-done.18, f32[8,128,128]{2,1,0:T(8,128)S(1)} %copy-done.35, f32[8,128,128]{2,1,0:T(8,128)} %collective-permute-done.13.refs_2_, ...), custom_call_target="tpu_custom_call" | custom-call | flops 1006632960 | bytes 4194304 | tf_op jit(solution)/shard_map/pallas_call | solution.py:139
  205.8 18.2 %collective-permute-done.7.refs_2_ = f32[8,128,128]{2,1,0:T(8,128)} collective-permute-done((f32[8,128,128]{2,1,0:T(8,128)}, f32[8,128,128]{2,1,0:T(8,128)}, u32[]{:S(2)}, u32[]{:S(2)}) %collective-permute-start.7) | collective-permute-done | bytes 524320 | tf_op jit(solution)/shard_map/ppermute | solution.py:340
  224.0 4.4 %shard_map.36 = (f32[1280,128]{1,0:T(8,128)S(1)}, bf16[512,1024]{1,0:T(8,128)(2,1)S(1)}, bf16[512,1024]{1,0:T(8,128)(2,1)S(1)}) custom-call(s32[1]{0:T(128)} %bitcast.me_ref, f32[8,128,128]{2,1,0:T(8,128)S(1)} %copy-done.16, f32[8,128,128]{2,1,0:T(8,128)} %collective-permute-done.6.refs_1_, f32[8,128,128]{2,1,0:T(8,128)} %collective-permute-done.7.refs_2_, ...), custom_call_target="tpu_custom_call" | custom-call | flops 1006632960 | bytes 4194304 | tf_op jit(solution)/shard_map/pallas_call | solution.py:139
  234.8 27.5 %all_to_all.10 = f32[16,40,128]{2,1,0:T(8,128)S(1)} all-to-all(f32[16,40,128]{2,1,0:T(8,128)S(1)} %bitcast.6), channel_id=1, replica_groups=mesh['gx'=4,'gy'=2,'gu'=2,'gc'=2] {'gx','gy','gu'}, dimensions={0} | all-to-all | bytes 655360 | tf_op jit(solution)/shard_map/all_to_all | solution.py:353
  262.4 14.1 %all_to_all.11 = f32[16,40,128]{2,1,0:T(8,128)S(1)} all-to-all(f32[16,40,128]{2,1,0:T(8,128)S(1)} %broadcast_in_dim.2), channel_id=1, replica_groups=mesh['gx'=4,'gy'=2,'gu'=2,'gc'=2] {'gx','gy','gu'}, dimensions={0} | all-to-all | bytes 655360 | tf_op jit(solution)/shard_map/all_to_all | solution.py:355
  278.2 17.5 %shard_map.37 = (f32[128,128]{1,0:T(8,128)}, f32[128,512]{1,0:T(8,128)S(1)}) custom-call(s32[1]{0:T(128)} %bitcast.me_ref, s32[1]{0:T(128)} %bitcast.1.core_ref, f32[640,128]{1,0:T(8,128)S(1)} %bitcast.5, f32[640,128]{1,0:T(8,128)S(1)} %collective-permute-done.16.other_ref), custom_call_target="tpu_custom_call" | custom-call | tf_op jit(solution)/shard_map/pallas_call | solution.py:245
  308.1 2.8 collective-permute-start.22
  314.2 2.6 collective-permute-done.18.refs_2_
  316.8 5.0 %collective-permute-start.23 = (f32[32,8,128]{2,1,0:T(8,128)S(1)}, f32[32,8,128]{2,1,0:T(8,128)S(1)}, u32[]{:S(2)}, u32[]{:S(2)}) collective-permute-start(f32[32,8,128]{2,1,0:T(8,128)S(1)} %get-tuple-element.143), channel_id=1, source_target_pairs={{0,8},{8,16},{16,24},{24,0},{1,9},{9,17},{17,25},{25,1},{2,10},{10... | collective-permute-start | bytes 393224 | tf_op jit(solution)/shard_map/ppermute | solution.py:340
  326.2 2.7 collective-permute-done.21.refs_6_
  328.8 3.4 collective-permute-start.26
  335.4 4.6 %collective-permute-done.24.refs_10_ = f32[32,8,128]{2,1,0:T(8,128)S(1)} collective-permute-done((f32[32,8,128]{2,1,0:T(8,128)S(1)}, f32[32,8,128]{2,1,0:T(8,128)S(1)}, u32[]{:S(2)}, u32[]{:S(2)}) %collective-permute-start.24) | collective-permute-done | bytes 131104 | tf_op jit(solution)/shard_map/ppermute | solution.py:340
  340.1 3.4 collective-permute-start.29
  345.8 5.5 %collective-permute-done.27.refs_14_ = f32[32,8,128]{2,1,0:T(8,128)S(1)} collective-permute-done((f32[32,8,128]{2,1,0:T(8,128)S(1)}, f32[32,8,128]{2,1,0:T(8,128)S(1)}, u32[]{:S(2)}, u32[]{:S(2)}) %collective-permute-start.27) | collective-permute-done | bytes 131104 | tf_op jit(solution)/shard_map/ppermute | solution.py:340
  351.3 5.6 %collective-permute-done.30.refs_18_ = f32[32,8,128]{2,1,0:T(8,128)S(1)} collective-permute-done((f32[32,8,128]{2,1,0:T(8,128)S(1)}, f32[32,8,128]{2,1,0:T(8,128)S(1)}, u32[]{:S(2)}, u32[]{:S(2)}) %collective-permute-start.30) | collective-permute-done | bytes 131104 | tf_op jit(solution)/shard_map/ppermute | solution.py:340
  (128 shorter events, 61.9 us)
Async XLA Ops:
  4.2 18.2 %collective-permute-start = (f32[8,128,128]{2,1,0:T(8,128)}, f32[8,128,128]{2,1,0:T(8,128)S(1)}, u32[]{:S(2)}, u32[]{:S(2)}) collective-permute-start(f32[8,128,128]{2,1,0:T(8,128)} %get-tuple-element.93), channel_id=1, source_target_pairs={{0,8},{8,16},{16,24},{24,0},{1,9},{9,17},{17,25},{25,1},{2,10},{10... | collective-permute-start | bytes 1572872 | tf_op jit(solution)/shard_map/ppermute | solution.py:340
  7.3 37.6 %collective-permute-start.1 = (f32[8,128,128]{2,1,0:T(8,128)}, f32[8,128,128]{2,1,0:T(8,128)S(1)}, u32[]{:S(2)}, u32[]{:S(2)}) collective-permute-start(f32[8,128,128]{2,1,0:T(8,128)} %get-tuple-element.94), channel_id=1, source_target_pairs={{0,16},{8,24},{16,0},{24,8},{1,17},{9,25},{17,1},{25,9},{2,18},{10... | collective-permute-start | bytes 1572872 | tf_op jit(solution)/shard_map/ppermute | solution.py:340
  9.9 35.1 %collective-permute-start.2 = (f32[8,128,128]{2,1,0:T(8,128)}, f32[8,128,128]{2,1,0:T(8,128)S(1)}, u32[]{:S(2)}, u32[]{:S(2)}) collective-permute-start(f32[8,128,128]{2,1,0:T(8,128)} %get-tuple-element.95), channel_id=1, source_target_pairs={{0,24},{8,0},{16,8},{24,16},{1,25},{9,1},{17,9},{25,17},{2,26},{10... | collective-permute-start | bytes 1572872 | tf_op jit(solution)/shard_map/ppermute | solution.py:340
  21.1 59.9 %collective-permute-start.9 = (f32[8,128,128]{2,1,0:T(8,128)S(1)}, f32[8,128,128]{2,1,0:T(8,128)S(1)}, u32[]{:S(2)}, u32[]{:S(2)}) collective-permute-start(f32[8,128,128]{2,1,0:T(8,128)S(1)} %get-tuple-element.109), channel_id=1, source_target_pairs={{0,8},{8,16},{16,24},{24,0},{1,9},{9,17},{17,25},{25,1},{2,10},{10... | collective-permute-start | bytes 1572872 | tf_op jit(solution)/shard_map/ppermute | solution.py:340
  21.7 89.8 %collective-permute-start.10 = (f32[8,128,128]{2,1,0:T(8,128)S(1)}, f32[8,128,128]{2,1,0:T(8,128)S(1)}, u32[]{:S(2)}, u32[]{:S(2)}) collective-permute-start(f32[8,128,128]{2,1,0:T(8,128)S(1)} %get-tuple-element.110), channel_id=1, source_target_pairs={{0,16},{8,24},{16,0},{24,8},{1,17},{9,25},{17,1},{25,9},{2,18},{10... | collective-permute-start | bytes 1572872 | tf_op jit(solution)/shard_map/ppermute | solution.py:340
  22.4 89.9 %collective-permute-start.11 = (f32[8,128,128]{2,1,0:T(8,128)S(1)}, f32[8,128,128]{2,1,0:T(8,128)S(1)}, u32[]{:S(2)}, u32[]{:S(2)}) collective-permute-start(f32[8,128,128]{2,1,0:T(8,128)S(1)} %get-tuple-element.111), channel_id=1, source_target_pairs={{0,24},{8,0},{16,8},{24,16},{1,25},{9,1},{17,9},{25,17},{2,26},{10... | collective-permute-start | bytes 1572872 | tf_op jit(solution)/shard_map/ppermute | solution.py:340
  44.9 82.7 %collective-permute-start.3 = (f32[8,128,128]{2,1,0:T(8,128)S(1)}, f32[8,128,128]{2,1,0:T(8,128)S(1)}, u32[]{:S(2)}, u32[]{:S(2)}) collective-permute-start(f32[8,128,128]{2,1,0:T(8,128)S(1)} %get-tuple-element.97), channel_id=1, source_target_pairs={{0,8},{8,16},{16,24},{24,0},{1,9},{9,17},{17,25},{25,1},{2,10},{10... | collective-permute-start | bytes 1572872 | tf_op jit(solution)/shard_map/ppermute | solution.py:340
  79.2 77.3 %collective-permute-start.4 = (f32[8,128,128]{2,1,0:T(8,128)S(1)}, f32[8,128,128]{2,1,0:T(8,128)S(1)}, u32[]{:S(2)}, u32[]{:S(2)}) collective-permute-start(f32[8,128,128]{2,1,0:T(8,128)S(1)} %get-tuple-element.98), channel_id=1, source_target_pairs={{0,16},{8,24},{16,0},{24,8},{1,17},{9,25},{17,1},{25,9},{2,18},{10... | collective-permute-start | bytes 1572872 | tf_op jit(solution)/shard_map/ppermute | solution.py:340
  81.8 75.5 %collective-permute-start.5 = (f32[8,128,128]{2,1,0:T(8,128)S(1)}, f32[8,128,128]{2,1,0:T(8,128)S(1)}, u32[]{:S(2)}, u32[]{:S(2)}) collective-permute-start(f32[8,128,128]{2,1,0:T(8,128)S(1)} %get-tuple-element.99), channel_id=1, source_target_pairs={{0,24},{8,0},{16,8},{24,16},{1,25},{9,1},{17,9},{25,17},{2,26},{10... | collective-permute-start | bytes 1572872 | tf_op jit(solution)/shard_map/ppermute | solution.py:340
  113.1 59.4 %collective-permute-start.12 = (f32[8,128,128]{2,1,0:T(8,128)S(1)}, f32[8,128,128]{2,1,0:T(8,128)S(1)}, u32[]{:S(2)}, u32[]{:S(2)}) collective-permute-start(f32[8,128,128]{2,1,0:T(8,128)S(1)} %get-tuple-element.113), channel_id=1, source_target_pairs={{0,8},{8,16},{16,24},{24,0},{1,9},{9,17},{17,25},{25,1},{2,10},{10... | collective-permute-start | bytes 1572872 | tf_op jit(solution)/shard_map/ppermute | solution.py:340
  124.2 77.3 %collective-permute-start.13 = (f32[8,128,128]{2,1,0:T(8,128)S(1)}, f32[8,128,128]{2,1,0:T(8,128)}, u32[]{:S(2)}, u32[]{:S(2)}) collective-permute-start(f32[8,128,128]{2,1,0:T(8,128)S(1)} %get-tuple-element.114), channel_id=1, source_target_pairs={{0,16},{8,24},{16,0},{24,8},{1,17},{9,25},{17,1},{25,9},{2,18},{10... | collective-permute-start | bytes 1572872 | tf_op jit(solution)/shard_map/ppermute | solution.py:340
  128.4 73.1 %collective-permute-start.14 = (f32[8,128,128]{2,1,0:T(8,128)S(1)}, f32[8,128,128]{2,1,0:T(8,128)}, u32[]{:S(2)}, u32[]{:S(2)}) collective-permute-start(f32[8,128,128]{2,1,0:T(8,128)S(1)} %get-tuple-element.115), channel_id=1, source_target_pairs={{0,24},{8,0},{16,8},{24,16},{1,25},{9,1},{17,9},{25,17},{2,26},{10... | collective-permute-start | bytes 1572872 | tf_op jit(solution)/shard_map/ppermute | solution.py:340
  158.1 47.7 %collective-permute-start.6 = (f32[8,128,128]{2,1,0:T(8,128)}, f32[8,128,128]{2,1,0:T(8,128)}, u32[]{:S(2)}, u32[]{:S(2)}) collective-permute-start(f32[8,128,128]{2,1,0:T(8,128)} %get-tuple-element.101), channel_id=1, source_target_pairs={{0,8},{8,16},{16,24},{24,0},{1,9},{9,17},{17,25},{25,1},{2,10},{10... | collective-permute-start | bytes 1572872 | tf_op jit(solution)/shard_map/ppermute | solution.py:340
  169.2 54.8 %collective-permute-start.7 = (f32[8,128,128]{2,1,0:T(8,128)}, f32[8,128,128]{2,1,0:T(8,128)}, u32[]{:S(2)}, u32[]{:S(2)}) collective-permute-start(f32[8,128,128]{2,1,0:T(8,128)} %get-tuple-element.102), channel_id=1, source_target_pairs={{0,16},{8,24},{16,0},{24,8},{1,17},{9,25},{17,1},{25,9},{2,18},{10... | collective-permute-start | bytes 1572872 | tf_op jit(solution)/shard_map/ppermute | solution.py:340
  173.4 50.6 %collective-permute-start.8 = (f32[8,128,128]{2,1,0:T(8,128)}, f32[8,128,128]{2,1,0:T(8,128)}, u32[]{:S(2)}, u32[]{:S(2)}) collective-permute-start(f32[8,128,128]{2,1,0:T(8,128)} %get-tuple-element.103), channel_id=1, source_target_pairs={{0,24},{8,0},{16,8},{24,16},{1,25},{9,1},{17,9},{25,17},{2,26},{10... | collective-permute-start | bytes 1572872 | tf_op jit(solution)/shard_map/ppermute | solution.py:340
  232.0 1.8 collective-permute-start.15
  276.5 1.6 collective-permute-start.16
  298.9 9.3 %collective-permute-start.17 = (f32[32,8,128]{2,1,0:T(8,128)S(1)}, f32[32,8,128]{2,1,0:T(8,128)S(1)}, u32[]{:S(2)}, u32[]{:S(2)}) collective-permute-start(f32[32,8,128]{2,1,0:T(8,128)S(1)} %get-tuple-element.126), channel_id=1, source_target_pairs={{0,8},{8,16},{16,24},{24,0},{1,9},{9,17},{17,25},{25,1},{2,10},{10... | collective-permute-start | bytes 393224 | tf_op jit(solution)/shard_map/ppermute | solution.py:340
  299.9 16.9 %collective-permute-start.18 = (f32[32,8,128]{2,1,0:T(8,128)S(1)}, f32[32,8,128]{2,1,0:T(8,128)S(1)}, u32[]{:S(2)}, u32[]{:S(2)}) collective-permute-start(f32[32,8,128]{2,1,0:T(8,128)S(1)} %get-tuple-element.127), channel_id=1, source_target_pairs={{0,16},{8,24},{16,0},{24,8},{1,17},{9,25},{17,1},{25,9},{2,18},{10... | collective-permute-start | bytes 393224 | tf_op jit(solution)/shard_map/ppermute | solution.py:340
  301.1 15.7 %collective-permute-start.19 = (f32[32,8,128]{2,1,0:T(8,128)S(1)}, f32[32,8,128]{2,1,0:T(8,128)S(1)}, u32[]{:S(2)}, u32[]{:S(2)}) collective-permute-start(f32[32,8,128]{2,1,0:T(8,128)S(1)} %get-tuple-element.128), channel_id=1, source_target_pairs={{0,24},{8,0},{16,8},{24,16},{1,25},{9,1},{17,9},{25,17},{2,26},{10... | collective-permute-start | bytes 393224 | tf_op jit(solution)/shard_map/ppermute | solution.py:340
  306.0 15.8 %collective-permute-start.20 = (f32[32,8,128]{2,1,0:T(8,128)S(1)}, f32[32,8,128]{2,1,0:T(8,128)S(1)}, u32[]{:S(2)}, u32[]{:S(2)}) collective-permute-start(f32[32,8,128]{2,1,0:T(8,128)S(1)} %get-tuple-element.133), channel_id=1, source_target_pairs={{0,8},{8,16},{16,24},{24,0},{1,9},{9,17},{17,25},{25,1},{2,10},{10... | collective-permute-start | bytes 393224 | tf_op jit(solution)/shard_map/ppermute | solution.py:340
  306.6 22.3 %collective-permute-start.21 = (f32[32,8,128]{2,1,0:T(8,128)S(1)}, f32[32,8,128]{2,1,0:T(8,128)S(1)}, u32[]{:S(2)}, u32[]{:S(2)}) collective-permute-start(f32[32,8,128]{2,1,0:T(8,128)S(1)} %get-tuple-element.134), channel_id=1, source_target_pairs={{0,16},{8,24},{16,0},{24,8},{1,17},{9,25},{17,1},{25,9},{2,18},{10... | collective-permute-start | bytes 393224 | tf_op jit(solution)/shard_map/ppermute | solution.py:340
  308.1 20.7 %collective-permute-start.22 = (f32[32,8,128]{2,1,0:T(8,128)S(1)}, f32[32,8,128]{2,1,0:T(8,128)S(1)}, u32[]{:S(2)}, u32[]{:S(2)}) collective-permute-start(f32[32,8,128]{2,1,0:T(8,128)S(1)} %get-tuple-element.135), channel_id=1, source_target_pairs={{0,24},{8,0},{16,8},{24,16},{1,25},{9,1},{17,9},{25,17},{2,26},{10... | collective-permute-start | bytes 393224 | tf_op jit(solution)/shard_map/ppermute | solution.py:340
  316.8 16.2 %collective-permute-start.23 = (f32[32,8,128]{2,1,0:T(8,128)S(1)}, f32[32,8,128]{2,1,0:T(8,128)S(1)}, u32[]{:S(2)}, u32[]{:S(2)}) collective-permute-start(f32[32,8,128]{2,1,0:T(8,128)S(1)} %get-tuple-element.143), channel_id=1, source_target_pairs={{0,8},{8,16},{16,24},{24,0},{1,9},{9,17},{17,25},{25,1},{2,10},{10... | collective-permute-start | bytes 393224 | tf_op jit(solution)/shard_map/ppermute | solution.py:340
  321.8 18.3 %collective-permute-start.24 = (f32[32,8,128]{2,1,0:T(8,128)S(1)}, f32[32,8,128]{2,1,0:T(8,128)S(1)}, u32[]{:S(2)}, u32[]{:S(2)}) collective-permute-start(f32[32,8,128]{2,1,0:T(8,128)S(1)} %get-tuple-element.144), channel_id=1, source_target_pairs={{0,16},{8,24},{16,0},{24,8},{1,17},{9,25},{17,1},{25,9},{2,18},{10... | collective-permute-start | bytes 393224 | tf_op jit(solution)/shard_map/ppermute | solution.py:340
  321.8 18.3 %collective-permute-start.25 = (f32[32,8,128]{2,1,0:T(8,128)S(1)}, f32[32,8,128]{2,1,0:T(8,128)S(1)}, u32[]{:S(2)}, u32[]{:S(2)}) collective-permute-start(f32[32,8,128]{2,1,0:T(8,128)S(1)} %get-tuple-element.145), channel_id=1, source_target_pairs={{0,24},{8,0},{16,8},{24,16},{1,25},{9,1},{17,9},{25,17},{2,26},{10... | collective-permute-start | bytes 393224 | tf_op jit(solution)/shard_map/ppermute | solution.py:340
  328.8 14.6 %collective-permute-start.26 = (f32[32,8,128]{2,1,0:T(8,128)S(1)}, f32[32,8,128]{2,1,0:T(8,128)S(1)}, u32[]{:S(2)}, u32[]{:S(2)}) collective-permute-start(f32[32,8,128]{2,1,0:T(8,128)S(1)} %get-tuple-element.153), channel_id=1, source_target_pairs={{0,8},{8,16},{16,24},{24,0},{1,9},{9,17},{17,25},{25,1},{2,10},{10... | collective-permute-start | bytes 393224 | tf_op jit(solution)/shard_map/ppermute | solution.py:340
  333.0 18.3 %collective-permute-start.27 = (f32[32,8,128]{2,1,0:T(8,128)S(1)}, f32[32,8,128]{2,1,0:T(8,128)S(1)}, u32[]{:S(2)}, u32[]{:S(2)}) collective-permute-start(f32[32,8,128]{2,1,0:T(8,128)S(1)} %get-tuple-element.154), channel_id=1, source_target_pairs={{0,16},{8,24},{16,0},{24,8},{1,17},{9,25},{17,1},{25,9},{2,18},{10... | collective-permute-start | bytes 393224 | tf_op jit(solution)/shard_map/ppermute | solution.py:340
  333.1 18.2 %collective-permute-start.28 = (f32[32,8,128]{2,1,0:T(8,128)S(1)}, f32[32,8,128]{2,1,0:T(8,128)S(1)}, u32[]{:S(2)}, u32[]{:S(2)}) collective-permute-start(f32[32,8,128]{2,1,0:T(8,128)S(1)} %get-tuple-element.155), channel_id=1, source_target_pairs={{0,24},{8,0},{16,8},{24,16},{1,25},{9,1},{17,9},{25,17},{2,26},{10... | collective-permute-start | bytes 393224 | tf_op jit(solution)/shard_map/ppermute | solution.py:340
  340.1 11.2 %collective-permute-start.29 = (f32[32,8,128]{2,1,0:T(8,128)S(1)}, f32[32,8,128]{2,1,0:T(8,128)S(1)}, u32[]{:S(2)}, u32[]{:S(2)}) collective-permute-start(f32[32,8,128]{2,1,0:T(8,128)S(1)} %get-tuple-element.163), channel_id=1, source_target_pairs={{0,8},{8,16},{16,24},{24,0},{1,9},{9,17},{17,25},{25,1},{2,10},{10... | collective-permute-start | bytes 393224 | tf_op jit(solution)/shard_map/ppermute | solution.py:340
  343.4 13.5 %collective-permute-start.30 = (f32[32,8,128]{2,1,0:T(8,128)S(1)}, f32[32,8,128]{2,1,0:T(8,128)S(1)}, u32[]{:S(2)}, u32[]{:S(2)}) collective-permute-start(f32[32,8,128]{2,1,0:T(8,128)S(1)} %get-tuple-element.164), channel_id=1, source_target_pairs={{0,16},{8,24},{16,0},{24,8},{1,17},{9,25},{17,1},{25,9},{2,18},{10... | collective-permute-start | bytes 393224 | tf_op jit(solution)/shard_map/ppermute | solution.py:340
  343.4 13.5 %collective-permute-start.31 = (f32[32,8,128]{2,1,0:T(8,128)S(1)}, f32[32,8,128]{2,1,0:T(8,128)S(1)}, u32[]{:S(2)}, u32[]{:S(2)}) collective-permute-start(f32[32,8,128]{2,1,0:T(8,128)S(1)} %get-tuple-element.165), channel_id=1, source_target_pairs={{0,24},{8,0},{16,8},{24,16},{1,25},{9,1},{17,9},{25,17},{2,26},{10... | collective-permute-start | bytes 393224 | tf_op jit(solution)/shard_map/ppermute | solution.py:340
  (38 other events, 324.2 us)

commit v7 on v6

--- a/solution.py
+++ b/solution.py
@@ -19,7 +19,7 @@
 SMEM = pl.BlockSpec(memory_space=pltpu.SMEM)
 ANY = pl.BlockSpec(memory_space=pl.ANY)
 HBM = pl.BlockSpec(memory_space=pltpu.HBM)
-SMALL, LARGE = 12 * 2**20, 56 * 2**20
+SMALL, LARGE = 12 * 2**20, 54 * 2**20
 PARAMS = pltpu.CompilerParams(vmem_limit_bytes=SMALL)
 
 
@@ -86,67 +86,70 @@
     return [list(parts[at : at + groups]) for at in range(0, len(parts), groups)]
 
 
-def gram_kernel(first, groups, chunks, earlier, me_ref, *refs):
+def gram_kernel(first, final, groups, me_ref, core_ref, *refs):
     parts, refs = refs[:groups], refs[groups:]
-    held, refs = refs[: 2 * chunks * earlier], refs[2 * chunks * earlier :]
     old_ref, refs = (None, refs) if first else (refs[0], refs[1:])
-    out_ref, made = refs[0], refs[1:]
-    wide, tall, zlocal = parts[0].shape
-    steps = wide // chunks
+    out_ref, (high_ref, low_ref) = (refs[-1], refs[2:4]) if final else (refs[0], refs[1:])
+    steps, tall, zlocal = parts[0].shape
     last = ((1,), (1,))
-    for chunk in range(chunks):
-        high_ref, low_ref = made[2 * chunk : 2 * chunk + 2]
-        for shift in range(groups):
-            owner = lax.rem(me_ref[0] + groups - shift, groups)
-            rows = pl.ds(pl.multiple_of(owner * tall, HALF), tall)
-            for step in range(steps):
-                high, low = split(parts[shift][chunk * steps + step])
-                columns = slice(step * zlocal, (step + 1) * zlocal)
-                high_ref[rows, columns] = high
-                low_ref[rows, columns] = low
-        pairs = held[2 * chunk * earlier : 2 * (chunk + 1) * earlier]
-        pairs = [*zip(pairs[::2], pairs[1::2]), (high_ref, low_ref)]
-        slot = 0
-        for row in range(groups * tall // BLOCK):
-            mine = slice(row * BLOCK, (row + 1) * BLOCK)
-            for other_high, other_low in pairs:
-                upto = slice(0, (row + 1) * BLOCK if other_high is high_ref else other_high.shape[0])
-                total = dot(high_ref[mine, :], other_high[upto, :], last)
-                total += dot(high_ref[mine, :], other_low[upto, :], last)
-                total += dot(low_ref[mine, :], other_high[upto, :], last)
-                for column in range(upto.stop // BLOCK):
-                    at = slice(slot * BLOCK, (slot + 1) * BLOCK)
-                    block = total[:, column * BLOCK : (column + 1) * BLOCK]
-                    if chunk:
-                        block += out_ref[at, :]
-                    elif not first:
-                        block += old_ref[at, :]
-                    out_ref[at, :] = block
-                    slot += 1
-
-
-def gram_step(me, parts, earlier, old, limit):
-    groups, chunks = len(parts), len(earlier)
-    wide, tall, zlocal = parts[0].shape
+    for shift in range(groups):
+        owner = lax.rem(me_ref[0] + groups - shift, groups)
+        rows = pl.ds(pl.multiple_of(owner * tall, HALF), tall)
+        for step in range(steps):
+            high, low = split(parts[shift][step])
+            columns = slice(step * zlocal, (step + 1) * zlocal)
+            high_ref[rows, columns] = high
+            low_ref[rows, columns] = low
+    slot = 0
+    for row in range(groups * tall // BLOCK):
+        mine = slice(row * BLOCK, (row + 1) * BLOCK)
+        upto = slice(0, (row + 1) * BLOCK)
+        total = dot(high_ref[mine, :], high_ref[upto, :], last)
+        total += dot(high_ref[mine, :], low_ref[upto, :], last)
+        total += dot(low_ref[mine, :], high_ref[upto, :], last)
+        for column in range(row + 1):
+            at = slice(slot * BLOCK, (slot + 1) * BLOCK)
+            block = total[:, column * BLOCK : (column + 1) * BLOCK]
+            out_ref[at, :] = block if first else block + old_ref[at, :]
+            slot += 1
+    if final:
+        own_ref, other_ref = refs[:2]
+        half = own_ref.shape[0]
+        if slot * BLOCK < 2 * half:
+            out_ref[slot * BLOCK :, :] = jnp.zeros((2 * half - slot * BLOCK, BLOCK), jnp.float32)
+        low, high = out_ref[:half, :], out_ref[half:, :]
+        own_ref[...] = jnp.where(core_ref[0] == 0, low, high)
+        other_ref[...] = jnp.where(core_ref[0] == 0, high, low)
+
+
+def gram_step(me, core, parts, old, unit):
+    groups = len(parts)
+    steps, tall, zlocal = parts[0].shape
     rows = groups * tall
-    before = sum(high.shape[0] for high, _ in earlier[0])
-    done, count = before // BLOCK, rows // BLOCK
-    slots = done * count + count * (count + 1) // 2
-    first = old is None
-    half = jax.ShapeDtypeStruct((rows, wide // chunks * zlocal), jnp.bfloat16)
-    operands = [me, *parts, *(half for held in earlier for pair in held for half in pair)]
-    operands += [] if first else [old]
-    total, *made = pl.pallas_call(
-        functools.partial(gram_kernel, first, groups, chunks, len(earlier[0])),
-        out_shape=(jax.ShapeDtypeStruct((slots * BLOCK, BLOCK), jnp.float32),) + (half,) * (2 * chunks),
-        in_specs=[SMEM] + [VMEM] * (len(operands) - 1),
-        out_specs=(VMEM,) * (1 + 2 * chunks),
-        compiler_params=pltpu.CompilerParams(vmem_limit_bytes=limit),
+    count = rows // BLOCK
+    slots = count * (count + 1) // 2
+    first, final = old is None, unit is not None
+    half = jax.ShapeDtypeStruct((rows, steps * zlocal), jnp.bfloat16)
+    operands = [me, core, *parts] + ([] if first else [old])
+    height = slots * BLOCK
+    sums = [jax.ShapeDtypeStruct((height, BLOCK), jnp.float32)]
+    scratch = []
+    if final:
+        height += -height % unit
+        sums = [jax.ShapeDtypeStruct((height // 2, BLOCK), jnp.float32)] * 2
+        scratch = [pltpu.VMEM((height, BLOCK), jnp.float32)]
+    *sums, high, low = pl.pallas_call(
+        functools.partial(gram_kernel, first, final, groups),
+        out_shape=(*sums, half, half),
+        in_specs=[SMEM, SMEM] + [VMEM] * (len(operands) - 2),
+        out_specs=(VMEM,) * (len(sums) + 2),
+        scratch_shapes=scratch,
+        compiler_params=PARAMS,
         cost_estimate=pl.CostEstimate(
-            flops=6 * slots * BLOCK * BLOCK * wide * zlocal, bytes_accessed=8 * rows * wide * zlocal, transcendentals=0
+            flops=6 * slots * BLOCK * BLOCK * steps * zlocal, bytes_accessed=8 * rows * steps * zlocal, transcendentals=0
         ),
     )(*operands)
-    return total, list(zip(made[::2], made[1::2]))
+    return sums, [(high, low)]
 
 
 def inverse_cholesky(a_ref, b_ref, w_ref):
@@ -341,18 +344,13 @@
     return moved
 
 
-def total_sum(blocks, core):
-    chips = lax.axis_size(CHIPS)
+def total_sum(own, other):
     swap = [(0, 1), (1, 0)]
-    unit = math.lcm(2 * chips, 2 * BLOCK)
-    blocks = jnp.pad(blocks, ((0, -blocks.shape[0] % unit), (0, 0)))
-    half = blocks.shape[0] // 2
-    other = lax.ppermute(lax.dynamic_slice_in_dim(blocks, (1 - core[0]) * half, half), CORES, swap)
-    own = lax.dynamic_slice_in_dim(blocks, core[0] * half, half) + other
-    parts = own.reshape(chips, -1, BLOCK)
+    own = own + lax.ppermute(other, CORES, swap)
+    parts = own.reshape(lax.axis_size(CHIPS), -1, BLOCK)
     share = jnp.sum(lax.all_to_all(parts, CHIPS, split_axis=0, concat_axis=0, tiled=True), axis=0)
     spread = jnp.broadcast_to(share[None], parts.shape)
-    own = lax.all_to_all(spread, CHIPS, split_axis=0, concat_axis=0, tiled=True).reshape(half, BLOCK)
+    own = lax.all_to_all(spread, CHIPS, split_axis=0, concat_axis=0, tiled=True).reshape(own.shape)
     return own, lax.ppermute(own, CORES, swap)
 
 
@@ -375,9 +373,9 @@
     core = lax.axis_index(CORES).astype(jnp.int32).reshape(1)
 
     pieces = [(0, xlocal, start, steps) for start in starts]
-    packed = pack(me, snapshot, groups, pieces[:1], 54 * 2**20)
+    packed = pack(me, snapshot, groups, pieces[:1], LARGE)
     if chunks > 1:
-        packed += pack(me, snapshot, groups, pieces[1:], 44 * 2**20)
+        packed += pack(me, snapshot, groups, pieces[1:], 16 * 2**20)
 
     moved = []
     for index, parts in enumerate(packed):
@@ -385,12 +383,13 @@
             parts = hold(parts, moved[index - 2])
         moved.append(exchange(parts))
 
+    unit = math.lcm(2 * lax.axis_size(CHIPS), 2 * BLOCK)
     halves = []
-    total = None
-    for parts in moved:
-        total, made = gram_step(me, parts, [[]], total, SMALL)
+    sums = [None]
+    for index, parts in enumerate(moved):
+        sums, made = gram_step(me, core, parts, sums[0], unit if index == chunks - 1 else None)
         halves.append(made)
-    own, other = total_sum(total, core)
+    own, other = total_sum(*sums)
     mine, turned = factor_step(me, core, own, other, groups, xlocal)
     outs = []
     for held in halves[-1:] + halves[:-1]:

time: 360 us -> 357 us (level)
  waiting for transfers between devices: 127 us -> 120 us
    ppermute x30, waiting for transfers between devices: 124 us -> 116 us  [exchange(): lax.ppermute(parts[shift], 'gx', [(i, (i + shift) % groups) for i in rang...]
  transfers between devices with their start and end apart: 32 -> 32, of which waited for: 13 -> 11; matrix products, arithmetic and copies ran while one was open for 0% -> 0% of each run, Pallas kernels for 6% -> 6%
where the time goes in v7:
time: 357 us; the launch traced here: 356 us
  waiting for transfers between devices  120 us (34%)
  starting transfers between devices  107 us (30%)
  Pallas kernels  50.6 us (14%)
  blocking collectives  41.7 us (12%)
  local copies, waits for them, and re-layouts  36.1 us (10%)
    ppermute x30, waiting for transfers between devices, exchange(): lax.ppermute(parts[shift], 'gx', [(i, (i + shift) % groups) for i in rang...  116 us
    ppermute x30, starting transfers between devices, exchange(): lax.ppermute(parts[shift], 'gx', [(i, (i + shift) % groups) for i in rang...  107 us
    unnamed x76, local copies, waits for them, and re-layouts  36.1 us
    all_to_all x1, blocking collectives, total_sum(): lax.all_to_all(parts, CHIPS, split_axis=0, concat_axis=0, tiled=True)  27.5 us
    pallas_call x1, Pallas kernels, factor_step(): pl.pallas_call(functools.partial(factor_kernel, groups, xlocal), out_shap...  17.5 us
    pallas_call x5, Pallas kernels, gram_step(): pl.pallas_call(functools.partial(gram_kernel, first, final, groups), out_...  17.4 us
    all_to_all x1, blocking collectives, total_sum(): lax.all_to_all(spread, CHIPS, split_axis=0, concat_axis=0, tiled=True)  14.1 us
    pallas_call x2, Pallas kernels, pack(): pl.pallas_call(functools.partial(pack_kernel, groups, per, tuple(pieces))...  10.3 us
  transfers between devices with their start and end apart: 32, of which 11 were waited for; matrix products, arithmetic and copies ran while one was open for 0% of the time, Pallas kernels for 6%

profile of v7, /device:TPU:0, one launch (start us, length us, event | category | flops | bytes accessed | tf_op | source)
XLA Modules:
  0.0 356.0 jit_solution(17746115092978509281)
XLA Ops:
  0.6 3.5 shard_map.31
  4.2 3.1 collective-permute-start
  7.3 2.6 collective-permute-start.1
  11.2 4.0 %copy-done = f32[128,160,128]{2,1,0:T(8,128)S(1)} copy-done((f32[128,160,128]{2,1,0:T(8,128)S(1)}, f32[128,160,128]{2,1,0:T(8,128)}, u32[]{:S(2)}) %copy-start) | copy-done | bytes 10485784
  15.2 6.7 %shard_map.30 = (f32[8,128,128]{2,1,0:T(8,128)S(1)}, f32[8,128,128]{2,1,0:T(8,128)S(1)}, f32[8,128,128]{2,1,0:T(8,128)S(1)}, f32[8,128,128]{2,1,0:T(8,128)S(1)},...) custom-call(s32[1]{0:T(128)} %bitcast.me_ref, ...), custom_call_target="tpu_custom_call" | custom-call | bytes 16777216 | tf_op jit(solution)/shard_map/pallas_call | solution.py:75
  26.2 2.8 collective-permute-start.11
  29.0 15.9 %collective-permute-done.1.refs_2_ = f32[8,128,128]{2,1,0:T(8,128)S(1)} collective-permute-done((f32[8,128,128]{2,1,0:T(8,128)}, f32[8,128,128]{2,1,0:T(8,128)S(1)}, u32[]{:S(2)}, u32[]{:S(2)}) %collective-permute-start.1) | collective-permute-done | bytes 524320 | tf_op jit(solution)/shard_map/ppermute | solution.py:343
  44.9 34.3 %collective-permute-start.3 = (f32[8,128,128]{2,1,0:T(8,128)S(1)}, f32[8,128,128]{2,1,0:T(8,128)S(1)}, u32[]{:S(2)}, u32[]{:S(2)}) collective-permute-start(f32[8,128,128]{2,1,0:T(8,128)S(1)} %get-tuple-element.98), channel_id=1, source_target_pairs={{0,8},{8,16},{16,24},{24,0},{1,9},{9,17},{17,25},{25,1},{2,10},{10... | collective-permute-start | bytes 1572872 | tf_op jit(solution)/shard_map/ppermute | solution.py:343
  82.3 29.2 %collective-permute-done.10.refs_2_ = f32[8,128,128]{2,1,0:T(8,128)S(1)} collective-permute-done((f32[8,128,128]{2,1,0:T(8,128)S(1)}, f32[8,128,128]{2,1,0:T(8,128)S(1)}, u32[]{:S(2)}, u32[]{:S(2)}) %collective-permute-start.10) | collective-permute-done | bytes 524320 | tf_op jit(solution)/shard_map/ppermute | solution.py:343
  113.1 11.0 %collective-permute-start.12 = (f32[8,128,128]{2,1,0:T(8,128)S(1)}, f32[8,128,128]{2,1,0:T(8,128)S(1)}, u32[]{:S(2)}, u32[]{:S(2)}) collective-permute-start(f32[8,128,128]{2,1,0:T(8,128)S(1)} %get-tuple-element.114), channel_id=1, source_target_pairs={{0,8},{8,16},{16,24},{24,0},{1,9},{9,17},{17,25},{25,1},{2,10},{10... | collective-permute-start | bytes 1572872 | tf_op jit(solution)/shard_map/ppermute | solution.py:343
  124.2 3.4 collective-permute-start.13
  128.4 28.1 %collective-permute-done.4.refs_2_ = f32[8,128,128]{2,1,0:T(8,128)S(1)} collective-permute-done((f32[8,128,128]{2,1,0:T(8,128)S(1)}, f32[8,128,128]{2,1,0:T(8,128)S(1)}, u32[]{:S(2)}, u32[]{:S(2)}) %collective-permute-start.4) | collective-permute-done | bytes 524320 | tf_op jit(solution)/shard_map/ppermute | solution.py:343
  158.1 11.1 %collective-permute-start.6 = (f32[8,128,128]{2,1,0:T(8,128)}, f32[8,128,128]{2,1,0:T(8,128)}, u32[]{:S(2)}, u32[]{:S(2)}) collective-permute-start(f32[8,128,128]{2,1,0:T(8,128)} %get-tuple-element.102), channel_id=1, source_target_pairs={{0,8},{8,16},{16,24},{24,0},{1,9},{9,17},{17,25},{25,1},{2,10},{10... | collective-permute-start | bytes 1572872 | tf_op jit(solution)/shard_map/ppermute | solution.py:343
  169.2 3.4 collective-permute-start.7
  173.4 2.8 shard_map.32
  182.3 3.0 shard_map.33
  190.9 3.0 shard_map.34
  194.9 6.6 %collective-permute-done.13.refs_2_ = f32[8,128,128]{2,1,0:T(8,128)} collective-permute-done((f32[8,128,128]{2,1,0:T(8,128)S(1)}, f32[8,128,128]{2,1,0:T(8,128)}, u32[]{:S(2)}, u32[]{:S(2)}) %collective-permute-start.13) | collective-permute-done | bytes 524320 | tf_op jit(solution)/shard_map/ppermute | solution.py:343
  201.5 4.2 %shard_map.35 = (f32[1280,128]{1,0:T(8,128)S(1)}, bf16[512,1024]{1,0:T(8,128)(2,1)S(1)}, bf16[512,1024]{1,0:T(8,128)(2,1)S(1)}) custom-call(s32[1]{0:T(128)} %bitcast.me_ref, s32[1]{0:T(128)} %bitcast.1.core_ref, f32[8,128,128]{2,1,0:T(8,128)S(1)} %copy-done.18, f32[8,128,128]{2,1,0:T(8,128)S(1)} %copy-done.35, ...), custom_call_target="tpu_custom_call" | custom-call | flops 1006632960 | bytes 4194304 | tf_op jit(solution)/shard_map/pallas_call | solution.py:141
  205.7 18.2 %collective-permute-done.7.refs_2_ = f32[8,128,128]{2,1,0:T(8,128)} collective-permute-done((f32[8,128,128]{2,1,0:T(8,128)}, f32[8,128,128]{2,1,0:T(8,128)}, u32[]{:S(2)}, u32[]{:S(2)}) %collective-permute-start.7) | collective-permute-done | bytes 524320 | tf_op jit(solution)/shard_map/ppermute | solution.py:343
  224.0 4.4 %shard_map.36 = (f32[640,128]{1,0:T(8,128)S(1)}, f32[640,128]{1,0:T(8,128)S(1)}, bf16[512,1024]{1,0:T(8,128)(2,1)S(1)}, bf16[512,1024]{1,0:T(8,128)(2,1)S(1)}) custom-call(s32[1]{0:T(128)} %bitcast.me_ref, s32[1]{0:T(128)} %bitcast.1.core_ref, f32[8,128,128]{2,1,0:T(8,128)S(1)} %copy-done.16, f32[8,128,128]{2,1,0:T(8,128)} %collective-permute-done.6.refs_1_, ...), custom_call_target="tpu_custom_call" | custom-call | flops 1006632960 | bytes 4194304 | tf_op jit(solution)/shard_map/pallas_call | solution.py:141
  232.0 27.5 %all_to_all.10 = f32[16,40,128]{2,1,0:T(8,128)S(1)} all-to-all(f32[16,40,128]{2,1,0:T(8,128)S(1)} %bitcast.6), channel_id=1, replica_groups=mesh['gx'=4,'gy'=2,'gu'=2,'gc'=2] {'gx','gy','gu'}, dimensions={0} | all-to-all | bytes 655360 | tf_op jit(solution)/shard_map/all_to_all | solution.py:351
  259.6 14.1 %all_to_all.11 = f32[16,40,128]{2,1,0:T(8,128)S(1)} all-to-all(f32[16,40,128]{2,1,0:T(8,128)S(1)} %broadcast_in_dim.2), channel_id=1, replica_groups=mesh['gx'=4,'gy'=2,'gu'=2,'gc'=2] {'gx','gy','gu'}, dimensions={0} | all-to-all | bytes 655360 | tf_op jit(solution)/shard_map/all_to_all | solution.py:353
  275.4 17.5 %shard_map.37 = (f32[128,128]{1,0:T(8,128)}, f32[128,512]{1,0:T(8,128)S(1)}) custom-call(s32[1]{0:T(128)} %bitcast.me_ref, s32[1]{0:T(128)} %bitcast.1.core_ref, f32[640,128]{1,0:T(8,128)S(1)} %bitcast.5, f32[640,128]{1,0:T(8,128)S(1)} %collective-permute-done.16.other_ref), custom_call_target="tpu_custom_call" | custom-call | tf_op jit(solution)/shard_map/pallas_call | solution.py:248
  305.4 2.8 collective-permute-start.22
  311.4 7.6 %collective-permute-start.23 = (f32[32,8,128]{2,1,0:T(8,128)S(1)}, f32[32,8,128]{2,1,0:T(8,128)S(1)}, u32[]{:S(2)}, u32[]{:S(2)}) collective-permute-start(f32[32,8,128]{2,1,0:T(8,128)S(1)} %get-tuple-element.145), channel_id=1, source_target_pairs={{0,8},{8,16},{16,24},{24,0},{1,9},{9,17},{17,25},{25,1},{2,10},{10... | collective-permute-start | bytes 393224 | tf_op jit(solution)/shard_map/ppermute | solution.py:343
  323.4 2.7 collective-permute-done.21.refs_6_
  326.1 3.4 collective-permute-start.26
  332.6 4.7 %collective-permute-done.24.refs_10_ = f32[32,8,128]{2,1,0:T(8,128)S(1)} collective-permute-done((f32[32,8,128]{2,1,0:T(8,128)S(1)}, f32[32,8,128]{2,1,0:T(8,128)S(1)}, u32[]{:S(2)}, u32[]{:S(2)}) %collective-permute-start.24) | collective-permute-done | bytes 131104 | tf_op jit(solution)/shard_map/ppermute | solution.py:343
  337.3 3.4 collective-permute-start.29
  343.0 5.5 %collective-permute-done.27.refs_14_ = f32[32,8,128]{2,1,0:T(8,128)S(1)} collective-permute-done((f32[32,8,128]{2,1,0:T(8,128)S(1)}, f32[32,8,128]{2,1,0:T(8,128)S(1)}, u32[]{:S(2)}, u32[]{:S(2)}) %collective-permute-start.27) | collective-permute-done | bytes 131104 | tf_op jit(solution)/shard_map/ppermute | solution.py:343
  348.5 5.6 %collective-permute-done.30.refs_18_ = f32[32,8,128]{2,1,0:T(8,128)S(1)} collective-permute-done((f32[32,8,128]{2,1,0:T(8,128)S(1)}, f32[32,8,128]{2,1,0:T(8,128)S(1)}, u32[]{:S(2)}, u32[]{:S(2)}) %collective-permute-start.30) | collective-permute-done | bytes 131104 | tf_op jit(solution)/shard_map/ppermute | solution.py:343
  (127 shorter events, 58.9 us)
Async XLA Ops:
  4.2 22.0 %collective-permute-start = (f32[8,128,128]{2,1,0:T(8,128)}, f32[8,128,128]{2,1,0:T(8,128)S(1)}, u32[]{:S(2)}, u32[]{:S(2)}) collective-permute-start(f32[8,128,128]{2,1,0:T(8,128)} %get-tuple-element.94), channel_id=1, source_target_pairs={{0,8},{8,16},{16,24},{24,0},{1,9},{9,17},{17,25},{25,1},{2,10},{10... | collective-permute-start | bytes 1572872 | tf_op jit(solution)/shard_map/ppermute | solution.py:343
  7.3 37.6 %collective-permute-start.1 = (f32[8,128,128]{2,1,0:T(8,128)}, f32[8,128,128]{2,1,0:T(8,128)S(1)}, u32[]{:S(2)}, u32[]{:S(2)}) collective-permute-start(f32[8,128,128]{2,1,0:T(8,128)} %get-tuple-element.95), channel_id=1, source_target_pairs={{0,16},{8,24},{16,0},{24,8},{1,17},{9,25},{17,1},{25,9},{2,18},{10... | collective-permute-start | bytes 1572872 | tf_op jit(solution)/shard_map/ppermute | solution.py:343
  9.8 35.1 %collective-permute-start.2 = (f32[8,128,128]{2,1,0:T(8,128)}, f32[8,128,128]{2,1,0:T(8,128)S(1)}, u32[]{:S(2)}, u32[]{:S(2)}) collective-permute-start(f32[8,128,128]{2,1,0:T(8,128)} %get-tuple-element.96), channel_id=1, source_target_pairs={{0,24},{8,0},{16,8},{24,16},{1,25},{9,1},{17,9},{25,17},{2,26},{10... | collective-permute-start | bytes 1572872 | tf_op jit(solution)/shard_map/ppermute | solution.py:343
  25.2 55.8 %collective-permute-start.9 = (f32[8,128,128]{2,1,0:T(8,128)S(1)}, f32[8,128,128]{2,1,0:T(8,128)S(1)}, u32[]{:S(2)}, u32[]{:S(2)}) collective-permute-start(f32[8,128,128]{2,1,0:T(8,128)S(1)} %get-tuple-element.110), channel_id=1, source_target_pairs={{0,8},{8,16},{16,24},{24,0},{1,9},{9,17},{17,25},{25,1},{2,10},{10... | collective-permute-start | bytes 1572872 | tf_op jit(solution)/shard_map/ppermute | solution.py:343
  25.9 85.6 %collective-permute-start.10 = (f32[8,128,128]{2,1,0:T(8,128)S(1)}, f32[8,128,128]{2,1,0:T(8,128)S(1)}, u32[]{:S(2)}, u32[]{:S(2)}) collective-permute-start(f32[8,128,128]{2,1,0:T(8,128)S(1)} %get-tuple-element.111), channel_id=1, source_target_pairs={{0,16},{8,24},{16,0},{24,8},{1,17},{9,25},{17,1},{25,9},{2,18},{10... | collective-permute-start | bytes 1572872 | tf_op jit(solution)/shard_map/ppermute | solution.py:343
  26.2 86.1 %collective-permute-start.11 = (f32[8,128,128]{2,1,0:T(8,128)S(1)}, f32[8,128,128]{2,1,0:T(8,128)S(1)}, u32[]{:S(2)}, u32[]{:S(2)}) collective-permute-start(f32[8,128,128]{2,1,0:T(8,128)S(1)} %get-tuple-element.112), channel_id=1, source_target_pairs={{0,24},{8,0},{16,8},{24,16},{1,25},{9,1},{17,9},{25,17},{2,26},{10... | collective-permute-start | bytes 1572872 | tf_op jit(solution)/shard_map/ppermute | solution.py:343
  44.9 82.7 %collective-permute-start.3 = (f32[8,128,128]{2,1,0:T(8,128)S(1)}, f32[8,128,128]{2,1,0:T(8,128)S(1)}, u32[]{:S(2)}, u32[]{:S(2)}) collective-permute-start(f32[8,128,128]{2,1,0:T(8,128)S(1)} %get-tuple-element.98), channel_id=1, source_target_pairs={{0,8},{8,16},{16,24},{24,0},{1,9},{9,17},{17,25},{25,1},{2,10},{10... | collective-permute-start | bytes 1572872 | tf_op jit(solution)/shard_map/ppermute | solution.py:343
  79.2 77.3 %collective-permute-start.4 = (f32[8,128,128]{2,1,0:T(8,128)S(1)}, f32[8,128,128]{2,1,0:T(8,128)S(1)}, u32[]{:S(2)}, u32[]{:S(2)}) collective-permute-start(f32[8,128,128]{2,1,0:T(8,128)S(1)} %get-tuple-element.99), channel_id=1, source_target_pairs={{0,16},{8,24},{16,0},{24,8},{1,17},{9,25},{17,1},{25,9},{2,18},{10... | collective-permute-start | bytes 1572872 | tf_op jit(solution)/shard_map/ppermute | solution.py:343
  81.8 75.5 %collective-permute-start.5 = (f32[8,128,128]{2,1,0:T(8,128)S(1)}, f32[8,128,128]{2,1,0:T(8,128)S(1)}, u32[]{:S(2)}, u32[]{:S(2)}) collective-permute-start(f32[8,128,128]{2,1,0:T(8,128)S(1)} %get-tuple-element.100), channel_id=1, source_target_pairs={{0,24},{8,0},{16,8},{24,16},{1,25},{9,1},{17,9},{25,17},{2,26},{10... | collective-permute-start | bytes 1572872 | tf_op jit(solution)/shard_map/ppermute | solution.py:343
  113.1 59.4 %collective-permute-start.12 = (f32[8,128,128]{2,1,0:T(8,128)S(1)}, f32[8,128,128]{2,1,0:T(8,128)S(1)}, u32[]{:S(2)}, u32[]{:S(2)}) collective-permute-start(f32[8,128,128]{2,1,0:T(8,128)S(1)} %get-tuple-element.114), channel_id=1, source_target_pairs={{0,8},{8,16},{16,24},{24,0},{1,9},{9,17},{17,25},{25,1},{2,10},{10... | collective-permute-start | bytes 1572872 | tf_op jit(solution)/shard_map/ppermute | solution.py:343
  124.2 77.3 %collective-permute-start.13 = (f32[8,128,128]{2,1,0:T(8,128)S(1)}, f32[8,128,128]{2,1,0:T(8,128)}, u32[]{:S(2)}, u32[]{:S(2)}) collective-permute-start(f32[8,128,128]{2,1,0:T(8,128)S(1)} %get-tuple-element.115), channel_id=1, source_target_pairs={{0,16},{8,24},{16,0},{24,8},{1,17},{9,25},{17,1},{25,9},{2,18},{10... | collective-permute-start | bytes 1572872 | tf_op jit(solution)/shard_map/ppermute | solution.py:343
  128.4 73.1 %collective-permute-start.14 = (f32[8,128,128]{2,1,0:T(8,128)S(1)}, f32[8,128,128]{2,1,0:T(8,128)}, u32[]{:S(2)}, u32[]{:S(2)}) collective-permute-start(f32[8,128,128]{2,1,0:T(8,128)S(1)} %get-tuple-element.116), channel_id=1, source_target_pairs={{0,24},{8,0},{16,8},{24,16},{1,25},{9,1},{17,9},{25,17},{2,26},{10... | collective-permute-start | bytes 1572872 | tf_op jit(solution)/shard_map/ppermute | solution.py:343
  158.1 47.7 %collective-permute-start.6 = (f32[8,128,128]{2,1,0:T(8,128)}, f32[8,128,128]{2,1,0:T(8,128)}, u32[]{:S(2)}, u32[]{:S(2)}) collective-permute-start(f32[8,128,128]{2,1,0:T(8,128)} %get-tuple-element.102), channel_id=1, source_target_pairs={{0,8},{8,16},{16,24},{24,0},{1,9},{9,17},{17,25},{25,1},{2,10},{10... | collective-permute-start | bytes 1572872 | tf_op jit(solution)/shard_map/ppermute | solution.py:343
  169.2 54.8 %collective-permute-start.7 = (f32[8,128,128]{2,1,0:T(8,128)}, f32[8,128,128]{2,1,0:T(8,128)}, u32[]{:S(2)}, u32[]{:S(2)}) collective-permute-start(f32[8,128,128]{2,1,0:T(8,128)} %get-tuple-element.103), channel_id=1, source_target_pairs={{0,16},{8,24},{16,0},{24,8},{1,17},{9,25},{17,1},{25,9},{2,18},{10... | collective-permute-start | bytes 1572872 | tf_op jit(solution)/shard_map/ppermute | solution.py:343
  173.3 50.6 %collective-permute-start.8 = (f32[8,128,128]{2,1,0:T(8,128)}, f32[8,128,128]{2,1,0:T(8,128)}, u32[]{:S(2)}, u32[]{:S(2)}) collective-permute-start(f32[8,128,128]{2,1,0:T(8,128)} %get-tuple-element.104), channel_id=1, source_target_pairs={{0,24},{8,0},{16,8},{24,16},{1,25},{9,1},{17,9},{25,17},{2,26},{10... | collective-permute-start | bytes 1572872 | tf_op jit(solution)/shard_map/ppermute | solution.py:343
  230.4 1.6 collective-permute-start.15
  273.7 1.6 collective-permute-start.16
  296.1 9.3 %collective-permute-start.17 = (f32[32,8,128]{2,1,0:T(8,128)S(1)}, f32[32,8,128]{2,1,0:T(8,128)S(1)}, u32[]{:S(2)}, u32[]{:S(2)}) collective-permute-start(f32[32,8,128]{2,1,0:T(8,128)S(1)} %get-tuple-element.128), channel_id=1, source_target_pairs={{0,8},{8,16},{16,24},{24,0},{1,9},{9,17},{17,25},{25,1},{2,10},{10... | collective-permute-start | bytes 393224 | tf_op jit(solution)/shard_map/ppermute | solution.py:343
  297.1 14.3 %collective-permute-start.18 = (f32[32,8,128]{2,1,0:T(8,128)S(1)}, f32[32,8,128]{2,1,0:T(8,128)S(1)}, u32[]{:S(2)}, u32[]{:S(2)}) collective-permute-start(f32[32,8,128]{2,1,0:T(8,128)S(1)} %get-tuple-element.129), channel_id=1, source_target_pairs={{0,16},{8,24},{16,0},{24,8},{1,17},{9,25},{17,1},{25,9},{2,18},{10... | collective-permute-start | bytes 393224 | tf_op jit(solution)/shard_map/ppermute | solution.py:343
  298.4 13.1 %collective-permute-start.19 = (f32[32,8,128]{2,1,0:T(8,128)S(1)}, f32[32,8,128]{2,1,0:T(8,128)S(1)}, u32[]{:S(2)}, u32[]{:S(2)}) collective-permute-start(f32[32,8,128]{2,1,0:T(8,128)S(1)} %get-tuple-element.130), channel_id=1, source_target_pairs={{0,24},{8,0},{16,8},{24,16},{1,25},{9,1},{17,9},{25,17},{2,26},{10... | collective-permute-start | bytes 393224 | tf_op jit(solution)/shard_map/ppermute | solution.py:343
  303.2 15.8 %collective-permute-start.20 = (f32[32,8,128]{2,1,0:T(8,128)S(1)}, f32[32,8,128]{2,1,0:T(8,128)S(1)}, u32[]{:S(2)}, u32[]{:S(2)}) collective-permute-start(f32[32,8,128]{2,1,0:T(8,128)S(1)} %get-tuple-element.135), channel_id=1, source_target_pairs={{0,8},{8,16},{16,24},{24,0},{1,9},{9,17},{17,25},{25,1},{2,10},{10... | collective-permute-start | bytes 393224 | tf_op jit(solution)/shard_map/ppermute | solution.py:343
  303.8 22.3 %collective-permute-start.21 = (f32[32,8,128]{2,1,0:T(8,128)S(1)}, f32[32,8,128]{2,1,0:T(8,128)S(1)}, u32[]{:S(2)}, u32[]{:S(2)}) collective-permute-start(f32[32,8,128]{2,1,0:T(8,128)S(1)} %get-tuple-element.136), channel_id=1, source_target_pairs={{0,16},{8,24},{16,0},{24,8},{1,17},{9,25},{17,1},{25,9},{2,18},{10... | collective-permute-start | bytes 393224 | tf_op jit(solution)/shard_map/ppermute | solution.py:343
  305.4 20.7 %collective-permute-start.22 = (f32[32,8,128]{2,1,0:T(8,128)S(1)}, f32[32,8,128]{2,1,0:T(8,128)S(1)}, u32[]{:S(2)}, u32[]{:S(2)}) collective-permute-start(f32[32,8,128]{2,1,0:T(8,128)S(1)} %get-tuple-element.137), channel_id=1, source_target_pairs={{0,24},{8,0},{16,8},{24,16},{1,25},{9,1},{17,9},{25,17},{2,26},{10... | collective-permute-start | bytes 393224 | tf_op jit(solution)/shard_map/ppermute | solution.py:343
  311.4 18.9 %collective-permute-start.23 = (f32[32,8,128]{2,1,0:T(8,128)S(1)}, f32[32,8,128]{2,1,0:T(8,128)S(1)}, u32[]{:S(2)}, u32[]{:S(2)}) collective-permute-start(f32[32,8,128]{2,1,0:T(8,128)S(1)} %get-tuple-element.145), channel_id=1, source_target_pairs={{0,8},{8,16},{16,24},{24,0},{1,9},{9,17},{17,25},{25,1},{2,10},{10... | collective-permute-start | bytes 393224 | tf_op jit(solution)/shard_map/ppermute | solution.py:343
  319.0 18.3 %collective-permute-start.24 = (f32[32,8,128]{2,1,0:T(8,128)S(1)}, f32[32,8,128]{2,1,0:T(8,128)S(1)}, u32[]{:S(2)}, u32[]{:S(2)}) collective-permute-start(f32[32,8,128]{2,1,0:T(8,128)S(1)} %get-tuple-element.146), channel_id=1, source_target_pairs={{0,16},{8,24},{16,0},{24,8},{1,17},{9,25},{17,1},{25,9},{2,18},{10... | collective-permute-start | bytes 393224 | tf_op jit(solution)/shard_map/ppermute | solution.py:343
  319.0 18.3 %collective-permute-start.25 = (f32[32,8,128]{2,1,0:T(8,128)S(1)}, f32[32,8,128]{2,1,0:T(8,128)S(1)}, u32[]{:S(2)}, u32[]{:S(2)}) collective-permute-start(f32[32,8,128]{2,1,0:T(8,128)S(1)} %get-tuple-element.147), channel_id=1, source_target_pairs={{0,24},{8,0},{16,8},{24,16},{1,25},{9,1},{17,9},{25,17},{2,26},{10... | collective-permute-start | bytes 393224 | tf_op jit(solution)/shard_map/ppermute | solution.py:343
  326.1 14.6 %collective-permute-start.26 = (f32[32,8,128]{2,1,0:T(8,128)S(1)}, f32[32,8,128]{2,1,0:T(8,128)S(1)}, u32[]{:S(2)}, u32[]{:S(2)}) collective-permute-start(f32[32,8,128]{2,1,0:T(8,128)S(1)} %get-tuple-element.155), channel_id=1, source_target_pairs={{0,8},{8,16},{16,24},{24,0},{1,9},{9,17},{17,25},{25,1},{2,10},{10... | collective-permute-start | bytes 393224 | tf_op jit(solution)/shard_map/ppermute | solution.py:343
  330.2 18.3 %collective-permute-start.27 = (f32[32,8,128]{2,1,0:T(8,128)S(1)}, f32[32,8,128]{2,1,0:T(8,128)S(1)}, u32[]{:S(2)}, u32[]{:S(2)}) collective-permute-start(f32[32,8,128]{2,1,0:T(8,128)S(1)} %get-tuple-element.156), channel_id=1, source_target_pairs={{0,16},{8,24},{16,0},{24,8},{1,17},{9,25},{17,1},{25,9},{2,18},{10... | collective-permute-start | bytes 393224 | tf_op jit(solution)/shard_map/ppermute | solution.py:343
  330.3 18.2 %collective-permute-start.28 = (f32[32,8,128]{2,1,0:T(8,128)S(1)}, f32[32,8,128]{2,1,0:T(8,128)S(1)}, u32[]{:S(2)}, u32[]{:S(2)}) collective-permute-start(f32[32,8,128]{2,1,0:T(8,128)S(1)} %get-tuple-element.157), channel_id=1, source_target_pairs={{0,24},{8,0},{16,8},{24,16},{1,25},{9,1},{17,9},{25,17},{2,26},{10... | collective-permute-start | bytes 393224 | tf_op jit(solution)/shard_map/ppermute | solution.py:343
  337.3 11.2 %collective-permute-start.29 = (f32[32,8,128]{2,1,0:T(8,128)S(1)}, f32[32,8,128]{2,1,0:T(8,128)S(1)}, u32[]{:S(2)}, u32[]{:S(2)}) collective-permute-start(f32[32,8,128]{2,1,0:T(8,128)S(1)} %get-tuple-element.165), channel_id=1, source_target_pairs={{0,8},{8,16},{16,24},{24,0},{1,9},{9,17},{17,25},{25,1},{2,10},{10... | collective-permute-start | bytes 393224 | tf_op jit(solution)/shard_map/ppermute | solution.py:343
  340.7 13.5 %collective-permute-start.30 = (f32[32,8,128]{2,1,0:T(8,128)S(1)}, f32[32,8,128]{2,1,0:T(8,128)S(1)}, u32[]{:S(2)}, u32[]{:S(2)}) collective-permute-start(f32[32,8,128]{2,1,0:T(8,128)S(1)} %get-tuple-element.166), channel_id=1, source_target_pairs={{0,16},{8,24},{16,0},{24,8},{1,17},{9,25},{17,1},{25,9},{2,18},{10... | collective-permute-start | bytes 393224 | tf_op jit(solution)/shard_map/ppermute | solution.py:343
  340.7 13.5 %collective-permute-start.31 = (f32[32,8,128]{2,1,0:T(8,128)S(1)}, f32[32,8,128]{2,1,0:T(8,128)S(1)}, u32[]{:S(2)}, u32[]{:S(2)}) collective-permute-start(f32[32,8,128]{2,1,0:T(8,128)S(1)} %get-tuple-element.167), channel_id=1, source_target_pairs={{0,24},{8,0},{16,8},{24,16},{1,25},{9,1},{17,9},{25,17},{2,26},{10... | collective-permute-start | bytes 393224 | tf_op jit(solution)/shard_map/ppermute | solution.py:343
  (38 other events, 316.4 us)

commit v8 on v7

--- a/solution.py
+++ b/solution.py
@@ -100,23 +100,31 @@
             columns = slice(step * zlocal, (step + 1) * zlocal)
             high_ref[rows, columns] = high
             low_ref[rows, columns] = low
-    slot = 0
-    for row in range(groups * tall // BLOCK):
-        mine = slice(row * BLOCK, (row + 1) * BLOCK)
-        upto = slice(0, (row + 1) * BLOCK)
-        total = dot(high_ref[mine, :], high_ref[upto, :], last)
-        total += dot(high_ref[mine, :], low_ref[upto, :], last)
-        total += dot(low_ref[mine, :], high_ref[upto, :], last)
+    order = groups * tall
+    height = order // BLOCK * (order // BLOCK + 1) // 2 * BLOCK
+    big = 2 * BLOCK if order % (2 * BLOCK) == 0 else BLOCK
+    ratio = big // BLOCK
+    for row in range(order // big):
+        left = slice(row * big, (row + 1) * big)
         for column in range(row + 1):
-            at = slice(slot * BLOCK, (slot + 1) * BLOCK)
-            block = total[:, column * BLOCK : (column + 1) * BLOCK]
-            out_ref[at, :] = block if first else block + old_ref[at, :]
-            slot += 1
+            right = slice(column * big, (column + 1) * big)
+            total = dot(high_ref[left, :], high_ref[right, :], last)
+            total += dot(high_ref[left, :], low_ref[right, :], last)
+            total += dot(low_ref[left, :], high_ref[right, :], last)
+            for i in range(ratio):
+                for j in range(ratio):
+                    r, c = row * ratio + i, column * ratio + j
+                    if r < c:
+                        continue
+                    at = (r * (r + 1) // 2 + c) * BLOCK
+                    at = slice(at, at + BLOCK)
+                    block = total[i * BLOCK : (i + 1) * BLOCK, j * BLOCK : (j + 1) * BLOCK]
+                    out_ref[at, :] = block if first else block + old_ref[at, :]
     if final:
         own_ref, other_ref = refs[:2]
         half = own_ref.shape[0]
-        if slot * BLOCK < 2 * half:
-            out_ref[slot * BLOCK :, :] = jnp.zeros((2 * half - slot * BLOCK, BLOCK), jnp.float32)
+        if height < 2 * half:
+            out_ref[height:, :] = jnp.zeros((2 * half - height, BLOCK), jnp.float32)
         low, high = out_ref[:half, :], out_ref[half:, :]
         own_ref[...] = jnp.where(core_ref[0] == 0, low, high)
         other_ref[...] = jnp.where(core_ref[0] == 0, high, low)
@@ -344,12 +352,30 @@
     return moved
 
 
+def add_kernel(left_ref, right_ref, out_ref):
+    out_ref[...] = left_ref[...] + right_ref[...]
+
+
+def spread_kernel(parts_ref, out_ref):
+    total = parts_ref[0]
+    for index in range(1, parts_ref.shape[0]):
+        total += parts_ref[index]
+    for index in range(parts_ref.shape[0]):
+        out_ref[index] = total
+
+
+def small_call(kernel, *operands):
+    shape = jax.ShapeDtypeStruct(operands[0].shape, jnp.float32)
+    specs = [VMEM] * len(operands)
+    return pl.pallas_call(kernel, out_shape=shape, in_specs=specs, out_specs=VMEM, compiler_params=PARAMS)(*operands)
+
+
 def total_sum(own, other):
     swap = [(0, 1), (1, 0)]
-    own = own + lax.ppermute(other, CORES, swap)
+    own = small_call(add_kernel, own, lax.ppermute(other, CORES, swap))
     parts = own.reshape(lax.axis_size(CHIPS), -1, BLOCK)
-    share = jnp.sum(lax.all_to_all(parts, CHIPS, split_axis=0, concat_axis=0, tiled=True), axis=0)
-    spread = jnp.broadcast_to(share[None], parts.shape)
+    parts = lax.all_to_all(parts, CHIPS, split_axis=0, concat_axis=0, tiled=True)
+    spread = small_call(spread_kernel, parts)
     own = lax.all_to_all(spread, CHIPS, split_axis=0, concat_axis=0, tiled=True).reshape(own.shape)
     return own, lax.ppermute(own, CORES, swap)
 

time: 357 us -> 351 us (0.983)
  waiting for transfers between devices: 120 us -> 131 us
  local copies, waits for them, and re-layouts: 36.1 us -> 26.2 us
  Pallas kernels: 50.6 us -> 44.3 us
    ppermute x30, waiting for transfers between devices: 116 us -> 128 us  [exchange(): lax.ppermute(parts[shift], 'gx', [(i, (i + shift) % groups) for i in rang...]
    unnamed x76 -> x52, local copies, waits for them, and re-layouts: 36.1 us -> 26.2 us
    pallas_call x5, Pallas kernels: 17.4 us -> 11.2 us  [gram_step(): pl.pallas_call(functools.partial(gram_kernel, first, final, groups), out_...]
  transfers between devices with their start and end apart: 32 -> 32, of which waited for: 11 -> 13; matrix products, arithmetic and copies ran while one was open for 0% -> 0% of each run, Pallas kernels for 6% -> 5%
where the time goes in v8:
time: 351 us; the launch traced here: 350 us
  waiting for transfers between devices  131 us (37%)
  starting transfers between devices  106 us (30%)
  Pallas kernels  44.3 us (13%)
  blocking collectives  41.7 us (12%)
  local copies, waits for them, and re-layouts  26.2 us (7%)
    ppermute x30, waiting for transfers between devices, exchange(): lax.ppermute(parts[shift], 'gx', [(i, (i + shift) % groups) for i in rang...  128 us
    ppermute x30, starting transfers between devices, exchange(): lax.ppermute(parts[shift], 'gx', [(i, (i + shift) % groups) for i in rang...  106 us
    all_to_all x1, blocking collectives, total_sum(): lax.all_to_all(parts, CHIPS, split_axis=0, concat_axis=0, tiled=True)  27.6 us
    unnamed x52, local copies, waits for them, and re-layouts  26.2 us
    pallas_call x1, Pallas kernels, factor_step(): pl.pallas_call(functools.partial(factor_kernel, groups, xlocal), out_shap...  17.5 us
    all_to_all x1, blocking collectives, total_sum(): lax.all_to_all(spread, CHIPS, split_axis=0, concat_axis=0, tiled=True)  14.1 us
    pallas_call x5, Pallas kernels, gram_step(): pl.pallas_call(functools.partial(gram_kernel, first, final, groups), out_...  11.2 us
    pallas_call x2, Pallas kernels, pack(): pl.pallas_call(functools.partial(pack_kernel, groups, per, tuple(pieces))...  10 us
  transfers between devices with their start and end apart: 32, of which 13 were waited for; matrix products, arithmetic and copies ran while one was open for 0% of the time, Pallas kernels for 5%

profile of v8, /device:TPU:0, one launch (start us, length us, event | category | flops | bytes accessed | tf_op | source)
XLA Modules:
  0.0 350.3 jit_solution(1782150301202273085)
XLA Ops:
  0.6 3.5 shard_map.31
  4.1 3.1 collective-permute-start
  7.2 2.6 collective-permute-start.1
  11.1 4.0 %copy-done = f32[128,160,128]{2,1,0:T(8,128)S(1)} copy-done((f32[128,160,128]{2,1,0:T(8,128)S(1)}, f32[128,160,128]{2,1,0:T(8,128)}, u32[]{:S(2)}) %copy-start) | copy-done | bytes 10485784
  15.1 6.5 %shard_map.30 = (f32[8,128,128]{2,1,0:T(8,128)S(1)}, f32[8,128,128]{2,1,0:T(8,128)S(1)}, f32[8,128,128]{2,1,0:T(8,128)S(1)}, f32[8,128,128]{2,1,0:T(8,128)S(1)},...) custom-call(s32[1]{0:T(128)} %bitcast.me_ref, ...), custom_call_target="tpu_custom_call" | custom-call | bytes 16777216 | tf_op jit(solution)/shard_map/pallas_call | solution.py:75
  25.1 2.8 collective-permute-start.11
  27.9 16.9 %collective-permute-done.1.refs_2_ = f32[8,128,128]{2,1,0:T(8,128)S(1)} collective-permute-done((f32[8,128,128]{2,1,0:T(8,128)}, f32[8,128,128]{2,1,0:T(8,128)S(1)}, u32[]{:S(2)}, u32[]{:S(2)}) %collective-permute-start.1) | collective-permute-done | bytes 524320 | tf_op jit(solution)/shard_map/ppermute | solution.py:351
  46.5 33.4 %collective-permute-start.3 = (f32[8,128,128]{2,1,0:T(8,128)S(1)}, f32[8,128,128]{2,1,0:T(8,128)S(1)}, u32[]{:S(2)}, u32[]{:S(2)}) collective-permute-start(f32[8,128,128]{2,1,0:T(8,128)S(1)} %get-tuple-element.98), channel_id=1, source_target_pairs={{0,8},{8,16},{16,24},{24,0},{1,9},{9,17},{17,25},{25,1},{2,10},{10... | collective-permute-start | bytes 1572872 | tf_op jit(solution)/shard_map/ppermute | solution.py:351
  79.9 2.6 collective-permute-start.4
  83.4 28.0 %collective-permute-done.10.refs_2_ = f32[8,128,128]{2,1,0:T(8,128)S(1)} collective-permute-done((f32[8,128,128]{2,1,0:T(8,128)S(1)}, f32[8,128,128]{2,1,0:T(8,128)S(1)}, u32[]{:S(2)}, u32[]{:S(2)}) %collective-permute-start.10) | collective-permute-done | bytes 524320 | tf_op jit(solution)/shard_map/ppermute | solution.py:351
  113.0 11.1 %collective-permute-start.12 = (f32[8,128,128]{2,1,0:T(8,128)S(1)}, f32[8,128,128]{2,1,0:T(8,128)S(1)}, u32[]{:S(2)}, u32[]{:S(2)}) collective-permute-start(f32[8,128,128]{2,1,0:T(8,128)S(1)} %get-tuple-element.114), channel_id=1, source_target_pairs={{0,8},{8,16},{16,24},{24,0},{1,9},{9,17},{17,25},{25,1},{2,10},{10... | collective-permute-start | bytes 1572872 | tf_op jit(solution)/shard_map/ppermute | solution.py:351
  124.1 3.4 collective-permute-start.13
  128.3 28.1 %collective-permute-done.4.refs_2_ = f32[8,128,128]{2,1,0:T(8,128)S(1)} collective-permute-done((f32[8,128,128]{2,1,0:T(8,128)S(1)}, f32[8,128,128]{2,1,0:T(8,128)S(1)}, u32[]{:S(2)}, u32[]{:S(2)}) %collective-permute-start.4) | collective-permute-done | bytes 524320 | tf_op jit(solution)/shard_map/ppermute | solution.py:351
  158.0 11.1 %collective-permute-start.6 = (f32[8,128,128]{2,1,0:T(8,128)S(1)}, f32[8,128,128]{2,1,0:T(8,128)}, u32[]{:S(2)}, u32[]{:S(2)}) collective-permute-start(f32[8,128,128]{2,1,0:T(8,128)S(1)} %get-tuple-element.102), channel_id=1, source_target_pairs={{0,8},{8,16},{16,24},{24,0},{1,9},{9,17},{17,25},{25,1},{2,10},{10... | collective-permute-start | bytes 1572872 | tf_op jit(solution)/shard_map/ppermute | solution.py:351
  169.2 3.4 collective-permute-start.7
  191.1 10.3 %collective-permute-done.13.refs_2_ = f32[8,128,128]{2,1,0:T(8,128)} collective-permute-done((f32[8,128,128]{2,1,0:T(8,128)}, f32[8,128,128]{2,1,0:T(8,128)}, u32[]{:S(2)}, u32[]{:S(2)}) %collective-permute-start.13) | collective-permute-done | bytes 524320 | tf_op jit(solution)/shard_map/ppermute | solution.py:351
  201.4 2.9 shard_map.35
  204.4 19.5 %collective-permute-done.7.refs_2_ = f32[8,128,128]{2,1,0:T(8,128)} collective-permute-done((f32[8,128,128]{2,1,0:T(8,128)S(1)}, f32[8,128,128]{2,1,0:T(8,128)}, u32[]{:S(2)}, u32[]{:S(2)}) %collective-permute-start.7) | collective-permute-done | bytes 524320 | tf_op jit(solution)/shard_map/ppermute | solution.py:351
  223.9 3.1 shard_map.36
  228.7 27.6 %all_to_all.10.parts_ref = f32[16,40,128]{2,1,0:T(8,128)S(1)} all-to-all(f32[16,40,128]{2,1,0:T(8,128)S(1)} %bitcast.6), channel_id=1, replica_groups=mesh['gx'=4,'gy'=2,'gu'=2,'gc'=2] {'gx','gy','gu'}, dimensions={0} | all-to-all | bytes 655360 | tf_op jit(solution)/shard_map/all_to_all | solution.py:377
  256.4 14.1 %all_to_all.11 = f32[16,40,128]{2,1,0:T(8,128)S(1)} all-to-all(f32[16,40,128]{2,1,0:T(8,128)S(1)} %shard_map.38), channel_id=1, replica_groups=mesh['gx'=4,'gy'=2,'gu'=2,'gc'=2] {'gx','gy','gu'}, dimensions={0} | all-to-all | bytes 655360 | tf_op jit(solution)/shard_map/all_to_all | solution.py:379
  272.1 17.5 %shard_map.39 = (f32[128,128]{1,0:T(8,128)}, f32[128,512]{1,0:T(8,128)S(1)}) custom-call(s32[1]{0:T(128)} %bitcast.me_ref, s32[1]{0:T(128)} %bitcast.1.core_ref, f32[640,128]{1,0:T(8,128)S(1)} %bitcast.5, f32[640,128]{1,0:T(8,128)S(1)} %collective-permute-done.16.other_ref), custom_call_target="tpu_custom_call" | custom-call | tf_op jit(solution)/shard_map/pallas_call | solution.py:256
  300.8 3.6 %collective-permute-done.18.refs_2_ = f32[32,8,128]{2,1,0:T(8,128)S(1)} collective-permute-done((f32[32,8,128]{2,1,0:T(8,128)S(1)}, f32[32,8,128]{2,1,0:T(8,128)S(1)}, u32[]{:S(2)}, u32[]{:S(2)}) %collective-permute-start.18) | collective-permute-done | bytes 131104 | tf_op jit(solution)/shard_map/ppermute | solution.py:351
  304.4 9.0 %collective-permute-start.23 = (f32[32,8,128]{2,1,0:T(8,128)S(1)}, f32[32,8,128]{2,1,0:T(8,128)S(1)}, u32[]{:S(2)}, u32[]{:S(2)}) collective-permute-start(f32[32,8,128]{2,1,0:T(8,128)S(1)} %get-tuple-element.145), channel_id=1, source_target_pairs={{0,8},{8,16},{16,24},{24,0},{1,9},{9,17},{17,25},{25,1},{2,10},{10... | collective-permute-start | bytes 393224 | tf_op jit(solution)/shard_map/ppermute | solution.py:351
  313.4 2.4 collective-permute-start.25
  316.5 3.9 %collective-permute-done.21.refs_6_ = f32[32,8,128]{2,1,0:T(8,128)S(1)} collective-permute-done((f32[32,8,128]{2,1,0:T(8,128)S(1)}, f32[32,8,128]{2,1,0:T(8,128)S(1)}, u32[]{:S(2)}, u32[]{:S(2)}) %collective-permute-start.21) | collective-permute-done | bytes 131104 | tf_op jit(solution)/shard_map/ppermute | solution.py:351
  320.4 3.4 collective-permute-start.26
  327.0 4.6 %collective-permute-done.24.refs_10_ = f32[32,8,128]{2,1,0:T(8,128)S(1)} collective-permute-done((f32[32,8,128]{2,1,0:T(8,128)S(1)}, f32[32,8,128]{2,1,0:T(8,128)S(1)}, u32[]{:S(2)}, u32[]{:S(2)}) %collective-permute-start.24) | collective-permute-done | bytes 131104 | tf_op jit(solution)/shard_map/ppermute | solution.py:351
  331.6 3.4 collective-permute-start.29
  335.0 2.4 collective-permute-start.31
  337.4 5.5 %collective-permute-done.27.refs_14_ = f32[32,8,128]{2,1,0:T(8,128)S(1)} collective-permute-done((f32[32,8,128]{2,1,0:T(8,128)S(1)}, f32[32,8,128]{2,1,0:T(8,128)S(1)}, u32[]{:S(2)}, u32[]{:S(2)}) %collective-permute-start.27) | collective-permute-done | bytes 131104 | tf_op jit(solution)/shard_map/ppermute | solution.py:351
  342.9 5.6 %collective-permute-done.30.refs_18_ = f32[32,8,128]{2,1,0:T(8,128)S(1)} collective-permute-done((f32[32,8,128]{2,1,0:T(8,128)S(1)}, f32[32,8,128]{2,1,0:T(8,128)S(1)}, u32[]{:S(2)}, u32[]{:S(2)}) %collective-permute-start.30) | collective-permute-done | bytes 131104 | tf_op jit(solution)/shard_map/ppermute | solution.py:351
  (102 shorter events, 50.0 us)
Async XLA Ops:
  4.1 20.2 %collective-permute-start = (f32[8,128,128]{2,1,0:T(8,128)}, f32[8,128,128]{2,1,0:T(8,128)S(1)}, u32[]{:S(2)}, u32[]{:S(2)}) collective-permute-start(f32[8,128,128]{2,1,0:T(8,128)} %get-tuple-element.94), channel_id=1, source_target_pairs={{0,8},{8,16},{16,24},{24,0},{1,9},{9,17},{17,25},{25,1},{2,10},{10... | collective-permute-start | bytes 1572872 | tf_op jit(solution)/shard_map/ppermute | solution.py:351
  7.2 37.6 %collective-permute-start.1 = (f32[8,128,128]{2,1,0:T(8,128)}, f32[8,128,128]{2,1,0:T(8,128)S(1)}, u32[]{:S(2)}, u32[]{:S(2)}) collective-permute-start(f32[8,128,128]{2,1,0:T(8,128)} %get-tuple-element.95), channel_id=1, source_target_pairs={{0,16},{8,24},{16,0},{24,8},{1,17},{9,25},{17,1},{25,9},{2,18},{10... | collective-permute-start | bytes 1572872 | tf_op jit(solution)/shard_map/ppermute | solution.py:351
  9.8 35.9 %collective-permute-start.2 = (f32[8,128,128]{2,1,0:T(8,128)}, f32[8,128,128]{2,1,0:T(8,128)S(1)}, u32[]{:S(2)}, u32[]{:S(2)}) collective-permute-start(f32[8,128,128]{2,1,0:T(8,128)} %get-tuple-element.96), channel_id=1, source_target_pairs={{0,24},{8,0},{16,8},{24,16},{1,25},{9,1},{17,9},{25,17},{2,26},{10... | collective-permute-start | bytes 1572872 | tf_op jit(solution)/shard_map/ppermute | solution.py:351
  23.3 59.3 %collective-permute-start.9 = (f32[8,128,128]{2,1,0:T(8,128)S(1)}, f32[8,128,128]{2,1,0:T(8,128)S(1)}, u32[]{:S(2)}, u32[]{:S(2)}) collective-permute-start(f32[8,128,128]{2,1,0:T(8,128)S(1)} %get-tuple-element.110), channel_id=1, source_target_pairs={{0,8},{8,16},{16,24},{24,0},{1,9},{9,17},{17,25},{25,1},{2,10},{10... | collective-permute-start | bytes 1572872 | tf_op jit(solution)/shard_map/ppermute | solution.py:351
  24.0 87.5 %collective-permute-start.10 = (f32[8,128,128]{2,1,0:T(8,128)S(1)}, f32[8,128,128]{2,1,0:T(8,128)S(1)}, u32[]{:S(2)}, u32[]{:S(2)}) collective-permute-start(f32[8,128,128]{2,1,0:T(8,128)S(1)} %get-tuple-element.111), channel_id=1, source_target_pairs={{0,16},{8,24},{16,0},{24,8},{1,17},{9,25},{17,1},{25,9},{2,18},{10... | collective-permute-start | bytes 1572872 | tf_op jit(solution)/shard_map/ppermute | solution.py:351
  25.1 87.1 %collective-permute-start.11 = (f32[8,128,128]{2,1,0:T(8,128)S(1)}, f32[8,128,128]{2,1,0:T(8,128)S(1)}, u32[]{:S(2)}, u32[]{:S(2)}) collective-permute-start(f32[8,128,128]{2,1,0:T(8,128)S(1)} %get-tuple-element.112), channel_id=1, source_target_pairs={{0,24},{8,0},{16,8},{24,16},{1,25},{9,1},{17,9},{25,17},{2,26},{10... | collective-permute-start | bytes 1572872 | tf_op jit(solution)/shard_map/ppermute | solution.py:351
  46.5 81.0 %collective-permute-start.3 = (f32[8,128,128]{2,1,0:T(8,128)S(1)}, f32[8,128,128]{2,1,0:T(8,128)S(1)}, u32[]{:S(2)}, u32[]{:S(2)}) collective-permute-start(f32[8,128,128]{2,1,0:T(8,128)S(1)} %get-tuple-element.98), channel_id=1, source_target_pairs={{0,8},{8,16},{16,24},{24,0},{1,9},{9,17},{17,25},{25,1},{2,10},{10... | collective-permute-start | bytes 1572872 | tf_op jit(solution)/shard_map/ppermute | solution.py:351
  79.9 76.4 %collective-permute-start.4 = (f32[8,128,128]{2,1,0:T(8,128)S(1)}, f32[8,128,128]{2,1,0:T(8,128)S(1)}, u32[]{:S(2)}, u32[]{:S(2)}) collective-permute-start(f32[8,128,128]{2,1,0:T(8,128)S(1)} %get-tuple-element.99), channel_id=1, source_target_pairs={{0,16},{8,24},{16,0},{24,8},{1,17},{9,25},{17,1},{25,9},{2,18},{10... | collective-permute-start | bytes 1572872 | tf_op jit(solution)/shard_map/ppermute | solution.py:351
  83.4 73.8 %collective-permute-start.5 = (f32[8,128,128]{2,1,0:T(8,128)S(1)}, f32[8,128,128]{2,1,0:T(8,128)S(1)}, u32[]{:S(2)}, u32[]{:S(2)}) collective-permute-start(f32[8,128,128]{2,1,0:T(8,128)S(1)} %get-tuple-element.100), channel_id=1, source_target_pairs={{0,24},{8,0},{16,8},{24,16},{1,25},{9,1},{17,9},{25,17},{2,26},{10... | collective-permute-start | bytes 1572872 | tf_op jit(solution)/shard_map/ppermute | solution.py:351
  113.0 59.5 %collective-permute-start.12 = (f32[8,128,128]{2,1,0:T(8,128)S(1)}, f32[8,128,128]{2,1,0:T(8,128)S(1)}, u32[]{:S(2)}, u32[]{:S(2)}) collective-permute-start(f32[8,128,128]{2,1,0:T(8,128)S(1)} %get-tuple-element.114), channel_id=1, source_target_pairs={{0,8},{8,16},{16,24},{24,0},{1,9},{9,17},{17,25},{25,1},{2,10},{10... | collective-permute-start | bytes 1572872 | tf_op jit(solution)/shard_map/ppermute | solution.py:351
  124.1 77.3 %collective-permute-start.13 = (f32[8,128,128]{2,1,0:T(8,128)}, f32[8,128,128]{2,1,0:T(8,128)}, u32[]{:S(2)}, u32[]{:S(2)}) collective-permute-start(f32[8,128,128]{2,1,0:T(8,128)} %get-tuple-element.115), channel_id=1, source_target_pairs={{0,16},{8,24},{16,0},{24,8},{1,17},{9,25},{17,1},{25,9},{2,18},{10... | collective-permute-start | bytes 1572872 | tf_op jit(solution)/shard_map/ppermute | solution.py:351
  128.3 73.1 %collective-permute-start.14 = (f32[8,128,128]{2,1,0:T(8,128)S(1)}, f32[8,128,128]{2,1,0:T(8,128)}, u32[]{:S(2)}, u32[]{:S(2)}) collective-permute-start(f32[8,128,128]{2,1,0:T(8,128)S(1)} %get-tuple-element.116), channel_id=1, source_target_pairs={{0,24},{8,0},{16,8},{24,16},{1,25},{9,1},{17,9},{25,17},{2,26},{10... | collective-permute-start | bytes 1572872 | tf_op jit(solution)/shard_map/ppermute | solution.py:351
  158.0 46.3 %collective-permute-start.6 = (f32[8,128,128]{2,1,0:T(8,128)S(1)}, f32[8,128,128]{2,1,0:T(8,128)}, u32[]{:S(2)}, u32[]{:S(2)}) collective-permute-start(f32[8,128,128]{2,1,0:T(8,128)S(1)} %get-tuple-element.102), channel_id=1, source_target_pairs={{0,8},{8,16},{16,24},{24,0},{1,9},{9,17},{17,25},{25,1},{2,10},{10... | collective-permute-start | bytes 1572872 | tf_op jit(solution)/shard_map/ppermute | solution.py:351
  169.2 54.7 %collective-permute-start.7 = (f32[8,128,128]{2,1,0:T(8,128)S(1)}, f32[8,128,128]{2,1,0:T(8,128)}, u32[]{:S(2)}, u32[]{:S(2)}) collective-permute-start(f32[8,128,128]{2,1,0:T(8,128)S(1)} %get-tuple-element.103), channel_id=1, source_target_pairs={{0,16},{8,24},{16,0},{24,8},{1,17},{9,25},{17,1},{25,9},{2,18},{10... | collective-permute-start | bytes 1572872 | tf_op jit(solution)/shard_map/ppermute | solution.py:351
  173.4 50.5 %collective-permute-start.8 = (f32[8,128,128]{2,1,0:T(8,128)S(1)}, f32[8,128,128]{2,1,0:T(8,128)}, u32[]{:S(2)}, u32[]{:S(2)}) collective-permute-start(f32[8,128,128]{2,1,0:T(8,128)S(1)} %get-tuple-element.104), channel_id=1, source_target_pairs={{0,24},{8,0},{16,8},{24,16},{1,25},{9,1},{17,9},{25,17},{2,26},{10... | collective-permute-start | bytes 1572872 | tf_op jit(solution)/shard_map/ppermute | solution.py:351
  227.0 1.7 collective-permute-start.15
  270.5 1.6 collective-permute-start.16
  290.4 8.3 %collective-permute-start.17 = (f32[32,8,128]{2,1,0:T(8,128)S(1)}, f32[32,8,128]{2,1,0:T(8,128)S(1)}, u32[]{:S(2)}, u32[]{:S(2)}) collective-permute-start(f32[32,8,128]{2,1,0:T(8,128)S(1)} %get-tuple-element.128), channel_id=1, source_target_pairs={{0,8},{8,16},{16,24},{24,0},{1,9},{9,17},{17,25},{25,1},{2,10},{10... | collective-permute-start | bytes 393224 | tf_op jit(solution)/shard_map/ppermute | solution.py:351
  291.4 13.0 %collective-permute-start.18 = (f32[32,8,128]{2,1,0:T(8,128)S(1)}, f32[32,8,128]{2,1,0:T(8,128)S(1)}, u32[]{:S(2)}, u32[]{:S(2)}) collective-permute-start(f32[32,8,128]{2,1,0:T(8,128)S(1)} %get-tuple-element.129), channel_id=1, source_target_pairs={{0,16},{8,24},{16,0},{24,8},{1,17},{9,25},{17,1},{25,9},{2,18},{10... | collective-permute-start | bytes 393224 | tf_op jit(solution)/shard_map/ppermute | solution.py:351
  292.7 11.7 %collective-permute-start.19 = (f32[32,8,128]{2,1,0:T(8,128)S(1)}, f32[32,8,128]{2,1,0:T(8,128)S(1)}, u32[]{:S(2)}, u32[]{:S(2)}) collective-permute-start(f32[32,8,128]{2,1,0:T(8,128)S(1)} %get-tuple-element.130), channel_id=1, source_target_pairs={{0,24},{8,0},{16,8},{24,16},{1,25},{9,1},{17,9},{25,17},{2,26},{10... | collective-permute-start | bytes 393224 | tf_op jit(solution)/shard_map/ppermute | solution.py:351
  295.0 18.3 %collective-permute-start.20 = (f32[32,8,128]{2,1,0:T(8,128)S(1)}, f32[32,8,128]{2,1,0:T(8,128)S(1)}, u32[]{:S(2)}, u32[]{:S(2)}) collective-permute-start(f32[32,8,128]{2,1,0:T(8,128)S(1)} %get-tuple-element.135), channel_id=1, source_target_pairs={{0,8},{8,16},{16,24},{24,0},{1,9},{9,17},{17,25},{25,1},{2,10},{10... | collective-permute-start | bytes 393224 | tf_op jit(solution)/shard_map/ppermute | solution.py:351
  295.6 24.8 %collective-permute-start.21 = (f32[32,8,128]{2,1,0:T(8,128)S(1)}, f32[32,8,128]{2,1,0:T(8,128)S(1)}, u32[]{:S(2)}, u32[]{:S(2)}) collective-permute-start(f32[32,8,128]{2,1,0:T(8,128)S(1)} %get-tuple-element.136), channel_id=1, source_target_pairs={{0,16},{8,24},{16,0},{24,8},{1,17},{9,25},{17,1},{25,9},{2,18},{10... | collective-permute-start | bytes 393224 | tf_op jit(solution)/shard_map/ppermute | solution.py:351
  298.7 21.7 %collective-permute-start.22 = (f32[32,8,128]{2,1,0:T(8,128)S(1)}, f32[32,8,128]{2,1,0:T(8,128)S(1)}, u32[]{:S(2)}, u32[]{:S(2)}) collective-permute-start(f32[32,8,128]{2,1,0:T(8,128)S(1)} %get-tuple-element.137), channel_id=1, source_target_pairs={{0,24},{8,0},{16,8},{24,16},{1,25},{9,1},{17,9},{25,17},{2,26},{10... | collective-permute-start | bytes 393224 | tf_op jit(solution)/shard_map/ppermute | solution.py:351
  304.4 20.3 %collective-permute-start.23 = (f32[32,8,128]{2,1,0:T(8,128)S(1)}, f32[32,8,128]{2,1,0:T(8,128)S(1)}, u32[]{:S(2)}, u32[]{:S(2)}) collective-permute-start(f32[32,8,128]{2,1,0:T(8,128)S(1)} %get-tuple-element.145), channel_id=1, source_target_pairs={{0,8},{8,16},{16,24},{24,0},{1,9},{9,17},{17,25},{25,1},{2,10},{10... | collective-permute-start | bytes 393224 | tf_op jit(solution)/shard_map/ppermute | solution.py:351
  313.4 18.3 %collective-permute-start.24 = (f32[32,8,128]{2,1,0:T(8,128)S(1)}, f32[32,8,128]{2,1,0:T(8,128)S(1)}, u32[]{:S(2)}, u32[]{:S(2)}) collective-permute-start(f32[32,8,128]{2,1,0:T(8,128)S(1)} %get-tuple-element.146), channel_id=1, source_target_pairs={{0,16},{8,24},{16,0},{24,8},{1,17},{9,25},{17,1},{25,9},{2,18},{10... | collective-permute-start | bytes 393224 | tf_op jit(solution)/shard_map/ppermute | solution.py:351
  313.4 18.3 %collective-permute-start.25 = (f32[32,8,128]{2,1,0:T(8,128)S(1)}, f32[32,8,128]{2,1,0:T(8,128)S(1)}, u32[]{:S(2)}, u32[]{:S(2)}) collective-permute-start(f32[32,8,128]{2,1,0:T(8,128)S(1)} %get-tuple-element.147), channel_id=1, source_target_pairs={{0,24},{8,0},{16,8},{24,16},{1,25},{9,1},{17,9},{25,17},{2,26},{10... | collective-permute-start | bytes 393224 | tf_op jit(solution)/shard_map/ppermute | solution.py:351
  320.4 14.6 %collective-permute-start.26 = (f32[32,8,128]{2,1,0:T(8,128)S(1)}, f32[32,8,128]{2,1,0:T(8,128)S(1)}, u32[]{:S(2)}, u32[]{:S(2)}) collective-permute-start(f32[32,8,128]{2,1,0:T(8,128)S(1)} %get-tuple-element.155), channel_id=1, source_target_pairs={{0,8},{8,16},{16,24},{24,0},{1,9},{9,17},{17,25},{25,1},{2,10},{10... | collective-permute-start | bytes 393224 | tf_op jit(solution)/shard_map/ppermute | solution.py:351
  324.6 18.3 %collective-permute-start.27 = (f32[32,8,128]{2,1,0:T(8,128)S(1)}, f32[32,8,128]{2,1,0:T(8,128)S(1)}, u32[]{:S(2)}, u32[]{:S(2)}) collective-permute-start(f32[32,8,128]{2,1,0:T(8,128)S(1)} %get-tuple-element.156), channel_id=1, source_target_pairs={{0,16},{8,24},{16,0},{24,8},{1,17},{9,25},{17,1},{25,9},{2,18},{10... | collective-permute-start | bytes 393224 | tf_op jit(solution)/shard_map/ppermute | solution.py:351
  324.7 18.2 %collective-permute-start.28 = (f32[32,8,128]{2,1,0:T(8,128)S(1)}, f32[32,8,128]{2,1,0:T(8,128)S(1)}, u32[]{:S(2)}, u32[]{:S(2)}) collective-permute-start(f32[32,8,128]{2,1,0:T(8,128)S(1)} %get-tuple-element.157), channel_id=1, source_target_pairs={{0,24},{8,0},{16,8},{24,16},{1,25},{9,1},{17,9},{25,17},{2,26},{10... | collective-permute-start | bytes 393224 | tf_op jit(solution)/shard_map/ppermute | solution.py:351
  331.6 11.2 %collective-permute-start.29 = (f32[32,8,128]{2,1,0:T(8,128)S(1)}, f32[32,8,128]{2,1,0:T(8,128)S(1)}, u32[]{:S(2)}, u32[]{:S(2)}) collective-permute-start(f32[32,8,128]{2,1,0:T(8,128)S(1)} %get-tuple-element.165), channel_id=1, source_target_pairs={{0,8},{8,16},{16,24},{24,0},{1,9},{9,17},{17,25},{25,1},{2,10},{10... | collective-permute-start | bytes 393224 | tf_op jit(solution)/shard_map/ppermute | solution.py:351
  335.0 13.5 %collective-permute-start.30 = (f32[32,8,128]{2,1,0:T(8,128)S(1)}, f32[32,8,128]{2,1,0:T(8,128)S(1)}, u32[]{:S(2)}, u32[]{:S(2)}) collective-permute-start(f32[32,8,128]{2,1,0:T(8,128)S(1)} %get-tuple-element.166), channel_id=1, source_target_pairs={{0,16},{8,24},{16,0},{24,8},{1,17},{9,25},{17,1},{25,9},{2,18},{10... | collective-permute-start | bytes 393224 | tf_op jit(solution)/shard_map/ppermute | solution.py:351
  335.0 13.5 %collective-permute-start.31 = (f32[32,8,128]{2,1,0:T(8,128)S(1)}, f32[32,8,128]{2,1,0:T(8,128)S(1)}, u32[]{:S(2)}, u32[]{:S(2)}) collective-permute-start(f32[32,8,128]{2,1,0:T(8,128)S(1)} %get-tuple-element.167), channel_id=1, source_target_pairs={{0,24},{8,0},{16,8},{24,16},{1,25},{9,1},{17,9},{25,17},{2,26},{10... | collective-permute-start | bytes 393224 | tf_op jit(solution)/shard_map/ppermute | solution.py:351
  (26 other events, 50.1 us)

commit v9 on v8

--- a/solution.py
+++ b/solution.py
@@ -401,7 +401,7 @@
     pieces = [(0, xlocal, start, steps) for start in starts]
     packed = pack(me, snapshot, groups, pieces[:1], LARGE)
     if chunks > 1:
-        packed += pack(me, snapshot, groups, pieces[1:], 16 * 2**20)
+        packed += [parts for piece in pieces[1:] for parts in pack(me, snapshot, groups, [piece], SMALL)]
 
     moved = []
     for index, parts in enumerate(packed):

time: 351 us -> 351 us (level)
  local copies, waits for them, and re-layouts: 26.2 us -> 15 us
  waiting for transfers between devices: 131 us -> 141 us
    unnamed x52 -> x40, local copies, waits for them, and re-layouts: 26.2 us -> 15 us
    ppermute x30, waiting for transfers between devices: 128 us -> 137 us  [exchange(): lax.ppermute(parts[shift], 'gx', [(i, (i + shift) % groups) for i in rang...]
    pallas_call x2 -> x5, Pallas kernels: 10 us -> 11.2 us  [pack(): pl.pallas_call(functools.partial(pack_kernel, groups, per, tuple(pieces))...]
  transfers between devices with their start and end apart: 32 -> 32, of which waited for: 13 -> 14; matrix products, arithmetic and copies ran while one was open for 0% -> 0% of each run, Pallas kernels for 5% -> 5%
where the time goes in v9:
time: 351 us; the launch traced here: 350 us
  waiting for transfers between devices  141 us (40%)
  starting transfers between devices  106 us (30%)
  Pallas kernels  45.5 us (13%)
  blocking collectives  41.7 us (12%)
  local copies, waits for them, and re-layouts  15 us (4%)
    ppermute x30, waiting for transfers between devices, exchange(): lax.ppermute(parts[shift], 'gx', [(i, (i + shift) % groups) for i in rang...  137 us
    ppermute x30, starting transfers between devices, exchange(): lax.ppermute(parts[shift], 'gx', [(i, (i + shift) % groups) for i in rang...  106 us
    all_to_all x1, blocking collectives, total_sum(): lax.all_to_all(parts, CHIPS, split_axis=0, concat_axis=0, tiled=True)  27.5 us
    pallas_call x1, Pallas kernels, factor_step(): pl.pallas_call(functools.partial(factor_kernel, groups, xlocal), out_shap...  17.5 us
    unnamed x40, local copies, waits for them, and re-layouts  15 us
    all_to_all x1, blocking collectives, total_sum(): lax.all_to_all(spread, CHIPS, split_axis=0, concat_axis=0, tiled=True)  14.1 us
    pallas_call x5, Pallas kernels, gram_step(): pl.pallas_call(functools.partial(gram_kernel, first, final, groups), out_...  11.2 us
    pallas_call x5, Pallas kernels, pack(): pl.pallas_call(functools.partial(pack_kernel, groups, per, tuple(pieces))...  11.2 us
  transfers between devices with their start and end apart: 32, of which 14 were waited for; matrix products, arithmetic and copies ran while one was open for 0% of the time, Pallas kernels for 5%

profile of v9, /device:TPU:0, one launch (start us, length us, event | category | flops | bytes accessed | tf_op | source)
XLA Modules:
  0.0 350.3 jit_solution(8484563861531377479)
XLA Ops:
  0.6 3.5 shard_map.32
  4.1 3.1 collective-permute-start
  7.2 2.6 collective-permute-start.1
  11.1 4.0 %copy-done = f32[128,160,128]{2,1,0:T(8,128)S(1)} copy-done((f32[128,160,128]{2,1,0:T(8,128)S(1)}, f32[128,160,128]{2,1,0:T(8,128)}, u32[]{:S(2)}) %copy-start) | copy-done | bytes 10485784
  17.6 4.7 %collective-permute-done.refs_1_ = f32[8,128,128]{2,1,0:T(8,128)S(1)} collective-permute-done((f32[8,128,128]{2,1,0:T(8,128)}, f32[8,128,128]{2,1,0:T(8,128)S(1)}, u32[]{:S(2)}, u32[]{:S(2)}) %collective-permute-start) | collective-permute-done | bytes 524320 | tf_op jit(solution)/shard_map/ppermute | solution.py:351
  22.3 2.5 collective-permute-start.11
  27.0 17.8 %collective-permute-done.1.refs_2_ = f32[8,128,128]{2,1,0:T(8,128)S(1)} collective-permute-done((f32[8,128,128]{2,1,0:T(8,128)}, f32[8,128,128]{2,1,0:T(8,128)S(1)}, u32[]{:S(2)}, u32[]{:S(2)}) %collective-permute-start.1) | collective-permute-done | bytes 524320 | tf_op jit(solution)/shard_map/ppermute | solution.py:351
  44.9 34.3 %collective-permute-start.3 = (f32[8,128,128]{2,1,0:T(8,128)S(1)}, f32[8,128,128]{2,1,0:T(8,128)S(1)}, u32[]{:S(2)}, u32[]{:S(2)}) collective-permute-start(f32[8,128,128]{2,1,0:T(8,128)S(1)} %get-tuple-element.98), channel_id=1, source_target_pairs={{0,8},{8,16},{16,24},{24,0},{1,9},{9,17},{17,25},{25,1},{2,10},{10... | collective-permute-start | bytes 1572872 | tf_op jit(solution)/shard_map/ppermute | solution.py:351
  81.5 2.4 shard_map.33
  84.7 26.7 %collective-permute-done.10.refs_2_ = f32[8,128,128]{2,1,0:T(8,128)S(1)} collective-permute-done((f32[8,128,128]{2,1,0:T(8,128)S(1)}, f32[8,128,128]{2,1,0:T(8,128)S(1)}, u32[]{:S(2)}, u32[]{:S(2)}) %collective-permute-start.10) | collective-permute-done | bytes 524320 | tf_op jit(solution)/shard_map/ppermute | solution.py:351
  111.5 11.8 %collective-permute-start.12 = (f32[8,128,128]{2,1,0:T(8,128)S(1)}, f32[8,128,128]{2,1,0:T(8,128)S(1)}, u32[]{:S(2)}, u32[]{:S(2)}) collective-permute-start(f32[8,128,128]{2,1,0:T(8,128)S(1)} %get-tuple-element.114), channel_id=1, source_target_pairs={{0,8},{8,16},{16,24},{24,0},{1,9},{9,17},{17,25},{25,1},{2,10},{10... | collective-permute-start | bytes 1572872 | tf_op jit(solution)/shard_map/ppermute | solution.py:351
  123.3 2.7 collective-permute-start.13
  126.0 2.4 shard_map.30
  129.2 27.2 %collective-permute-done.4.refs_2_ = f32[8,128,128]{2,1,0:T(8,128)S(1)} collective-permute-done((f32[8,128,128]{2,1,0:T(8,128)S(1)}, f32[8,128,128]{2,1,0:T(8,128)S(1)}, u32[]{:S(2)}, u32[]{:S(2)}) %collective-permute-start.4) | collective-permute-done | bytes 524320 | tf_op jit(solution)/shard_map/ppermute | solution.py:351
  158.0 11.1 %collective-permute-start.6 = (f32[8,128,128]{2,1,0:T(8,128)}, f32[8,128,128]{2,1,0:T(8,128)}, u32[]{:S(2)}, u32[]{:S(2)}) collective-permute-start(f32[8,128,128]{2,1,0:T(8,128)} %get-tuple-element.102), channel_id=1, source_target_pairs={{0,8},{8,16},{16,24},{24,0},{1,9},{9,17},{17,25},{25,1},{2,10},{10... | collective-permute-start | bytes 1572872 | tf_op jit(solution)/shard_map/ppermute | solution.py:351
  169.1 3.4 collective-permute-start.7
  184.8 16.7 %collective-permute-done.13.refs_2_ = f32[8,128,128]{2,1,0:T(8,128)} collective-permute-done((f32[8,128,128]{2,1,0:T(8,128)}, f32[8,128,128]{2,1,0:T(8,128)}, u32[]{:S(2)}, u32[]{:S(2)}) %collective-permute-start.13) | collective-permute-done | bytes 524320 | tf_op jit(solution)/shard_map/ppermute | solution.py:351
  201.5 2.9 shard_map.38
  204.4 19.5 %collective-permute-done.7.refs_2_ = f32[8,128,128]{2,1,0:T(8,128)} collective-permute-done((f32[8,128,128]{2,1,0:T(8,128)}, f32[8,128,128]{2,1,0:T(8,128)}, u32[]{:S(2)}, u32[]{:S(2)}) %collective-permute-start.7) | collective-permute-done | bytes 524320 | tf_op jit(solution)/shard_map/ppermute | solution.py:351
  223.9 3.1 shard_map.39
  228.8 27.5 %all_to_all.10.parts_ref = f32[16,40,128]{2,1,0:T(8,128)S(1)} all-to-all(f32[16,40,128]{2,1,0:T(8,128)S(1)} %bitcast.6), channel_id=1, replica_groups=mesh['gx'=4,'gy'=2,'gu'=2,'gc'=2] {'gx','gy','gu'}, dimensions={0} | all-to-all | bytes 655360 | tf_op jit(solution)/shard_map/all_to_all | solution.py:377
  256.4 14.1 %all_to_all.11 = f32[16,40,128]{2,1,0:T(8,128)S(1)} all-to-all(f32[16,40,128]{2,1,0:T(8,128)S(1)} %shard_map.41), channel_id=1, replica_groups=mesh['gx'=4,'gy'=2,'gu'=2,'gc'=2] {'gx','gy','gu'}, dimensions={0} | all-to-all | bytes 655360 | tf_op jit(solution)/shard_map/all_to_all | solution.py:379
  272.1 17.5 %shard_map.42 = (f32[128,128]{1,0:T(8,128)}, f32[128,512]{1,0:T(8,128)S(1)}) custom-call(s32[1]{0:T(128)} %bitcast.me_ref, s32[1]{0:T(128)} %bitcast.1.core_ref, f32[640,128]{1,0:T(8,128)S(1)} %bitcast.5, f32[640,128]{1,0:T(8,128)S(1)} %collective-permute-done.16.other_ref), custom_call_target="tpu_custom_call" | custom-call | tf_op jit(solution)/shard_map/pallas_call | solution.py:256
  300.8 3.6 %collective-permute-done.18.refs_2_ = f32[32,8,128]{2,1,0:T(8,128)S(1)} collective-permute-done((f32[32,8,128]{2,1,0:T(8,128)S(1)}, f32[32,8,128]{2,1,0:T(8,128)S(1)}, u32[]{:S(2)}, u32[]{:S(2)}) %collective-permute-start.18) | collective-permute-done | bytes 131104 | tf_op jit(solution)/shard_map/ppermute | solution.py:351
  304.4 9.0 %collective-permute-start.23 = (f32[32,8,128]{2,1,0:T(8,128)S(1)}, f32[32,8,128]{2,1,0:T(8,128)S(1)}, u32[]{:S(2)}, u32[]{:S(2)}) collective-permute-start(f32[32,8,128]{2,1,0:T(8,128)S(1)} %get-tuple-element.145), channel_id=1, source_target_pairs={{0,8},{8,16},{16,24},{24,0},{1,9},{9,17},{17,25},{25,1},{2,10},{10... | collective-permute-start | bytes 393224 | tf_op jit(solution)/shard_map/ppermute | solution.py:351
  313.4 2.4 collective-permute-start.25
  316.5 3.9 %collective-permute-done.21.refs_6_ = f32[32,8,128]{2,1,0:T(8,128)S(1)} collective-permute-done((f32[32,8,128]{2,1,0:T(8,128)S(1)}, f32[32,8,128]{2,1,0:T(8,128)S(1)}, u32[]{:S(2)}, u32[]{:S(2)}) %collective-permute-start.21) | collective-permute-done | bytes 131104 | tf_op jit(solution)/shard_map/ppermute | solution.py:351
  320.4 3.4 collective-permute-start.26
  327.0 4.6 %collective-permute-done.24.refs_10_ = f32[32,8,128]{2,1,0:T(8,128)S(1)} collective-permute-done((f32[32,8,128]{2,1,0:T(8,128)S(1)}, f32[32,8,128]{2,1,0:T(8,128)S(1)}, u32[]{:S(2)}, u32[]{:S(2)}) %collective-permute-start.24) | collective-permute-done | bytes 131104 | tf_op jit(solution)/shard_map/ppermute | solution.py:351
  331.6 3.4 collective-permute-start.29
  337.4 5.5 %collective-permute-done.27.refs_14_ = f32[32,8,128]{2,1,0:T(8,128)S(1)} collective-permute-done((f32[32,8,128]{2,1,0:T(8,128)S(1)}, f32[32,8,128]{2,1,0:T(8,128)S(1)}, u32[]{:S(2)}, u32[]{:S(2)}) %collective-permute-start.27) | collective-permute-done | bytes 131104 | tf_op jit(solution)/shard_map/ppermute | solution.py:351
  342.9 5.6 %collective-permute-done.30.refs_18_ = f32[32,8,128]{2,1,0:T(8,128)S(1)} collective-permute-done((f32[32,8,128]{2,1,0:T(8,128)S(1)}, f32[32,8,128]{2,1,0:T(8,128)S(1)}, u32[]{:S(2)}, u32[]{:S(2)}) %collective-permute-start.30) | collective-permute-done | bytes 131104 | tf_op jit(solution)/shard_map/ppermute | solution.py:351
  (93 shorter events, 46.5 us)
Async XLA Ops:
  4.1 18.2 %collective-permute-start = (f32[8,128,128]{2,1,0:T(8,128)}, f32[8,128,128]{2,1,0:T(8,128)S(1)}, u32[]{:S(2)}, u32[]{:S(2)}) collective-permute-start(f32[8,128,128]{2,1,0:T(8,128)} %get-tuple-element.94), channel_id=1, source_target_pairs={{0,8},{8,16},{16,24},{24,0},{1,9},{9,17},{17,25},{25,1},{2,10},{10... | collective-permute-start | bytes 1572872 | tf_op jit(solution)/shard_map/ppermute | solution.py:351
  7.2 37.6 %collective-permute-start.1 = (f32[8,128,128]{2,1,0:T(8,128)}, f32[8,128,128]{2,1,0:T(8,128)S(1)}, u32[]{:S(2)}, u32[]{:S(2)}) collective-permute-start(f32[8,128,128]{2,1,0:T(8,128)} %get-tuple-element.95), channel_id=1, source_target_pairs={{0,16},{8,24},{16,0},{24,8},{1,17},{9,25},{17,1},{25,9},{2,18},{10... | collective-permute-start | bytes 1572872 | tf_op jit(solution)/shard_map/ppermute | solution.py:351
  9.8 35.1 %collective-permute-start.2 = (f32[8,128,128]{2,1,0:T(8,128)}, f32[8,128,128]{2,1,0:T(8,128)S(1)}, u32[]{:S(2)}, u32[]{:S(2)}) collective-permute-start(f32[8,128,128]{2,1,0:T(8,128)} %get-tuple-element.96), channel_id=1, source_target_pairs={{0,24},{8,0},{16,8},{24,16},{1,25},{9,1},{17,9},{25,17},{2,26},{10... | collective-permute-start | bytes 1572872 | tf_op jit(solution)/shard_map/ppermute | solution.py:351
  16.6 64.3 %collective-permute-start.9 = (f32[8,128,128]{2,1,0:T(8,128)S(1)}, f32[8,128,128]{2,1,0:T(8,128)S(1)}, u32[]{:S(2)}, u32[]{:S(2)}) collective-permute-start(f32[8,128,128]{2,1,0:T(8,128)S(1)} %get-tuple-element.110), channel_id=1, source_target_pairs={{0,8},{8,16},{16,24},{24,0},{1,9},{9,17},{17,25},{25,1},{2,10},{10... | collective-permute-start | bytes 1572872 | tf_op jit(solution)/shard_map/ppermute | solution.py:351
  17.3 94.2 %collective-permute-start.10 = (f32[8,128,128]{2,1,0:T(8,128)S(1)}, f32[8,128,128]{2,1,0:T(8,128)S(1)}, u32[]{:S(2)}, u32[]{:S(2)}) collective-permute-start(f32[8,128,128]{2,1,0:T(8,128)S(1)} %get-tuple-element.111), channel_id=1, source_target_pairs={{0,16},{8,24},{16,0},{24,8},{1,17},{9,25},{17,1},{25,9},{2,18},{10... | collective-permute-start | bytes 1572872 | tf_op jit(solution)/shard_map/ppermute | solution.py:351
  22.3 89.1 %collective-permute-start.11 = (f32[8,128,128]{2,1,0:T(8,128)S(1)}, f32[8,128,128]{2,1,0:T(8,128)S(1)}, u32[]{:S(2)}, u32[]{:S(2)}) collective-permute-start(f32[8,128,128]{2,1,0:T(8,128)S(1)} %get-tuple-element.112), channel_id=1, source_target_pairs={{0,24},{8,0},{16,8},{24,16},{1,25},{9,1},{17,9},{25,17},{2,26},{10... | collective-permute-start | bytes 1572872 | tf_op jit(solution)/shard_map/ppermute | solution.py:351
  44.9 81.1 %collective-permute-start.3 = (f32[8,128,128]{2,1,0:T(8,128)S(1)}, f32[8,128,128]{2,1,0:T(8,128)S(1)}, u32[]{:S(2)}, u32[]{:S(2)}) collective-permute-start(f32[8,128,128]{2,1,0:T(8,128)S(1)} %get-tuple-element.98), channel_id=1, source_target_pairs={{0,8},{8,16},{16,24},{24,0},{1,9},{9,17},{17,25},{25,1},{2,10},{10... | collective-permute-start | bytes 1572872 | tf_op jit(solution)/shard_map/ppermute | solution.py:351
  79.1 77.3 %collective-permute-start.4 = (f32[8,128,128]{2,1,0:T(8,128)S(1)}, f32[8,128,128]{2,1,0:T(8,128)S(1)}, u32[]{:S(2)}, u32[]{:S(2)}) collective-permute-start(f32[8,128,128]{2,1,0:T(8,128)S(1)} %get-tuple-element.99), channel_id=1, source_target_pairs={{0,16},{8,24},{16,0},{24,8},{1,17},{9,25},{17,1},{25,9},{2,18},{10... | collective-permute-start | bytes 1572872 | tf_op jit(solution)/shard_map/ppermute | solution.py:351
  80.9 76.3 %collective-permute-start.5 = (f32[8,128,128]{2,1,0:T(8,128)S(1)}, f32[8,128,128]{2,1,0:T(8,128)S(1)}, u32[]{:S(2)}, u32[]{:S(2)}) collective-permute-start(f32[8,128,128]{2,1,0:T(8,128)S(1)} %get-tuple-element.100), channel_id=1, source_target_pairs={{0,24},{8,0},{16,8},{24,16},{1,25},{9,1},{17,9},{25,17},{2,26},{10... | collective-permute-start | bytes 1572872 | tf_op jit(solution)/shard_map/ppermute | solution.py:351
  111.5 61.0 %collective-permute-start.12 = (f32[8,128,128]{2,1,0:T(8,128)S(1)}, f32[8,128,128]{2,1,0:T(8,128)S(1)}, u32[]{:S(2)}, u32[]{:S(2)}) collective-permute-start(f32[8,128,128]{2,1,0:T(8,128)S(1)} %get-tuple-element.114), channel_id=1, source_target_pairs={{0,8},{8,16},{16,24},{24,0},{1,9},{9,17},{17,25},{25,1},{2,10},{10... | collective-permute-start | bytes 1572872 | tf_op jit(solution)/shard_map/ppermute | solution.py:351
  123.3 78.2 %collective-permute-start.13 = (f32[8,128,128]{2,1,0:T(8,128)}, f32[8,128,128]{2,1,0:T(8,128)}, u32[]{:S(2)}, u32[]{:S(2)}) collective-permute-start(f32[8,128,128]{2,1,0:T(8,128)} %get-tuple-element.115), channel_id=1, source_target_pairs={{0,16},{8,24},{16,0},{24,8},{1,17},{9,25},{17,1},{25,9},{2,18},{10... | collective-permute-start | bytes 1572872 | tf_op jit(solution)/shard_map/ppermute | solution.py:351
  126.0 75.5 %collective-permute-start.14 = (f32[8,128,128]{2,1,0:T(8,128)}, f32[8,128,128]{2,1,0:T(8,128)}, u32[]{:S(2)}, u32[]{:S(2)}) collective-permute-start(f32[8,128,128]{2,1,0:T(8,128)} %get-tuple-element.116), channel_id=1, source_target_pairs={{0,24},{8,0},{16,8},{24,16},{1,25},{9,1},{17,9},{25,17},{2,26},{10... | collective-permute-start | bytes 1572872 | tf_op jit(solution)/shard_map/ppermute | solution.py:351
  158.0 46.4 %collective-permute-start.6 = (f32[8,128,128]{2,1,0:T(8,128)}, f32[8,128,128]{2,1,0:T(8,128)}, u32[]{:S(2)}, u32[]{:S(2)}) collective-permute-start(f32[8,128,128]{2,1,0:T(8,128)} %get-tuple-element.102), channel_id=1, source_target_pairs={{0,8},{8,16},{16,24},{24,0},{1,9},{9,17},{17,25},{25,1},{2,10},{10... | collective-permute-start | bytes 1572872 | tf_op jit(solution)/shard_map/ppermute | solution.py:351
  169.1 54.8 %collective-permute-start.7 = (f32[8,128,128]{2,1,0:T(8,128)}, f32[8,128,128]{2,1,0:T(8,128)}, u32[]{:S(2)}, u32[]{:S(2)}) collective-permute-start(f32[8,128,128]{2,1,0:T(8,128)} %get-tuple-element.103), channel_id=1, source_target_pairs={{0,16},{8,24},{16,0},{24,8},{1,17},{9,25},{17,1},{25,9},{2,18},{10... | collective-permute-start | bytes 1572872 | tf_op jit(solution)/shard_map/ppermute | solution.py:351
  173.3 50.7 %collective-permute-start.8 = (f32[8,128,128]{2,1,0:T(8,128)}, f32[8,128,128]{2,1,0:T(8,128)}, u32[]{:S(2)}, u32[]{:S(2)}) collective-permute-start(f32[8,128,128]{2,1,0:T(8,128)} %get-tuple-element.104), channel_id=1, source_target_pairs={{0,24},{8,0},{16,8},{24,16},{1,25},{9,1},{17,9},{25,17},{2,26},{10... | collective-permute-start | bytes 1572872 | tf_op jit(solution)/shard_map/ppermute | solution.py:351
  227.0 1.7 collective-permute-start.15
  270.5 1.6 collective-permute-start.16
  290.4 8.3 %collective-permute-start.17 = (f32[32,8,128]{2,1,0:T(8,128)S(1)}, f32[32,8,128]{2,1,0:T(8,128)S(1)}, u32[]{:S(2)}, u32[]{:S(2)}) collective-permute-start(f32[32,8,128]{2,1,0:T(8,128)S(1)} %get-tuple-element.128), channel_id=1, source_target_pairs={{0,8},{8,16},{16,24},{24,0},{1,9},{9,17},{17,25},{25,1},{2,10},{10... | collective-permute-start | bytes 393224 | tf_op jit(solution)/shard_map/ppermute | solution.py:351
  291.4 12.9 %collective-permute-start.18 = (f32[32,8,128]{2,1,0:T(8,128)S(1)}, f32[32,8,128]{2,1,0:T(8,128)S(1)}, u32[]{:S(2)}, u32[]{:S(2)}) collective-permute-start(f32[32,8,128]{2,1,0:T(8,128)S(1)} %get-tuple-element.129), channel_id=1, source_target_pairs={{0,16},{8,24},{16,0},{24,8},{1,17},{9,25},{17,1},{25,9},{2,18},{10... | collective-permute-start | bytes 393224 | tf_op jit(solution)/shard_map/ppermute | solution.py:351
  292.7 11.7 %collective-permute-start.19 = (f32[32,8,128]{2,1,0:T(8,128)S(1)}, f32[32,8,128]{2,1,0:T(8,128)S(1)}, u32[]{:S(2)}, u32[]{:S(2)}) collective-permute-start(f32[32,8,128]{2,1,0:T(8,128)S(1)} %get-tuple-element.130), channel_id=1, source_target_pairs={{0,24},{8,0},{16,8},{24,16},{1,25},{9,1},{17,9},{25,17},{2,26},{10... | collective-permute-start | bytes 393224 | tf_op jit(solution)/shard_map/ppermute | solution.py:351
  295.0 18.3 %collective-permute-start.20 = (f32[32,8,128]{2,1,0:T(8,128)S(1)}, f32[32,8,128]{2,1,0:T(8,128)S(1)}, u32[]{:S(2)}, u32[]{:S(2)}) collective-permute-start(f32[32,8,128]{2,1,0:T(8,128)S(1)} %get-tuple-element.135), channel_id=1, source_target_pairs={{0,8},{8,16},{16,24},{24,0},{1,9},{9,17},{17,25},{25,1},{2,10},{10... | collective-permute-start | bytes 393224 | tf_op jit(solution)/shard_map/ppermute | solution.py:351
  295.6 24.8 %collective-permute-start.21 = (f32[32,8,128]{2,1,0:T(8,128)S(1)}, f32[32,8,128]{2,1,0:T(8,128)S(1)}, u32[]{:S(2)}, u32[]{:S(2)}) collective-permute-start(f32[32,8,128]{2,1,0:T(8,128)S(1)} %get-tuple-element.136), channel_id=1, source_target_pairs={{0,16},{8,24},{16,0},{24,8},{1,17},{9,25},{17,1},{25,9},{2,18},{10... | collective-permute-start | bytes 393224 | tf_op jit(solution)/shard_map/ppermute | solution.py:351
  298.7 21.7 %collective-permute-start.22 = (f32[32,8,128]{2,1,0:T(8,128)S(1)}, f32[32,8,128]{2,1,0:T(8,128)S(1)}, u32[]{:S(2)}, u32[]{:S(2)}) collective-permute-start(f32[32,8,128]{2,1,0:T(8,128)S(1)} %get-tuple-element.137), channel_id=1, source_target_pairs={{0,24},{8,0},{16,8},{24,16},{1,25},{9,1},{17,9},{25,17},{2,26},{10... | collective-permute-start | bytes 393224 | tf_op jit(solution)/shard_map/ppermute | solution.py:351
  304.4 20.3 %collective-permute-start.23 = (f32[32,8,128]{2,1,0:T(8,128)S(1)}, f32[32,8,128]{2,1,0:T(8,128)S(1)}, u32[]{:S(2)}, u32[]{:S(2)}) collective-permute-start(f32[32,8,128]{2,1,0:T(8,128)S(1)} %get-tuple-element.145), channel_id=1, source_target_pairs={{0,8},{8,16},{16,24},{24,0},{1,9},{9,17},{17,25},{25,1},{2,10},{10... | collective-permute-start | bytes 393224 | tf_op jit(solution)/shard_map/ppermute | solution.py:351
  313.3 18.3 %collective-permute-start.24 = (f32[32,8,128]{2,1,0:T(8,128)S(1)}, f32[32,8,128]{2,1,0:T(8,128)S(1)}, u32[]{:S(2)}, u32[]{:S(2)}) collective-permute-start(f32[32,8,128]{2,1,0:T(8,128)S(1)} %get-tuple-element.146), channel_id=1, source_target_pairs={{0,16},{8,24},{16,0},{24,8},{1,17},{9,25},{17,1},{25,9},{2,18},{10... | collective-permute-start | bytes 393224 | tf_op jit(solution)/shard_map/ppermute | solution.py:351
  313.4 18.3 %collective-permute-start.25 = (f32[32,8,128]{2,1,0:T(8,128)S(1)}, f32[32,8,128]{2,1,0:T(8,128)S(1)}, u32[]{:S(2)}, u32[]{:S(2)}) collective-permute-start(f32[32,8,128]{2,1,0:T(8,128)S(1)} %get-tuple-element.147), channel_id=1, source_target_pairs={{0,24},{8,0},{16,8},{24,16},{1,25},{9,1},{17,9},{25,17},{2,26},{10... | collective-permute-start | bytes 393224 | tf_op jit(solution)/shard_map/ppermute | solution.py:351
  320.4 14.6 %collective-permute-start.26 = (f32[32,8,128]{2,1,0:T(8,128)S(1)}, f32[32,8,128]{2,1,0:T(8,128)S(1)}, u32[]{:S(2)}, u32[]{:S(2)}) collective-permute-start(f32[32,8,128]{2,1,0:T(8,128)S(1)} %get-tuple-element.155), channel_id=1, source_target_pairs={{0,8},{8,16},{16,24},{24,0},{1,9},{9,17},{17,25},{25,1},{2,10},{10... | collective-permute-start | bytes 393224 | tf_op jit(solution)/shard_map/ppermute | solution.py:351
  324.6 18.3 %collective-permute-start.27 = (f32[32,8,128]{2,1,0:T(8,128)S(1)}, f32[32,8,128]{2,1,0:T(8,128)S(1)}, u32[]{:S(2)}, u32[]{:S(2)}) collective-permute-start(f32[32,8,128]{2,1,0:T(8,128)S(1)} %get-tuple-element.156), channel_id=1, source_target_pairs={{0,16},{8,24},{16,0},{24,8},{1,17},{9,25},{17,1},{25,9},{2,18},{10... | collective-permute-start | bytes 393224 | tf_op jit(solution)/shard_map/ppermute | solution.py:351
  324.6 18.2 %collective-permute-start.28 = (f32[32,8,128]{2,1,0:T(8,128)S(1)}, f32[32,8,128]{2,1,0:T(8,128)S(1)}, u32[]{:S(2)}, u32[]{:S(2)}) collective-permute-start(f32[32,8,128]{2,1,0:T(8,128)S(1)} %get-tuple-element.157), channel_id=1, source_target_pairs={{0,24},{8,0},{16,8},{24,16},{1,25},{9,1},{17,9},{25,17},{2,26},{10... | collective-permute-start | bytes 393224 | tf_op jit(solution)/shard_map/ppermute | solution.py:351
  331.6 11.2 %collective-permute-start.29 = (f32[32,8,128]{2,1,0:T(8,128)S(1)}, f32[32,8,128]{2,1,0:T(8,128)S(1)}, u32[]{:S(2)}, u32[]{:S(2)}) collective-permute-start(f32[32,8,128]{2,1,0:T(8,128)S(1)} %get-tuple-element.165), channel_id=1, source_target_pairs={{0,8},{8,16},{16,24},{24,0},{1,9},{9,17},{17,25},{25,1},{2,10},{10... | collective-permute-start | bytes 393224 | tf_op jit(solution)/shard_map/ppermute | solution.py:351
  335.0 13.5 %collective-permute-start.30 = (f32[32,8,128]{2,1,0:T(8,128)S(1)}, f32[32,8,128]{2,1,0:T(8,128)S(1)}, u32[]{:S(2)}, u32[]{:S(2)}) collective-permute-start(f32[32,8,128]{2,1,0:T(8,128)S(1)} %get-tuple-element.166), channel_id=1, source_target_pairs={{0,16},{8,24},{16,0},{24,8},{1,17},{9,25},{17,1},{25,9},{2,18},{10... | collective-permute-start | bytes 393224 | tf_op jit(solution)/shard_map/ppermute | solution.py:351
  335.0 13.5 %collective-permute-start.31 = (f32[32,8,128]{2,1,0:T(8,128)S(1)}, f32[32,8,128]{2,1,0:T(8,128)S(1)}, u32[]{:S(2)}, u32[]{:S(2)}) collective-permute-start(f32[32,8,128]{2,1,0:T(8,128)S(1)} %get-tuple-element.167), channel_id=1, source_target_pairs={{0,24},{8,0},{16,8},{24,16},{1,25},{9,1},{17,9},{25,17},{2,26},{10... | collective-permute-start | bytes 393224 | tf_op jit(solution)/shard_map/ppermute | solution.py:351
  (20 other events, 343.6 us)

commit v10 on v9

--- a/solution.py
+++ b/solution.py
@@ -422,7 +422,7 @@
         if len(outs) == 1:
             (turned,) = hold([turned], parts[0])
         parts = core_step(me, turned, held, groups, zlocal)
-        outs.append(exchange(hold(parts, outs[-2]) if len(outs) >= 2 else parts))
+        outs.append(exchange(hold(parts, outs[-3]) if len(outs) >= 3 else parts))
     return (mine, place(me, outs, starts[-1:] + starts[:-1], ylocal))
 
 

time: 351 us -> 352 us (level)
  no operation moved by 1% of the time
where the time goes in v10:
time: 352 us; the launch traced here: 351 us
  waiting for transfers between devices  142 us (40%)
  starting transfers between devices  106 us (30%)
  Pallas kernels  45.5 us (13%)
  blocking collectives  41.7 us (12%)
  local copies, waits for them, and re-layouts  15 us (4%)
    ppermute x30, waiting for transfers between devices, exchange(): lax.ppermute(parts[shift], 'gx', [(i, (i + shift) % groups) for i in rang...  138 us
    ppermute x30, starting transfers between devices, exchange(): lax.ppermute(parts[shift], 'gx', [(i, (i + shift) % groups) for i in rang...  106 us
    all_to_all x1, blocking collectives, total_sum(): lax.all_to_all(parts, CHIPS, split_axis=0, concat_axis=0, tiled=True)  27.5 us
    pallas_call x1, Pallas kernels, factor_step(): pl.pallas_call(functools.partial(factor_kernel, groups, xlocal), out_shap...  17.5 us
    unnamed x40, local copies, waits for them, and re-layouts  15 us
    all_to_all x1, blocking collectives, total_sum(): lax.all_to_all(spread, CHIPS, split_axis=0, concat_axis=0, tiled=True)  14.1 us
    pallas_call x5, Pallas kernels, gram_step(): pl.pallas_call(functools.partial(gram_kernel, first, final, groups), out_...  11.2 us
    pallas_call x5, Pallas kernels, pack(): pl.pallas_call(functools.partial(pack_kernel, groups, per, tuple(pieces))...  11.2 us
  transfers between devices with their start and end apart: 32, of which 14 were waited for; matrix products, arithmetic and copies ran while one was open for 0% of the time, Pallas kernels for 5%

profile of v10, /device:TPU:0, one launch (start us, length us, event | category | flops | bytes accessed | tf_op | source)
XLA Modules:
  0.0 351.2 jit_solution(6492071211305999247)
XLA Ops:
  0.6 3.5 shard_map.32
  4.1 3.1 collective-permute-start
  7.2 2.6 collective-permute-start.1
  11.1 4.0 %copy-done = f32[128,160,128]{2,1,0:T(8,128)S(1)} copy-done((f32[128,160,128]{2,1,0:T(8,128)S(1)}, f32[128,160,128]{2,1,0:T(8,128)}, u32[]{:S(2)}) %copy-start) | copy-done | bytes 10485784
  17.6 4.7 %collective-permute-done.refs_1_ = f32[8,128,128]{2,1,0:T(8,128)S(1)} collective-permute-done((f32[8,128,128]{2,1,0:T(8,128)}, f32[8,128,128]{2,1,0:T(8,128)S(1)}, u32[]{:S(2)}, u32[]{:S(2)}) %collective-permute-start) | collective-permute-done | bytes 524320 | tf_op jit(solution)/shard_map/ppermute | solution.py:351
  22.3 2.5 collective-permute-start.11
  27.0 17.8 %collective-permute-done.1.refs_2_ = f32[8,128,128]{2,1,0:T(8,128)S(1)} collective-permute-done((f32[8,128,128]{2,1,0:T(8,128)}, f32[8,128,128]{2,1,0:T(8,128)S(1)}, u32[]{:S(2)}, u32[]{:S(2)}) %collective-permute-start.1) | collective-permute-done | bytes 524320 | tf_op jit(solution)/shard_map/ppermute | solution.py:351
  44.9 34.3 %collective-permute-start.3 = (f32[8,128,128]{2,1,0:T(8,128)S(1)}, f32[8,128,128]{2,1,0:T(8,128)S(1)}, u32[]{:S(2)}, u32[]{:S(2)}) collective-permute-start(f32[8,128,128]{2,1,0:T(8,128)S(1)} %get-tuple-element.94), channel_id=1, source_target_pairs={{0,8},{8,16},{16,24},{24,0},{1,9},{9,17},{17,25},{25,1},{2,10},{10... | collective-permute-start | bytes 1572872 | tf_op jit(solution)/shard_map/ppermute | solution.py:351
  81.5 2.4 shard_map.33
  84.7 26.7 %collective-permute-done.10.refs_2_ = f32[8,128,128]{2,1,0:T(8,128)S(1)} collective-permute-done((f32[8,128,128]{2,1,0:T(8,128)S(1)}, f32[8,128,128]{2,1,0:T(8,128)S(1)}, u32[]{:S(2)}, u32[]{:S(2)}) %collective-permute-start.10) | collective-permute-done | bytes 524320 | tf_op jit(solution)/shard_map/ppermute | solution.py:351
  111.5 11.8 %collective-permute-start.12 = (f32[8,128,128]{2,1,0:T(8,128)S(1)}, f32[8,128,128]{2,1,0:T(8,128)S(1)}, u32[]{:S(2)}, u32[]{:S(2)}) collective-permute-start(f32[8,128,128]{2,1,0:T(8,128)S(1)} %get-tuple-element.110), channel_id=1, source_target_pairs={{0,8},{8,16},{16,24},{24,0},{1,9},{9,17},{17,25},{25,1},{2,10},{10... | collective-permute-start | bytes 1572872 | tf_op jit(solution)/shard_map/ppermute | solution.py:351
  123.3 2.7 collective-permute-start.13
  126.0 2.4 shard_map.30
  129.2 27.2 %collective-permute-done.4.refs_2_ = f32[8,128,128]{2,1,0:T(8,128)S(1)} collective-permute-done((f32[8,128,128]{2,1,0:T(8,128)S(1)}, f32[8,128,128]{2,1,0:T(8,128)S(1)}, u32[]{:S(2)}, u32[]{:S(2)}) %collective-permute-start.4) | collective-permute-done | bytes 524320 | tf_op jit(solution)/shard_map/ppermute | solution.py:351
  158.0 11.1 %collective-permute-start.6 = (f32[8,128,128]{2,1,0:T(8,128)}, f32[8,128,128]{2,1,0:T(8,128)}, u32[]{:S(2)}, u32[]{:S(2)}) collective-permute-start(f32[8,128,128]{2,1,0:T(8,128)} %get-tuple-element.98), channel_id=1, source_target_pairs={{0,8},{8,16},{16,24},{24,0},{1,9},{9,17},{17,25},{25,1},{2,10},{10... | collective-permute-start | bytes 1572872 | tf_op jit(solution)/shard_map/ppermute | solution.py:351
  169.1 3.4 collective-permute-start.7
  184.8 16.7 %collective-permute-done.13.refs_2_ = f32[8,128,128]{2,1,0:T(8,128)} collective-permute-done((f32[8,128,128]{2,1,0:T(8,128)}, f32[8,128,128]{2,1,0:T(8,128)}, u32[]{:S(2)}, u32[]{:S(2)}) %collective-permute-start.13) | collective-permute-done | bytes 524320 | tf_op jit(solution)/shard_map/ppermute | solution.py:351
  201.5 2.9 shard_map.38
  204.4 19.5 %collective-permute-done.7.refs_2_ = f32[8,128,128]{2,1,0:T(8,128)} collective-permute-done((f32[8,128,128]{2,1,0:T(8,128)}, f32[8,128,128]{2,1,0:T(8,128)}, u32[]{:S(2)}, u32[]{:S(2)}) %collective-permute-start.7) | collective-permute-done | bytes 524320 | tf_op jit(solution)/shard_map/ppermute | solution.py:351
  223.9 3.1 shard_map.39
  228.8 27.5 %all_to_all.10.parts_ref = f32[16,40,128]{2,1,0:T(8,128)S(1)} all-to-all(f32[16,40,128]{2,1,0:T(8,128)S(1)} %bitcast.6), channel_id=1, replica_groups=mesh['gx'=4,'gy'=2,'gu'=2,'gc'=2] {'gx','gy','gu'}, dimensions={0} | all-to-all | bytes 655360 | tf_op jit(solution)/shard_map/all_to_all | solution.py:377
  256.4 14.1 %all_to_all.11 = f32[16,40,128]{2,1,0:T(8,128)S(1)} all-to-all(f32[16,40,128]{2,1,0:T(8,128)S(1)} %shard_map.41), channel_id=1, replica_groups=mesh['gx'=4,'gy'=2,'gu'=2,'gc'=2] {'gx','gy','gu'}, dimensions={0} | all-to-all | bytes 655360 | tf_op jit(solution)/shard_map/all_to_all | solution.py:379
  272.1 17.5 %shard_map.42 = (f32[128,128]{1,0:T(8,128)}, f32[128,512]{1,0:T(8,128)S(1)}) custom-call(s32[1]{0:T(128)} %bitcast.me_ref, s32[1]{0:T(128)} %bitcast.1.core_ref, f32[640,128]{1,0:T(8,128)S(1)} %bitcast.5, f32[640,128]{1,0:T(8,128)S(1)} %collective-permute-done.16.other_ref), custom_call_target="tpu_custom_call" | custom-call | tf_op jit(solution)/shard_map/pallas_call | solution.py:256
  301.6 3.5 %collective-permute-done.21.refs_6_ = f32[32,8,128]{2,1,0:T(8,128)S(1)} collective-permute-done((f32[32,8,128]{2,1,0:T(8,128)S(1)}, f32[32,8,128]{2,1,0:T(8,128)S(1)}, u32[]{:S(2)}, u32[]{:S(2)}) %collective-permute-start.21) | collective-permute-done | bytes 131104 | tf_op jit(solution)/shard_map/ppermute | solution.py:351
  305.1 7.5 %collective-permute-start.24 = (f32[32,8,128]{2,1,0:T(8,128)S(1)}, f32[32,8,128]{2,1,0:T(8,128)S(1)}, u32[]{:S(2)}, u32[]{:S(2)}) collective-permute-start(f32[32,8,128]{2,1,0:T(8,128)S(1)} %get-tuple-element.138), channel_id=1, source_target_pairs={{0,16},{8,24},{16,0},{24,8},{1,17},{9,25},{17,1},{25,9},{2,18},{10... | collective-permute-start | bytes 393224 | tf_op jit(solution)/shard_map/ppermute | solution.py:351
  312.7 3.8 %collective-permute-start.25 = (f32[32,8,128]{2,1,0:T(8,128)S(1)}, f32[32,8,128]{2,1,0:T(8,128)S(1)}, u32[]{:S(2)}, u32[]{:S(2)}) collective-permute-start(f32[32,8,128]{2,1,0:T(8,128)S(1)} %get-tuple-element.139), channel_id=1, source_target_pairs={{0,24},{8,0},{16,8},{24,16},{1,25},{9,1},{17,9},{25,17},{2,26},{10... | collective-permute-start | bytes 393224 | tf_op jit(solution)/shard_map/ppermute | solution.py:351
  316.5 4.7 %collective-permute-done.18.refs_2_ = f32[32,8,128]{2,1,0:T(8,128)S(1)} collective-permute-done((f32[32,8,128]{2,1,0:T(8,128)S(1)}, f32[32,8,128]{2,1,0:T(8,128)S(1)}, u32[]{:S(2)}, u32[]{:S(2)}) %collective-permute-start.18) | collective-permute-done | bytes 131104 | tf_op jit(solution)/shard_map/ppermute | solution.py:351
  322.4 3.5 collective-permute-start.30
  327.0 5.5 %collective-permute-done.24.refs_10_ = f32[32,8,128]{2,1,0:T(8,128)S(1)} collective-permute-done((f32[32,8,128]{2,1,0:T(8,128)S(1)}, f32[32,8,128]{2,1,0:T(8,128)S(1)}, u32[]{:S(2)}, u32[]{:S(2)}) %collective-permute-start.24) | collective-permute-done | bytes 131104 | tf_op jit(solution)/shard_map/ppermute | solution.py:351
  332.7 3.5 %collective-permute-start.27 = (f32[32,8,128]{2,1,0:T(8,128)S(1)}, f32[32,8,128]{2,1,0:T(8,128)S(1)}, u32[]{:S(2)}, u32[]{:S(2)}) collective-permute-start(f32[32,8,128]{2,1,0:T(8,128)S(1)} %get-tuple-element.148), channel_id=1, source_target_pairs={{0,16},{8,24},{16,0},{24,8},{1,17},{9,25},{17,1},{25,9},{2,18},{10... | collective-permute-start | bytes 393224 | tf_op jit(solution)/shard_map/ppermute | solution.py:351
  338.2 5.5 %collective-permute-done.30.refs_18_ = f32[32,8,128]{2,1,0:T(8,128)S(1)} collective-permute-done((f32[32,8,128]{2,1,0:T(8,128)S(1)}, f32[32,8,128]{2,1,0:T(8,128)S(1)}, u32[]{:S(2)}, u32[]{:S(2)}) %collective-permute-start.30) | collective-permute-done | bytes 131104 | tf_op jit(solution)/shard_map/ppermute | solution.py:351
  343.7 5.6 %collective-permute-done.27.refs_14_ = f32[32,8,128]{2,1,0:T(8,128)S(1)} collective-permute-done((f32[32,8,128]{2,1,0:T(8,128)S(1)}, f32[32,8,128]{2,1,0:T(8,128)S(1)}, u32[]{:S(2)}, u32[]{:S(2)}) %collective-permute-start.27) | collective-permute-done | bytes 131104 | tf_op jit(solution)/shard_map/ppermute | solution.py:351
  (93 shorter events, 45.4 us)
Async XLA Ops:
  4.1 18.2 %collective-permute-start = (f32[8,128,128]{2,1,0:T(8,128)}, f32[8,128,128]{2,1,0:T(8,128)S(1)}, u32[]{:S(2)}, u32[]{:S(2)}) collective-permute-start(f32[8,128,128]{2,1,0:T(8,128)} %get-tuple-element.90), channel_id=1, source_target_pairs={{0,8},{8,16},{16,24},{24,0},{1,9},{9,17},{17,25},{25,1},{2,10},{10... | collective-permute-start | bytes 1572872 | tf_op jit(solution)/shard_map/ppermute | solution.py:351
  7.2 37.6 %collective-permute-start.1 = (f32[8,128,128]{2,1,0:T(8,128)}, f32[8,128,128]{2,1,0:T(8,128)S(1)}, u32[]{:S(2)}, u32[]{:S(2)}) collective-permute-start(f32[8,128,128]{2,1,0:T(8,128)} %get-tuple-element.91), channel_id=1, source_target_pairs={{0,16},{8,24},{16,0},{24,8},{1,17},{9,25},{17,1},{25,9},{2,18},{10... | collective-permute-start | bytes 1572872 | tf_op jit(solution)/shard_map/ppermute | solution.py:351
  9.8 35.1 %collective-permute-start.2 = (f32[8,128,128]{2,1,0:T(8,128)}, f32[8,128,128]{2,1,0:T(8,128)S(1)}, u32[]{:S(2)}, u32[]{:S(2)}) collective-permute-start(f32[8,128,128]{2,1,0:T(8,128)} %get-tuple-element.92), channel_id=1, source_target_pairs={{0,24},{8,0},{16,8},{24,16},{1,25},{9,1},{17,9},{25,17},{2,26},{10... | collective-permute-start | bytes 1572872 | tf_op jit(solution)/shard_map/ppermute | solution.py:351
  16.6 64.3 %collective-permute-start.9 = (f32[8,128,128]{2,1,0:T(8,128)S(1)}, f32[8,128,128]{2,1,0:T(8,128)S(1)}, u32[]{:S(2)}, u32[]{:S(2)}) collective-permute-start(f32[8,128,128]{2,1,0:T(8,128)S(1)} %get-tuple-element.106), channel_id=1, source_target_pairs={{0,8},{8,16},{16,24},{24,0},{1,9},{9,17},{17,25},{25,1},{2,10},{10... | collective-permute-start | bytes 1572872 | tf_op jit(solution)/shard_map/ppermute | solution.py:351
  17.3 94.2 %collective-permute-start.10 = (f32[8,128,128]{2,1,0:T(8,128)S(1)}, f32[8,128,128]{2,1,0:T(8,128)S(1)}, u32[]{:S(2)}, u32[]{:S(2)}) collective-permute-start(f32[8,128,128]{2,1,0:T(8,128)S(1)} %get-tuple-element.107), channel_id=1, source_target_pairs={{0,16},{8,24},{16,0},{24,8},{1,17},{9,25},{17,1},{25,9},{2,18},{10... | collective-permute-start | bytes 1572872 | tf_op jit(solution)/shard_map/ppermute | solution.py:351
  22.3 89.1 %collective-permute-start.11 = (f32[8,128,128]{2,1,0:T(8,128)S(1)}, f32[8,128,128]{2,1,0:T(8,128)S(1)}, u32[]{:S(2)}, u32[]{:S(2)}) collective-permute-start(f32[8,128,128]{2,1,0:T(8,128)S(1)} %get-tuple-element.108), channel_id=1, source_target_pairs={{0,24},{8,0},{16,8},{24,16},{1,25},{9,1},{17,9},{25,17},{2,26},{10... | collective-permute-start | bytes 1572872 | tf_op jit(solution)/shard_map/ppermute | solution.py:351
  44.9 81.1 %collective-permute-start.3 = (f32[8,128,128]{2,1,0:T(8,128)S(1)}, f32[8,128,128]{2,1,0:T(8,128)S(1)}, u32[]{:S(2)}, u32[]{:S(2)}) collective-permute-start(f32[8,128,128]{2,1,0:T(8,128)S(1)} %get-tuple-element.94), channel_id=1, source_target_pairs={{0,8},{8,16},{16,24},{24,0},{1,9},{9,17},{17,25},{25,1},{2,10},{10... | collective-permute-start | bytes 1572872 | tf_op jit(solution)/shard_map/ppermute | solution.py:351
  79.1 77.3 %collective-permute-start.4 = (f32[8,128,128]{2,1,0:T(8,128)S(1)}, f32[8,128,128]{2,1,0:T(8,128)S(1)}, u32[]{:S(2)}, u32[]{:S(2)}) collective-permute-start(f32[8,128,128]{2,1,0:T(8,128)S(1)} %get-tuple-element.95), channel_id=1, source_target_pairs={{0,16},{8,24},{16,0},{24,8},{1,17},{9,25},{17,1},{25,9},{2,18},{10... | collective-permute-start | bytes 1572872 | tf_op jit(solution)/shard_map/ppermute | solution.py:351
  80.9 76.3 %collective-permute-start.5 = (f32[8,128,128]{2,1,0:T(8,128)S(1)}, f32[8,128,128]{2,1,0:T(8,128)S(1)}, u32[]{:S(2)}, u32[]{:S(2)}) collective-permute-start(f32[8,128,128]{2,1,0:T(8,128)S(1)} %get-tuple-element.96), channel_id=1, source_target_pairs={{0,24},{8,0},{16,8},{24,16},{1,25},{9,1},{17,9},{25,17},{2,26},{10... | collective-permute-start | bytes 1572872 | tf_op jit(solution)/shard_map/ppermute | solution.py:351
  111.5 61.0 %collective-permute-start.12 = (f32[8,128,128]{2,1,0:T(8,128)S(1)}, f32[8,128,128]{2,1,0:T(8,128)S(1)}, u32[]{:S(2)}, u32[]{:S(2)}) collective-permute-start(f32[8,128,128]{2,1,0:T(8,128)S(1)} %get-tuple-element.110), channel_id=1, source_target_pairs={{0,8},{8,16},{16,24},{24,0},{1,9},{9,17},{17,25},{25,1},{2,10},{10... | collective-permute-start | bytes 1572872 | tf_op jit(solution)/shard_map/ppermute | solution.py:351
  123.3 78.2 %collective-permute-start.13 = (f32[8,128,128]{2,1,0:T(8,128)}, f32[8,128,128]{2,1,0:T(8,128)}, u32[]{:S(2)}, u32[]{:S(2)}) collective-permute-start(f32[8,128,128]{2,1,0:T(8,128)} %get-tuple-element.111), channel_id=1, source_target_pairs={{0,16},{8,24},{16,0},{24,8},{1,17},{9,25},{17,1},{25,9},{2,18},{10... | collective-permute-start | bytes 1572872 | tf_op jit(solution)/shard_map/ppermute | solution.py:351
  126.0 75.5 %collective-permute-start.14 = (f32[8,128,128]{2,1,0:T(8,128)}, f32[8,128,128]{2,1,0:T(8,128)}, u32[]{:S(2)}, u32[]{:S(2)}) collective-permute-start(f32[8,128,128]{2,1,0:T(8,128)} %get-tuple-element.112), channel_id=1, source_target_pairs={{0,24},{8,0},{16,8},{24,16},{1,25},{9,1},{17,9},{25,17},{2,26},{10... | collective-permute-start | bytes 1572872 | tf_op jit(solution)/shard_map/ppermute | solution.py:351
  158.0 46.4 %collective-permute-start.6 = (f32[8,128,128]{2,1,0:T(8,128)}, f32[8,128,128]{2,1,0:T(8,128)}, u32[]{:S(2)}, u32[]{:S(2)}) collective-permute-start(f32[8,128,128]{2,1,0:T(8,128)} %get-tuple-element.98), channel_id=1, source_target_pairs={{0,8},{8,16},{16,24},{24,0},{1,9},{9,17},{17,25},{25,1},{2,10},{10... | collective-permute-start | bytes 1572872 | tf_op jit(solution)/shard_map/ppermute | solution.py:351
  169.1 54.8 %collective-permute-start.7 = (f32[8,128,128]{2,1,0:T(8,128)}, f32[8,128,128]{2,1,0:T(8,128)}, u32[]{:S(2)}, u32[]{:S(2)}) collective-permute-start(f32[8,128,128]{2,1,0:T(8,128)} %get-tuple-element.99), channel_id=1, source_target_pairs={{0,16},{8,24},{16,0},{24,8},{1,17},{9,25},{17,1},{25,9},{2,18},{10... | collective-permute-start | bytes 1572872 | tf_op jit(solution)/shard_map/ppermute | solution.py:351
  173.3 50.7 %collective-permute-start.8 = (f32[8,128,128]{2,1,0:T(8,128)}, f32[8,128,128]{2,1,0:T(8,128)}, u32[]{:S(2)}, u32[]{:S(2)}) collective-permute-start(f32[8,128,128]{2,1,0:T(8,128)} %get-tuple-element.100), channel_id=1, source_target_pairs={{0,24},{8,0},{16,8},{24,16},{1,25},{9,1},{17,9},{25,17},{2,26},{10... | collective-permute-start | bytes 1572872 | tf_op jit(solution)/shard_map/ppermute | solution.py:351
  227.0 1.7 collective-permute-start.15
  270.5 1.6 collective-permute-start.16
  291.1 8.3 %collective-permute-start.20 = (f32[32,8,128]{2,1,0:T(8,128)S(1)}, f32[32,8,128]{2,1,0:T(8,128)S(1)}, u32[]{:S(2)}, u32[]{:S(2)}) collective-permute-start(f32[32,8,128]{2,1,0:T(8,128)S(1)} %get-tuple-element.131), channel_id=1, source_target_pairs={{0,8},{8,16},{16,24},{24,0},{1,9},{9,17},{17,25},{25,1},{2,10},{10... | collective-permute-start | bytes 393224 | tf_op jit(solution)/shard_map/ppermute | solution.py:351
  292.2 12.9 %collective-permute-start.21 = (f32[32,8,128]{2,1,0:T(8,128)S(1)}, f32[32,8,128]{2,1,0:T(8,128)S(1)}, u32[]{:S(2)}, u32[]{:S(2)}) collective-permute-start(f32[32,8,128]{2,1,0:T(8,128)S(1)} %get-tuple-element.132), channel_id=1, source_target_pairs={{0,16},{8,24},{16,0},{24,8},{1,17},{9,25},{17,1},{25,9},{2,18},{10... | collective-permute-start | bytes 393224 | tf_op jit(solution)/shard_map/ppermute | solution.py:351
  293.4 11.7 %collective-permute-start.22 = (f32[32,8,128]{2,1,0:T(8,128)S(1)}, f32[32,8,128]{2,1,0:T(8,128)S(1)}, u32[]{:S(2)}, u32[]{:S(2)}) collective-permute-start(f32[32,8,128]{2,1,0:T(8,128)S(1)} %get-tuple-element.133), channel_id=1, source_target_pairs={{0,24},{8,0},{16,8},{24,16},{1,25},{9,1},{17,9},{25,17},{2,26},{10... | collective-permute-start | bytes 393224 | tf_op jit(solution)/shard_map/ppermute | solution.py:351
  295.0 17.6 %collective-permute-start.17 = (f32[32,8,128]{2,1,0:T(8,128)S(1)}, f32[32,8,128]{2,1,0:T(8,128)S(1)}, u32[]{:S(2)}, u32[]{:S(2)}) collective-permute-start(f32[32,8,128]{2,1,0:T(8,128)S(1)} %get-tuple-element.124), channel_id=1, source_target_pairs={{0,8},{8,16},{16,24},{24,0},{1,9},{9,17},{17,25},{25,1},{2,10},{10... | collective-permute-start | bytes 393224 | tf_op jit(solution)/shard_map/ppermute | solution.py:351
  295.6 25.6 %collective-permute-start.18 = (f32[32,8,128]{2,1,0:T(8,128)S(1)}, f32[32,8,128]{2,1,0:T(8,128)S(1)}, u32[]{:S(2)}, u32[]{:S(2)}) collective-permute-start(f32[32,8,128]{2,1,0:T(8,128)S(1)} %get-tuple-element.125), channel_id=1, source_target_pairs={{0,16},{8,24},{16,0},{24,8},{1,17},{9,25},{17,1},{25,9},{2,18},{10... | collective-permute-start | bytes 393224 | tf_op jit(solution)/shard_map/ppermute | solution.py:351
  299.5 22.9 %collective-permute-start.19 = (f32[32,8,128]{2,1,0:T(8,128)S(1)}, f32[32,8,128]{2,1,0:T(8,128)S(1)}, u32[]{:S(2)}, u32[]{:S(2)}) collective-permute-start(f32[32,8,128]{2,1,0:T(8,128)S(1)} %get-tuple-element.126), channel_id=1, source_target_pairs={{0,24},{8,0},{16,8},{24,16},{1,25},{9,1},{17,9},{25,17},{2,26},{10... | collective-permute-start | bytes 393224 | tf_op jit(solution)/shard_map/ppermute | solution.py:351
  305.1 20.7 %collective-permute-start.23 = (f32[32,8,128]{2,1,0:T(8,128)S(1)}, f32[32,8,128]{2,1,0:T(8,128)S(1)}, u32[]{:S(2)}, u32[]{:S(2)}) collective-permute-start(f32[32,8,128]{2,1,0:T(8,128)S(1)} %get-tuple-element.137), channel_id=1, source_target_pairs={{0,8},{8,16},{16,24},{24,0},{1,9},{9,17},{17,25},{25,1},{2,10},{10... | collective-permute-start | bytes 393224 | tf_op jit(solution)/shard_map/ppermute | solution.py:351
  305.1 27.3 %collective-permute-start.24 = (f32[32,8,128]{2,1,0:T(8,128)S(1)}, f32[32,8,128]{2,1,0:T(8,128)S(1)}, u32[]{:S(2)}, u32[]{:S(2)}) collective-permute-start(f32[32,8,128]{2,1,0:T(8,128)S(1)} %get-tuple-element.138), channel_id=1, source_target_pairs={{0,16},{8,24},{16,0},{24,8},{1,17},{9,25},{17,1},{25,9},{2,18},{10... | collective-permute-start | bytes 393224 | tf_op jit(solution)/shard_map/ppermute | solution.py:351
  312.7 20.1 %collective-permute-start.25 = (f32[32,8,128]{2,1,0:T(8,128)S(1)}, f32[32,8,128]{2,1,0:T(8,128)S(1)}, u32[]{:S(2)}, u32[]{:S(2)}) collective-permute-start(f32[32,8,128]{2,1,0:T(8,128)S(1)} %get-tuple-element.139), channel_id=1, source_target_pairs={{0,24},{8,0},{16,8},{24,16},{1,25},{9,1},{17,9},{25,17},{2,26},{10... | collective-permute-start | bytes 393224 | tf_op jit(solution)/shard_map/ppermute | solution.py:351
  321.2 15.0 %collective-permute-start.29 = (f32[32,8,128]{2,1,0:T(8,128)S(1)}, f32[32,8,128]{2,1,0:T(8,128)S(1)}, u32[]{:S(2)}, u32[]{:S(2)}) collective-permute-start(f32[32,8,128]{2,1,0:T(8,128)S(1)} %get-tuple-element.157), channel_id=1, source_target_pairs={{0,8},{8,16},{16,24},{24,0},{1,9},{9,17},{17,25},{25,1},{2,10},{10... | collective-permute-start | bytes 393224 | tf_op jit(solution)/shard_map/ppermute | solution.py:351
  322.4 21.3 %collective-permute-start.30 = (f32[32,8,128]{2,1,0:T(8,128)S(1)}, f32[32,8,128]{2,1,0:T(8,128)S(1)}, u32[]{:S(2)}, u32[]{:S(2)}) collective-permute-start(f32[32,8,128]{2,1,0:T(8,128)S(1)} %get-tuple-element.158), channel_id=1, source_target_pairs={{0,16},{8,24},{16,0},{24,8},{1,17},{9,25},{17,1},{25,9},{2,18},{10... | collective-permute-start | bytes 393224 | tf_op jit(solution)/shard_map/ppermute | solution.py:351
  325.8 17.9 %collective-permute-start.31 = (f32[32,8,128]{2,1,0:T(8,128)S(1)}, f32[32,8,128]{2,1,0:T(8,128)S(1)}, u32[]{:S(2)}, u32[]{:S(2)}) collective-permute-start(f32[32,8,128]{2,1,0:T(8,128)S(1)} %get-tuple-element.159), channel_id=1, source_target_pairs={{0,24},{8,0},{16,8},{24,16},{1,25},{9,1},{17,9},{25,17},{2,26},{10... | collective-permute-start | bytes 393224 | tf_op jit(solution)/shard_map/ppermute | solution.py:351
  332.5 11.3 %collective-permute-start.26 = (f32[32,8,128]{2,1,0:T(8,128)S(1)}, f32[32,8,128]{2,1,0:T(8,128)S(1)}, u32[]{:S(2)}, u32[]{:S(2)}) collective-permute-start(f32[32,8,128]{2,1,0:T(8,128)S(1)} %get-tuple-element.147), channel_id=1, source_target_pairs={{0,8},{8,16},{16,24},{24,0},{1,9},{9,17},{17,25},{25,1},{2,10},{10... | collective-permute-start | bytes 393224 | tf_op jit(solution)/shard_map/ppermute | solution.py:351
  332.7 16.6 %collective-permute-start.27 = (f32[32,8,128]{2,1,0:T(8,128)S(1)}, f32[32,8,128]{2,1,0:T(8,128)S(1)}, u32[]{:S(2)}, u32[]{:S(2)}) collective-permute-start(f32[32,8,128]{2,1,0:T(8,128)S(1)} %get-tuple-element.148), channel_id=1, source_target_pairs={{0,16},{8,24},{16,0},{24,8},{1,17},{9,25},{17,1},{25,9},{2,18},{10... | collective-permute-start | bytes 393224 | tf_op jit(solution)/shard_map/ppermute | solution.py:351
  336.2 13.1 %collective-permute-start.28 = (f32[32,8,128]{2,1,0:T(8,128)S(1)}, f32[32,8,128]{2,1,0:T(8,128)S(1)}, u32[]{:S(2)}, u32[]{:S(2)}) collective-permute-start(f32[32,8,128]{2,1,0:T(8,128)S(1)} %get-tuple-element.149), channel_id=1, source_target_pairs={{0,24},{8,0},{16,8},{24,16},{1,25},{9,1},{17,9},{25,17},{2,26},{10... | collective-permute-start | bytes 393224 | tf_op jit(solution)/shard_map/ppermute | solution.py:351
  (20 other events, 343.6 us)
